TPU v7x, 32 devices: a whole 2x2x4 slice. The times are simulated.
32 devices in a mesh: fsdp: 16 (over z, y, core), blk: 2 (over x).
Axes of the slice: x: 2, y: 2, z: 4, core: 2. Of those that a mesh axis runs over, the one named last changes fastest.
Arguments:
- x_resp: bfloat16 [16, 256, 5120], P('fsdp', 'blk'), may hold values from -6 to 6
- queries: bfloat16 [16, 256, 4096], P('fsdp', 'blk'), may hold values from -12 to 12
- prompt_cache: bfloat16 [16, 1024, 1024], P('fsdp', 'blk'), may hold values from -6 to 6
- kv_weight: bfloat16 [5120, 1024], P('fsdp'), may hold values from -0.078125 to 0.078125
- key_gain: float32 [128], replicated, may hold values from 0.1 to 1.9
- prompt_lengths: int32 [16], P('fsdp'), may hold values from 512 to 1024, as said below
- block_table: int32 [16, 4, 2], P('fsdp', 'blk'), may hold values from 0 to 1
- resp_lengths: int32 [16, 4], P('fsdp', 'blk'), may hold values from 16 to 64, as said below
Outputs:
- context: bfloat16 [16, 256, 4096], P('fsdp', 'blk')
Inputs may be any that keep to these rules, and one draw needn't show every extreme that they name: `prompt_lengths`: the first group's prompt has 1024 tokens. `resp_lengths`: the first response of every group has 64 tokens.
All inputs are finite; a program needn't handle non-finite values.
Results may differ from a plain program's by a relative error of at most 0.0039.
Values may be sent and summed in bfloat16 or wider, within the bound.
No kernel may reach another device: no remote copies, remote signals or barrier semaphores. Data moves between devices by JAX's collectives and lax.ppermute only.
A program may use at most 192 MiB of HBM per device.

v0:
```python
import jax
import jax.numpy as jnp
from jax import lax
from jax.sharding import PartitionSpec as P

HQ = 32
KVH = 4
HD = 128
BLOCK = 512
RESP_DEV = 2
RLEN = 64


def passed_along(shard, axis, by):
    count = lax.axis_size(axis)
    return lax.ppermute(shard, axis, [(i, (i + by) % count) for i in range(count)])


def per_device(
    x_resp, queries, prompt_cache, kv_weight, key_gain, prompt_lengths, block_table, resp_lengths
):
    row_count = x_resp.shape[1]
    local_x = x_resp[0]
    heads_shared = HQ // KVH
    score_scale = HD ** (-0.5)
    projected = jnp.dot(
        local_x,
        lax.all_gather(kv_weight, "fsdp", axis=0, tiled=True),
        preferred_element_type=jnp.float32,
    )
    keys_raw = projected[:, : KVH * HD].reshape(row_count, KVH, HD)
    scaled = keys_raw * lax.rsqrt(jnp.mean(keys_raw * keys_raw, axis=-1, keepdims=True) + 1e-06)
    own_keys = (scaled * key_gain).astype(jnp.bfloat16)
    own_values = projected[:, KVH * HD :].reshape(row_count, KVH, HD).astype(jnp.bfloat16)
    query = queries[0].reshape(row_count, KVH, heads_shared, HD)
    lengths = resp_lengths[0]
    owner_of = jnp.arange(row_count) // RLEN
    slot_of = jnp.arange(row_count) % RLEN
    pick_len = (owner_of[:, None] == jnp.arange(RESP_DEV)[None, :]).astype(jnp.int32)
    row_len = jnp.sum(pick_len * lengths[None, :], axis=1)
    own_mask = (
        (owner_of[:, None] == owner_of[None, :])
        & (slot_of[None, :] <= slot_of[:, None])
        & (slot_of[None, :] < row_len[:, None])
    )
    scores = (
        jnp.einsum("rkgd,skd->kgrs", query, own_keys, preferred_element_type=jnp.float32)
        * score_scale
    )
    scores = jnp.where(own_mask[None, None], scores, -jnp.inf)
    running_max = jnp.max(scores, axis=-1)
    weights = jnp.exp(scores - running_max[..., None])
    running_sum = jnp.sum(weights, axis=-1)
    context_sum = jnp.einsum(
        "kgrs,skd->kgrd",
        weights.astype(jnp.bfloat16),
        own_values,
        preferred_element_type=jnp.float32,
    )
    state = (running_max, running_sum, context_sum)
    table = block_table[0].astype(jnp.float32)
    limit = prompt_lengths[0]
    own_cache = prompt_cache[0]
    span_rows = own_cache.shape[0]
    cycle_size = lax.axis_size("blk")
    holder = lax.axis_index("blk")
    current_cache = own_cache
    for stride in range(cycle_size):
        place_count = current_cache.shape[0]
        places = (holder - stride) % cycle_size * span_rows + jnp.arange(place_count)
        onehot = ((places // BLOCK)[None, :] == jnp.arange(table.shape[1])[:, None]).astype(
            jnp.float32
        )
        listed = jnp.dot(table, onehot) > 0.5
        allowed = listed & (places < limit)[None, :]
        row_allowed = jnp.broadcast_to(allowed[:, None, :], (RESP_DEV, RLEN, place_count)).reshape(
            row_count, place_count
        )
        old_max, old_sum, old_context = state
        cache_keys = current_cache[:, : KVH * HD].reshape(place_count, KVH, HD)
        cache_values = current_cache[:, KVH * HD :].reshape(place_count, KVH, HD)
        block_scores = (
            jnp.einsum("rkgd,skd->kgrs", query, cache_keys, preferred_element_type=jnp.float32)
            * score_scale
        )
        block_scores = jnp.where(row_allowed[None, None], block_scores, -jnp.inf)
        new_max = jnp.maximum(old_max, jnp.max(block_scores, axis=-1))
        faded = jnp.exp(old_max - new_max)
        block_weights = jnp.exp(block_scores - new_max[..., None])
        new_sum = old_sum * faded + jnp.sum(block_weights, axis=-1)
        new_context = old_context * faded[..., None] + jnp.einsum(
            "kgrs,skd->kgrd",
            block_weights.astype(jnp.bfloat16),
            cache_values,
            preferred_element_type=jnp.float32,
        )
        state = (new_max, new_sum, new_context)
        if stride + 1 < cycle_size:
            current_cache = passed_along(current_cache, "blk", 1)
    final_max, final_sum, final_context = state
    result = final_context / final_sum[..., None]
    result = jnp.transpose(result, (2, 0, 1, 3)).reshape(row_count, HQ * HD)
    live = (slot_of < row_len).astype(jnp.float32)
    return (result * live[:, None]).astype(jnp.bfloat16)[None]


def solution(mesh):
    return jax.shard_map(
        per_device,
        mesh=mesh,
        in_specs=(
            P("fsdp", "blk", None),
            P("fsdp", "blk", None),
            P("fsdp", "blk", None),
            P("fsdp", None),
            P(),
            P("fsdp"),
            P("fsdp", "blk", None),
            P("fsdp", "blk"),
        ),
        out_specs=P("fsdp", "blk", None),
        check_vma=False,
    )
```

profile of v0, /device:TPU:0, one launch (start us, length us, event | category | flops | bytes accessed | tf_op | source)
XLA Modules:
  0.0 132.8 jit_solution(17319009619594090459)
XLA Ops:
  6.5 0.7 all-gather.2.cloned.1.call-update
  7.3 1.5 %copy.71 = bf16[1,512,1024]{1,2,0:T(8,128)(2,1)S(1)} copy(bf16[1,512,1024]{2,1,0:T(8,128)(2,1)} %param.10) | data formatting | bytes 2097152 | tf_op args[2]
  8.8 3.0 %collective-permute-start = (bf16[512,1024]{0,1:T(8,128)(2,1)S(1)}, bf16[512,1024]{0,1:T(8,128)(2,1)}, u32[]{:S(2)}, u32[]{:S(2)}) collective-permute-start(bf16[512,1024]{0,1:T(8,128)(2,1)S(1)} %bitcast.132), channel_id=1, source_target_pairs={{0,1},{1,0},{2,3},{3,2},{4,5},{5,4},{6,7},{7,6},{8,9},{9,8},{10,11... | collective-permute-start | bytes 3145736 | tf_op jit(solution)/shard_map/ppermute | solution.py:16
  12.5 0.7 fusion.57
  13.2 0.8 fusion.27
  14.0 0.8 fusion.29
  14.8 0.5 compare_convert_fusion
  15.8 1.4 %copy.96 = bf16[16,8,32,128]{3,2,1,0:T(8,128)(2,1)S(1)} copy(bf16[16,8,32,128]{3,1,2,0:T(8,128)(2,1)} %bitcast.137) | data formatting | bytes 2097152
  17.2 0.7 compare_and_fusion
  17.9 0.9 fusion.66
  18.8 5.1 %fusion.4 = (f32[4,8,128]{2,1,0:T(8,128)S(1)}, f32[4,512,128,8]{2,1,3,0:T(8,128)}) fusion(pred[128,512]{0,1:T(8,128)(4,1)S(1)} %copy.70, bf16[512,4,128,1]{0,2,3,1:T(8,128)(2,1)S(1)} %bitcast.135, bf16[128,4,8,128]{3,2,1,0:T(8,128)(2,1)S(1)} %bitcast.129), kind=kOutput, calls=%fused_computation.8 | convolution fusion | flops 543158272 | bytes 10043392 | tf_op jit(solution)/shard_map/rkgd,skd->kgrs/dot_general | solution.py:83
  23.8 11.2 %collective-permute-done = bf16[512,1024]{0,1:T(8,128)(2,1)} collective-permute-done((bf16[512,1024]{0,1:T(8,128)(2,1)S(1)}, bf16[512,1024]{0,1:T(8,128)(2,1)}, u32[]{:S(2)}, u32[]{:S(2)}) %collective-permute-start) | collective-permute-done | bytes 1048608 | tf_op jit(solution)/shard_map/ppermute | solution.py:16
  35.0 2.1 %fusion.65 = (bf16[512,512]{0,1:T(8,128)(2,1)}, bf16[512,512]{0,1:T(8,128)(2,1)S(1)}) fusion(bf16[512,1024]{0,1:T(8,128)(2,1)} %collective-permute-done), kind=kLoop, calls=%fused_computation.101 | loop fusion | bytes 2097152 | tf_op jit(solution)/shard_map/slice | solution.py:81
  37.1 5.8 %fusion.5 = (f32[4,8,128]{2,1,0:T(8,128)}, f32[4,512,128,8]{2,1,3,0:T(8,128)}) fusion(pred[128,512]{0,1:T(8,128)(4,1)S(1)} %copy.75, bf16[512,4,128,1]{0,2,3,1:T(8,128)(2,1)S(1)} %bitcast.134, bf16[128,4,8,128]{3,2,1,0:T(8,128)(2,1)S(1)} %bitcast.130), kind=kOutput, calls=%fused_computation.9 | convolution fusion | flops 543158272 | bytes 10043392 | tf_op jit(solution)/shard_map/rkgd,skd->kgrs/dot_general | solution.py:83
  42.9 57.4 %all-gather.2.cloned.1.call-done = bf16[5120,1024]{1,0:T(8,128)(2,1)} async-done(((bf16[320,1024]{1,0:T(8,128)(2,1)}), bf16[5120,1024]{1,0:T(8,128)(2,1)}) %all-gather.2.cloned.1.call-update) | async-done | bytes 10485776 | tf_op jit(solution)/shard_map/all_gather | solution.py:28
  100.3 5.5 %fusion.24 = f32[128,1024]{1,0:T(8,128)S(1)} fusion(bf16[5120,1024]{1,0:T(8,128)(2,1)} %all-gather.2.cloned.1.call-done, bf16[1,128,5120]{2,1,0:T(8,128)(2,1)S(1)} %copy-done), kind=kOutput, calls=%fused_computation.30 | convolution fusion | flops 1342177280 | bytes 12320768 | tf_op jit(solution)/shard_map/dot_general | solution.py:26
  106.5 1.5 %fusion.67 = (f32[4,8,128]{2,1,0:T(8,128)S(1)}, f32[4,8,128,128]{2,3,1,0:T(8,128)S(1)}) fusion(bf16[128,4,8,128]{3,2,1,0:T(8,128)(2,1)S(1)} %bitcast.131, bf16[128,4,128,1]{2,1,0,3:T(4,128)(2,1)S(1)} %fusion.38, pred[128,128]{0,1:T(8,128)(4,1)} %compare_and_fusion), kind=kOutput, calls=%fused_computation.103 | convolution fusion | flops 135786496 | bytes 3309568 | tf_op jit(solution)/shard_map/rkgd,skd->kgrs/dot_general | solution.py:47
  108.9 0.9 fusion.64
  109.9 5.2 %fusion = f32[4,8,128]{2,1,0:T(8,128)S(1)} fusion(f32[4,512,128,8]{2,1,3,0:T(8,128)} %get-tuple-element.19, f32[4,8,128]{2,1,0:T(8,128)S(1)} %get-tuple-element.9, pred[128,512]{0,1:T(8,128)(4,1)S(1)} %copy.70), kind=kLoop, calls=%fused_computation.4 | loop fusion | flops 8384512 | bytes 8486912 | tf_op jit(solution)/shard_map/reduce_sum | solution.py:90
  115.1 2.1 %fusion.8 = f32[4,8,128,128]{2,3,1,0:T(8,128)S(1)} fusion(bf16[512,4,128,1]{0,2,3,1:T(8,128)(2,1)S(1)} %bitcast.140, f32[4,512,128,8]{2,1,3,0:T(8,128)S(1)} %bitcast.128, f32[4,8,128]{2,1,0:T(8,128)S(1)} %get-tuple-element.9, pred[128,512]{0,1:T(8,128)(4,1)S(1)} %copy.70), kind=kOutput, calls=%fused_computation.11 | convolution fusion | flops 545259520 | bytes 11091968 | tf_op jit(solution)/shard_map/kgrs,skd->kgrd/dot_general | solution.py:91
  117.3 2.0 %fusion.2 = f32[4,8,128]{2,1,0:T(8,128)S(1)} fusion(f32[4,512,128,8]{2,1,3,0:T(8,128)S(1)} %bitcast.126, f32[4,8,128]{2,1,0:T(8,128)S(1)} %get-tuple-element.8, pred[128,512]{0,1:T(8,128)(4,1)S(1)} %copy.75), kind=kLoop, calls=%fused_computation.6 | loop fusion | flops 8384512 | bytes 8486912 | tf_op jit(solution)/shard_map/reduce_sum | solution.py:90
  119.4 3.5 %fusion.18 = f32[128,4,8,128]{0,3,2,1:T(8,128)} fusion(f32[4,8,128,128]{2,3,1,0:T(8,128)S(1)} %fusion.8, f32[4,8,128,128]{2,3,1,0:T(8,128)S(1)} %fusion.30, bf16[512,4,128,1]{0,2,3,1:T(8,128)(2,1)S(1)} %bitcast.139, f32[4,512,128,8]{2,1,3,0:T(8,128)S(1)} %bitcast.126, f32[4,8,128]{2,1,0:T(8,128)S(1)} %get-tuple-element.8, pred[128,512]{0,1:T(8,128)(4,1)S(1)} %copy.75, ...), kind=kOutput, calls=%fused_computation.21 | convolution fusion | flops 547880960 | bytes 15335424 | tf_op jit(solution)/shard_map/kgrs,skd->kgrd/dot_general | solution.py:91
  122.8 1.9 %copy.79 = f32[1,128,4096]{2,1,0:T(8,128)S(1)} copy(f32[1,128,4096]{1,2,0:T(8,128)} %bitcast.136) | data formatting | bytes 4194304 | tf_op jit(solution)/shard_map/reshape | solution.py:102
  124.8 1.2 multiply_convert_fusion
  (41 shorter events, 2.1 us)
Async XLA Ops:
  6.5 93.7 %copy-start = (bf16[1,128,5120]{2,1,0:T(8,128)(2,1)S(1)}, bf16[1,128,5120]{2,1,0:T(8,128)(2,1)}, u32[]{:S(2)}) copy-start(bf16[1,128,5120]{2,1,0:T(8,128)(2,1)} %param.8) | copy-start | bytes 3932164
  6.5 93.7 %all-gather.2.cloned.1.call-start = ((), (), s32[]{:S(2)}) async-start(), calls=%async_computation | async-start | bytes 11141120 | tf_op jit(solution)/shard_map/all_gather | solution.py:28
  8.8 26.3 %collective-permute-start = (bf16[512,1024]{0,1:T(8,128)(2,1)S(1)}, bf16[512,1024]{0,1:T(8,128)(2,1)}, u32[]{:S(2)}, u32[]{:S(2)}) collective-permute-start(bf16[512,1024]{0,1:T(8,128)(2,1)S(1)} %bitcast.132), channel_id=1, source_target_pairs={{0,1},{1,0},{2,3},{3,2},{4,5},{5,4},{6,7},{7,6},{8,9},{9,8},{10,11... | collective-permute-start | bytes 3145736 | tf_op jit(solution)/shard_map/ppermute | solution.py:16
  42.9 63.4 %copy-start.4 = (f32[128]{0:T(128)S(1)}, f32[128]{0:T(128)}, u32[]{:S(2)}) copy-start(f32[128]{0:T(128)} %param.12) | copy-start | bytes 1540
  106.5 8.6 %slice-start.2 = ((s8[8388608]{0:T(1024)(128)(4,1)}), s8[4194304]{0:T(1024)(128)(4,1)S(1)}, s32[]{:S(2)}) async-start(s8[8388608]{0:T(1024)(128)(4,1)} %bitcast.127), calls=%async_computation.3 | async-start | bytes 8388608
  106.5 8.6 %copy-start.2 = (bf16[512,512]{0,1:T(8,128)(2,1)S(1)}, bf16[512,512]{0,1:T(8,128)(2,1)}, u32[]{:S(2)}) copy-start(bf16[512,512]{0,1:T(8,128)(2,1)} %get-tuple-element.13) | copy-start | bytes 1572868
  108.5 6.6 %slice-start.3 = ((s8[8388608]{0:T(1024)(128)(4,1)}), s8[4194304]{0:T(1024)(128)(4,1)S(1)}, s32[]{:S(2)}) async-start(s8[8388608]{0:T(1024)(128)(4,1)} %bitcast.127), calls=%async_computation.4 | async-start | bytes 8388608
  109.8 7.3 %slice-start = ((s8[8388608]{0:T(1024)(128)(4,1)}), s8[4194304]{0:T(1024)(128)(4,1)S(1)}, s32[]{:S(2)}) async-start(s8[8388608]{0:T(1024)(128)(4,1)} %bitcast.125), calls=%async_computation.1 | async-start | bytes 8388608
  115.1 2.2 %slice-start.1 = ((s8[8388608]{0:T(1024)(128)(4,1)}), s8[4194304]{0:T(1024)(128)(4,1)S(1)}, s32[]{:S(2)}) async-start(s8[8388608]{0:T(1024)(128)(4,1)} %bitcast.125), calls=%async_computation.2 | async-start | bytes 8388608
  115.1 4.2 %copy-start.3 = (f32[4,8,128]{2,1,0:T(8,128)S(1)}, f32[4,8,128]{2,1,0:T(8,128)}, u32[]{:S(2)}) copy-start(f32[4,8,128]{2,1,0:T(8,128)} %get-tuple-element.14) | copy-start | bytes 49156
  115.1 4.2 %copy-start.1 = (bf16[512,512]{0,1:T(8,128)(2,1)S(1)}, bf16[512,512]{0,1:T(8,128)(2,1)}, u32[]{:S(2)}) copy-start(bf16[512,512]{0,1:T(8,128)(2,1)} %get-tuple-element.10) | copy-start | bytes 1572868
  119.3 5.4 %copy-start.5 = (f32[128]{0:T(128)S(1)}, f32[128]{0:T(128)}, u32[]{:S(2)}) copy-start(f32[128]{0:T(128)} %compare_convert_fusion) | copy-start | bytes 1540
Sparse Core Ops, SparseCore 0:
  9.6 90.5 all-gather.1
where the time goes:
time: 133 us
  waiting for transfers between devices  69.3 us (52%)
  matrix products  25.5 us (19%)
  between operations  14.3 us (11%)
  other arithmetic  12.2 us (9%)
  local copies, waits for them, and re-layouts  8.55 us (6%)
  starting transfers between devices  3.01 us (2%)
    all_gather x1, waiting for transfers between devices, per_device(): lax.all_gather(kv_weight, 'fsdp', axis=0, tiled=True)  57.4 us
    ppermute x1, waiting for transfers between devices, passed_along(): lax.ppermute(shard, axis, [(i, (i + by) % count) for i in range(count)])  11.2 us
    dot_general x2, matrix products, per_device(): jnp.einsum('rkgd,skd->kgrs', query, cache_keys, preferred_element_type=jn...  10.8 us
    reduce_sum x2, other arithmetic, per_device(): new_sum = old_sum * faded + jnp.sum(block_weights, axis=-1)  7.21 us
    dot_general x2, matrix products, per_device(): jnp.einsum('kgrs,skd->kgrd', block_weights.astype(jnp.bfloat16), cache_va...  5.52 us
    dot_general x1, matrix products, per_device(): jnp.dot(local_x, lax.all_gather(kv_weight, 'fsdp', axis=0, tiled=True), p...  5.49 us
    unnamed x22, local copies, waits for them, and re-layouts  3.06 us
    ppermute x1, starting transfers between devices, passed_along(): lax.ppermute(shard, axis, [(i, (i + by) % count) for i in range(count)])  3 us
  transfers between devices with their start and end apart: 2, of which 2 were waited for; matrix products, arithmetic and copies ran while one was open for 16% of the time, Pallas kernels for 0%

commit v1 on v0

v1 whole, which is shorter than its diff:
```python
import functools

import jax
import jax.numpy as jnp
from jax import lax
from jax.experimental import pallas as pl
from jax.experimental.pallas import tpu as pltpu
from jax.sharding import Mesh
from jax.sharding import PartitionSpec as P

HQ = 32
KVH = 4
HD = 128
SHARED = HQ // KVH
BLOCK = 512
RESP_DEV = 2
RLEN = 64
ROWS = RESP_DEV * RLEN
GROUP = SHARED * HD
SCALE = HD ** (-0.5) * 1.4426950408889634
HIDDEN = -1e30
NT = (((1,), (1,)), ((), ()))


def prompt_kernel(first, info, q_ref, k_ref, v_ref, *refs):
    if first:
        acc_ref, ml_ref = refs
    else:
        old_acc, old_ml, acc_ref, ml_ref = refs
    count = k_ref.shape[0]
    place = info[0] + lax.broadcasted_iota(jnp.int32, (1, count), 1)
    inside = place < info[1]
    biases = []
    for r in range(RESP_DEV):
        seen = inside & (jnp.full((1, count), info[2 + r]) == 1)
        biases.append(jnp.broadcast_to(jnp.where(seen, 0.0, HIDDEN), (RLEN, count)))
    bias = jnp.concatenate(biases, axis=0)
    keys = k_ref[...]
    values = v_ref[...]
    lane = lax.broadcasted_iota(jnp.int32, (ROWS, HD), 1)
    ml = jnp.zeros((ROWS, HD), jnp.float32)
    for g in range(SHARED):
        cols = slice(g * HD, (g + 1) * HD)
        scores = lax.dot_general(q_ref[:, cols], keys, NT, preferred_element_type=jnp.float32)
        scores = scores * SCALE + bias
        largest = jnp.max(scores, axis=1, keepdims=True)
        if not first:
            before = old_ml[0, :, g : g + 1]
            largest = jnp.maximum(largest, before)
            faded = jnp.exp2(before - largest)
        weights = jnp.exp2(scores - largest)
        total = jnp.sum(weights, axis=1, keepdims=True)
        acc = jnp.dot(weights.astype(jnp.bfloat16), values, preferred_element_type=jnp.float32)
        if not first:
            total = total + faded * old_ml[0, :, SHARED + g : SHARED + g + 1]
            acc = acc + faded * old_acc[:, cols]
        acc_ref[:, cols] = acc
        ml = jnp.where(lane == g, largest, ml)
        ml = jnp.where(lane == SHARED + g, total, ml)
    ml_ref[0] = ml


def prompt_attention(info, query, cache, state):
    count = cache.shape[0]
    first = state is None
    wide = pl.BlockSpec((ROWS, GROUP), lambda k, s: (0, k))
    small = pl.BlockSpec((1, ROWS, HD), lambda k, s: (k, 0, 0))
    specs = [
        wide,
        pl.BlockSpec((count, HD), lambda k, s: (0, k)),
        pl.BlockSpec((count, HD), lambda k, s: (0, KVH + k)),
    ]
    operands = [query, cache, cache]
    if not first:
        specs += [wide, small]
        operands += list(state)
    return pl.pallas_call(
        functools.partial(prompt_kernel, first),
        grid_spec=pltpu.PrefetchScalarGridSpec(
            num_scalar_prefetch=1, grid=(KVH,), in_specs=specs, out_specs=[wide, small]
        ),
        out_shape=[
            jax.ShapeDtypeStruct((ROWS, HQ * HD), jnp.float32),
            jax.ShapeDtypeStruct((KVH, ROWS, HD), jnp.float32),
        ],
        compiler_params=pltpu.CompilerParams(vmem_limit_bytes=32 * 2**20),
        cost_estimate=pl.CostEstimate(
            flops=8 * ROWS * HQ * count * HD, bytes_accessed=6 * 2**20, transcendentals=ROWS * HQ * count
        ),
        name="prompt_attention",
    )(info, *operands)


def project_kernel(where, x_ref, other_ref, same_ref, cross_ref, mine_ref, theirs_ref, both):
    rows = same_ref.shape[0]
    core = where[1]
    both[pl.ds(pl.multiple_of(core * rows, 16), rows), :] = same_ref[...]
    both[pl.ds(pl.multiple_of((1 - core) * rows, 16), rows), :] = cross_ref[...]
    left = jnp.concatenate([x_ref[...], other_ref[...]], axis=0)
    product = jnp.dot(left, both[...], preferred_element_type=jnp.float32)
    start = pl.program_id(0) == 0

    @pl.when(start)
    def _():
        mine_ref[...] = product[:ROWS]
        theirs_ref[...] = product[ROWS:]

    @pl.when(jnp.logical_not(start))
    def _():
        mine_ref[...] += product[:ROWS]
        theirs_ref[...] += product[ROWS:]


def project(where, x, other, same, cross, steps):
    rows = same.shape[0] // steps
    columns = same.shape[1]
    out = pl.BlockSpec((ROWS, columns), lambda z, w: (0, 0))
    weight = pl.BlockSpec((rows, columns), lambda z, w: (z, 0))
    return pl.pallas_call(
        project_kernel,
        grid_spec=pltpu.PrefetchScalarGridSpec(
            num_scalar_prefetch=1,
            grid=(steps,),
            in_specs=[
                pl.BlockSpec((None, ROWS, 2 * rows), lambda z, w: (z, 0, 0)),
                pl.BlockSpec((None, ROWS, 2 * rows), lambda z, w: (z, 0, 0)),
                weight,
                weight,
            ],
            out_specs=[out, out],
            scratch_shapes=[pltpu.VMEM((2 * rows, columns), jnp.bfloat16)],
        ),
        out_shape=[jax.ShapeDtypeStruct((ROWS, columns), jnp.float32)] * 2,
        compiler_params=pltpu.CompilerParams(vmem_limit_bytes=32 * 2**20),
        cost_estimate=pl.CostEstimate(
            flops=8 * ROWS * rows * steps * columns, bytes_accessed=8 * 2**20, transcendentals=0
        ),
        name="project",
    )(where, x, other, same, cross)


def final_kernel(lengths, gain_ref, q_ref, ka_ref, kb_ref, va_ref, vb_ref, acc_ref, ml_ref, out_ref):
    raw = ka_ref[...] + kb_ref[...]
    mean = jnp.mean(raw * raw, axis=1, keepdims=True)
    keys = (raw * lax.rsqrt(mean + 1e-06) * gain_ref[...]).astype(jnp.bfloat16)
    values = (va_ref[...] + vb_ref[...]).astype(jnp.bfloat16)
    row = lax.broadcasted_iota(jnp.int32, (ROWS, ROWS), 0)
    col = lax.broadcasted_iota(jnp.int32, (ROWS, ROWS), 1)
    length = jnp.where(row < RLEN, lengths[0], lengths[1])
    base = jnp.where(row < RLEN, 0, RLEN)
    seen = (col >= base) & (col <= row) & (col - base < length)
    live = (row - base < length).astype(jnp.float32)
    for g in range(SHARED):
        cols = slice(g * HD, (g + 1) * HD)
        scores = lax.dot_general(q_ref[:, cols], keys, NT, preferred_element_type=jnp.float32)
        scores = jnp.where(seen, scores * SCALE, HIDDEN)
        before = ml_ref[0, :, g : g + 1]
        largest = jnp.maximum(jnp.max(scores, axis=1, keepdims=True), before)
        faded = jnp.exp2(before - largest)
        weights = jnp.exp2(scores - largest)
        total = jnp.sum(weights, axis=1, keepdims=True) + faded * ml_ref[0, :, SHARED + g : SHARED + g + 1]
        acc = jnp.dot(weights.astype(jnp.bfloat16), values, preferred_element_type=jnp.float32)
        acc = acc + faded * acc_ref[:, cols]
        out_ref[:, cols] = (acc / total * live).astype(jnp.bfloat16)


def final_attention(lengths, gain, query, mine, theirs, acc, ml):
    wide = pl.BlockSpec((ROWS, GROUP), lambda k, s: (0, k))
    key = pl.BlockSpec((ROWS, HD), lambda k, s: (0, k))
    value = pl.BlockSpec((ROWS, HD), lambda k, s: (0, KVH + k))
    return pl.pallas_call(
        final_kernel,
        grid_spec=pltpu.PrefetchScalarGridSpec(
            num_scalar_prefetch=1,
            grid=(KVH,),
            in_specs=[
                pl.BlockSpec((1, HD), lambda k, s: (0, 0)),
                wide,
                key,
                key,
                value,
                value,
                wide,
                pl.BlockSpec((1, ROWS, HD), lambda k, s: (k, 0, 0)),
            ],
            out_specs=wide,
        ),
        out_shape=jax.ShapeDtypeStruct((ROWS, HQ * HD), jnp.bfloat16),
        compiler_params=pltpu.CompilerParams(vmem_limit_bytes=32 * 2**20),
        cost_estimate=pl.CostEstimate(
            flops=8 * ROWS * HQ * ROWS * HD, bytes_accessed=6 * 2**20, transcendentals=ROWS * HQ * ROWS
        ),
        name="final_attention",
    )(lengths, gain, query, mine, theirs, mine, theirs, acc, ml)


def swap(array, axis):
    return lax.ppermute(array, axis, [(0, 1), (1, 0)])


def per_device(
    x_resp, queries, prompt_cache, kv_weight, key_gain, prompt_lengths, block_table, resp_lengths
):
    x, query, cache = x_resp[0], queries[0], prompt_cache[0]
    steps = lax.axis_size("z")
    y, core = lax.axis_index("y"), lax.axis_index("core")
    holder, cycle = lax.axis_index("blk"), lax.axis_size("blk")
    part = x.shape[1] // (2 * steps)

    same = lax.all_gather(kv_weight, "z", axis=0, tiled=True)
    halves = jnp.transpose(x.reshape(ROWS, steps, 2, part), (2, 1, 0, 3))
    other = swap(lax.dynamic_index_in_dim(halves, 1 - y, axis=0, keepdims=False), "y")
    x = lax.dynamic_index_in_dim(halves, y, axis=0, keepdims=False)

    state = None
    for stride in range(cycle):
        owner = lax.rem(holder + cycle - stride, cycle)
        first_place = owner * cache.shape[0]
        listed = lax.dynamic_index_in_dim(block_table[0], first_place // BLOCK, axis=1, keepdims=False)
        info = jnp.concatenate([first_place[None], prompt_lengths, listed]).astype(jnp.int32)
        if stride + 1 < cycle:
            following = lax.ppermute(cache, "blk", [(i, (i + 1) % cycle) for i in range(cycle)])
        state = prompt_attention(info, query, cache, state)
        cache = following

    same, other, x, state = lax.optimization_barrier((same, other, x, state))
    cross = swap(same, "core")
    where = jnp.stack([y, core]).astype(jnp.int32)
    mine, theirs = project(where, x, other, same, cross, steps)
    theirs = swap(theirs, "y")
    return final_attention(resp_lengths[0], key_gain[None], query, mine, theirs, *state)[None]


def solution(mesh):
    groups, blocks = mesh.devices.shape
    split = Mesh(mesh.devices.reshape(groups // 4, 2, 2, blocks), ("z", "y", "core", "blk"))
    fsdp = ("z", "y", "core")
    return jax.shard_map(
        per_device,
        mesh=split,
        in_specs=(
            P(fsdp, "blk", None),
            P(fsdp, "blk", None),
            P(fsdp, "blk", None),
            P(fsdp, None),
            P(),
            P(fsdp),
            P(fsdp, "blk", None),
            P(fsdp, "blk"),
        ),
        out_specs=P(fsdp, "blk", None),
        check_vma=False,
    )
```

time: 133 us -> 113 us (0.85)
  Pallas kernels: 0 us -> 41.5 us
  waiting for transfers between devices: 69.3 us -> 38.6 us
  matrix products: 25.5 us -> 0 us
  other arithmetic: 12.2 us -> 0.23 us
  local copies, waits for them, and re-layouts: 8.55 us -> 11.7 us
  starting transfers between devices: 3.01 us -> 6.07 us
    pallas_call x0 -> x4, Pallas kernels: none -> 41.5 us  [the longest x2 24.5 us: prompt_attention(): pl.pallas_call(functools.partial(prompt_kernel, first), grid_spec=pltpu.P...]
    all_gather x1, waiting for transfers between devices: 57.4 us -> 16 us  [per_device(): same = lax.all_gather(kv_weight, 'z', axis=0, tiled=True)]
    dot_general x9 -> x0, matrix products: 25.5 us -> none  [the longest x2 10.8 us: per_device(): jnp.einsum('rkgd,skd->kgrs', query, cache_keys, preferred_element_type=jn...]
    ppermute x1 -> x4, waiting for transfers between devices: 11.2 us -> 21.9 us  [the longest x3 17.5 us: swap(): return lax.ppermute(array, axis, [(0, 1), (1, 0)])]
    reduce_sum x5 -> x0, other arithmetic: 8.53 us -> none  [the longest x2 7.21 us: per_device(): new_sum = old_sum * faded + jnp.sum(block_weights, axis=-1)]
    unnamed x22 -> x25, local copies, waits for them, and re-layouts: 3.06 us -> 10.6 us
    ppermute x1 -> x4, starting transfers between devices: 3 us -> 6.07 us  [the longest x3 3.07 us: swap(): return lax.ppermute(array, axis, [(0, 1), (1, 0)])]
    slice x4 -> x0, local copies, waits for them, and re-layouts: 2.98 us -> none  [the longest x1 2.08 us: per_device(): cache_values = current_cache[:, KVH * HD:].reshape(place_count, KVH, HD)]
  transfers between devices with their start and end apart: 2 -> 5, of which waited for: 2 -> 4; matrix products, arithmetic and copies ran while one was open for 16% -> 5% of each run, Pallas kernels for 0% -> 22%
where the time goes in v1:
time: 113 us; the launch traced here: 112 us
  Pallas kernels  41.5 us (37%)
  waiting for transfers between devices  38.6 us (34%)
  between operations  14.1 us (12%)
  local copies, waits for them, and re-layouts  11.7 us (10%)
  starting transfers between devices  6.07 us (5%)
    pallas_call x2, Pallas kernels, prompt_attention(): pl.pallas_call(functools.partial(prompt_kernel, first), grid_spec=pltpu.P...  24.5 us
    ppermute x3, waiting for transfers between devices, swap(): return lax.ppermute(array, axis, [(0, 1), (1, 0)])  17.5 us
    all_gather x1, waiting for transfers between devices, per_device(): same = lax.all_gather(kv_weight, 'z', axis=0, tiled=True)  16 us
    pallas_call x1, Pallas kernels, final_attention(): pl.pallas_call(final_kernel, grid_spec=pltpu.PrefetchScalarGridSpec(num_s...  13.3 us
    unnamed x25, local copies, waits for them, and re-layouts  10.6 us
    ppermute x1, waiting for transfers between devices, per_device(): lax.ppermute(cache, 'blk', [(i, (i + 1) % cycle) for i in range(cycle)])  4.33 us
    pallas_call x1, Pallas kernels, project(): pl.pallas_call(project_kernel, grid_spec=pltpu.PrefetchScalarGridSpec(num...  3.63 us
    ppermute x3, starting transfers between devices, swap(): return lax.ppermute(array, axis, [(0, 1), (1, 0)])  3.07 us
  transfers between devices with their start and end apart: 5, of which 4 were waited for; matrix products, arithmetic and copies ran while one was open for 5% of the time, Pallas kernels for 22%

profile of v1, /device:TPU:0, one launch (start us, length us, event | category | flops | bytes accessed | tf_op | source)
XLA Modules:
  0.0 112.3 jit_solution(11115605931020437118)
XLA Ops:
  6.5 0.7 all-gather.2.cloned.1.call-update
  7.3 3.0 %collective-permute-start.1 = (bf16[512,1024]{1,0:T(8,128)(2,1)}, bf16[512,1024]{1,0:T(8,128)(2,1)}, u32[]{:S(2)}, u32[]{:S(2)}) collective-permute-start(bf16[512,1024]{1,0:T(8,128)(2,1)} %bitcast.22), channel_id=1, source_target_pairs={{0,1},{1,0},{2,3},{3,2},{4,5},{5,4},{6,7},{7,6},{8,9},{9,8},{10,11... | collective-permute-start | bytes 3145736 | tf_op jit(solution)/shard_map/ppermute | solution.py:222
  10.3 1.8 %copy.9 = bf16[1,128,5120]{1,2,0:T(8,128)(2,1)S(1)} copy(bf16[1,128,5120]{2,1,0:T(8,128)(2,1)} %param.8) | data formatting | bytes 2621440 | tf_op args[0]
  12.1 0.9 constant_dynamic-slice_fusion
  13.0 1.1 copy.12
  14.1 1.5 %collective-permute-start = (bf16[4,128,640]{2,1,0:T(8,128)(2,1)}, bf16[4,128,640]{2,1,0:T(8,128)(2,1)S(1)}, u32[]{:S(2)}, u32[]{:S(2)}) collective-permute-start(bf16[4,128,640]{2,1,0:T(8,128)(2,1)} %bitcast.7), channel_id=1, source_target_pairs={{0,4},{4,0},{1,5},{5,1},{2,6},{6,2},{3,7},{7,3},{8,12},{12,8},{9,1... | collective-permute-start | bytes 1966088 | tf_op jit(solution)/shard_map/ppermute | solution.py:198
  16.3 1.4 %copy.13 = bf16[128,4,1,640]{3,0,1,2:T(8,128)(2,1)S(1)} copy(bf16[128,4,1,640]{0,3,2,1:T(8,128)(2,1)} %get-tuple-element.29) | data formatting | bytes 1310720
  17.7 0.2 dynamic-slice_reduce_fusion
  17.9 0.1 pad_add_fusion.2.info
  18.0 0.1 pad_add_fusion.1.info
  18.0 1.3 %copy-done.9 = bf16[1,512,1024]{2,1,0:T(8,128)(2,1)S(1)} copy-done((bf16[1,512,1024]{2,1,0:T(8,128)(2,1)S(1)}, bf16[1,512,1024]{2,1,0:T(8,128)(2,1)}, u32[]{:S(2)}) %copy-start.9) | copy-done | bytes 1048600
  19.4 10.0 %prompt_attention.2 = (f32[128,4096]{1,0:T(8,128)S(1)}, f32[4,128,128]{2,1,0:T(8,128)S(1)}) custom-call(s32[4]{0:T(128)S(1)} %pad_add_fusion.2.info, bf16[128,4096]{1,0:T(8,128)(2,1)S(1)} %bitcast.17, bf16[512,1024]{1,0:T(8,128)(2,1)S(1)} %bitcast.23, bf16[512,1024]{1,0:T(8,128)(2,1)S(1)} %bitcast.24), custom_call_target="tpu_custom_call" | custom-call | flops 2147483648 | bytes 6291456 | tf_op jit(solution)/shard_map/prompt_attention/pallas_call | solution.py:77
  29.4 4.3 %collective-permute-done.1.k_ref.v_ref = bf16[512,1024]{1,0:T(8,128)(2,1)} collective-permute-done((bf16[512,1024]{1,0:T(8,128)(2,1)}, bf16[512,1024]{1,0:T(8,128)(2,1)}, u32[]{:S(2)}, u32[]{:S(2)}) %collective-permute-start.1) | collective-permute-done | bytes 1048608 | tf_op jit(solution)/shard_map/ppermute | solution.py:222
  33.7 14.5 %prompt_attention.3 = (f32[128,4096]{1,0:T(8,128)S(1)}, f32[4,128,128]{2,1,0:T(8,128)S(1)}) custom-call(s32[4]{0:T(128)S(1)} %pad_add_fusion.1.info, bf16[128,4096]{1,0:T(8,128)(2,1)S(1)} %bitcast.18, bf16[512,1024]{1,0:T(8,128)(2,1)} %collective-permute-done.1.k_ref.v_ref, bf16[512,1024]{1,0:T(8,128)(2,1)} %collective-permute-done.1.k_ref.v_ref, ...), custom_call_target="tpu_custom_call" | custom-call | flops 2147483648 | bytes 6291456 | tf_op jit(solution)/shard_map/prompt_attention/pallas_call | solution.py:77
  48.3 1.3 %copy-done.1 = f32[128,4096]{1,0:T(8,128)} copy-done((f32[128,4096]{1,0:T(8,128)}, f32[128,4096]{1,0:T(8,128)S(1)}, u32[]{:S(2)}) %copy-start.1) | copy-done | bytes 2097176
  49.6 0.8 copy-done.5
  50.4 16.0 %all-gather.2.cloned.1.call-done.same_ref = bf16[1280,1024]{1,0:T(8,128)(2,1)} async-done(((bf16[320,1024]{1,0:T(8,128)(2,1)}), bf16[1280,1024]{1,0:T(8,128)(2,1)}) %all-gather.2.cloned.1.call-update) | async-done | bytes 2621456 | tf_op jit(solution)/shard_map/all_gather | solution.py:210
  66.5 5.0 %collective-permute-done.2.cross_ref = bf16[1280,1024]{1,0:T(8,128)(2,1)S(1)} collective-permute-done((bf16[1280,1024]{1,0:T(8,128)(2,1)}, bf16[1280,1024]{1,0:T(8,128)(2,1)S(1)}, u32[]{:S(2)}, u32[]{:S(2)}) %collective-permute-start.2) | collective-permute-done | bytes 2621472 | tf_op jit(solution)/shard_map/ppermute | solution.py:198
  71.6 1.7 %copy-done = bf16[1280,1024]{1,0:T(8,128)(2,1)S(1)} copy-done((bf16[1280,1024]{1,0:T(8,128)(2,1)S(1)}, bf16[1280,1024]{1,0:T(8,128)(2,1)}, u32[]{:S(2)}) %copy-start) | copy-done | bytes 2621464
  73.3 1.1 copy-done.6
  74.4 3.6 %project.1 = (f32[128,1024]{1,0:T(8,128)S(1)}, f32[128,1024]{1,0:T(8,128)S(1)}) custom-call(s32[2]{0:T(128)S(1)} %pad_add_fusion.where, bf16[4,128,640]{2,1,0:T(8,128)(2,1)S(1)} %bitcast.16, bf16[4,128,640]{2,1,0:T(8,128)(2,1)S(1)} %copy-done.6, bf16[1280,1024]{1,0:T(8,128)(2,1)S(1)} %copy-done, bf16[1280,1024]{1,0:T(8,128)(2,1)S(1)} %collective-permute-done.2.cross_ref), custom_call_target="tpu_custom_call" | custom-call | flops 1342177280 | bytes 8388608 | tf_op jit(solution)/shard_map/project/pallas_call | solution.py:119
  78.1 1.5 %collective-permute-start.3 = (f32[128,1024]{1,0:T(8,128)S(1)}, f32[128,1024]{1,0:T(8,128)S(1)}, u32[]{:S(2)}, u32[]{:S(2)}) collective-permute-start(f32[128,1024]{1,0:T(8,128)S(1)} %get-tuple-element.24), channel_id=1, source_target_pairs={{0,4},{4,0},{1,5},{5,1},{2,6},{6,2},{3,7},{7,3},{8,12},{12,8},{9,1... | collective-permute-start | bytes 1572872 | tf_op jit(solution)/shard_map/ppermute | solution.py:198
  79.6 12.5 %collective-permute-done.3.kb_ref.vb_ref = f32[128,1024]{1,0:T(8,128)S(1)} collective-permute-done((f32[128,1024]{1,0:T(8,128)S(1)}, f32[128,1024]{1,0:T(8,128)S(1)}, u32[]{:S(2)}, u32[]{:S(2)}) %collective-permute-start.3) | collective-permute-done | bytes 524320 | tf_op jit(solution)/shard_map/ppermute | solution.py:198
  92.1 13.3 %final_attention.1 = bf16[128,4096]{1,0:T(8,128)(2,1)} custom-call(s32[2]{0:T(128)S(1)} %bitcast.20, f32[1,128]{1,0:T(1,128)S(1)} %bitcast.21, bf16[128,4096]{1,0:T(8,128)(2,1)S(1)} %bitcast.19, f32[128,1024]{1,0:T(8,128)S(1)} %get-tuple-element.23.ka_ref.va_ref, f32[128,1024]{1,0:T(8,128)S(1)} %collective-permute-done.3.kb_ref.vb_ref, ...), custom_call_target="tpu_custom_call" | custom-call | flops 536870912 | bytes 6291456 | tf_op jit(solution)/shard_map/final_attention/pallas_call | solution.py:171
  (21 shorter events, 0.1 us)
Async XLA Ops:
  6.5 59.9 %all-gather.2.cloned.1.call-start = ((), (), s32[]{:S(2)}) async-start(), calls=%async_computation | async-start | bytes 3276800 | tf_op jit(solution)/shard_map/all_gather | solution.py:210
  7.3 26.5 %collective-permute-start.1 = (bf16[512,1024]{1,0:T(8,128)(2,1)}, bf16[512,1024]{1,0:T(8,128)(2,1)}, u32[]{:S(2)}, u32[]{:S(2)}) collective-permute-start(bf16[512,1024]{1,0:T(8,128)(2,1)} %bitcast.22), channel_id=1, source_target_pairs={{0,1},{1,0},{2,3},{3,2},{4,5},{5,4},{6,7},{7,6},{8,9},{9,8},{10,11... | collective-permute-start | bytes 3145736 | tf_op jit(solution)/shard_map/ppermute | solution.py:222
  12.0 5.6 %copy-start.10 = (s32[1,2,2]{2,1,0:T(2,128)S(1)}, s32[1,2,2]{2,1,0:T(2,128)}, u32[]{:S(2)}) copy-start(s32[1,2,2]{2,1,0:T(2,128)} %param.14) | copy-start | bytes 52
  12.0 6.0 %copy-start.3 = (bf16[1,128,4096]{2,1,0:T(8,128)(2,1)S(1)}, bf16[1,128,4096]{2,1,0:T(8,128)(2,1)}, u32[]{:S(2)}) copy-start(bf16[1,128,4096]{2,1,0:T(8,128)(2,1)} %param.9) | copy-start | bytes 3145732
  14.1 35.5 %collective-permute-start = (bf16[4,128,640]{2,1,0:T(8,128)(2,1)}, bf16[4,128,640]{2,1,0:T(8,128)(2,1)S(1)}, u32[]{:S(2)}, u32[]{:S(2)}) collective-permute-start(bf16[4,128,640]{2,1,0:T(8,128)(2,1)} %bitcast.7), channel_id=1, source_target_pairs={{0,4},{4,0},{1,5},{5,1},{2,6},{6,2},{3,7},{7,3},{8,12},{12,8},{9,1... | collective-permute-start | bytes 1966088 | tf_op jit(solution)/shard_map/ppermute | solution.py:198
  18.0 1.3 %copy-start.9 = (bf16[1,512,1024]{2,1,0:T(8,128)(2,1)S(1)}, bf16[1,512,1024]{2,1,0:T(8,128)(2,1)}, u32[]{:S(2)}) copy-start(bf16[1,512,1024]{2,1,0:T(8,128)(2,1)} %param.10) | copy-start | bytes 3145732
  48.3 1.3 %copy-start.1 = (f32[128,4096]{1,0:T(8,128)}, f32[128,4096]{1,0:T(8,128)S(1)}, u32[]{:S(2)}) copy-start(f32[128,4096]{1,0:T(8,128)S(1)} %get-tuple-element.25.acc_ref) | copy-start | bytes 6291460
  49.6 0.8 copy-start.5
  66.5 5.1 %collective-permute-start.2 = (bf16[1280,1024]{1,0:T(8,128)(2,1)}, bf16[1280,1024]{1,0:T(8,128)(2,1)S(1)}, u32[]{:S(2)}, u32[]{:S(2)}) collective-permute-start(bf16[1280,1024]{1,0:T(8,128)(2,1)} %all-gather.2.cloned.1.call-done.same_ref), channel_id=1, source_target_pairs={{0,2},{2,0},{1,3},{3,1},{4,6},{6,4},{5,7},{7,5},{8,10},{10,8},{9,1... | collective-permute-start | bytes 7864328 | tf_op jit(solution)/shard_map/ppermute | solution.py:198
  71.6 1.7 %copy-start = (bf16[1280,1024]{1,0:T(8,128)(2,1)S(1)}, bf16[1280,1024]{1,0:T(8,128)(2,1)}, u32[]{:S(2)}) copy-start(bf16[1280,1024]{1,0:T(8,128)(2,1)} %all-gather.2.cloned.1.call-done.same_ref) | copy-start | bytes 7864324
  73.3 1.1 copy-start.6
  74.4 17.7 %copy-start.2 = (f32[128,4096]{1,0:T(8,128)S(1)}, f32[128,4096]{1,0:T(8,128)}, u32[]{:S(2)}) copy-start(f32[128,4096]{1,0:T(8,128)} %copy-done.1) | copy-start | bytes 6291460
  74.4 17.7 %copy-start.4 = (bf16[1,128,4096]{2,1,0:T(8,128)(2,1)S(1)}, bf16[1,128,4096]{2,1,0:T(8,128)(2,1)}, u32[]{:S(2)}) copy-start(bf16[1,128,4096]{2,1,0:T(8,128)(2,1)} %param.9) | copy-start | bytes 3145732
  74.4 17.7 %copy-start.7 = (s32[1,2]{1,0:T(1,128)S(1)}, s32[1,2]{1,0:T(1,128)}, u32[]{:S(2)}) copy-start(s32[1,2]{1,0:T(1,128)} %param.15) | copy-start | bytes 28
  74.4 17.7 %copy-start.8 = (f32[128]{0:T(128)S(1)}, f32[128]{0:T(128)}, u32[]{:S(2)}) copy-start(f32[128]{0:T(128)} %param.12) | copy-start | bytes 1540
  78.1 14.0 %collective-permute-start.3 = (f32[128,1024]{1,0:T(8,128)S(1)}, f32[128,1024]{1,0:T(8,128)S(1)}, u32[]{:S(2)}, u32[]{:S(2)}) collective-permute-start(f32[128,1024]{1,0:T(8,128)S(1)} %get-tuple-element.24), channel_id=1, source_target_pairs={{0,4},{4,0},{1,5},{5,1},{2,6},{6,2},{3,7},{7,3},{8,12},{12,8},{9,1... | collective-permute-start | bytes 1572872 | tf_op jit(solution)/shard_map/ppermute | solution.py:198
Sparse Core Ops, SparseCore 0:
  8.9 57.4 all-gather.1

commit v2 on v1

--- a/solution.py
+++ b/solution.py
@@ -16,10 +16,17 @@
 RESP_DEV = 2
 RLEN = 64
 ROWS = RESP_DEV * RLEN
+PAIR = 2 * ROWS
 GROUP = SHARED * HD
 SCALE = HD ** (-0.5) * 1.4426950408889634
 HIDDEN = -1e30
 NT = (((1,), (1,)), ((), ()))
+
+
+def pair_scores(keys, q_ref, g):
+    heads = [q_ref[:, i * HD : (i + 1) * HD] for i in (g, g + 1)]
+    scores = lax.dot_general(keys, jnp.concatenate(heads, axis=0), NT, preferred_element_type=jnp.float32)
+    return scores * SCALE
 
 
 def prompt_kernel(first, info, q_ref, k_ref, v_ref, *refs):
@@ -28,43 +35,37 @@
     else:
         old_acc, old_ml, acc_ref, ml_ref = refs
     count = k_ref.shape[0]
-    place = info[0] + lax.broadcasted_iota(jnp.int32, (1, count), 1)
-    inside = place < info[1]
-    biases = []
-    for r in range(RESP_DEV):
-        seen = inside & (jnp.full((1, count), info[2 + r]) == 1)
-        biases.append(jnp.broadcast_to(jnp.where(seen, 0.0, HIDDEN), (RLEN, count)))
-    bias = jnp.concatenate(biases, axis=0)
+    place = info[0] + lax.broadcasted_iota(jnp.int32, (count, PAIR), 0)
+    lane = lax.broadcasted_iota(jnp.int32, (count, PAIR), 1)
+    listed = jnp.where(lane % ROWS < RLEN, info[2], info[3])
+    bias = jnp.where((place < info[1]) & (listed == 1), 0.0, HIDDEN)
     keys = k_ref[...]
-    values = v_ref[...]
-    lane = lax.broadcasted_iota(jnp.int32, (ROWS, HD), 1)
-    ml = jnp.zeros((ROWS, HD), jnp.float32)
-    for g in range(SHARED):
-        cols = slice(g * HD, (g + 1) * HD)
-        scores = lax.dot_general(q_ref[:, cols], keys, NT, preferred_element_type=jnp.float32)
-        scores = scores * SCALE + bias
-        largest = jnp.max(scores, axis=1, keepdims=True)
+    values = v_ref[...].T
+    for g in range(0, SHARED, 2):
+        cols = slice(g * HD, (g + 2) * HD)
+        scores = pair_scores(keys, q_ref, g) + bias
+        largest = jnp.max(scores, axis=0, keepdims=True)
         if not first:
-            before = old_ml[0, :, g : g + 1]
+            before = old_ml[0:1, cols]
             largest = jnp.maximum(largest, before)
             faded = jnp.exp2(before - largest)
         weights = jnp.exp2(scores - largest)
-        total = jnp.sum(weights, axis=1, keepdims=True)
-        acc = jnp.dot(weights.astype(jnp.bfloat16), values, preferred_element_type=jnp.float32)
+        total = jnp.sum(weights, axis=0, keepdims=True)
+        acc = jnp.dot(values, weights.astype(jnp.bfloat16), preferred_element_type=jnp.float32)
         if not first:
-            total = total + faded * old_ml[0, :, SHARED + g : SHARED + g + 1]
+            total = total + faded * old_ml[1:2, cols]
             acc = acc + faded * old_acc[:, cols]
         acc_ref[:, cols] = acc
-        ml = jnp.where(lane == g, largest, ml)
-        ml = jnp.where(lane == SHARED + g, total, ml)
-    ml_ref[0] = ml
+        ml_ref[0:1, cols] = largest
+        ml_ref[1:2, cols] = total
 
 
 def prompt_attention(info, query, cache, state):
     count = cache.shape[0]
     first = state is None
     wide = pl.BlockSpec((ROWS, GROUP), lambda k, s: (0, k))
-    small = pl.BlockSpec((1, ROWS, HD), lambda k, s: (k, 0, 0))
+    turned = pl.BlockSpec((HD, SHARED * ROWS), lambda k, s: (0, k))
+    small = pl.BlockSpec((8, SHARED * ROWS), lambda k, s: (0, k))
     specs = [
         wide,
         pl.BlockSpec((count, HD), lambda k, s: (0, k)),
@@ -72,16 +73,16 @@
     ]
     operands = [query, cache, cache]
     if not first:
-        specs += [wide, small]
+        specs += [turned, small]
         operands += list(state)
     return pl.pallas_call(
         functools.partial(prompt_kernel, first),
         grid_spec=pltpu.PrefetchScalarGridSpec(
-            num_scalar_prefetch=1, grid=(KVH,), in_specs=specs, out_specs=[wide, small]
+            num_scalar_prefetch=1, grid=(KVH,), in_specs=specs, out_specs=[turned, small]
         ),
         out_shape=[
-            jax.ShapeDtypeStruct((ROWS, HQ * HD), jnp.float32),
-            jax.ShapeDtypeStruct((KVH, ROWS, HD), jnp.float32),
+            jax.ShapeDtypeStruct((HD, HQ * ROWS), jnp.float32),
+            jax.ShapeDtypeStruct((8, HQ * ROWS), jnp.float32),
         ],
         compiler_params=pltpu.CompilerParams(vmem_limit_bytes=32 * 2**20),
         cost_estimate=pl.CostEstimate(
@@ -143,25 +144,25 @@
     raw = ka_ref[...] + kb_ref[...]
     mean = jnp.mean(raw * raw, axis=1, keepdims=True)
     keys = (raw * lax.rsqrt(mean + 1e-06) * gain_ref[...]).astype(jnp.bfloat16)
-    values = (va_ref[...] + vb_ref[...]).astype(jnp.bfloat16)
-    row = lax.broadcasted_iota(jnp.int32, (ROWS, ROWS), 0)
-    col = lax.broadcasted_iota(jnp.int32, (ROWS, ROWS), 1)
+    values = (va_ref[...] + vb_ref[...]).T.astype(jnp.bfloat16)
+    slot = lax.broadcasted_iota(jnp.int32, (ROWS, PAIR), 0)
+    row = lax.broadcasted_iota(jnp.int32, (ROWS, PAIR), 1) % ROWS
     length = jnp.where(row < RLEN, lengths[0], lengths[1])
     base = jnp.where(row < RLEN, 0, RLEN)
-    seen = (col >= base) & (col <= row) & (col - base < length)
-    live = (row - base < length).astype(jnp.float32)
-    for g in range(SHARED):
-        cols = slice(g * HD, (g + 1) * HD)
-        scores = lax.dot_general(q_ref[:, cols], keys, NT, preferred_element_type=jnp.float32)
-        scores = jnp.where(seen, scores * SCALE, HIDDEN)
-        before = ml_ref[0, :, g : g + 1]
-        largest = jnp.maximum(jnp.max(scores, axis=1, keepdims=True), before)
+    seen = (slot >= base) & (slot <= row) & (slot - base < length)
+    live = jnp.where(row - base < length, 1.0, 0.0)[0:1]
+    for g in range(0, SHARED, 2):
+        cols = slice(g * HD, (g + 2) * HD)
+        scores = jnp.where(seen, pair_scores(keys, q_ref, g), HIDDEN)
+        before = ml_ref[0:1, cols]
+        largest = jnp.maximum(jnp.max(scores, axis=0, keepdims=True), before)
         faded = jnp.exp2(before - largest)
         weights = jnp.exp2(scores - largest)
-        total = jnp.sum(weights, axis=1, keepdims=True) + faded * ml_ref[0, :, SHARED + g : SHARED + g + 1]
-        acc = jnp.dot(weights.astype(jnp.bfloat16), values, preferred_element_type=jnp.float32)
-        acc = acc + faded * acc_ref[:, cols]
-        out_ref[:, cols] = (acc / total * live).astype(jnp.bfloat16)
+        total = jnp.sum(weights, axis=0, keepdims=True) + faded * ml_ref[1:2, cols]
+        acc = jnp.dot(values, weights.astype(jnp.bfloat16), preferred_element_type=jnp.float32)
+        acc = (acc + faded * acc_ref[:, cols]) * (live / total)
+        out_ref[:, g * HD : (g + 1) * HD] = acc[:, :ROWS].T.astype(jnp.bfloat16)
+        out_ref[:, (g + 1) * HD : (g + 2) * HD] = acc[:, ROWS:].T.astype(jnp.bfloat16)
 
 
 def final_attention(lengths, gain, query, mine, theirs, acc, ml):
@@ -180,8 +181,8 @@
                 key,
                 value,
                 value,
-                wide,
-                pl.BlockSpec((1, ROWS, HD), lambda k, s: (k, 0, 0)),
+                pl.BlockSpec((HD, SHARED * ROWS), lambda k, s: (0, k)),
+                pl.BlockSpec((8, SHARED * ROWS), lambda k, s: (0, k)),
             ],
             out_specs=wide,
         ),

time: 113 us -> 104 us (0.920)
  Pallas kernels: 41.5 us -> 25.7 us
  waiting for transfers between devices: 38.6 us -> 46 us
    pallas_call x1, Pallas kernels: 13.3 us -> 4.96 us  [final_attention(): pl.pallas_call(final_kernel, grid_spec=pltpu.PrefetchScalarGridSpec(num_s...]
    pallas_call x2, Pallas kernels: 24.5 us -> 17.2 us  [prompt_attention(): pl.pallas_call(functools.partial(prompt_kernel, first), grid_spec=pltpu.P...]
    all_gather x1, waiting for transfers between devices: 16 us -> 21.5 us  [per_device(): same = lax.all_gather(kv_weight, 'z', axis=0, tiled=True)]
    ppermute x1, waiting for transfers between devices: 4.33 us -> 6.21 us  [per_device(): lax.ppermute(cache, 'blk', [(i, (i + 1) % cycle) for i in range(cycle)])]
  transfers between devices with their start and end apart: 5 -> 5, of which waited for: 4 -> 4; matrix products, arithmetic and copies ran while one was open for 5% -> 5% of each run, Pallas kernels for 22% -> 17%
where the time goes in v2:
time: 104 us
  waiting for transfers between devices  46 us (44%)
  Pallas kernels  25.7 us (25%)
  between operations  14.1 us (14%)
  local copies, waits for them, and re-layouts  11.7 us (11%)
  starting transfers between devices  6.07 us (6%)
    all_gather x1, waiting for transfers between devices, per_device(): same = lax.all_gather(kv_weight, 'z', axis=0, tiled=True)  21.5 us
    ppermute x3, waiting for transfers between devices, swap(): return lax.ppermute(array, axis, [(0, 1), (1, 0)])  17.5 us
    pallas_call x2, Pallas kernels, prompt_attention(): pl.pallas_call(functools.partial(prompt_kernel, first), grid_spec=pltpu.P...  17.2 us
    unnamed x25, local copies, waits for them, and re-layouts  10.6 us
    ppermute x1, waiting for transfers between devices, per_device(): lax.ppermute(cache, 'blk', [(i, (i + 1) % cycle) for i in range(cycle)])  6.21 us
    pallas_call x1, Pallas kernels, final_attention(): pl.pallas_call(final_kernel, grid_spec=pltpu.PrefetchScalarGridSpec(num_s...  4.96 us
    pallas_call x1, Pallas kernels, project(): pl.pallas_call(project_kernel, grid_spec=pltpu.PrefetchScalarGridSpec(num...  3.61 us
    ppermute x3, starting transfers between devices, swap(): return lax.ppermute(array, axis, [(0, 1), (1, 0)])  3.07 us
  transfers between devices with their start and end apart: 5, of which 4 were waited for; matrix products, arithmetic and copies ran while one was open for 5% of the time, Pallas kernels for 17%

profile of v2, /device:TPU:0, one launch (start us, length us, event | category | flops | bytes accessed | tf_op | source)
XLA Modules:
  0.0 103.9 jit_solution(7944689659462215681)
XLA Ops:
  6.5 0.7 all-gather.2.cloned.1.call-update
  7.3 3.0 %collective-permute-start.1 = (bf16[512,1024]{1,0:T(8,128)(2,1)}, bf16[512,1024]{1,0:T(8,128)(2,1)}, u32[]{:S(2)}, u32[]{:S(2)}) collective-permute-start(bf16[512,1024]{1,0:T(8,128)(2,1)} %bitcast.22), channel_id=1, source_target_pairs={{0,1},{1,0},{2,3},{3,2},{4,5},{5,4},{6,7},{7,6},{8,9},{9,8},{10,11... | collective-permute-start | bytes 3145736 | tf_op jit(solution)/shard_map/ppermute | solution.py:223
  10.3 1.8 %copy.9 = bf16[1,128,5120]{1,2,0:T(8,128)(2,1)S(1)} copy(bf16[1,128,5120]{2,1,0:T(8,128)(2,1)} %param.8) | data formatting | bytes 2621440 | tf_op args[0]
  12.1 0.9 constant_dynamic-slice_fusion
  13.0 1.1 %copy.12 = bf16[128,4,1,640]{3,0,1,2:T(8,128)(2,1)} copy(bf16[128,4,1,640]{0,3,2,1:T(8,128)(2,1)S(1)} %get-tuple-element.30) | data formatting | bytes 1310720
  14.1 1.5 %collective-permute-start = (bf16[4,128,640]{2,1,0:T(8,128)(2,1)}, bf16[4,128,640]{2,1,0:T(8,128)(2,1)S(1)}, u32[]{:S(2)}, u32[]{:S(2)}) collective-permute-start(bf16[4,128,640]{2,1,0:T(8,128)(2,1)} %bitcast.7), channel_id=1, source_target_pairs={{0,4},{4,0},{1,5},{5,1},{2,6},{6,2},{3,7},{7,3},{8,12},{12,8},{9,1... | collective-permute-start | bytes 1966088 | tf_op jit(solution)/shard_map/ppermute | solution.py:199
  16.3 1.4 %copy.13 = bf16[128,4,1,640]{3,0,1,2:T(8,128)(2,1)S(1)} copy(bf16[128,4,1,640]{0,3,2,1:T(8,128)(2,1)} %get-tuple-element.29) | data formatting | bytes 1310720
  17.7 0.2 dynamic-slice_reduce_fusion
  17.9 0.1 pad_add_fusion.2.info
  18.0 0.1 pad_add_fusion.1.info
  18.0 1.3 %copy-done.9 = bf16[1,512,1024]{2,1,0:T(8,128)(2,1)S(1)} copy-done((bf16[1,512,1024]{2,1,0:T(8,128)(2,1)S(1)}, bf16[1,512,1024]{2,1,0:T(8,128)(2,1)}, u32[]{:S(2)}) %copy-start.9) | copy-done | bytes 1048600
  19.4 8.2 %prompt_attention.2 = (f32[128,4096]{1,0:T(8,128)S(1)}, f32[8,4096]{1,0:T(8,128)S(1)}) custom-call(s32[4]{0:T(128)S(1)} %pad_add_fusion.2.info, bf16[128,4096]{1,0:T(8,128)(2,1)S(1)} %bitcast.17, bf16[512,1024]{1,0:T(8,128)(2,1)S(1)} %bitcast.23, bf16[512,1024]{1,0:T(8,128)(2,1)S(1)} %bitcast.24), custom_call_target="tpu_custom_call" | custom-call | flops 2147483648 | bytes 6291456 | tf_op jit(solution)/shard_map/prompt_attention/pallas_call | solution.py:78
  27.5 6.2 %collective-permute-done.1.k_ref.v_ref = bf16[512,1024]{1,0:T(8,128)(2,1)} collective-permute-done((bf16[512,1024]{1,0:T(8,128)(2,1)}, bf16[512,1024]{1,0:T(8,128)(2,1)}, u32[]{:S(2)}, u32[]{:S(2)}) %collective-permute-start.1) | collective-permute-done | bytes 1048608 | tf_op jit(solution)/shard_map/ppermute | solution.py:223
  33.7 9.0 %prompt_attention.3 = (f32[128,4096]{1,0:T(8,128)S(1)}, f32[8,4096]{1,0:T(8,128)S(1)}) custom-call(s32[4]{0:T(128)S(1)} %pad_add_fusion.1.info, bf16[128,4096]{1,0:T(8,128)(2,1)S(1)} %bitcast.18, bf16[512,1024]{1,0:T(8,128)(2,1)} %collective-permute-done.1.k_ref.v_ref, bf16[512,1024]{1,0:T(8,128)(2,1)} %collective-permute-done.1.k_ref.v_ref, ...), custom_call_target="tpu_custom_call" | custom-call | flops 2147483648 | bytes 6291456 | tf_op jit(solution)/shard_map/prompt_attention/pallas_call | solution.py:78
  42.8 1.3 %copy-done.1 = f32[128,4096]{1,0:T(8,128)} copy-done((f32[128,4096]{1,0:T(8,128)}, f32[128,4096]{1,0:T(8,128)S(1)}, u32[]{:S(2)}) %copy-start.1) | copy-done | bytes 2097176
  44.1 0.8 copy-done.5
  44.9 21.5 %all-gather.2.cloned.1.call-done.same_ref = bf16[1280,1024]{1,0:T(8,128)(2,1)} async-done(((bf16[320,1024]{1,0:T(8,128)(2,1)}), bf16[1280,1024]{1,0:T(8,128)(2,1)}) %all-gather.2.cloned.1.call-update) | async-done | bytes 2621456 | tf_op jit(solution)/shard_map/all_gather | solution.py:211
  66.5 5.0 %collective-permute-done.2.cross_ref = bf16[1280,1024]{1,0:T(8,128)(2,1)S(1)} collective-permute-done((bf16[1280,1024]{1,0:T(8,128)(2,1)}, bf16[1280,1024]{1,0:T(8,128)(2,1)S(1)}, u32[]{:S(2)}, u32[]{:S(2)}) %collective-permute-start.2) | collective-permute-done | bytes 2621472 | tf_op jit(solution)/shard_map/ppermute | solution.py:199
  71.6 1.7 %copy-done = bf16[1280,1024]{1,0:T(8,128)(2,1)S(1)} copy-done((bf16[1280,1024]{1,0:T(8,128)(2,1)S(1)}, bf16[1280,1024]{1,0:T(8,128)(2,1)}, u32[]{:S(2)}) %copy-start) | copy-done | bytes 2621464
  73.3 1.1 %copy-done.6 = bf16[4,128,640]{2,1,0:T(8,128)(2,1)S(1)} copy-done((bf16[4,128,640]{2,1,0:T(8,128)(2,1)S(1)}, bf16[4,128,640]{2,1,0:T(8,128)(2,1)}, u32[]{:S(2)}) %copy-start.6) | copy-done | bytes 655384
  74.4 3.6 %project.1 = (f32[128,1024]{1,0:T(8,128)S(1)}, f32[128,1024]{1,0:T(8,128)S(1)}) custom-call(s32[2]{0:T(128)S(1)} %pad_add_fusion.where, bf16[4,128,640]{2,1,0:T(8,128)(2,1)S(1)} %bitcast.16, bf16[4,128,640]{2,1,0:T(8,128)(2,1)S(1)} %copy-done.6, bf16[1280,1024]{1,0:T(8,128)(2,1)S(1)} %copy-done, bf16[1280,1024]{1,0:T(8,128)(2,1)S(1)} %collective-permute-done.2.cross_ref), custom_call_target="tpu_custom_call" | custom-call | flops 1342177280 | bytes 8388608 | tf_op jit(solution)/shard_map/project/pallas_call | solution.py:120
  78.0 1.5 %collective-permute-start.3 = (f32[128,1024]{1,0:T(8,128)S(1)}, f32[128,1024]{1,0:T(8,128)S(1)}, u32[]{:S(2)}, u32[]{:S(2)}) collective-permute-start(f32[128,1024]{1,0:T(8,128)S(1)} %get-tuple-element.24), channel_id=1, source_target_pairs={{0,4},{4,0},{1,5},{5,1},{2,6},{6,2},{3,7},{7,3},{8,12},{12,8},{9,1... | collective-permute-start | bytes 1572872 | tf_op jit(solution)/shard_map/ppermute | solution.py:199
  79.6 12.5 %collective-permute-done.3.kb_ref.vb_ref = f32[128,1024]{1,0:T(8,128)S(1)} collective-permute-done((f32[128,1024]{1,0:T(8,128)S(1)}, f32[128,1024]{1,0:T(8,128)S(1)}, u32[]{:S(2)}, u32[]{:S(2)}) %collective-permute-start.3) | collective-permute-done | bytes 524320 | tf_op jit(solution)/shard_map/ppermute | solution.py:199
  92.1 5.0 %final_attention.1 = bf16[128,4096]{1,0:T(8,128)(2,1)} custom-call(s32[2]{0:T(128)S(1)} %bitcast.20, f32[1,128]{1,0:T(1,128)S(1)} %bitcast.21, bf16[128,4096]{1,0:T(8,128)(2,1)S(1)} %bitcast.19, f32[128,1024]{1,0:T(8,128)S(1)} %get-tuple-element.23.ka_ref.va_ref, f32[128,1024]{1,0:T(8,128)S(1)} %collective-permute-done.3.kb_ref.vb_ref, ...), custom_call_target="tpu_custom_call" | custom-call | flops 536870912 | bytes 6291456 | tf_op jit(solution)/shard_map/final_attention/pallas_call | solution.py:172
  (21 shorter events, 0.1 us)
Async XLA Ops:
  6.5 59.9 %all-gather.2.cloned.1.call-start = ((), (), s32[]{:S(2)}) async-start(), calls=%async_computation | async-start | bytes 3276800 | tf_op jit(solution)/shard_map/all_gather | solution.py:211
  7.3 26.5 %collective-permute-start.1 = (bf16[512,1024]{1,0:T(8,128)(2,1)}, bf16[512,1024]{1,0:T(8,128)(2,1)}, u32[]{:S(2)}, u32[]{:S(2)}) collective-permute-start(bf16[512,1024]{1,0:T(8,128)(2,1)} %bitcast.22), channel_id=1, source_target_pairs={{0,1},{1,0},{2,3},{3,2},{4,5},{5,4},{6,7},{7,6},{8,9},{9,8},{10,11... | collective-permute-start | bytes 3145736 | tf_op jit(solution)/shard_map/ppermute | solution.py:223
  12.0 5.6 %copy-start.10 = (s32[1,2,2]{2,1,0:T(2,128)S(1)}, s32[1,2,2]{2,1,0:T(2,128)}, u32[]{:S(2)}) copy-start(s32[1,2,2]{2,1,0:T(2,128)} %param.14) | copy-start | bytes 52
  12.0 6.0 %copy-start.3 = (bf16[1,128,4096]{2,1,0:T(8,128)(2,1)S(1)}, bf16[1,128,4096]{2,1,0:T(8,128)(2,1)}, u32[]{:S(2)}) copy-start(bf16[1,128,4096]{2,1,0:T(8,128)(2,1)} %param.9) | copy-start | bytes 3145732
  14.1 30.0 %collective-permute-start = (bf16[4,128,640]{2,1,0:T(8,128)(2,1)}, bf16[4,128,640]{2,1,0:T(8,128)(2,1)S(1)}, u32[]{:S(2)}, u32[]{:S(2)}) collective-permute-start(bf16[4,128,640]{2,1,0:T(8,128)(2,1)} %bitcast.7), channel_id=1, source_target_pairs={{0,4},{4,0},{1,5},{5,1},{2,6},{6,2},{3,7},{7,3},{8,12},{12,8},{9,1... | collective-permute-start | bytes 1966088 | tf_op jit(solution)/shard_map/ppermute | solution.py:199
  18.0 1.3 %copy-start.9 = (bf16[1,512,1024]{2,1,0:T(8,128)(2,1)S(1)}, bf16[1,512,1024]{2,1,0:T(8,128)(2,1)}, u32[]{:S(2)}) copy-start(bf16[1,512,1024]{2,1,0:T(8,128)(2,1)} %param.10) | copy-start | bytes 3145732
  42.8 1.3 %copy-start.1 = (f32[128,4096]{1,0:T(8,128)}, f32[128,4096]{1,0:T(8,128)S(1)}, u32[]{:S(2)}) copy-start(f32[128,4096]{1,0:T(8,128)S(1)} %get-tuple-element.25.acc_ref) | copy-start | bytes 6291460
  44.1 0.8 copy-start.5
  66.5 5.1 %collective-permute-start.2 = (bf16[1280,1024]{1,0:T(8,128)(2,1)}, bf16[1280,1024]{1,0:T(8,128)(2,1)S(1)}, u32[]{:S(2)}, u32[]{:S(2)}) collective-permute-start(bf16[1280,1024]{1,0:T(8,128)(2,1)} %all-gather.2.cloned.1.call-done.same_ref), channel_id=1, source_target_pairs={{0,2},{2,0},{1,3},{3,1},{4,6},{6,4},{5,7},{7,5},{8,10},{10,8},{9,1... | collective-permute-start | bytes 7864328 | tf_op jit(solution)/shard_map/ppermute | solution.py:199
  71.6 1.7 %copy-start = (bf16[1280,1024]{1,0:T(8,128)(2,1)S(1)}, bf16[1280,1024]{1,0:T(8,128)(2,1)}, u32[]{:S(2)}) copy-start(bf16[1280,1024]{1,0:T(8,128)(2,1)} %all-gather.2.cloned.1.call-done.same_ref) | copy-start | bytes 7864324
  73.3 1.1 %copy-start.6 = (bf16[4,128,640]{2,1,0:T(8,128)(2,1)S(1)}, bf16[4,128,640]{2,1,0:T(8,128)(2,1)}, u32[]{:S(2)}) copy-start(bf16[4,128,640]{2,1,0:T(8,128)(2,1)} %copy-done.5) | copy-start | bytes 1966084
  74.4 17.7 %copy-start.2 = (f32[128,4096]{1,0:T(8,128)S(1)}, f32[128,4096]{1,0:T(8,128)}, u32[]{:S(2)}) copy-start(f32[128,4096]{1,0:T(8,128)} %copy-done.1) | copy-start | bytes 6291460
  74.4 17.7 %copy-start.4 = (bf16[1,128,4096]{2,1,0:T(8,128)(2,1)S(1)}, bf16[1,128,4096]{2,1,0:T(8,128)(2,1)}, u32[]{:S(2)}) copy-start(bf16[1,128,4096]{2,1,0:T(8,128)(2,1)} %param.9) | copy-start | bytes 3145732
  74.4 17.7 %copy-start.7 = (s32[1,2]{1,0:T(1,128)S(1)}, s32[1,2]{1,0:T(1,128)}, u32[]{:S(2)}) copy-start(s32[1,2]{1,0:T(1,128)} %param.15) | copy-start | bytes 28
  74.4 17.7 %copy-start.8 = (f32[128]{0:T(128)S(1)}, f32[128]{0:T(128)}, u32[]{:S(2)}) copy-start(f32[128]{0:T(128)} %param.12) | copy-start | bytes 1540
  78.0 14.0 %collective-permute-start.3 = (f32[128,1024]{1,0:T(8,128)S(1)}, f32[128,1024]{1,0:T(8,128)S(1)}, u32[]{:S(2)}, u32[]{:S(2)}) collective-permute-start(f32[128,1024]{1,0:T(8,128)S(1)} %get-tuple-element.24), channel_id=1, source_target_pairs={{0,4},{4,0},{1,5},{5,1},{2,6},{6,2},{3,7},{7,3},{8,12},{12,8},{9,1... | collective-permute-start | bytes 1572872 | tf_op jit(solution)/shard_map/ppermute | solution.py:199
Sparse Core Ops, SparseCore 0:
  8.9 57.4 all-gather.1

commit v3 on v2

v3 whole, which is shorter than its diff:
```python
import functools

import jax
import jax.numpy as jnp
from jax import lax
from jax.experimental import pallas as pl
from jax.experimental.pallas import tpu as pltpu
from jax.sharding import Mesh
from jax.sharding import PartitionSpec as P

HQ = 32
KVH = 4
HD = 128
SHARED = HQ // KVH
BLOCK = 512
RESP_DEV = 2
RLEN = 64
ROWS = RESP_DEV * RLEN
PAIR = 2 * ROWS
GROUP = SHARED * HD
SCALE = HD ** (-0.5) * 1.4426950408889634
HIDDEN = -1e30
NT = (((1,), (1,)), ((), ()))
HINT = pl.CostEstimate(flops=1024, bytes_accessed=1024, transcendentals=0)


def pair_scores(keys, q_ref, g):
    heads = [q_ref[:, i * HD : (i + 1) * HD] for i in (g, g + 1)]
    scores = lax.dot_general(keys, jnp.concatenate(heads, axis=0), NT, preferred_element_type=jnp.float32)
    return scores * SCALE


def prompt_kernel(first, info, q_ref, k_ref, v_ref, *refs):
    if first:
        acc_ref, ml_ref = refs
    else:
        old_acc, old_ml, acc_ref, ml_ref = refs
    count = k_ref.shape[0]
    place = info[0] + lax.broadcasted_iota(jnp.int32, (count, PAIR), 0)
    lane = lax.broadcasted_iota(jnp.int32, (count, PAIR), 1)
    listed = jnp.where(lane % ROWS < RLEN, info[2], info[3])
    bias = jnp.where((place < info[1]) & (listed == 1), 0.0, HIDDEN)
    keys = k_ref[...]
    values = v_ref[...].T
    for g in range(0, SHARED, 2):
        cols = slice(g * HD, (g + 2) * HD)
        scores = pair_scores(keys, q_ref, g) + bias
        largest = jnp.max(scores, axis=0, keepdims=True)
        if not first:
            before = old_ml[0:1, cols]
            largest = jnp.maximum(largest, before)
            faded = jnp.exp2(before - largest)
        weights = jnp.exp2(scores - largest)
        total = jnp.sum(weights, axis=0, keepdims=True)
        acc = jnp.dot(values, weights.astype(jnp.bfloat16), preferred_element_type=jnp.float32)
        if not first:
            total = total + faded * old_ml[1:2, cols]
            acc = acc + faded * old_acc[:, cols]
        acc_ref[:, cols] = acc
        ml_ref[0:1, cols] = largest
        ml_ref[1:2, cols] = total


def prompt_attention(info, query, cache, state, head, heads):
    count = cache.shape[0]
    first = state is None
    wide = pl.BlockSpec((ROWS, GROUP), lambda k, s: (0, head + k))
    turned = pl.BlockSpec((HD, SHARED * ROWS), lambda k, s: (0, k))
    small = pl.BlockSpec((8, SHARED * ROWS), lambda k, s: (0, k))
    specs = [
        wide,
        pl.BlockSpec((count, HD), lambda k, s: (0, head + k)),
        pl.BlockSpec((count, HD), lambda k, s: (0, KVH + head + k)),
    ]
    operands = [query, cache, cache]
    if not first:
        specs += [turned, small]
        operands += list(state)
    return pl.pallas_call(
        functools.partial(prompt_kernel, first),
        grid_spec=pltpu.PrefetchScalarGridSpec(
            num_scalar_prefetch=1, grid=(heads,), in_specs=specs, out_specs=[turned, small]
        ),
        out_shape=[
            jax.ShapeDtypeStruct((HD, heads * SHARED * ROWS), jnp.float32),
            jax.ShapeDtypeStruct((8, heads * SHARED * ROWS), jnp.float32),
        ],
        compiler_params=pltpu.CompilerParams(vmem_limit_bytes=32 * 2**20),
        cost_estimate=HINT,
        name="prompt_attention",
    )(info, *operands)


def pack_rows_kernel(where, keep_ref, send_ref, keep_out, send_out):
    keep_out[...] = keep_ref[...]
    send_out[...] = send_ref[...]


def pack_rows(where, x, y, steps):
    part = x.shape[1] // (2 * steps)
    if part % 128:
        halves = jnp.transpose(x.reshape(ROWS, steps, 2, part), (2, 1, 0, 3))
        return [lax.dynamic_index_in_dim(halves, i, axis=0, keepdims=False) for i in (y, 1 - y)]
    out = pl.BlockSpec((None, ROWS, part), lambda z, w: (z, 0, 0))
    return pl.pallas_call(
        pack_rows_kernel,
        grid_spec=pltpu.PrefetchScalarGridSpec(
            num_scalar_prefetch=1,
            grid=(steps,),
            in_specs=[
                pl.BlockSpec((ROWS, part), lambda z, w: (0, 2 * z + w[1])),
                pl.BlockSpec((ROWS, part), lambda z, w: (0, 2 * z + 1 - w[1])),
            ],
            out_specs=[out, out],
        ),
        out_shape=[jax.ShapeDtypeStruct((steps, ROWS, part), x.dtype)] * 2,
        cost_estimate=HINT,
        name="pack_rows",
    )(where, x, x)


def pack_weight_kernel(chunks, where, own_ref, got_ref, *outs):
    rows = own_ref.shape[0]
    helped, direct = row_split(2 * rows)
    core, plane = where[2], where[3]
    own_place = pl.ds(pl.multiple_of(core * rows, 16), rows)
    got_place = pl.ds(pl.multiple_of((1 - core) * rows, 16), rows)
    direct_place = pl.ds(pl.multiple_of(plane * helped, 16), direct)
    for i, (head, heads) in enumerate(chunks):
        columns = slice(head * HD, (head + heads) * HD)
        whole, far = outs[2 * i], outs[2 * i + 1]
        whole[own_place, :] = own_ref[:, columns]
        whole[got_place, :] = got_ref[:, columns]
        far[...] = whole[direct_place, :]


def row_split(rows):
    helped = rows * 2 // 5
    return helped, rows - helped


def pack_weight(where, own, got, chunks):
    rows = own.shape[0]
    shapes = []
    for _, heads in chunks:
        shapes.append(jax.ShapeDtypeStruct((2 * rows, heads * HD), own.dtype))
        shapes.append(jax.ShapeDtypeStruct((row_split(2 * rows)[1], heads * HD), own.dtype))
    outs = pl.pallas_call(
        functools.partial(pack_weight_kernel, chunks),
        grid_spec=pltpu.PrefetchScalarGridSpec(
            num_scalar_prefetch=1,
            grid=(1,),
            in_specs=[pl.BlockSpec((rows, KVH * HD), lambda i, w: (0, 0))] * 2,
            out_specs=[pl.BlockSpec(shape.shape, lambda i, w: (0, 0)) for shape in shapes],
        ),
        out_shape=shapes,
        cost_estimate=HINT,
        name="pack_weight",
    )(where, own, got)
    return outs[0::2], outs[1::2]


def project_kernel(steps, where, *refs):
    groups, refs = refs[:4], refs[4:]
    near, direct, forwarded, outs, whole = refs[:2], refs[2:steps], refs[steps], refs[steps + 1 : -1], refs[-1]
    plane = where[3]
    total = None
    for j in range(steps):
        if j < 2:
            weight = near[j][...]
        else:
            count, extra = direct[j - 2].shape[0], forwarded.shape[1]
            whole[j - 2, pl.ds(pl.multiple_of(plane * extra, 16), count), :] = direct[j - 2][...]
            whole[j - 2, pl.ds(pl.multiple_of((1 - plane) * count, 16), extra), :] = forwarded[j - 2]
            weight = whole[j - 2]
        place = where[0] ^ j
        left = jnp.concatenate([group[place] for group in groups], axis=0)
        product = jnp.dot(left, weight, preferred_element_type=jnp.float32)
        total = product if total is None else total + product
    for i, out in enumerate(outs):
        out[...] = total[i * ROWS : (i + 1) * ROWS]


def project(where, groups, near, direct, forwarded):
    steps = 2 + len(direct)
    rows, columns = near[0].shape
    operands = [*groups, *near, *direct, forwarded]
    out = jax.ShapeDtypeStruct((ROWS, columns), jnp.float32)

    def full(array):
        return pl.BlockSpec(array.shape, lambda i, w: (0,) * len(array.shape))

    return pl.pallas_call(
        functools.partial(project_kernel, steps),
        grid_spec=pltpu.PrefetchScalarGridSpec(
            num_scalar_prefetch=1,
            grid=(1,),
            in_specs=[full(array) for array in operands],
            out_specs=[full(out)] * 4,
            scratch_shapes=[pltpu.VMEM((steps - 2, rows, columns), jnp.bfloat16)],
        ),
        out_shape=[out] * 4,
        compiler_params=pltpu.CompilerParams(vmem_limit_bytes=32 * 2**20),
        cost_estimate=HINT,
        name="project",
    )(where, *operands)


def final_kernel(info, gain_ref, q_ref, here_a, here_b, there_a, there_b, acc_ref, ml_ref, *refs):
    out_ref = refs[-1]
    here = here_a[...] + here_b[...]
    there = there_a[...] + there_b[...]
    first_core = jnp.full(here.shape, info[2]) == 0
    raw = jnp.where(first_core, here, there)
    mean = jnp.mean(raw * raw, axis=1, keepdims=True)
    keys = (raw * lax.rsqrt(mean + 1e-06) * gain_ref[...]).astype(jnp.bfloat16)
    values = jnp.where(first_core, there, here).T.astype(jnp.bfloat16)
    slot = lax.broadcasted_iota(jnp.int32, (ROWS, PAIR), 0)
    row = lax.broadcasted_iota(jnp.int32, (ROWS, PAIR), 1) % ROWS
    length = jnp.where(row < RLEN, info[0], info[1])
    base = jnp.where(row < RLEN, 0, RLEN)
    seen = (slot >= base) & (slot <= row) & (slot - base < length)
    live = jnp.where(row - base < length, 1.0, 0.0)[0:1]
    for g in range(0, SHARED, 2):
        cols = slice(g * HD, (g + 2) * HD)
        scores = jnp.where(seen, pair_scores(keys, q_ref, g), HIDDEN)
        before = ml_ref[0:1, cols]
        largest = jnp.maximum(jnp.max(scores, axis=0, keepdims=True), before)
        faded = jnp.exp2(before - largest)
        weights = jnp.exp2(scores - largest)
        total = jnp.sum(weights, axis=0, keepdims=True) + faded * ml_ref[1:2, cols]
        acc = jnp.dot(values, weights.astype(jnp.bfloat16), preferred_element_type=jnp.float32)
        acc = (acc + faded * acc_ref[:, cols]) * (live / total)
        out_ref[:, g * HD : (g + 1) * HD] = acc[:, :ROWS].T.astype(jnp.bfloat16)
        out_ref[:, (g + 1) * HD : (g + 2) * HD] = acc[:, ROWS:].T.astype(jnp.bfloat16)


def final_attention(info, gain, query, sums, state, offset, chunk, result):
    head, heads = chunk
    wide = pl.BlockSpec((ROWS, GROUP), lambda k, s: (0, head + k))
    part = pl.BlockSpec((ROWS, HD), lambda k, s: (0, k))
    operands = [gain, query, *sums, *state]
    specs = [
        pl.BlockSpec((1, HD), lambda k, s: (0, 0)),
        wide,
        part,
        part,
        part,
        part,
        pl.BlockSpec((HD, SHARED * ROWS), lambda k, s: (0, offset + k)),
        pl.BlockSpec((8, SHARED * ROWS), lambda k, s: (0, offset + k)),
    ]
    aliases = {}
    if result is not None:
        operands.append(result)
        specs.append(pl.BlockSpec(memory_space=pl.ANY))
        aliases = {len(operands): 0}
    return pl.pallas_call(
        final_kernel,
        grid_spec=pltpu.PrefetchScalarGridSpec(
            num_scalar_prefetch=1, grid=(heads,), in_specs=specs, out_specs=wide
        ),
        out_shape=jax.ShapeDtypeStruct((ROWS, HQ * HD), jnp.bfloat16),
        input_output_aliases=aliases,
        compiler_params=pltpu.CompilerParams(vmem_limit_bytes=32 * 2**20),
        cost_estimate=HINT,
        name="final_attention",
    )(info, *operands)


def xor_swap(array, axis, by):
    return lax.ppermute(array, axis, [(i, i ^ by) for i in range(lax.axis_size(axis))])


CHUNKS = ((0, 2), (2, 1), (3, 1))
HALVES = ((0, 2), (2, 2))


def per_device(
    x_resp, queries, prompt_cache, kv_weight, key_gain, prompt_lengths, block_table, resp_lengths
):
    x, query = x_resp[0], queries[0]
    steps = lax.axis_size("z")
    z, y, core = lax.axis_index("z"), lax.axis_index("y"), lax.axis_index("core")
    holder, cycle = lax.axis_index("blk"), lax.axis_size("blk")
    plane = holder % 2
    where = jnp.stack([z, y, core, plane]).astype(jnp.int32)

    caches = [prompt_cache[0]]
    for _ in range(cycle - 1):
        caches.append(lax.ppermute(caches[-1], "blk", [(i, (i + 1) % cycle) for i in range(cycle)]))

    half = KVH * HD
    own = lax.dynamic_slice_in_dim(kv_weight, core * half, half, axis=1)
    got = xor_swap(lax.dynamic_slice_in_dim(kv_weight, (1 - core) * half, half, axis=1), "core", 1)
    whole, far = pack_weight(where, own, got, CHUNKS)
    helped, direct = row_split(2 * kv_weight.shape[0])

    def send(chunk, whole, far):
        pieces = [xor_swap(far, "z", j) for j in range(steps - 1, 1, -1)][::-1]
        return xor_swap(whole, "z", 1), pieces

    def forward(pieces):
        parts = [lax.dynamic_slice_in_dim(p, plane * (direct - helped), helped, axis=0) for p in pieces]
        return xor_swap(jnp.stack(parts), "blk", 1)

    sent = [send(0, whole[0], far[0])]
    query, _ = lax.optimization_barrier((query, whole[0]))
    keep, other = pack_rows(where, x, y, steps)
    other = xor_swap(other, "y", 1)
    groups = [keep, other, xor_swap(keep, "core", 1), xor_swap(other, "core", 1)]

    infos = []
    for stride in range(cycle):
        owner = lax.rem(holder + cycle - stride, cycle)
        place = owner * prompt_cache.shape[1]
        listed = lax.dynamic_index_in_dim(block_table[0], place // BLOCK, axis=1, keepdims=False)
        infos.append(jnp.concatenate([place[None], prompt_lengths, listed]).astype(jnp.int32))

    states = [prompt_attention(infos[0], query, caches[0], None, *heads) for heads in HALVES]

    def rest(i):
        for stride in range(1, cycle):
            states[i] = prompt_attention(infos[stride], query, caches[stride], states[i], *HALVES[i])

    sent[0], ahead, states = lax.optimization_barrier((sent[0], (whole[1], far[1]), states))
    forwarded = [forward(sent[0][1])]
    sent.append(send(1, *ahead))
    rest(0)
    sent[1], ahead, states[0] = lax.optimization_barrier((sent[1], (whole[2], far[2]), states[0]))
    forwarded.append(forward(sent[1][1]))
    sent.append(send(2, *ahead))
    rest(1)
    sent[2], states[1] = lax.optimization_barrier((sent[2], states[1]))
    forwarded.append(forward(sent[2][1]))

    info = jnp.concatenate([resp_lengths[0], core[None]]).astype(jnp.int32)
    result = None
    for i, chunk in enumerate(CHUNKS):
        near, pieces = sent[i]
        sums = project(where, groups, [whole[i], near], pieces, forwarded[i])
        sums = [
            sums[0],
            xor_swap(sums[1], "y", 1),
            xor_swap(sums[2], "core", 1),
            xor_swap(sums[3], ("y", "core"), 3),
        ]
        at = [n for n, (head, heads) in enumerate(HALVES) if head <= chunk[0] < head + heads][0]
        result = final_attention(
            info, key_gain[None], query, sums, states[at], chunk[0] - HALVES[at][0], chunk, result
        )
    return result[None]


def solution(mesh):
    groups, blocks = mesh.devices.shape
    split = Mesh(mesh.devices.reshape(groups // 4, 2, 2, blocks), ("z", "y", "core", "blk"))
    fsdp = ("z", "y", "core")
    return jax.shard_map(
        per_device,
        mesh=split,
        in_specs=(
            P(fsdp, "blk", None),
            P(fsdp, "blk", None),
            P(fsdp, "blk", None),
            P(fsdp, None),
            P(),
            P(fsdp),
            P(fsdp, "blk", None),
            P(fsdp, "blk"),
        ),
        out_specs=P(fsdp, "blk", None),
        check_vma=False,
    )
```

time: 104 us -> 86.6 us (0.83)
  waiting for transfers between devices: 46 us -> 18.9 us
  starting transfers between devices: 6.07 us -> 23 us
  Pallas kernels: 25.7 us -> 39.6 us
  between operations: 14.1 us -> 0.89 us
  local copies, waits for them, and re-layouts: 11.7 us -> 3.03 us
    all_gather x1 -> x0, waiting for transfers between devices: 21.5 us -> none  [per_device(): same = lax.all_gather(kv_weight, 'z', axis=0, tiled=True)]
    ppermute x4 -> x26, starting transfers between devices: 6.07 us -> 23 us  [the longest x25 20 us: xor_swap(): lax.ppermute(array, axis, [(i, i ^ by) for i in range(lax.axis_size(axis))])]
    pallas_call x1 -> x5, Pallas kernels: 3.61 us -> 14.7 us  [the longest x3 7.55 us: project(): pl.pallas_call(functools.partial(project_kernel, steps), grid_spec=pltpu....]
    unnamed x25 -> x26, local copies, waits for them, and re-layouts: 10.6 us -> 0.79 us
    ppermute x4 -> x26, waiting for transfers between devices: 23.7 us -> 18.9 us  [the longest x25 18.9 us: xor_swap(): lax.ppermute(array, axis, [(i, i ^ by) for i in range(lax.axis_size(axis))])]
    pallas_call x1 -> x3, Pallas kernels: 4.96 us -> 7.19 us  [final_attention(): pl.pallas_call(final_kernel, grid_spec=pltpu.PrefetchScalarGridSpec(num_s...]
    dynamic_slice x1 -> x2, local copies, waits for them, and re-layouts: 0.21 us -> 2.19 us  [the longest x1 1.97 us: per_device(): lax.dynamic_slice_in_dim(kv_weight, (1 - core) * half, half, axis=1)]
    pallas_call x2 -> x4, Pallas kernels: 17.2 us -> 17.7 us  [prompt_attention(): pl.pallas_call(functools.partial(prompt_kernel, first), grid_spec=pltpu.P...]
  transfers between devices with their start and end apart: 5 -> 26, of which waited for: 4 -> 7; matrix products, arithmetic and copies ran while one was open for 5% -> 4% of each run, Pallas kernels for 17% -> 44%
where the time goes in v3:
time: 86.6 us; the launch traced here: 86.2 us
  Pallas kernels  39.6 us (46%)
  starting transfers between devices  23 us (27%)
  waiting for transfers between devices  18.9 us (22%)
  local copies, waits for them, and re-layouts  3.03 us (3%)
  between operations  0.89 us (1%)
  other arithmetic  0.88 us (1%)
    ppermute x25, starting transfers between devices, xor_swap(): lax.ppermute(array, axis, [(i, i ^ by) for i in range(lax.axis_size(axis))])  20 us
    ppermute x25, waiting for transfers between devices, xor_swap(): lax.ppermute(array, axis, [(i, i ^ by) for i in range(lax.axis_size(axis))])  18.9 us
    pallas_call x4, Pallas kernels, prompt_attention(): pl.pallas_call(functools.partial(prompt_kernel, first), grid_spec=pltpu.P...  17.7 us
    pallas_call x3, Pallas kernels, project(): pl.pallas_call(functools.partial(project_kernel, steps), grid_spec=pltpu....  7.55 us
    pallas_call x3, Pallas kernels, final_attention(): pl.pallas_call(final_kernel, grid_spec=pltpu.PrefetchScalarGridSpec(num_s...  7.19 us
    pallas_call x1, Pallas kernels, pack_rows(): pl.pallas_call(pack_rows_kernel, grid_spec=pltpu.PrefetchScalarGridSpec(n...  4.34 us
    ppermute x1, starting transfers between devices, per_device(): lax.ppermute(caches[-1], 'blk', [(i, (i + 1) % cycle) for i in range(cycl...  2.94 us
    pallas_call x1, Pallas kernels, pack_weight(): pl.pallas_call(functools.partial(pack_weight_kernel, chunks), grid_spec=p...  2.79 us
  transfers between devices with their start and end apart: 26, of which 7 were waited for; matrix products, arithmetic and copies ran while one was open for 4% of the time, Pallas kernels for 44%

profile of v3, /device:TPU:0, one launch (start us, length us, event | category | flops | bytes accessed | tf_op | source)
XLA Modules:
  0.0 86.2 jit_solution(7856960324333938994)
XLA Ops:
  0.0 2.9 %collective-permute-start.10 = (bf16[512,1024]{1,0:T(8,128)(2,1)}, bf16[512,1024]{1,0:T(8,128)(2,1)S(1)}, u32[]{:S(2)}, u32[]{:S(2)}) collective-permute-start(bf16[512,1024]{1,0:T(8,128)(2,1)} %bitcast.31), channel_id=1, source_target_pairs={{0,1},{1,0},{2,3},{3,2},{4,5},{5,4},{6,7},{7,6},{8,9},{9,8},{10,11... | collective-permute-start | bytes 3145736 | tf_op jit(solution)/shard_map/ppermute | solution.py:291
  2.9 2.0 %constant_dynamic-slice_fusion.2 = (bf16[320,512]{1,0:T(8,128)(2,1)}, bf16[320,512]{1,0:T(8,128)(2,1)}) fusion(bf16[320,1024]{1,0:T(8,128)(2,1)} %param.11, s32[]{:T(128)S(6)} %select_n.37, s32[]{:T(128)S(6)} %select_n.36), kind=kLoop, calls=%fused_computation.11 | loop fusion | bytes 1310728 | tf_op jit(solution)/shard_map/dynamic_slice | solution.py:295
  5.5 4.3 %pack_rows.1 = (bf16[4,128,640]{2,1,0:T(8,128)(2,1)}, bf16[4,128,640]{2,1,0:T(8,128)(2,1)}) custom-call(s32[4]{0:T(128)} %pad_add_fusion.1.where, bf16[128,5120]{1,0:T(8,128)(2,1)} %bitcast.39, bf16[128,5120]{1,0:T(8,128)(2,1)} %bitcast.40), custom_call_target="tpu_custom_call" | custom-call | flops 1024 | bytes 1024 | tf_op jit(solution)/shard_map/pack_rows/pallas_call | solution.py:105
  9.9 1.5 %collective-permute-start.1 = (bf16[4,128,640]{2,1,0:T(8,128)(2,1)}, bf16[4,128,640]{2,1,0:T(8,128)(2,1)}, u32[]{:S(2)}, u32[]{:S(2)}) collective-permute-start(bf16[4,128,640]{2,1,0:T(8,128)(2,1)} %get-tuple-element.58), channel_id=1, source_target_pairs={{0,4},{4,0},{1,5},{5,1},{2,6},{6,2},{3,7},{7,3},{8,12},{12,8},{9,1... | collective-permute-start | bytes 1966088 | tf_op jit(solution)/shard_map/ppermute | solution.py:272
  12.1 2.8 %pack_weight.1 = (bf16[640,256]{1,0:T(8,128)(2,1)}, bf16[384,256]{1,0:T(8,128)(2,1)}, bf16[640,128]{1,0:T(8,128)(2,1)}, bf16[384,128]{1,0:T(8,128)(2,1)}, bf16[6...) custom-call(s32[4]{0:T(128)} %pad_add_fusion.1.where, bf16[320,512]{1,0:T(8,128)(2,1)} %get-tuple-element.108.own_ref, ...), custom_call_target="tpu_custom_call" | custom-call | flops 1024 | bytes 1024 | tf_op jit(solution)/shard_map/pack_weight/pallas_call | solution.py:148
  14.9 1.6 %collective-permute-start.4 = (bf16[640,256]{1,0:T(8,128)(2,1)}, bf16[640,256]{1,0:T(8,128)(2,1)S(1)}, u32[]{:S(2)}, u32[]{:S(2)}) collective-permute-start(bf16[640,256]{1,0:T(8,128)(2,1)} %get-tuple-element.55.refs_4_), channel_id=1, source_target_pairs={{0,8},{8,0},{16,24},{24,16},{1,9},{9,1},{17,25},{25,17},{2,10},{10... | collective-permute-start | bytes 983048 | tf_op jit(solution)/shard_map/ppermute | solution.py:272
  17.4 2.5 %collective-permute-start.6 = (bf16[384,256]{1,0:T(8,128)(2,1)}, bf16[384,256]{1,0:T(8,128)(2,1)S(1)}, u32[]{:S(2)}, u32[]{:S(2)}) collective-permute-start(bf16[384,256]{1,0:T(8,128)(2,1)} %get-tuple-element.60), channel_id=1, source_target_pairs={{0,24},{8,16},{16,8},{24,0},{1,25},{9,17},{17,9},{25,1},{2,26},{10... | collective-permute-start | bytes 589832 | tf_op jit(solution)/shard_map/ppermute | solution.py:272
  20.3 4.4 %prompt_attention.5 = (f32[128,2048]{1,0:T(8,128)S(1)}, f32[8,2048]{1,0:T(8,128)S(1)}) custom-call(s32[4]{0:T(128)S(1)} %pad_add_fusion.2.info, bf16[128,4096]{1,0:T(8,128)(2,1)S(1)} %bitcast.24, bf16[512,1024]{1,0:T(8,128)(2,1)S(1)} %bitcast.32, bf16[512,1024]{1,0:T(8,128)(2,1)S(1)} %bitcast.33), custom_call_target="tpu_custom_call" | custom-call | flops 1024 | bytes 1024 | tf_op jit(solution)/shard_map/prompt_attention/pallas_call | solution.py:79
  24.7 4.4 %prompt_attention.4 = (f32[128,2048]{1,0:T(8,128)S(1)}, f32[8,2048]{1,0:T(8,128)S(1)}) custom-call(s32[4]{0:T(128)S(1)} %pad_add_fusion.2.info, bf16[128,4096]{1,0:T(8,128)(2,1)S(1)} %bitcast.25, bf16[512,1024]{1,0:T(8,128)(2,1)S(1)} %bitcast.34, bf16[512,1024]{1,0:T(8,128)(2,1)S(1)} %bitcast.35), custom_call_target="tpu_custom_call" | custom-call | flops 1024 | bytes 1024 | tf_op jit(solution)/shard_map/prompt_attention/pallas_call | solution.py:79
  29.1 2.9 %collective-permute-done.6.refs_7_ = bf16[384,256]{1,0:T(8,128)(2,1)S(1)} collective-permute-done((bf16[384,256]{1,0:T(8,128)(2,1)}, bf16[384,256]{1,0:T(8,128)(2,1)S(1)}, u32[]{:S(2)}, u32[]{:S(2)}) %collective-permute-start.6) | collective-permute-done | bytes 196640 | tf_op jit(solution)/shard_map/ppermute | solution.py:272
  32.0 5.9 %collective-permute-done.5.refs_6_ = bf16[384,256]{1,0:T(8,128)(2,1)S(1)} collective-permute-done((bf16[384,256]{1,0:T(8,128)(2,1)}, bf16[384,256]{1,0:T(8,128)(2,1)S(1)}, u32[]{:S(2)}, u32[]{:S(2)}) %collective-permute-start.5) | collective-permute-done | bytes 196640 | tf_op jit(solution)/shard_map/ppermute | solution.py:272
  37.9 2.6 %collective-permute-start.9 = (bf16[384,128]{1,0:T(8,128)(2,1)S(1)}, bf16[384,128]{1,0:T(8,128)(2,1)S(1)}, u32[]{:S(2)}, u32[]{:S(2)}) collective-permute-start(bf16[384,128]{1,0:T(8,128)(2,1)S(1)} %copy-done.11), channel_id=1, source_target_pairs={{0,24},{8,16},{16,8},{24,0},{1,25},{9,17},{17,9},{25,1},{2,26},{10... | collective-permute-start | bytes 294920 | tf_op jit(solution)/shard_map/ppermute | solution.py:272
  40.7 1.7 %collective-permute-start.8 = (bf16[384,128]{1,0:T(8,128)(2,1)S(1)}, bf16[384,128]{1,0:T(8,128)(2,1)S(1)}, u32[]{:S(2)}, u32[]{:S(2)}) collective-permute-start(bf16[384,128]{1,0:T(8,128)(2,1)S(1)} %copy-done.11), channel_id=1, source_target_pairs={{0,16},{8,24},{16,0},{24,8},{1,17},{9,25},{17,1},{25,9},{2,18},{10... | collective-permute-start | bytes 294920 | tf_op jit(solution)/shard_map/ppermute | solution.py:272
  42.4 4.5 %prompt_attention.6 = (f32[128,2048]{1,0:T(8,128)S(1)}, f32[8,2048]{1,0:T(8,128)S(1)}) custom-call(s32[4]{0:T(128)S(1)} %pad_add_fusion.3.info, bf16[128,4096]{1,0:T(8,128)(2,1)S(1)} %bitcast.26, bf16[512,1024]{1,0:T(8,128)(2,1)S(1)} %collective-permute-done.10.k_ref.v_ref, bf16[512,1024]{1,0:T(8,128)(2,1)S(1)} %collective-permute-done.10.k_ref.v_ref, ...), custom_call_target="tpu_custom_call" | custom-call | flops 1024 | bytes 1024 | tf_op jit(solution)/shard_map/prompt_attention/pallas_call | solution.py:79
  49.5 1.6 %collective-permute-start.13 = (bf16[384,128]{1,0:T(8,128)(2,1)S(1)}, bf16[384,128]{1,0:T(8,128)(2,1)S(1)}, u32[]{:S(2)}, u32[]{:S(2)}) collective-permute-start(bf16[384,128]{1,0:T(8,128)(2,1)S(1)} %copy-done.10), channel_id=1, source_target_pairs={{0,24},{8,16},{16,8},{24,0},{1,25},{9,17},{17,9},{25,1},{2,26},{10... | collective-permute-start | bytes 294920 | tf_op jit(solution)/shard_map/ppermute | solution.py:272
  51.4 5.6 %collective-permute-done.13.refs_7_ = bf16[384,128]{1,0:T(8,128)(2,1)S(1)} collective-permute-done((bf16[384,128]{1,0:T(8,128)(2,1)S(1)}, bf16[384,128]{1,0:T(8,128)(2,1)S(1)}, u32[]{:S(2)}, u32[]{:S(2)}) %collective-permute-start.13) | collective-permute-done | bytes 98336 | tf_op jit(solution)/shard_map/ppermute | solution.py:272
  57.1 4.5 %prompt_attention.7 = (f32[128,2048]{1,0:T(8,128)S(1)}, f32[8,2048]{1,0:T(8,128)S(1)}) custom-call(s32[4]{0:T(128)S(1)} %pad_add_fusion.3.info, bf16[128,4096]{1,0:T(8,128)(2,1)S(1)} %bitcast.27, bf16[512,1024]{1,0:T(8,128)(2,1)S(1)} %collective-permute-done.10.k_ref.v_ref, bf16[512,1024]{1,0:T(8,128)(2,1)S(1)} %collective-permute-done.10.k_ref.v_ref, ...), custom_call_target="tpu_custom_call" | custom-call | flops 1024 | bytes 1024 | tf_op jit(solution)/shard_map/prompt_attention/pallas_call | solution.py:79
  64.7 2.6 %project.5 = (f32[128,256]{1,0:T(8,128)S(1)}, f32[128,256]{1,0:T(8,128)S(1)}, f32[128,256]{1,0:T(8,128)S(1)}, f32[128,256]{1,0:T(8,128)S(1)}) custom-call(s32[4]{0:T(128)S(1)} %copy-done.6, bf16[4,128,640]{2,1,0:T(8,128)(2,1)S(1)} %copy-done.2, bf16[4,128,640]{2,1,0:T(8,128)(2,1)} %collective-permute-done.1.refs_1_, ...), custom_call_target="tpu_custom_call" | custom-call | flops 1024 | bytes 1024 | tf_op jit(solution)/shard_map/project/pallas_call | solution.py:193
  67.9 1.6 %collective-permute-start.25 = (f32[128,256]{1,0:T(8,128)S(1)}, f32[128,256]{1,0:T(8,128)S(1)}, u32[]{:S(2)}, u32[]{:S(2)}) collective-permute-start(f32[128,256]{1,0:T(8,128)S(1)} %get-tuple-element.102), channel_id=1, source_target_pairs={{0,6},{2,4},{4,2},{6,0},{1,7},{3,5},{5,3},{7,1},{8,14},{10,12},{12... | collective-permute-start | bytes 393224 | tf_op jit(solution)/shard_map/ppermute | solution.py:272
  69.6 2.5 %project.4 = (f32[128,128]{1,0:T(8,128)S(1)}, f32[128,128]{1,0:T(8,128)S(1)}, f32[128,128]{1,0:T(8,128)S(1)}, f32[128,128]{1,0:T(8,128)S(1)}) custom-call(s32[4]{0:T(128)S(1)} %copy-done.6, bf16[4,128,640]{2,1,0:T(8,128)(2,1)S(1)} %copy-done.2, bf16[4,128,640]{2,1,0:T(8,128)(2,1)} %collective-permute-done.1.refs_1_, ...), custom_call_target="tpu_custom_call" | custom-call | flops 1024 | bytes 1024 | tf_op jit(solution)/shard_map/project/pallas_call | solution.py:193
  72.6 2.5 %project.3 = (f32[128,128]{1,0:T(8,128)S(1)}, f32[128,128]{1,0:T(8,128)S(1)}, f32[128,128]{1,0:T(8,128)S(1)}, f32[128,128]{1,0:T(8,128)S(1)}) custom-call(s32[4]{0:T(128)S(1)} %copy-done.6, bf16[4,128,640]{2,1,0:T(8,128)(2,1)S(1)} %copy-done.2, bf16[4,128,640]{2,1,0:T(8,128)(2,1)} %collective-permute-done.1.refs_1_, ...), custom_call_target="tpu_custom_call" | custom-call | flops 1024 | bytes 1024 | tf_op jit(solution)/shard_map/project/pallas_call | solution.py:193
  79.0 3.1 %final_attention.3.refs_0_ = bf16[128,4096]{1,0:T(8,128)(2,1)} custom-call(s32[3]{0:T(128)S(1)} %pad_add_fusion.info, f32[1,128]{1,0:T(1,128)S(1)} %bitcast.36, bf16[128,4096]{1,0:T(8,128)(2,1)S(1)} %bitcast.28, f32[128,256]{1,0:T(8,128)S(1)} %get-tuple-element.99.here_a, f32[128,256]{1,0:T(8,128)S(1)} %collective-permute-done.23.here_b, ...), custom_call_target="tpu_custom_call" | custom-call | flops 1024 | bytes 1024 | tf_op jit(solution)/shard_map/final_attention/pallas_call | solution.py:258
  82.1 2.1 %final_attention.4.refs_0_ = bf16[128,4096]{1,0:T(8,128)(2,1)} custom-call(s32[3]{0:T(128)S(1)} %pad_add_fusion.info, f32[1,128]{1,0:T(1,128)S(1)} %bitcast.37, bf16[128,4096]{1,0:T(8,128)(2,1)S(1)} %bitcast.29, f32[128,128]{1,0:T(8,128)S(1)} %get-tuple-element.92.here_a, ...), custom_call_target="tpu_custom_call", output_to_operand_aliasing={{}: (9, {})} | custom-call | flops 1024 | bytes 1024 | tf_op jit(solution)/shard_map/final_attention/pallas_call | solution.py:258
  84.2 2.1 %final_attention.5 = bf16[128,4096]{1,0:T(8,128)(2,1)} custom-call(s32[3]{0:T(128)S(1)} %pad_add_fusion.info, f32[1,128]{1,0:T(1,128)S(1)} %bitcast.38, bf16[128,4096]{1,0:T(8,128)(2,1)S(1)} %bitcast.30, f32[128,128]{1,0:T(8,128)S(1)} %get-tuple-element.83.here_a, f32[128,128]{1,0:T(8,128)S(1)} %collective-permute-done.15.here_b, ...), custom_call_target="tpu_custom_call", output_to_operand_aliasing={{}: (9, {})} | custom-call | flops 1024 | bytes 1024 | tf_op jit(solution)/shard_map/final_attention/pallas_call | solution.py:258
  (78 shorter events, 13.1 us)
Async XLA Ops:
  0.0 40.7 %collective-permute-start.10 = (bf16[512,1024]{1,0:T(8,128)(2,1)}, bf16[512,1024]{1,0:T(8,128)(2,1)S(1)}, u32[]{:S(2)}, u32[]{:S(2)}) collective-permute-start(bf16[512,1024]{1,0:T(8,128)(2,1)} %bitcast.31), channel_id=1, source_target_pairs={{0,1},{1,0},{2,3},{3,2},{4,5},{5,4},{6,7},{7,6},{8,9},{9,8},{10,11... | collective-permute-start | bytes 3145736 | tf_op jit(solution)/shard_map/ppermute | solution.py:291
  4.9 6.5 %collective-permute-start = (bf16[320,512]{1,0:T(8,128)(2,1)}, bf16[320,512]{1,0:T(8,128)(2,1)S(1)}, u32[]{:S(2)}, u32[]{:S(2)}) collective-permute-start(bf16[320,512]{1,0:T(8,128)(2,1)} %get-tuple-element.107), channel_id=1, source_target_pairs={{0,2},{2,0},{1,3},{3,1},{4,6},{6,4},{5,7},{7,5},{8,10},{10,8},{9,1... | collective-permute-start | bytes 983048 | tf_op jit(solution)/shard_map/ppermute | solution.py:272
  9.9 30.7 %collective-permute-start.1 = (bf16[4,128,640]{2,1,0:T(8,128)(2,1)}, bf16[4,128,640]{2,1,0:T(8,128)(2,1)}, u32[]{:S(2)}, u32[]{:S(2)}) collective-permute-start(bf16[4,128,640]{2,1,0:T(8,128)(2,1)} %get-tuple-element.58), channel_id=1, source_target_pairs={{0,4},{4,0},{1,5},{5,1},{2,6},{6,2},{3,7},{7,3},{8,12},{12,8},{9,1... | collective-permute-start | bytes 1966088 | tf_op jit(solution)/shard_map/ppermute | solution.py:272
  14.9 23.0 %collective-permute-start.4 = (bf16[640,256]{1,0:T(8,128)(2,1)}, bf16[640,256]{1,0:T(8,128)(2,1)S(1)}, u32[]{:S(2)}, u32[]{:S(2)}) collective-permute-start(bf16[640,256]{1,0:T(8,128)(2,1)} %get-tuple-element.55.refs_4_), channel_id=1, source_target_pairs={{0,8},{8,0},{16,24},{24,16},{1,9},{9,1},{17,25},{25,17},{2,10},{10... | collective-permute-start | bytes 983048 | tf_op jit(solution)/shard_map/ppermute | solution.py:272
  17.4 14.6 %collective-permute-start.6 = (bf16[384,256]{1,0:T(8,128)(2,1)}, bf16[384,256]{1,0:T(8,128)(2,1)S(1)}, u32[]{:S(2)}, u32[]{:S(2)}) collective-permute-start(bf16[384,256]{1,0:T(8,128)(2,1)} %get-tuple-element.60), channel_id=1, source_target_pairs={{0,24},{8,16},{16,8},{24,0},{1,25},{9,17},{17,9},{25,1},{2,26},{10... | collective-permute-start | bytes 589832 | tf_op jit(solution)/shard_map/ppermute | solution.py:272
  19.9 18.0 %collective-permute-start.5 = (bf16[384,256]{1,0:T(8,128)(2,1)}, bf16[384,256]{1,0:T(8,128)(2,1)S(1)}, u32[]{:S(2)}, u32[]{:S(2)}) collective-permute-start(bf16[384,256]{1,0:T(8,128)(2,1)} %get-tuple-element.60), channel_id=1, source_target_pairs={{0,16},{8,24},{16,0},{24,8},{1,17},{9,25},{17,1},{25,9},{2,18},{10... | collective-permute-start | bytes 589832 | tf_op jit(solution)/shard_map/ppermute | solution.py:272
  32.0 32.7 %collective-permute-start.2 = (bf16[4,128,640]{2,1,0:T(8,128)(2,1)S(1)}, bf16[4,128,640]{2,1,0:T(8,128)(2,1)S(1)}, u32[]{:S(2)}, u32[]{:S(2)}) collective-permute-start(bf16[4,128,640]{2,1,0:T(8,128)(2,1)S(1)} %copy-done.2), channel_id=1, source_target_pairs={{0,2},{2,0},{1,3},{3,1},{4,6},{6,4},{5,7},{7,5},{8,10},{10,8},{9,1... | collective-permute-start | bytes 1966088 | tf_op jit(solution)/shard_map/ppermute | solution.py:272
  37.9 9.0 %collective-permute-start.9 = (bf16[384,128]{1,0:T(8,128)(2,1)S(1)}, bf16[384,128]{1,0:T(8,128)(2,1)S(1)}, u32[]{:S(2)}, u32[]{:S(2)}) collective-permute-start(bf16[384,128]{1,0:T(8,128)(2,1)S(1)} %copy-done.11), channel_id=1, source_target_pairs={{0,24},{8,16},{16,8},{24,0},{1,25},{9,17},{17,9},{25,1},{2,26},{10... | collective-permute-start | bytes 294920 | tf_op jit(solution)/shard_map/ppermute | solution.py:272
  40.5 9.0 %collective-permute-start.7 = (bf16[640,128]{1,0:T(8,128)(2,1)S(1)}, bf16[640,128]{1,0:T(8,128)(2,1)S(1)}, u32[]{:S(2)}, u32[]{:S(2)}) collective-permute-start(bf16[640,128]{1,0:T(8,128)(2,1)S(1)} %copy-done.5), channel_id=1, source_target_pairs={{0,8},{8,0},{16,24},{24,16},{1,9},{9,1},{17,25},{25,17},{2,10},{10... | collective-permute-start | bytes 491528 | tf_op jit(solution)/shard_map/ppermute | solution.py:272
  40.5 24.2 %collective-permute-start.3 = (bf16[4,128,640]{2,1,0:T(8,128)(2,1)}, bf16[4,128,640]{2,1,0:T(8,128)(2,1)S(1)}, u32[]{:S(2)}, u32[]{:S(2)}) collective-permute-start(bf16[4,128,640]{2,1,0:T(8,128)(2,1)} %collective-permute-done.1.refs_1_), channel_id=1, source_target_pairs={{0,2},{2,0},{1,3},{3,1},{4,6},{6,4},{5,7},{7,5},{8,10},{10,8},{9,1... | collective-permute-start | bytes 1966088 | tf_op jit(solution)/shard_map/ppermute | solution.py:272
  40.7 7.5 %collective-permute-start.8 = (bf16[384,128]{1,0:T(8,128)(2,1)S(1)}, bf16[384,128]{1,0:T(8,128)(2,1)S(1)}, u32[]{:S(2)}, u32[]{:S(2)}) collective-permute-start(bf16[384,128]{1,0:T(8,128)(2,1)S(1)} %copy-done.11), channel_id=1, source_target_pairs={{0,16},{8,24},{16,0},{24,8},{1,17},{9,25},{17,1},{25,9},{2,18},{10... | collective-permute-start | bytes 294920 | tf_op jit(solution)/shard_map/ppermute | solution.py:272
  46.9 17.8 %collective-permute-start.22 = (bf16[2,256,256]{2,1,0:T(8,128)(2,1)S(1)}, bf16[2,256,256]{2,1,0:T(8,128)(2,1)S(1)}, u32[]{:S(2)}, u32[]{:S(2)}) collective-permute-start(bf16[2,256,256]{2,1,0:T(8,128)(2,1)S(1)} %pad_maximum_fusion), channel_id=1, source_target_pairs={{0,1},{1,0},{2,3},{3,2},{4,5},{5,4},{6,7},{7,6},{8,9},{9,8},{10,11... | collective-permute-start | bytes 786440 | tf_op jit(solution)/shard_map/ppermute | solution.py:272
  49.5 7.5 %collective-permute-start.13 = (bf16[384,128]{1,0:T(8,128)(2,1)S(1)}, bf16[384,128]{1,0:T(8,128)(2,1)S(1)}, u32[]{:S(2)}, u32[]{:S(2)}) collective-permute-start(bf16[384,128]{1,0:T(8,128)(2,1)S(1)} %copy-done.10), channel_id=1, source_target_pairs={{0,24},{8,16},{16,8},{24,0},{1,25},{9,17},{17,9},{25,1},{2,26},{10... | collective-permute-start | bytes 294920 | tf_op jit(solution)/shard_map/ppermute | solution.py:272
  51.2 12.0 %collective-permute-start.11 = (bf16[640,128]{1,0:T(8,128)(2,1)S(1)}, bf16[640,128]{1,0:T(8,128)(2,1)S(1)}, u32[]{:S(2)}, u32[]{:S(2)}) collective-permute-start(bf16[640,128]{1,0:T(8,128)(2,1)S(1)} %copy-done.4), channel_id=1, source_target_pairs={{0,8},{8,0},{16,24},{24,16},{1,9},{9,1},{17,25},{25,17},{2,10},{10... | collective-permute-start | bytes 491528 | tf_op jit(solution)/shard_map/ppermute | solution.py:272
  62.6 7.0 %collective-permute-start.18 = (bf16[2,256,128]{2,1,0:T(8,128)(2,1)S(1)}, bf16[2,256,128]{2,1,0:T(8,128)(2,1)S(1)}, u32[]{:S(2)}, u32[]{:S(2)}) collective-permute-start(bf16[2,256,128]{2,1,0:T(8,128)(2,1)S(1)} %pad_maximum_fusion.2), channel_id=1, source_target_pairs={{0,1},{1,0},{2,3},{3,2},{4,5},{5,4},{6,7},{7,6},{8,9},{9,8},{10,11... | collective-permute-start | bytes 393224 | tf_op jit(solution)/shard_map/ppermute | solution.py:272
  63.2 9.4 %collective-permute-start.14 = (bf16[2,256,128]{2,1,0:T(8,128)(2,1)S(1)}, bf16[2,256,128]{2,1,0:T(8,128)(2,1)S(1)}, u32[]{:S(2)}, u32[]{:S(2)}) collective-permute-start(bf16[2,256,128]{2,1,0:T(8,128)(2,1)S(1)} %pad_maximum_fusion.1), channel_id=1, source_target_pairs={{0,1},{1,0},{2,3},{3,2},{4,5},{5,4},{6,7},{7,6},{8,9},{9,8},{10,11... | collective-permute-start | bytes 393224 | tf_op jit(solution)/shard_map/ppermute | solution.py:272
  67.3 9.5 %collective-permute-start.23 = (f32[128,256]{1,0:T(8,128)S(1)}, f32[128,256]{1,0:T(8,128)S(1)}, u32[]{:S(2)}, u32[]{:S(2)}) collective-permute-start(f32[128,256]{1,0:T(8,128)S(1)} %get-tuple-element.100), channel_id=1, source_target_pairs={{0,4},{4,0},{1,5},{5,1},{2,6},{6,2},{3,7},{7,3},{8,12},{12,8},{9,1... | collective-permute-start | bytes 393224 | tf_op jit(solution)/shard_map/ppermute | solution.py:272
  67.9 9.8 %collective-permute-start.24 = (f32[128,256]{1,0:T(8,128)S(1)}, f32[128,256]{1,0:T(8,128)S(1)}, u32[]{:S(2)}, u32[]{:S(2)}) collective-permute-start(f32[128,256]{1,0:T(8,128)S(1)} %get-tuple-element.101), channel_id=1, source_target_pairs={{0,2},{2,0},{1,3},{3,1},{4,6},{6,4},{5,7},{7,5},{8,10},{10,8},{9,1... | collective-permute-start | bytes 393224 | tf_op jit(solution)/shard_map/ppermute | solution.py:272
  67.9 10.5 %collective-permute-start.25 = (f32[128,256]{1,0:T(8,128)S(1)}, f32[128,256]{1,0:T(8,128)S(1)}, u32[]{:S(2)}, u32[]{:S(2)}) collective-permute-start(f32[128,256]{1,0:T(8,128)S(1)} %get-tuple-element.102), channel_id=1, source_target_pairs={{0,6},{2,4},{4,2},{6,0},{1,7},{3,5},{5,3},{7,1},{8,14},{10,12},{12... | collective-permute-start | bytes 393224 | tf_op jit(solution)/shard_map/ppermute | solution.py:272
  72.6 9.5 %collective-permute-start.20 = (f32[128,128]{1,0:T(8,128)S(1)}, f32[128,128]{1,0:T(8,128)S(1)}, u32[]{:S(2)}, u32[]{:S(2)}) collective-permute-start(f32[128,128]{1,0:T(8,128)S(1)} %get-tuple-element.94), channel_id=1, source_target_pairs={{0,2},{2,0},{1,3},{3,1},{4,6},{6,4},{5,7},{7,5},{8,10},{10,8},{9,1... | collective-permute-start | bytes 196616 | tf_op jit(solution)/shard_map/ppermute | solution.py:272
  76.5 5.6 %collective-permute-start.21 = (f32[128,128]{1,0:T(8,128)S(1)}, f32[128,128]{1,0:T(8,128)S(1)}, u32[]{:S(2)}, u32[]{:S(2)}) collective-permute-start(f32[128,128]{1,0:T(8,128)S(1)} %get-tuple-element.95), channel_id=1, source_target_pairs={{0,6},{2,4},{4,2},{6,0},{1,7},{3,5},{5,3},{7,1},{8,14},{10,12},{12... | collective-permute-start | bytes 196616 | tf_op jit(solution)/shard_map/ppermute | solution.py:272
  76.8 7.4 %collective-permute-start.15 = (f32[128,128]{1,0:T(8,128)S(1)}, f32[128,128]{1,0:T(8,128)S(1)}, u32[]{:S(2)}, u32[]{:S(2)}) collective-permute-start(f32[128,128]{1,0:T(8,128)S(1)} %get-tuple-element.84), channel_id=1, source_target_pairs={{0,4},{4,0},{1,5},{5,1},{2,6},{6,2},{3,7},{7,3},{8,12},{12,8},{9,1... | collective-permute-start | bytes 196616 | tf_op jit(solution)/shard_map/ppermute | solution.py:272
  77.8 6.4 %collective-permute-start.16 = (f32[128,128]{1,0:T(8,128)S(1)}, f32[128,128]{1,0:T(8,128)S(1)}, u32[]{:S(2)}, u32[]{:S(2)}) collective-permute-start(f32[128,128]{1,0:T(8,128)S(1)} %get-tuple-element.85), channel_id=1, source_target_pairs={{0,2},{2,0},{1,3},{3,1},{4,6},{6,4},{5,7},{7,5},{8,10},{10,8},{9,1... | collective-permute-start | bytes 196616 | tf_op jit(solution)/shard_map/ppermute | solution.py:272
  78.4 5.8 %collective-permute-start.17 = (f32[128,128]{1,0:T(8,128)S(1)}, f32[128,128]{1,0:T(8,128)S(1)}, u32[]{:S(2)}, u32[]{:S(2)}) collective-permute-start(f32[128,128]{1,0:T(8,128)S(1)} %get-tuple-element.86), channel_id=1, source_target_pairs={{0,6},{2,4},{4,2},{6,0},{1,7},{3,5},{5,3},{7,1},{8,14},{10,12},{12... | collective-permute-start | bytes 196616 | tf_op jit(solution)/shard_map/ppermute | solution.py:272
  (15 other events, 132.2 us)

commit v4 on v2

v4 whole, which is shorter than its diff:
```python
import functools

import jax
import jax.numpy as jnp
from jax import lax
from jax.experimental import pallas as pl
from jax.experimental.pallas import tpu as pltpu
from jax.sharding import Mesh
from jax.sharding import PartitionSpec as P

HQ = 32
KVH = 4
HD = 128
SHARED = HQ // KVH
BLOCK = 512
RESP_DEV = 2
RLEN = 64
ROWS = RESP_DEV * RLEN
PAIR = 2 * ROWS
GROUP = SHARED * HD
SCALE = HD ** (-0.5) * 1.4426950408889634
HIDDEN = -1e30
NT = (((1,), (1,)), ((), ()))
HINT = pl.CostEstimate(flops=1024, bytes_accessed=1024, transcendentals=0)
LONG = pl.CostEstimate(flops=2**33, bytes_accessed=2**23, transcendentals=2**22)

CHUNKS = ((0, 2), (2, 1), (3, 1))
HELP = (3, 4, 4)


def pair_scores(keys, q_ref, g):
    heads = [q_ref[:, i * HD : (i + 1) * HD] for i in (g, g + 1)]
    scores = lax.dot_general(keys, jnp.concatenate(heads, axis=0), NT, preferred_element_type=jnp.float32)
    return scores * SCALE


def prompt_kernel(first, info, q_ref, k_ref, v_ref, *refs):
    if first:
        acc_ref, ml_ref = refs
    else:
        old_acc, old_ml, acc_ref, ml_ref = refs
    count = k_ref.shape[0]
    place = info[0] + lax.broadcasted_iota(jnp.int32, (count, PAIR), 0)
    lane = lax.broadcasted_iota(jnp.int32, (count, PAIR), 1)
    listed = jnp.where(lane % ROWS < RLEN, info[2], info[3])
    bias = jnp.where((place < info[1]) & (listed == 1), 0.0, HIDDEN)
    keys = k_ref[...]
    values = v_ref[...].T
    for g in range(0, SHARED, 2):
        cols = slice(g * HD, (g + 2) * HD)
        scores = pair_scores(keys, q_ref, g) + bias
        largest = jnp.max(scores, axis=0, keepdims=True)
        if not first:
            before = old_ml[0:1, cols]
            largest = jnp.maximum(largest, before)
            faded = jnp.exp2(before - largest)
        weights = jnp.exp2(scores - largest)
        total = jnp.sum(weights, axis=0, keepdims=True)
        acc = jnp.dot(values, weights.astype(jnp.bfloat16), preferred_element_type=jnp.float32)
        if not first:
            total = total + faded * old_ml[1:2, cols]
            acc = acc + faded * old_acc[:, cols]
        acc_ref[:, cols] = acc
        ml_ref[0:1, cols] = largest
        ml_ref[1:2, cols] = total


def prompt_attention(info, query, cache, state, head, heads, offset=0):
    count = cache.shape[0]
    first = state is None
    wide = pl.BlockSpec((ROWS, GROUP), lambda k, s: (0, head + k))
    turned = pl.BlockSpec((HD, SHARED * ROWS), lambda k, s: (0, k))
    small = pl.BlockSpec((8, SHARED * ROWS), lambda k, s: (0, k))
    specs = [
        wide,
        pl.BlockSpec((count, HD), lambda k, s: (0, head + k)),
        pl.BlockSpec((count, HD), lambda k, s: (0, KVH + head + k)),
    ]
    operands = [query, cache, cache]
    if not first:
        specs += [
            pl.BlockSpec((HD, SHARED * ROWS), lambda k, s: (0, offset + k)),
            pl.BlockSpec((8, SHARED * ROWS), lambda k, s: (0, offset + k)),
        ]
        operands += list(state)
    return pl.pallas_call(
        functools.partial(prompt_kernel, first),
        grid_spec=pltpu.PrefetchScalarGridSpec(
            num_scalar_prefetch=1, grid=(heads,), in_specs=specs, out_specs=[turned, small]
        ),
        out_shape=[
            jax.ShapeDtypeStruct((HD, heads * SHARED * ROWS), jnp.float32),
            jax.ShapeDtypeStruct((8, heads * SHARED * ROWS), jnp.float32),
        ],
        compiler_params=pltpu.CompilerParams(vmem_limit_bytes=32 * 2**20),
        cost_estimate=LONG,
        name="prompt_attention",
    )(info, *operands)


VMEM = pl.BlockSpec(memory_space=pltpu.VMEM)
SMEM = pl.BlockSpec(memory_space=pltpu.SMEM)
PARAMS = pltpu.CompilerParams(vmem_limit_bytes=32 * 2**20)


def on_chip(kernel, name, outs, scalars, *operands, scratch=()):
    return pl.pallas_call(
        kernel,
        in_specs=[SMEM] + [VMEM] * len(operands),
        out_specs=[VMEM] * len(outs),
        out_shape=outs,
        scratch_shapes=scratch,
        compiler_params=PARAMS,
        cost_estimate=HINT,
        name=name,
    )(scalars, *operands)


def pack_rows_kernel(where, own_ref, got_ref, keep, send):
    steps, part = keep.shape[1], keep.shape[3]
    for z in range(steps):
        for out, y in ((keep, where[1]), (send, 1 - where[1])):
            columns = pl.ds(pl.multiple_of((2 * z + y) * part, 128), part)
            out[0, z] = own_ref[:, columns]
            out[1, z] = got_ref[:, columns]


def pack_rows(where, own, got, y, steps):
    part = own.shape[1] // (2 * steps)
    if part % 128:
        halves = jnp.stack([own, got]).reshape(2, ROWS, steps, 2, part)
        halves = jnp.transpose(halves, (3, 0, 2, 1, 4))
        return [lax.dynamic_index_in_dim(halves, i, axis=0, keepdims=False) for i in (y, 1 - y)]
    outs = [jax.ShapeDtypeStruct((2, steps, ROWS, part), own.dtype)] * 2
    return on_chip(pack_rows_kernel, "pack_rows", outs, where, own, got)


def row_split(rows, i):
    helped = rows * HELP[i] // 10
    return helped, rows - helped


def columns_of(chunk):
    return slice(chunk[0] * HD, (chunk[0] + chunk[1]) * HD)


def pack_weight_kernel(where, own_ref, got_ref, *outs):
    rows = own_ref.shape[0]
    core, plane = where[2], where[3]
    half = pl.ds(pl.multiple_of(core * KVH * HD, 128), KVH * HD)
    own, got = own_ref[:, half], got_ref[:, half]
    for whole, far, chunk in zip(outs[0::2], outs[1::2], CHUNKS):
        whole[pl.ds(pl.multiple_of(core * rows, 16), rows), :] = own[:, columns_of(chunk)]
        whole[pl.ds(pl.multiple_of((1 - core) * rows, 16), rows), :] = got[:, columns_of(chunk)]
        direct = far.shape[0]
        far[...] = whole[pl.ds(pl.multiple_of(plane * (2 * rows - direct), 16), direct), :]


def pack_weight(where, own, got):
    rows = 2 * own.shape[0]
    shapes = []
    for i, (_, heads) in enumerate(CHUNKS):
        shapes += [(rows, heads * HD), (row_split(rows, i)[1], heads * HD)]
    outs = [jax.ShapeDtypeStruct(shape, own.dtype) for shape in shapes]
    outs = on_chip(pack_weight_kernel, "pack_weight", outs, where, own, got)
    return list(outs[0::2]), list(outs[1::2])


def project_kernel(where, keep, other, own, near, forwarded, *refs):
    direct, mine, theirs, whole = refs[:-3], refs[-3], refs[-2], refs[-1]
    plane = where[3]
    count, extra = direct[0].shape[0], forwarded.shape[1]
    total = None
    for j in range(2 + len(direct)):
        if j == 0:
            weight = own[...]
        elif j == 1:
            weight = near[...]
        else:
            far = whole.at[j - 2]
            far[pl.ds(pl.multiple_of(plane * extra, 16), count), :] = direct[j - 2][...]
            far[pl.ds(pl.multiple_of((1 - plane) * count, 16), extra), :] = forwarded[j - 2]
            weight = far[...]
        place = where[0] ^ j
        left = jnp.concatenate([x[core, place] for x in (keep, other) for core in range(2)], axis=0)
        product = jnp.dot(left, weight, preferred_element_type=jnp.float32)
        total = product if total is None else total + product
    for i in range(2):
        mine[i] = total[i * ROWS : (i + 1) * ROWS]
        theirs[i] = total[(2 + i) * ROWS : (3 + i) * ROWS]


def project(where, keep, other, own, near, direct, forwarded):
    width = own.shape[1]
    out = jax.ShapeDtypeStruct((2, ROWS, width), jnp.float32)
    return on_chip(
        project_kernel,
        "project",
        [out, out],
        where,
        keep,
        other,
        own,
        near,
        forwarded,
        *direct,
        scratch=[pltpu.VMEM((len(direct), own.shape[0], width), jnp.bfloat16)],
    )


def final_kernel(chunk, offset, info, gain_ref, q_ref, acc_ref, ml_ref, mine, theirs, there, *refs):
    result, built, sem = refs[-3:]
    head, heads = chunk
    slot = lax.broadcasted_iota(jnp.int32, (ROWS, PAIR), 0)
    row = lax.broadcasted_iota(jnp.int32, (ROWS, PAIR), 1) % ROWS
    length = jnp.where(row < RLEN, info[0], info[1])
    base = jnp.where(row < RLEN, 0, RLEN)
    seen = (slot >= base) & (slot <= row) & (slot - base < length)
    live = jnp.where(row - base < length, 1.0, 0.0)[0:1]
    copies = []
    for k in range(heads):
        part = slice(k * HD, (k + 1) * HD)
        here = mine[0, :, part] + theirs[0, :, part]
        away = there[0, :, part] if there.shape[0] == 1 else there[0, :, part] + there[1, :, part]
        first_core = jnp.full(here.shape, info[2]) == 0
        raw = jnp.where(first_core, here, away)
        mean = jnp.mean(raw * raw, axis=1, keepdims=True)
        keys = (raw * lax.rsqrt(mean + 1e-06) * gain_ref[...]).astype(jnp.bfloat16)
        values = jnp.where(first_core, away, here).T.astype(jnp.bfloat16)
        for g in range(0, SHARED, 2):
            cols = slice(((offset + k) * SHARED + g) * HD, ((offset + k) * SHARED + g + 2) * HD)
            scores = jnp.where(seen, pair_scores(keys, q_ref, (head + k) * SHARED + g), HIDDEN)
            before = ml_ref[0:1, cols]
            largest = jnp.maximum(jnp.max(scores, axis=0, keepdims=True), before)
            faded = jnp.exp2(before - largest)
            weights = jnp.exp2(scores - largest)
            total = jnp.sum(weights, axis=0, keepdims=True) + faded * ml_ref[1:2, cols]
            acc = jnp.dot(values, weights.astype(jnp.bfloat16), preferred_element_type=jnp.float32)
            acc = (acc + faded * acc_ref[:, cols]) * (live / total)
            built[k, :, g * HD : (g + 1) * HD] = acc[:, :ROWS].T.astype(jnp.bfloat16)
            built[k, :, (g + 1) * HD : (g + 2) * HD] = acc[:, ROWS:].T.astype(jnp.bfloat16)
        place = result.at[:, pl.ds((head + k) * GROUP, GROUP)]
        copies.append(pltpu.make_async_copy(built.at[k], place, sem.at[k]))
        copies[-1].start()
    for copy in copies:
        copy.wait()


def final_attention(info, gain, query, state, offset, chunk, mine, theirs, there, result):
    heads = chunk[1]
    operands = [gain, query, *state, mine, theirs, there]
    specs = [SMEM] + [VMEM] * len(operands)
    aliases = {}
    if result is not None:
        operands.append(result)
        specs.append(pl.BlockSpec(memory_space=pl.ANY))
        aliases = {len(operands): 0}
    return pl.pallas_call(
        functools.partial(final_kernel, chunk, offset),
        in_specs=specs,
        out_specs=pl.BlockSpec(memory_space=pl.ANY),
        out_shape=jax.ShapeDtypeStruct((ROWS, HQ * HD), jnp.bfloat16),
        scratch_shapes=[pltpu.VMEM((heads, ROWS, GROUP), jnp.bfloat16), pltpu.SemaphoreType.DMA((heads,))],
        input_output_aliases=aliases,
        compiler_params=PARAMS,
        cost_estimate=HINT,
        name="final_attention",
    )(info, *operands)


def xor_swap(array, axis, by):
    return lax.ppermute(array, axis, [(i, i ^ by) for i in range(lax.axis_size(axis))])


def per_device(
    x_resp, queries, prompt_cache, kv_weight, key_gain, prompt_lengths, block_table, resp_lengths
):
    x, query = x_resp[0], queries[0]
    steps = lax.axis_size("z")
    z, y, core = lax.axis_index("z"), lax.axis_index("y"), lax.axis_index("core")
    holder, cycle = lax.axis_index("blk"), lax.axis_size("blk")
    plane = holder % 2
    where = jnp.stack([z, y, core, plane]).astype(jnp.int32)

    tie = lax.optimization_barrier

    got_weight = xor_swap(kv_weight, "core", 1)
    got_x = xor_swap(x, "core", 1)
    caches = [prompt_cache[0]]
    for _ in range(cycle - 1):
        caches.append(lax.ppermute(caches[-1], "blk", [(i, (i + 1) % cycle) for i in range(cycle)]))

    whole, far = pack_weight(where, kv_weight, got_weight)

    def send(whole, far):
        return xor_swap(whole, "z", 1), [xor_swap(far, "z", j) for j in range(2, steps)]

    def forward(i):
        helped, direct = row_split(whole[0].shape[0], i)
        parts = [lax.dynamic_slice_in_dim(p, plane * (direct - helped), helped, axis=0) for p in sent[i][1]]
        return xor_swap(jnp.stack(parts), "blk", 1)

    sent = [send(whole[0], far[0])]
    keep, given = pack_rows(where, x, got_x, y, steps)
    other = xor_swap(given, "y", 1)

    infos = []
    for stride in range(cycle):
        owner = lax.rem(holder + cycle - stride, cycle)
        place = owner * prompt_cache.shape[1]
        listed = lax.dynamic_index_in_dim(block_table[0], place // BLOCK, axis=1, keepdims=False)
        infos.append(jnp.concatenate([place[None], prompt_lengths, listed]).astype(jnp.int32))

    def rest(head, heads, state, offset):
        for stride in range(1, cycle):
            state = prompt_attention(infos[stride], query, caches[stride], state, head, heads, offset)
            offset = 0
        return state

    query, _, _ = tie((query, whole[0], given))
    state = prompt_attention(infos[0], query, caches[0], None, 0, KVH)

    sent[0], caches, state, next_chunk = tie((sent[0], caches, state, (whole[1], far[1])))
    sent.append(send(*next_chunk))
    forwarded = [forward(0)]
    halves = [rest(0, 2, state, 0)]
    sent[1], forwarded[0], halves[0], next_chunk = tie((sent[1], forwarded[0], halves[0], (whole[2], far[2])))
    sent.append(send(*next_chunk))
    forwarded.append(forward(1))

    def sums(i):
        return project(where, keep, other, whole[i], *sent[i], forwarded[i])

    info = jnp.concatenate([resp_lengths[0], core[None]]).astype(jnp.int32)
    gain = key_gain[None]
    mine_0, theirs_0 = sums(0)
    theirs_0 = xor_swap(theirs_0, "y", 1)
    mine_0, forwarded[1] = tie((mine_0, forwarded[1]))
    mine_1, theirs_1 = sums(1)
    theirs_1 = xor_swap(theirs_1, "y", 1)
    sent[2], mine_1, state = tie((sent[2], mine_1, state))
    forwarded.append(forward(2))
    halves.append(rest(2, 2, state, 2))
    theirs_0, theirs_1, halves[1] = tie((theirs_0, theirs_1, halves[1]))
    there_0 = xor_swap(mine_0[1:] + theirs_0[1:], "core", 1)
    there_1 = xor_swap(mine_1[1:] + theirs_1[1:], "core", 1)
    result = final_attention(info, gain, query, halves[0], 0, CHUNKS[0], mine_0, theirs_0, there_0, None)
    mine_2, theirs_2 = sums(2)
    there_2 = [xor_swap(mine_2[1], "core", 1), xor_swap(theirs_2[1], ("y", "core"), 3)]
    theirs_2 = xor_swap(theirs_2[:1], "y", 1)
    result = final_attention(info, gain, query, halves[1], 0, CHUNKS[1], mine_1, theirs_1, there_1, result)
    result = final_attention(
        info, gain, query, halves[1], 1, CHUNKS[2], mine_2, theirs_2, jnp.stack(there_2), result
    )
    return result[None]


def solution(mesh):
    groups, blocks = mesh.devices.shape
    split = Mesh(mesh.devices.reshape(groups // 4, 2, 2, blocks), ("z", "y", "core", "blk"))
    fsdp = ("z", "y", "core")
    return jax.shard_map(
        per_device,
        mesh=split,
        in_specs=(
            P(fsdp, "blk", None),
            P(fsdp, "blk", None),
            P(fsdp, "blk", None),
            P(fsdp, None),
            P(),
            P(fsdp),
            P(fsdp, "blk", None),
            P(fsdp, "blk"),
        ),
        out_specs=P(fsdp, "blk", None),
        check_vma=False,
    )
```

time: 104 us -> 75.5 us (0.73)
  waiting for transfers between devices: 46 us -> 12.8 us
  starting transfers between devices: 6.07 us -> 27.7 us
  between operations: 14.1 us -> 0.93 us
  local copies, waits for them, and re-layouts: 11.7 us -> 2.16 us
  Pallas kernels: 25.7 us -> 30.7 us
    ppermute x4 -> x23, starting transfers between devices: 6.07 us -> 27.7 us  [the longest x22 24.8 us: xor_swap(): lax.ppermute(array, axis, [(i, i ^ by) for i in range(lax.axis_size(axis))])]
    all_gather x1 -> x0, waiting for transfers between devices: 21.5 us -> none  [per_device(): same = lax.all_gather(kv_weight, 'z', axis=0, tiled=True)]
    ppermute x4 -> x23, waiting for transfers between devices: 23.7 us -> 12.8 us  [the longest x22 12.8 us: xor_swap(): lax.ppermute(array, axis, [(i, i ^ by) for i in range(lax.axis_size(axis))])]
    unnamed x25 -> x12, local copies, waits for them, and re-layouts: 10.6 us -> 1.12 us
    pallas_call x2 -> x8, Pallas kernels: 8.57 us -> 12.1 us  [the longest x3 6.43 us: final_attention(): pl.pallas_call(functools.partial(final_kernel, chunk, offset), in_specs=s...]
    pallas_call x2 -> x3, Pallas kernels: 17.2 us -> 18.6 us  [prompt_attention(): pl.pallas_call(functools.partial(prompt_kernel, first), grid_spec=pltpu.P...]
  transfers between devices with their start and end apart: 5 -> 23, of which waited for: 4 -> 4; matrix products, arithmetic and copies ran while one was open for 5% -> 2% of each run, Pallas kernels for 17% -> 38%
where the time goes in v4:
time: 75.5 us; the launch traced here: 74.6 us
  Pallas kernels  30.7 us (41%)
  starting transfers between devices  27.7 us (37%)
  waiting for transfers between devices  12.8 us (17%)
  local copies, waits for them, and re-layouts  2.16 us (3%)
  between operations  0.93 us (1%)
    ppermute x22, starting transfers between devices, xor_swap(): lax.ppermute(array, axis, [(i, i ^ by) for i in range(lax.axis_size(axis))])  24.8 us
    pallas_call x3, Pallas kernels, prompt_attention(): pl.pallas_call(functools.partial(prompt_kernel, first), grid_spec=pltpu.P...  18.6 us
    ppermute x22, waiting for transfers between devices, xor_swap(): lax.ppermute(array, axis, [(i, i ^ by) for i in range(lax.axis_size(axis))])  12.8 us
    pallas_call x3, Pallas kernels, final_attention(): pl.pallas_call(functools.partial(final_kernel, chunk, offset), in_specs=s...  6.43 us
    pallas_call x5, Pallas kernels, on_chip(): pl.pallas_call(kernel, in_specs=[SMEM] + [VMEM] * len(operands), out_spec...  5.69 us
    ppermute x1, starting transfers between devices, per_device(): lax.ppermute(caches[-1], 'blk', [(i, (i + 1) % cycle) for i in range(cycl...  2.93 us
  transfers between devices with their start and end apart: 23, of which 4 were waited for; matrix products, arithmetic and copies ran while one was open for 2% of the time, Pallas kernels for 38%

profile of v4, /device:TPU:0, one launch (start us, length us, event | category | flops | bytes accessed | tf_op | source)
XLA Modules:
  0.0 74.6 jit_solution(17303743258859053869)
XLA Ops:
  0.5 2.9 %collective-permute-start.6 = (bf16[512,1024]{1,0:T(8,128)(2,1)}, bf16[512,1024]{1,0:T(8,128)(2,1)}, u32[]{:S(2)}, u32[]{:S(2)}) collective-permute-start(bf16[512,1024]{1,0:T(8,128)(2,1)} %bitcast.41), channel_id=1, source_target_pairs={{0,1},{1,0},{2,3},{3,2},{4,5},{5,4},{6,7},{7,6},{8,9},{9,8},{10,11... | collective-permute-start | bytes 3145736 | tf_op jit(solution)/shard_map/ppermute | solution.py:291
  5.2 1.1 %copy-done.2 = bf16[320,1024]{1,0:T(8,128)(2,1)S(1)} copy-done((bf16[320,1024]{1,0:T(8,128)(2,1)S(1)}, bf16[320,1024]{1,0:T(8,128)(2,1)}, u32[]{:S(2)}) %copy-start.2) | copy-done | bytes 655384
  7.0 4.0 %collective-permute-start.5 = (bf16[448,256]{1,0:T(8,128)(2,1)S(1)}, bf16[448,256]{1,0:T(8,128)(2,1)S(1)}, u32[]{:S(2)}, u32[]{:S(2)}) collective-permute-start(bf16[448,256]{1,0:T(8,128)(2,1)S(1)} %get-tuple-element.58), channel_id=1, source_target_pairs={{0,24},{8,16},{16,8},{24,0},{1,25},{9,17},{17,9},{25,1},{2,26},{10... | collective-permute-start | bytes 688136 | tf_op jit(solution)/shard_map/ppermute | solution.py:272
  12.4 1.7 %collective-permute-start.2 = (bf16[2,4,128,640]{3,2,1,0:T(8,128)(2,1)S(1)}, bf16[2,4,128,640]{3,2,1,0:T(8,128)(2,1)S(1)}, u32[]{:S(2)}, u32[]{:S(2)}) collective-permute-start(bf16[2,4,128,640]{3,2,1,0:T(8,128)(2,1)S(1)} %get-tuple-element.55), channel_id=1, source_target_pairs={{0,4},{4,0},{1,5},{5,1},{2,6},{6,2},{3,7},{7,3},{8,12},{12,8},{9,1... | collective-permute-start | bytes 3932168 | tf_op jit(solution)/shard_map/ppermute | solution.py:272
  14.2 8.2 %prompt_attention.3 = (f32[128,4096]{1,0:T(8,128)S(1)}, f32[8,4096]{1,0:T(8,128)S(1)}) custom-call(s32[4]{0:T(128)S(1)} %get-tuple-element.107.info, bf16[128,4096]{1,0:T(8,128)(2,1)S(1)} %bitcast.30, bf16[512,1024]{1,0:T(8,128)(2,1)S(1)} %bitcast.42, bf16[512,1024]{1,0:T(8,128)(2,1)S(1)} %bitcast.43), custom_call_target="tpu_custom_call" | custom-call | flops 8589934592 | bytes 8388608 | tf_op jit(solution)/shard_map/prompt_attention/pallas_call | solution.py:86
  22.4 8.5 %collective-permute-done.4.refs_0_ = bf16[448,256]{1,0:T(8,128)(2,1)S(1)} collective-permute-done((bf16[448,256]{1,0:T(8,128)(2,1)S(1)}, bf16[448,256]{1,0:T(8,128)(2,1)S(1)}, u32[]{:S(2)}, u32[]{:S(2)}) %collective-permute-start.4) | collective-permute-done | bytes 229408 | tf_op jit(solution)/shard_map/ppermute | solution.py:272
  30.8 2.5 %collective-permute-start.9 = (bf16[384,128]{1,0:T(8,128)(2,1)S(1)}, bf16[384,128]{1,0:T(8,128)(2,1)S(1)}, u32[]{:S(2)}, u32[]{:S(2)}) collective-permute-start(bf16[384,128]{1,0:T(8,128)(2,1)S(1)} %get-tuple-element.65), channel_id=1, source_target_pairs={{0,24},{8,16},{16,8},{24,0},{1,25},{9,17},{17,9},{25,1},{2,26},{10... | collective-permute-start | bytes 294920 | tf_op jit(solution)/shard_map/ppermute | solution.py:272
  33.4 2.0 %collective-permute-start.7 = (bf16[640,128]{1,0:T(8,128)(2,1)S(1)}, bf16[640,128]{1,0:T(8,128)(2,1)S(1)}, u32[]{:S(2)}, u32[]{:S(2)}) collective-permute-start(bf16[640,128]{1,0:T(8,128)(2,1)S(1)} %get-tuple-element.64.own), channel_id=1, source_target_pairs={{0,8},{8,0},{16,24},{24,16},{1,9},{9,1},{17,25},{25,17},{2,10},{10... | collective-permute-start | bytes 491528 | tf_op jit(solution)/shard_map/ppermute | solution.py:272
  35.4 1.6 %collective-permute-start.10 = (bf16[2,192,256]{2,1,0:T(8,128)(2,1)S(1)}, bf16[2,192,256]{2,1,0:T(8,128)(2,1)S(1)}, u32[]{:S(2)}, u32[]{:S(2)}) collective-permute-start(bf16[2,192,256]{2,1,0:T(8,128)(2,1)S(1)} %pad_maximum_fusion), channel_id=1, source_target_pairs={{0,1},{1,0},{2,3},{3,2},{4,5},{5,4},{6,7},{7,6},{8,9},{9,8},{10,11... | collective-permute-start | bytes 589832 | tf_op jit(solution)/shard_map/ppermute | solution.py:272
  36.9 5.2 %prompt_attention.4 = (f32[128,2048]{1,0:T(8,128)S(1)}, f32[8,2048]{1,0:T(8,128)S(1)}) custom-call(s32[4]{0:T(128)S(1)} %get-tuple-element.108.info, bf16[128,4096]{1,0:T(8,128)(2,1)S(1)} %bitcast.31, bf16[512,1024]{1,0:T(8,128)(2,1)} %collective-permute-done.6.k_ref.v_ref, bf16[512,1024]{1,0:T(8,128)(2,1)} %collective-permute-done.6.k_ref.v_ref, ...), custom_call_target="tpu_custom_call" | custom-call | flops 8589934592 | bytes 8388608 | tf_op jit(solution)/shard_map/prompt_attention/pallas_call | solution.py:86
  43.0 1.6 %collective-permute-start.12 = (bf16[2,256,128]{2,1,0:T(8,128)(2,1)S(1)}, bf16[2,256,128]{2,1,0:T(8,128)(2,1)S(1)}, u32[]{:S(2)}, u32[]{:S(2)}) collective-permute-start(bf16[2,256,128]{2,1,0:T(8,128)(2,1)S(1)} %pad_maximum_fusion.1), channel_id=1, source_target_pairs={{0,1},{1,0},{2,3},{3,2},{4,5},{5,4},{6,7},{7,6},{8,9},{9,8},{10,11... | collective-permute-start | bytes 393224 | tf_op jit(solution)/shard_map/ppermute | solution.py:272
  44.6 1.8 %collective-permute-start.16 = (bf16[384,128]{1,0:T(8,128)(2,1)S(1)}, bf16[384,128]{1,0:T(8,128)(2,1)S(1)}, u32[]{:S(2)}, u32[]{:S(2)}) collective-permute-start(bf16[384,128]{1,0:T(8,128)(2,1)S(1)} %get-tuple-element.84), channel_id=1, source_target_pairs={{0,24},{8,16},{16,8},{24,0},{1,25},{9,17},{17,9},{25,1},{2,26},{10... | collective-permute-start | bytes 294920 | tf_op jit(solution)/shard_map/ppermute | solution.py:272
  46.4 1.1 %collective-permute-start.15 = (bf16[384,128]{1,0:T(8,128)(2,1)S(1)}, bf16[384,128]{1,0:T(8,128)(2,1)S(1)}, u32[]{:S(2)}, u32[]{:S(2)}) collective-permute-start(bf16[384,128]{1,0:T(8,128)(2,1)S(1)} %get-tuple-element.84), channel_id=1, source_target_pairs={{0,16},{8,24},{16,0},{24,8},{1,17},{9,25},{17,1},{25,9},{2,18},{10... | collective-permute-start | bytes 294920 | tf_op jit(solution)/shard_map/ppermute | solution.py:272
  47.5 1.5 %project.3 = (f32[2,128,256]{2,1,0:T(8,128)S(1)}, f32[2,128,256]{2,1,0:T(8,128)S(1)}) custom-call(s32[4]{0:T(128)S(1)} %pad_add_fusion.1.where, bf16[2,4,128,640]{3,2,1,0:T(8,128)(2,1)S(1)} %get-tuple-element.57.keep, bf16[2,4,128,640]{3,2,1,0:T(8,128)(2,1)S(1)} %collective-permute-done.2.other, bf16[640,256]{1,0:T(8,128)(2,1)S(1)} %get-tuple-element.54.own, ...), custom_call_target="tpu_custom_call" | custom-call | flops 1024 | bytes 1024 | tf_op jit(solution)/shard_map/project/pallas_call | solution.py:107
  49.1 1.4 %project.4 = (f32[2,128,128]{2,1,0:T(8,128)S(1)}, f32[2,128,128]{2,1,0:T(8,128)S(1)}) custom-call(s32[4]{0:T(128)S(1)} %pad_add_fusion.1.where, bf16[2,4,128,640]{3,2,1,0:T(8,128)(2,1)S(1)} %get-tuple-element.57.keep, bf16[2,4,128,640]{3,2,1,0:T(8,128)(2,1)S(1)} %collective-permute-done.2.other, bf16[640,128]{1,0:T(8,128)(2,1)S(1)} %get-tuple-element.64.own, ...), custom_call_target="tpu_custom_call" | custom-call | flops 1024 | bytes 1024 | tf_op jit(solution)/shard_map/project/pallas_call | solution.py:107
  50.5 1.6 %collective-permute-start.13 = (f32[2,128,128]{2,1,0:T(8,128)S(1)}, f32[2,128,128]{2,1,0:T(8,128)S(1)}, u32[]{:S(2)}, u32[]{:S(2)}) collective-permute-start(f32[2,128,128]{2,1,0:T(8,128)S(1)} %get-tuple-element.82), channel_id=1, source_target_pairs={{0,4},{4,0},{1,5},{5,1},{2,6},{6,2},{3,7},{7,3},{8,12},{12,8},{9,1... | collective-permute-start | bytes 393224 | tf_op jit(solution)/shard_map/ppermute | solution.py:272
  52.1 3.1 %collective-permute-done.15.refs_0_ = bf16[384,128]{1,0:T(8,128)(2,1)S(1)} collective-permute-done((bf16[384,128]{1,0:T(8,128)(2,1)S(1)}, bf16[384,128]{1,0:T(8,128)(2,1)S(1)}, u32[]{:S(2)}, u32[]{:S(2)}) %collective-permute-start.15) | collective-permute-done | bytes 98336 | tf_op jit(solution)/shard_map/ppermute | solution.py:272
  56.0 1.5 %collective-permute-start.11 = (f32[2,128,256]{2,1,0:T(8,128)S(1)}, f32[2,128,256]{2,1,0:T(8,128)S(1)}, u32[]{:S(2)}, u32[]{:S(2)}) collective-permute-start(f32[2,128,256]{2,1,0:T(8,128)S(1)} %get-tuple-element.76), channel_id=1, source_target_pairs={{0,4},{4,0},{1,5},{5,1},{2,6},{6,2},{3,7},{7,3},{8,12},{12,8},{9,1... | collective-permute-start | bytes 786440 | tf_op jit(solution)/shard_map/ppermute | solution.py:272
  57.5 5.2 %prompt_attention.5 = (f32[128,2048]{1,0:T(8,128)S(1)}, f32[8,2048]{1,0:T(8,128)S(1)}) custom-call(s32[4]{0:T(128)S(1)} %get-tuple-element.108.info, bf16[128,4096]{1,0:T(8,128)(2,1)S(1)} %bitcast.32, bf16[512,1024]{1,0:T(8,128)(2,1)} %collective-permute-done.6.k_ref.v_ref, bf16[512,1024]{1,0:T(8,128)(2,1)} %collective-permute-done.6.k_ref.v_ref, ...), custom_call_target="tpu_custom_call" | custom-call | flops 8589934592 | bytes 8388608 | tf_op jit(solution)/shard_map/prompt_attention/pallas_call | solution.py:86
  62.8 1.4 %project.5 = (f32[2,128,128]{2,1,0:T(8,128)S(1)}, f32[2,128,128]{2,1,0:T(8,128)S(1)}) custom-call(s32[4]{0:T(128)S(1)} %pad_add_fusion.1.where, bf16[2,4,128,640]{3,2,1,0:T(8,128)(2,1)S(1)} %get-tuple-element.57.keep, bf16[2,4,128,640]{3,2,1,0:T(8,128)(2,1)S(1)} %collective-permute-done.2.other, bf16[640,128]{1,0:T(8,128)(2,1)S(1)} %get-tuple-element.83.own, ...), custom_call_target="tpu_custom_call" | custom-call | flops 1024 | bytes 1024 | tf_op jit(solution)/shard_map/project/pallas_call | solution.py:107
  65.0 1.5 %collective-permute-start.18 = (f32[1,128,128]{2,1,0:T(8,128)S(1)}, f32[1,128,128]{2,1,0:T(8,128)S(1)}, u32[]{:S(2)}, u32[]{:S(2)}) collective-permute-start(f32[1,128,128]{2,1,0:T(8,128)S(1)} %get-tuple-element.106), channel_id=1, source_target_pairs={{0,4},{4,0},{1,5},{5,1},{2,6},{6,2},{3,7},{7,3},{8,12},{12,8},{9,1... | collective-permute-start | bytes 196616 | tf_op jit(solution)/shard_map/ppermute | solution.py:272
  68.2 2.3 %final_attention.3.refs_0_ = bf16[128,4096]{1,0:T(8,128)(2,1)} custom-call(s32[3]{0:T(128)S(1)} %pad_add_fusion.info, f32[1,128]{1,0:T(1,128)S(1)} %bitcast.38, bf16[128,4096]{1,0:T(8,128)(2,1)S(1)} %bitcast.33, f32[128,2048]{1,0:T(8,128)S(1)} %get-tuple-element.99.acc_ref, f32[8,2048]{1,0:T(8,128)S(1)} %get-tuple-element.100.ml_ref, ...), custom_call_target="tpu_custom_call" | custom-call | flops 1024 | bytes 1024 | tf_op jit(solution)/shard_map/final_attention/pallas_call | solution.py:258
  70.5 2.1 %final_attention.4.refs_0_ = bf16[128,4096]{1,0:T(8,128)(2,1)} custom-call(s32[3]{0:T(128)S(1)} %pad_add_fusion.info, f32[1,128]{1,0:T(1,128)S(1)} %bitcast.39, bf16[128,4096]{1,0:T(8,128)(2,1)S(1)} %bitcast.34, f32[128,2048]{1,0:T(8,128)S(1)} %get-tuple-element.90.acc_ref, f32[8,2048]{1,0:T(8,128)S(1)} %get-tuple-element.91.ml_ref, ...), custom_call_target="tpu_custom_call", output_to_operand_aliasing={{}: (8, {})} | custom-call | flops 1024 | bytes 1024 | tf_op jit(solution)/shard_map/final_attention/pallas_call | solution.py:258
  72.6 2.1 %final_attention.5 = bf16[128,4096]{1,0:T(8,128)(2,1)} custom-call(s32[3]{0:T(128)S(1)} %pad_add_fusion.info, f32[1,128]{1,0:T(1,128)S(1)} %bitcast.40, bf16[128,4096]{1,0:T(8,128)(2,1)S(1)} %bitcast.35, f32[128,2048]{1,0:T(8,128)S(1)} %get-tuple-element.90.acc_ref, f32[8,2048]{1,0:T(8,128)S(1)} %get-tuple-element.91.ml_ref, ...), custom_call_target="tpu_custom_call", output_to_operand_aliasing={{}: (8, {})} | custom-call | flops 1024 | bytes 1024 | tf_op jit(solution)/shard_map/final_attention/pallas_call | solution.py:258
  (63 shorter events, 7.9 us)
Async XLA Ops:
  0.0 11.7 %copy-start.1 = (bf16[1,128,5120]{2,1,0:T(8,128)(2,1)S(1)}, bf16[1,128,5120]{2,1,0:T(8,128)(2,1)}, u32[]{:S(2)}) copy-start(bf16[1,128,5120]{2,1,0:T(8,128)(2,1)} %param.8) | copy-start | bytes 3932164
  0.0 11.7 %collective-permute-start.1 = (bf16[128,5120]{1,0:T(8,128)(2,1)}, bf16[128,5120]{1,0:T(8,128)(2,1)S(1)}, u32[]{:S(2)}, u32[]{:S(2)}) collective-permute-start(bf16[128,5120]{1,0:T(8,128)(2,1)} %bitcast.36), channel_id=1, source_target_pairs={{0,2},{2,0},{1,3},{3,1},{4,6},{6,4},{5,7},{7,5},{8,10},{10,8},{9,1... | collective-permute-start | bytes 3932168 | tf_op jit(solution)/shard_map/ppermute | solution.py:272
  0.5 4.8 %collective-permute-start = (bf16[320,1024]{1,0:T(8,128)(2,1)}, bf16[320,1024]{1,0:T(8,128)(2,1)S(1)}, u32[]{:S(2)}, u32[]{:S(2)}) collective-permute-start(bf16[320,1024]{1,0:T(8,128)(2,1)} %own_ref.1), channel_id=1, source_target_pairs={{0,2},{2,0},{1,3},{3,1},{4,6},{6,4},{5,7},{7,5},{8,10},{10,8},{9,1... | collective-permute-start | bytes 1966088 | tf_op jit(solution)/shard_map/ppermute | solution.py:272
  0.5 30.3 %collective-permute-start.6 = (bf16[512,1024]{1,0:T(8,128)(2,1)}, bf16[512,1024]{1,0:T(8,128)(2,1)}, u32[]{:S(2)}, u32[]{:S(2)}) collective-permute-start(bf16[512,1024]{1,0:T(8,128)(2,1)} %bitcast.41), channel_id=1, source_target_pairs={{0,1},{1,0},{2,3},{3,2},{4,5},{5,4},{6,7},{7,6},{8,9},{9,8},{10,11... | collective-permute-start | bytes 3145736 | tf_op jit(solution)/shard_map/ppermute | solution.py:291
  7.0 15.4 %collective-permute-start.5 = (bf16[448,256]{1,0:T(8,128)(2,1)S(1)}, bf16[448,256]{1,0:T(8,128)(2,1)S(1)}, u32[]{:S(2)}, u32[]{:S(2)}) collective-permute-start(bf16[448,256]{1,0:T(8,128)(2,1)S(1)} %get-tuple-element.58), channel_id=1, source_target_pairs={{0,24},{8,16},{16,8},{24,0},{1,25},{9,17},{17,9},{25,1},{2,26},{10... | collective-permute-start | bytes 688136 | tf_op jit(solution)/shard_map/ppermute | solution.py:272
  11.0 19.8 %collective-permute-start.4 = (bf16[448,256]{1,0:T(8,128)(2,1)S(1)}, bf16[448,256]{1,0:T(8,128)(2,1)S(1)}, u32[]{:S(2)}, u32[]{:S(2)}) collective-permute-start(bf16[448,256]{1,0:T(8,128)(2,1)S(1)} %get-tuple-element.58), channel_id=1, source_target_pairs={{0,16},{8,24},{16,0},{24,8},{1,17},{9,25},{17,1},{25,9},{2,18},{10... | collective-permute-start | bytes 688136 | tf_op jit(solution)/shard_map/ppermute | solution.py:272
  11.0 19.8 %collective-permute-start.3 = (bf16[640,256]{1,0:T(8,128)(2,1)S(1)}, bf16[640,256]{1,0:T(8,128)(2,1)S(1)}, u32[]{:S(2)}, u32[]{:S(2)}) collective-permute-start(bf16[640,256]{1,0:T(8,128)(2,1)S(1)} %get-tuple-element.54.own), channel_id=1, source_target_pairs={{0,8},{8,0},{16,24},{24,16},{1,9},{9,1},{17,25},{25,17},{2,10},{10... | collective-permute-start | bytes 983048 | tf_op jit(solution)/shard_map/ppermute | solution.py:272
  12.4 35.1 %collective-permute-start.2 = (bf16[2,4,128,640]{3,2,1,0:T(8,128)(2,1)S(1)}, bf16[2,4,128,640]{3,2,1,0:T(8,128)(2,1)S(1)}, u32[]{:S(2)}, u32[]{:S(2)}) collective-permute-start(bf16[2,4,128,640]{3,2,1,0:T(8,128)(2,1)S(1)} %get-tuple-element.55), channel_id=1, source_target_pairs={{0,4},{4,0},{1,5},{5,1},{2,6},{6,2},{3,7},{7,3},{8,12},{12,8},{9,1... | collective-permute-start | bytes 3932168 | tf_op jit(solution)/shard_map/ppermute | solution.py:272
  30.8 11.3 %collective-permute-start.9 = (bf16[384,128]{1,0:T(8,128)(2,1)S(1)}, bf16[384,128]{1,0:T(8,128)(2,1)S(1)}, u32[]{:S(2)}, u32[]{:S(2)}) collective-permute-start(bf16[384,128]{1,0:T(8,128)(2,1)S(1)} %get-tuple-element.65), channel_id=1, source_target_pairs={{0,24},{8,16},{16,8},{24,0},{1,25},{9,17},{17,9},{25,1},{2,26},{10... | collective-permute-start | bytes 294920 | tf_op jit(solution)/shard_map/ppermute | solution.py:272
  33.3 8.8 %collective-permute-start.8 = (bf16[384,128]{1,0:T(8,128)(2,1)S(1)}, bf16[384,128]{1,0:T(8,128)(2,1)S(1)}, u32[]{:S(2)}, u32[]{:S(2)}) collective-permute-start(bf16[384,128]{1,0:T(8,128)(2,1)S(1)} %get-tuple-element.65), channel_id=1, source_target_pairs={{0,16},{8,24},{16,0},{24,8},{1,17},{9,25},{17,1},{25,9},{2,18},{10... | collective-permute-start | bytes 294920 | tf_op jit(solution)/shard_map/ppermute | solution.py:272
  33.4 9.0 %collective-permute-start.7 = (bf16[640,128]{1,0:T(8,128)(2,1)S(1)}, bf16[640,128]{1,0:T(8,128)(2,1)S(1)}, u32[]{:S(2)}, u32[]{:S(2)}) collective-permute-start(bf16[640,128]{1,0:T(8,128)(2,1)S(1)} %get-tuple-element.64.own), channel_id=1, source_target_pairs={{0,8},{8,0},{16,24},{24,16},{1,9},{9,1},{17,25},{25,17},{2,10},{10... | collective-permute-start | bytes 491528 | tf_op jit(solution)/shard_map/ppermute | solution.py:272
  35.4 7.0 %collective-permute-start.10 = (bf16[2,192,256]{2,1,0:T(8,128)(2,1)S(1)}, bf16[2,192,256]{2,1,0:T(8,128)(2,1)S(1)}, u32[]{:S(2)}, u32[]{:S(2)}) collective-permute-start(bf16[2,192,256]{2,1,0:T(8,128)(2,1)S(1)} %pad_maximum_fusion), channel_id=1, source_target_pairs={{0,1},{1,0},{2,3},{3,2},{4,5},{5,4},{6,7},{7,6},{8,9},{9,8},{10,11... | collective-permute-start | bytes 589832 | tf_op jit(solution)/shard_map/ppermute | solution.py:272
  42.4 12.8 %collective-permute-start.14 = (bf16[640,128]{1,0:T(8,128)(2,1)S(1)}, bf16[640,128]{1,0:T(8,128)(2,1)S(1)}, u32[]{:S(2)}, u32[]{:S(2)}) collective-permute-start(bf16[640,128]{1,0:T(8,128)(2,1)S(1)} %get-tuple-element.83.own), channel_id=1, source_target_pairs={{0,8},{8,0},{16,24},{24,16},{1,9},{9,1},{17,25},{25,17},{2,10},{10... | collective-permute-start | bytes 491528 | tf_op jit(solution)/shard_map/ppermute | solution.py:272
  43.0 6.0 %collective-permute-start.12 = (bf16[2,256,128]{2,1,0:T(8,128)(2,1)S(1)}, bf16[2,256,128]{2,1,0:T(8,128)(2,1)S(1)}, u32[]{:S(2)}, u32[]{:S(2)}) collective-permute-start(bf16[2,256,128]{2,1,0:T(8,128)(2,1)S(1)} %pad_maximum_fusion.1), channel_id=1, source_target_pairs={{0,1},{1,0},{2,3},{3,2},{4,5},{5,4},{6,7},{7,6},{8,9},{9,8},{10,11... | collective-permute-start | bytes 393224 | tf_op jit(solution)/shard_map/ppermute | solution.py:272
  44.6 7.5 %collective-permute-start.16 = (bf16[384,128]{1,0:T(8,128)(2,1)S(1)}, bf16[384,128]{1,0:T(8,128)(2,1)S(1)}, u32[]{:S(2)}, u32[]{:S(2)}) collective-permute-start(bf16[384,128]{1,0:T(8,128)(2,1)S(1)} %get-tuple-element.84), channel_id=1, source_target_pairs={{0,24},{8,16},{16,8},{24,0},{1,25},{9,17},{17,9},{25,1},{2,26},{10... | collective-permute-start | bytes 294920 | tf_op jit(solution)/shard_map/ppermute | solution.py:272
  46.4 8.8 %collective-permute-start.15 = (bf16[384,128]{1,0:T(8,128)(2,1)S(1)}, bf16[384,128]{1,0:T(8,128)(2,1)S(1)}, u32[]{:S(2)}, u32[]{:S(2)}) collective-permute-start(bf16[384,128]{1,0:T(8,128)(2,1)S(1)} %get-tuple-element.84), channel_id=1, source_target_pairs={{0,16},{8,24},{16,0},{24,8},{1,17},{9,25},{17,1},{25,9},{2,18},{10... | collective-permute-start | bytes 294920 | tf_op jit(solution)/shard_map/ppermute | solution.py:272
  50.5 16.0 %collective-permute-start.13 = (f32[2,128,128]{2,1,0:T(8,128)S(1)}, f32[2,128,128]{2,1,0:T(8,128)S(1)}, u32[]{:S(2)}, u32[]{:S(2)}) collective-permute-start(f32[2,128,128]{2,1,0:T(8,128)S(1)} %get-tuple-element.82), channel_id=1, source_target_pairs={{0,4},{4,0},{1,5},{5,1},{2,6},{6,2},{3,7},{7,3},{8,12},{12,8},{9,1... | collective-permute-start | bytes 393224 | tf_op jit(solution)/shard_map/ppermute | solution.py:272
  55.2 7.6 %collective-permute-start.17 = (bf16[2,256,128]{2,1,0:T(8,128)(2,1)S(1)}, bf16[2,256,128]{2,1,0:T(8,128)(2,1)S(1)}, u32[]{:S(2)}, u32[]{:S(2)}) collective-permute-start(bf16[2,256,128]{2,1,0:T(8,128)(2,1)S(1)} %pad_maximum_fusion.2), channel_id=1, source_target_pairs={{0,1},{1,0},{2,3},{3,2},{4,5},{5,4},{6,7},{7,6},{8,9},{9,8},{10,11... | collective-permute-start | bytes 393224 | tf_op jit(solution)/shard_map/ppermute | solution.py:272
  56.0 10.5 %collective-permute-start.11 = (f32[2,128,256]{2,1,0:T(8,128)S(1)}, f32[2,128,256]{2,1,0:T(8,128)S(1)}, u32[]{:S(2)}, u32[]{:S(2)}) collective-permute-start(f32[2,128,256]{2,1,0:T(8,128)S(1)} %get-tuple-element.76), channel_id=1, source_target_pairs={{0,4},{4,0},{1,5},{5,1},{2,6},{6,2},{3,7},{7,3},{8,12},{12,8},{9,1... | collective-permute-start | bytes 786440 | tf_op jit(solution)/shard_map/ppermute | solution.py:272
  64.2 3.0 %collective-permute-start.19 = (f32[128,128]{1,0:T(8,128)S(1)}, f32[128,128]{1,0:T(8,128)S(1)}, u32[]{:S(2)}, u32[]{:S(2)}) collective-permute-start(f32[128,128]{1,0:T(8,128)S(1)} %slice_bitcast_fusion.1), channel_id=1, source_target_pairs={{0,2},{2,0},{1,3},{3,1},{4,6},{6,4},{5,7},{7,5},{8,10},{10,8},{9,1... | collective-permute-start | bytes 196616 | tf_op jit(solution)/shard_map/ppermute | solution.py:272
  64.3 3.8 %collective-permute-start.20 = (f32[128,128]{1,0:T(8,128)S(1)}, f32[128,128]{1,0:T(8,128)S(1)}, u32[]{:S(2)}, u32[]{:S(2)}) collective-permute-start(f32[128,128]{1,0:T(8,128)S(1)} %get-tuple-element.105), channel_id=1, source_target_pairs={{0,6},{2,4},{4,2},{6,0},{1,7},{3,5},{5,3},{7,1},{8,14},{10,12},{12... | collective-permute-start | bytes 196616 | tf_op jit(solution)/shard_map/ppermute | solution.py:272
  65.0 7.6 %collective-permute-start.18 = (f32[1,128,128]{2,1,0:T(8,128)S(1)}, f32[1,128,128]{2,1,0:T(8,128)S(1)}, u32[]{:S(2)}, u32[]{:S(2)}) collective-permute-start(f32[1,128,128]{2,1,0:T(8,128)S(1)} %get-tuple-element.106), channel_id=1, source_target_pairs={{0,4},{4,0},{1,5},{5,1},{2,6},{6,2},{3,7},{7,3},{8,12},{12,8},{9,1... | collective-permute-start | bytes 196616 | tf_op jit(solution)/shard_map/ppermute | solution.py:272
  66.5 1.6 %collective-permute-start.22 = (f32[1,128,256]{2,1,0:T(8,128)S(1)}, f32[1,128,256]{2,1,0:T(8,128)S(1)}, u32[]{:S(2)}, u32[]{:S(2)}) collective-permute-start(f32[1,128,256]{2,1,0:T(8,128)S(1)} %slice_add_fusion), channel_id=1, source_target_pairs={{0,2},{2,0},{1,3},{3,1},{4,6},{6,4},{5,7},{7,5},{8,10},{10,8},{9,1... | collective-permute-start | bytes 393224 | tf_op jit(solution)/shard_map/ppermute | solution.py:272
  66.6 3.8 %collective-permute-start.21 = (f32[1,128,128]{2,1,0:T(8,128)S(1)}, f32[1,128,128]{2,1,0:T(8,128)S(1)}, u32[]{:S(2)}, u32[]{:S(2)}) collective-permute-start(f32[1,128,128]{2,1,0:T(8,128)S(1)} %slice_add_fusion.1), channel_id=1, source_target_pairs={{0,2},{2,0},{1,3},{3,1},{4,6},{6,4},{5,7},{7,5},{8,10},{10,8},{9,1... | collective-permute-start | bytes 196616 | tf_op jit(solution)/shard_map/ppermute | solution.py:272
  (5 other events, 23.3 us)

commit v5 on v4

--- a/solution.py
+++ b/solution.py
@@ -22,16 +22,21 @@
 HIDDEN = -1e30
 NT = (((1,), (1,)), ((), ()))
 HINT = pl.CostEstimate(flops=1024, bytes_accessed=1024, transcendentals=0)
-LONG = pl.CostEstimate(flops=2**33, bytes_accessed=2**23, transcendentals=2**22)
-
-CHUNKS = ((0, 2), (2, 1), (3, 1))
-HELP = (3, 4, 4)
-
-
-def pair_scores(keys, q_ref, g):
+LONG = pl.CostEstimate(flops=2**32, bytes_accessed=1024, transcendentals=0)
+
+CHUNKS = ((0, 2), (2, 2))
+HELP = (4, 5)
+
+
+def pair_queries(q_ref, g, extra=None):
     heads = [q_ref[:, i * HD : (i + 1) * HD] for i in (g, g + 1)]
-    scores = lax.dot_general(keys, jnp.concatenate(heads, axis=0), NT, preferred_element_type=jnp.float32)
-    return scores * SCALE
+    if extra is not None:
+        heads = [jnp.concatenate([head, extra], axis=1) for head in heads]
+    return jnp.concatenate(heads, axis=0)
+
+
+def scores_of(keys, queries):
+    return lax.dot_general(keys, queries, NT, preferred_element_type=jnp.float32)
 
 
 def prompt_kernel(first, info, q_ref, k_ref, v_ref, *refs):
@@ -40,21 +45,26 @@
     else:
         old_acc, old_ml, acc_ref, ml_ref = refs
     count = k_ref.shape[0]
-    place = info[0] + lax.broadcasted_iota(jnp.int32, (count, PAIR), 0)
-    lane = lax.broadcasted_iota(jnp.int32, (count, PAIR), 1)
-    listed = jnp.where(lane % ROWS < RLEN, info[2], info[3])
-    bias = jnp.where((place < info[1]) & (listed == 1), 0.0, HIDDEN)
-    keys = k_ref[...]
+    place = info[0] + lax.broadcasted_iota(jnp.int32, (count, HD), 0)
+    column = lax.broadcasted_iota(jnp.int32, (count, HD), 1)
+    listed = jnp.where(column == 0, info[2], info[3])
+    hidden = (column < RESP_DEV) & ((place >= info[1]) | (listed != 1))
+    keys = jnp.concatenate([k_ref[...], jnp.where(hidden, HIDDEN, 0.0).astype(jnp.bfloat16)], axis=1)
+    owner = lax.broadcasted_iota(jnp.int32, (ROWS, HD), 0) // RLEN
+    ours = jnp.where(owner == lax.broadcasted_iota(jnp.int32, (ROWS, HD), 1), 1.0, 0.0).astype(jnp.bfloat16)
     values = v_ref[...].T
+    ahead = scores_of(keys, pair_queries(q_ref, 0, ours))
     for g in range(0, SHARED, 2):
         cols = slice(g * HD, (g + 2) * HD)
-        scores = pair_scores(keys, q_ref, g) + bias
+        scores = ahead
+        if g + 2 < SHARED:
+            ahead = scores_of(keys, pair_queries(q_ref, g + 2, ours))
         largest = jnp.max(scores, axis=0, keepdims=True)
         if not first:
             before = old_ml[0:1, cols]
             largest = jnp.maximum(largest, before)
-            faded = jnp.exp2(before - largest)
-        weights = jnp.exp2(scores - largest)
+            faded = jnp.exp2((before - largest) * SCALE)
+        weights = jnp.exp2((scores - largest) * SCALE)
         total = jnp.sum(weights, axis=0, keepdims=True)
         acc = jnp.dot(values, weights.astype(jnp.bfloat16), preferred_element_type=jnp.float32)
         if not first:
@@ -227,13 +237,15 @@
         mean = jnp.mean(raw * raw, axis=1, keepdims=True)
         keys = (raw * lax.rsqrt(mean + 1e-06) * gain_ref[...]).astype(jnp.bfloat16)
         values = jnp.where(first_core, away, here).T.astype(jnp.bfloat16)
-        for g in range(0, SHARED, 2):
+        pairs = range(0, SHARED, 2)
+        products = [scores_of(keys, pair_queries(q_ref, (head + k) * SHARED + g)) for g in pairs]
+        for g, scores in zip(pairs, products):
             cols = slice(((offset + k) * SHARED + g) * HD, ((offset + k) * SHARED + g + 2) * HD)
-            scores = jnp.where(seen, pair_scores(keys, q_ref, (head + k) * SHARED + g), HIDDEN)
+            scores = jnp.where(seen, scores, HIDDEN)
             before = ml_ref[0:1, cols]
             largest = jnp.maximum(jnp.max(scores, axis=0, keepdims=True), before)
-            faded = jnp.exp2(before - largest)
-            weights = jnp.exp2(scores - largest)
+            faded = jnp.exp2((before - largest) * SCALE)
+            weights = jnp.exp2((scores - largest) * SCALE)
             total = jnp.sum(weights, axis=0, keepdims=True) + faded * ml_ref[1:2, cols]
             acc = jnp.dot(values, weights.astype(jnp.bfloat16), preferred_element_type=jnp.float32)
             acc = (acc + faded * acc_ref[:, cols]) * (live / total)
@@ -311,21 +323,15 @@
         listed = lax.dynamic_index_in_dim(block_table[0], place // BLOCK, axis=1, keepdims=False)
         infos.append(jnp.concatenate([place[None], prompt_lengths, listed]).astype(jnp.int32))
 
-    def rest(head, heads, state, offset):
-        for stride in range(1, cycle):
-            state = prompt_attention(infos[stride], query, caches[stride], state, head, heads, offset)
-            offset = 0
-        return state
-
     query, _, _ = tie((query, whole[0], given))
     state = prompt_attention(infos[0], query, caches[0], None, 0, KVH)
 
-    sent[0], caches, state, next_chunk = tie((sent[0], caches, state, (whole[1], far[1])))
-    sent.append(send(*next_chunk))
+    sent[0], caches, state, second = tie((sent[0], caches, state, (whole[1], far[1])))
+    sent.append(send(*second))
     forwarded = [forward(0)]
-    halves = [rest(0, 2, state, 0)]
-    sent[1], forwarded[0], halves[0], next_chunk = tie((sent[1], forwarded[0], halves[0], (whole[2], far[2])))
-    sent.append(send(*next_chunk))
+    for stride in range(1, cycle):
+        state = prompt_attention(infos[stride], query, caches[stride], state, 0, KVH)
+    sent[1], forwarded[0], state = tie((sent[1], forwarded[0], state))
     forwarded.append(forward(1))
 
     def sums(i):
@@ -335,23 +341,15 @@
     gain = key_gain[None]
     mine_0, theirs_0 = sums(0)
     theirs_0 = xor_swap(theirs_0, "y", 1)
-    mine_0, forwarded[1] = tie((mine_0, forwarded[1]))
+    forwarded[1], mine_0 = tie((forwarded[1], mine_0))
     mine_1, theirs_1 = sums(1)
+    theirs_0, theirs_1 = tie((theirs_0, theirs_1))
     theirs_1 = xor_swap(theirs_1, "y", 1)
-    sent[2], mine_1, state = tie((sent[2], mine_1, state))
-    forwarded.append(forward(2))
-    halves.append(rest(2, 2, state, 2))
-    theirs_0, theirs_1, halves[1] = tie((theirs_0, theirs_1, halves[1]))
     there_0 = xor_swap(mine_0[1:] + theirs_0[1:], "core", 1)
+    result = final_attention(info, gain, query, state, 0, CHUNKS[0], mine_0, theirs_0, there_0, None)
+    theirs_1, result = tie((theirs_1, result))
     there_1 = xor_swap(mine_1[1:] + theirs_1[1:], "core", 1)
-    result = final_attention(info, gain, query, halves[0], 0, CHUNKS[0], mine_0, theirs_0, there_0, None)
-    mine_2, theirs_2 = sums(2)
-    there_2 = [xor_swap(mine_2[1], "core", 1), xor_swap(theirs_2[1], ("y", "core"), 3)]
-    theirs_2 = xor_swap(theirs_2[:1], "y", 1)
-    result = final_attention(info, gain, query, halves[1], 0, CHUNKS[1], mine_1, theirs_1, there_1, result)
-    result = final_attention(
-        info, gain, query, halves[1], 1, CHUNKS[2], mine_2, theirs_2, jnp.stack(there_2), result
-    )
+    result = final_attention(info, gain, query, state, 2, CHUNKS[1], mine_1, theirs_1, there_1, result)
     return result[None]
 
 

time: 75.5 us -> 69.1 us (0.915)
  waiting for transfers between devices: 12.8 us -> 25.7 us
  Pallas kernels: 30.7 us -> 20.8 us
  starting transfers between devices: 27.7 us -> 19.2 us
    ppermute x22 -> x15, waiting for transfers between devices: 12.8 us -> 25.7 us  [xor_swap(): lax.ppermute(array, axis, [(i, i ^ by) for i in range(lax.axis_size(axis))])]
    ppermute x22 -> x15, starting transfers between devices: 24.8 us -> 16.3 us  [xor_swap(): lax.ppermute(array, axis, [(i, i ^ by) for i in range(lax.axis_size(axis))])]
    pallas_call x3 -> x2, Pallas kernels: 18.6 us -> 11.7 us  [prompt_attention(): pl.pallas_call(functools.partial(prompt_kernel, first), grid_spec=pltpu.P...]
    pallas_call x3 -> x2, Pallas kernels: 6.43 us -> 4.67 us  [final_attention(): pl.pallas_call(functools.partial(final_kernel, chunk, offset), in_specs=s...]
    pallas_call x5 -> x4, Pallas kernels: 5.69 us -> 4.38 us  [on_chip(): pl.pallas_call(kernel, in_specs=[SMEM] + [VMEM] * len(operands), out_spec...]
  transfers between devices with their start and end apart: 23 -> 16, of which waited for: 4 -> 8; matrix products, arithmetic and copies ran while one was open for 2% -> 2% of each run, Pallas kernels for 38% -> 27%
where the time goes in v5:
time: 69.1 us; the launch traced here: 68.9 us
  waiting for transfers between devices  25.7 us (37%)
  Pallas kernels  20.8 us (30%)
  starting transfers between devices  19.2 us (28%)
  local copies, waits for them, and re-layouts  2.11 us (3%)
  between operations  0.81 us (1%)
    ppermute x15, waiting for transfers between devices, xor_swap(): lax.ppermute(array, axis, [(i, i ^ by) for i in range(lax.axis_size(axis))])  25.7 us
    ppermute x15, starting transfers between devices, xor_swap(): lax.ppermute(array, axis, [(i, i ^ by) for i in range(lax.axis_size(axis))])  16.3 us
    pallas_call x2, Pallas kernels, prompt_attention(): pl.pallas_call(functools.partial(prompt_kernel, first), grid_spec=pltpu.P...  11.7 us
    pallas_call x2, Pallas kernels, final_attention(): pl.pallas_call(functools.partial(final_kernel, chunk, offset), in_specs=s...  4.67 us
    pallas_call x4, Pallas kernels, on_chip(): pl.pallas_call(kernel, in_specs=[SMEM] + [VMEM] * len(operands), out_spec...  4.38 us
    ppermute x1, starting transfers between devices, per_device(): lax.ppermute(caches[-1], 'blk', [(i, (i + 1) % cycle) for i in range(cycl...  2.93 us
  transfers between devices with their start and end apart: 16, of which 8 were waited for; matrix products, arithmetic and copies ran while one was open for 2% of the time, Pallas kernels for 27%

profile of v5, /device:TPU:0, one launch (start us, length us, event | category | flops | bytes accessed | tf_op | source)
XLA Modules:
  0.0 68.9 jit_solution(17258070087464419668)
XLA Ops:
  0.5 2.9 %collective-permute-start.5 = (bf16[512,1024]{1,0:T(8,128)(2,1)}, bf16[512,1024]{1,0:T(8,128)(2,1)}, u32[]{:S(2)}, u32[]{:S(2)}) collective-permute-start(bf16[512,1024]{1,0:T(8,128)(2,1)} %bitcast.28), channel_id=1, source_target_pairs={{0,1},{1,0},{2,3},{3,2},{4,5},{5,4},{6,7},{7,6},{8,9},{9,8},{10,11... | collective-permute-start | bytes 3145736 | tf_op jit(solution)/shard_map/ppermute | solution.py:303
  4.1 1.0 %dynamic-slice_reduce_fusion = (s32[2]{0:T(128)S(1)}, s32[2]{0:T(128)S(1)}) fusion(s32[1,2,2]{2,1,0:T(2,128)} %param.14, s32[]{:T(128)S(6)} %select_n.30, s32[]{:T(128)S(6)} %select_n.27), kind=kLoop, calls=%fused_computation.6 | loop fusion | bytes 40 | tf_op jit(solution)/shard_map/jit(dynamic_index_in_dim)/dynamic_slice | solution.py:323
  5.3 1.1 %copy-done.2 = bf16[320,1024]{1,0:T(8,128)(2,1)S(1)} copy-done((bf16[320,1024]{1,0:T(8,128)(2,1)S(1)}, bf16[320,1024]{1,0:T(8,128)(2,1)}, u32[]{:S(2)}) %copy-start.2) | copy-done | bytes 655384
  7.0 3.0 %collective-permute-start.3 = (bf16[384,256]{1,0:T(8,128)(2,1)S(1)}, bf16[384,256]{1,0:T(8,128)(2,1)S(1)}, u32[]{:S(2)}, u32[]{:S(2)}) collective-permute-start(bf16[384,256]{1,0:T(8,128)(2,1)S(1)} %get-tuple-element.43), channel_id=1, source_target_pairs={{0,16},{8,24},{16,0},{24,8},{1,17},{9,25},{17,1},{25,9},{2,18},{10... | collective-permute-start | bytes 589832 | tf_op jit(solution)/shard_map/ppermute | solution.py:284
  10.0 1.3 %collective-permute-start.4 = (bf16[384,256]{1,0:T(8,128)(2,1)S(1)}, bf16[384,256]{1,0:T(8,128)(2,1)S(1)}, u32[]{:S(2)}, u32[]{:S(2)}) collective-permute-start(bf16[384,256]{1,0:T(8,128)(2,1)S(1)} %get-tuple-element.43), channel_id=1, source_target_pairs={{0,24},{8,16},{16,8},{24,0},{1,25},{9,17},{17,9},{25,1},{2,26},{10... | collective-permute-start | bytes 589832 | tf_op jit(solution)/shard_map/ppermute | solution.py:284
  12.3 1.6 %collective-permute-start.10 = (bf16[2,4,128,640]{3,2,1,0:T(8,128)(2,1)S(1)}, bf16[2,4,128,640]{3,2,1,0:T(8,128)(2,1)S(1)}, u32[]{:S(2)}, u32[]{:S(2)}) collective-permute-start(bf16[2,4,128,640]{3,2,1,0:T(8,128)(2,1)S(1)} %get-tuple-element.41), channel_id=1, source_target_pairs={{0,4},{4,0},{1,5},{5,1},{2,6},{6,2},{3,7},{7,3},{8,12},{12,8},{9,1... | collective-permute-start | bytes 3932168 | tf_op jit(solution)/shard_map/ppermute | solution.py:284
  13.9 5.4 %prompt_attention.2 = (f32[128,4096]{1,0:T(8,128)S(1)}, f32[8,4096]{1,0:T(8,128)S(1)}) custom-call(s32[4]{0:T(128)S(1)} %get-tuple-element.77.info, bf16[128,4096]{1,0:T(8,128)(2,1)S(1)} %bitcast.18, bf16[512,1024]{1,0:T(8,128)(2,1)S(1)} %bitcast.29, bf16[512,1024]{1,0:T(8,128)(2,1)S(1)} %bitcast.30), custom_call_target="tpu_custom_call" | custom-call | flops 4294967296 | bytes 1024 | tf_op jit(solution)/shard_map/prompt_attention/pallas_call | solution.py:96
  19.4 4.8 %collective-permute-done.3.refs_0_ = bf16[384,256]{1,0:T(8,128)(2,1)S(1)} collective-permute-done((bf16[384,256]{1,0:T(8,128)(2,1)S(1)}, bf16[384,256]{1,0:T(8,128)(2,1)S(1)}, u32[]{:S(2)}, u32[]{:S(2)}) %collective-permute-start.3) | collective-permute-done | bytes 196640 | tf_op jit(solution)/shard_map/ppermute | solution.py:284
  24.2 3.7 %collective-permute-done.2.near = bf16[640,256]{1,0:T(8,128)(2,1)S(1)} collective-permute-done((bf16[640,256]{1,0:T(8,128)(2,1)S(1)}, bf16[640,256]{1,0:T(8,128)(2,1)S(1)}, u32[]{:S(2)}, u32[]{:S(2)}) %collective-permute-start.2) | collective-permute-done | bytes 327712 | tf_op jit(solution)/shard_map/ppermute | solution.py:284
  27.8 2.7 %collective-permute-start.7 = (bf16[320,256]{1,0:T(8,128)(2,1)S(1)}, bf16[320,256]{1,0:T(8,128)(2,1)S(1)}, u32[]{:S(2)}, u32[]{:S(2)}) collective-permute-start(bf16[320,256]{1,0:T(8,128)(2,1)S(1)} %get-tuple-element.49), channel_id=1, source_target_pairs={{0,16},{8,24},{16,0},{24,8},{1,17},{9,25},{17,1},{25,9},{2,18},{10... | collective-permute-start | bytes 491528 | tf_op jit(solution)/shard_map/ppermute | solution.py:284
  31.4 1.6 %collective-permute-start.9 = (bf16[2,256,256]{2,1,0:T(8,128)(2,1)S(1)}, bf16[2,256,256]{2,1,0:T(8,128)(2,1)S(1)}, u32[]{:S(2)}, u32[]{:S(2)}) collective-permute-start(bf16[2,256,256]{2,1,0:T(8,128)(2,1)S(1)} %pad_maximum_fusion.1), channel_id=1, source_target_pairs={{0,1},{1,0},{2,3},{3,2},{4,5},{5,4},{6,7},{7,6},{8,9},{9,8},{10,11... | collective-permute-start | bytes 786440 | tf_op jit(solution)/shard_map/ppermute | solution.py:284
  33.5 6.3 %prompt_attention.3 = (f32[128,4096]{1,0:T(8,128)S(1)}, f32[8,4096]{1,0:T(8,128)S(1)}) custom-call(s32[4]{0:T(128)S(1)} %get-tuple-element.78.info, bf16[128,4096]{1,0:T(8,128)(2,1)S(1)} %bitcast.19, bf16[512,1024]{1,0:T(8,128)(2,1)} %collective-permute-done.5.k_ref.v_ref, bf16[512,1024]{1,0:T(8,128)(2,1)} %collective-permute-done.5.k_ref.v_ref, ...), custom_call_target="tpu_custom_call" | custom-call | flops 4294967296 | bytes 1024 | tf_op jit(solution)/shard_map/prompt_attention/pallas_call | solution.py:96
  39.8 2.4 %collective-permute-done.7.refs_0_ = bf16[320,256]{1,0:T(8,128)(2,1)S(1)} collective-permute-done((bf16[320,256]{1,0:T(8,128)(2,1)S(1)}, bf16[320,256]{1,0:T(8,128)(2,1)S(1)}, u32[]{:S(2)}, u32[]{:S(2)}) %collective-permute-start.7) | collective-permute-done | bytes 163872 | tf_op jit(solution)/shard_map/ppermute | solution.py:284
  42.3 5.9 %collective-permute-done.6.near = bf16[640,256]{1,0:T(8,128)(2,1)S(1)} collective-permute-done((bf16[640,256]{1,0:T(8,128)(2,1)S(1)}, bf16[640,256]{1,0:T(8,128)(2,1)S(1)}, u32[]{:S(2)}, u32[]{:S(2)}) %collective-permute-start.6) | collective-permute-done | bytes 327712 | tf_op jit(solution)/shard_map/ppermute | solution.py:284
  48.8 1.5 %project.2 = (f32[2,128,256]{2,1,0:T(8,128)S(1)}, f32[2,128,256]{2,1,0:T(8,128)S(1)}) custom-call(s32[4]{0:T(128)S(1)} %pad_add_fusion.1.where, bf16[2,4,128,640]{3,2,1,0:T(8,128)(2,1)S(1)} %get-tuple-element.59.keep, bf16[2,4,128,640]{3,2,1,0:T(8,128)(2,1)S(1)} %collective-permute-done.10.other, bf16[640,256]{1,0:T(8,128)(2,1)S(1)} %get-tuple-element.40.own, ...), custom_call_target="tpu_custom_call" | custom-call | flops 1024 | bytes 1024 | tf_op jit(solution)/shard_map/project/pallas_call | solution.py:117
  50.3 1.6 %collective-permute-start.12 = (f32[2,128,256]{2,1,0:T(8,128)S(1)}, f32[2,128,256]{2,1,0:T(8,128)S(1)}, u32[]{:S(2)}, u32[]{:S(2)}) collective-permute-start(f32[2,128,256]{2,1,0:T(8,128)S(1)} %get-tuple-element.68), channel_id=1, source_target_pairs={{0,4},{4,0},{1,5},{5,1},{2,6},{6,2},{3,7},{7,3},{8,12},{12,8},{9,1... | collective-permute-start | bytes 786440 | tf_op jit(solution)/shard_map/ppermute | solution.py:284
  51.9 5.1 %collective-permute-done.11.forwarded = bf16[2,320,256]{2,1,0:T(8,128)(2,1)S(1)} collective-permute-done((bf16[2,320,256]{2,1,0:T(8,128)(2,1)S(1)}, bf16[2,320,256]{2,1,0:T(8,128)(2,1)S(1)}, u32[]{:S(2)}, u32[]{:S(2)}) %collective-permute-start.11) | collective-permute-done | bytes 327712 | tf_op jit(solution)/shard_map/ppermute | solution.py:284
  57.1 1.5 %project.3 = (f32[2,128,256]{2,1,0:T(8,128)S(1)}, f32[2,128,256]{2,1,0:T(8,128)S(1)}) custom-call(s32[4]{0:T(128)S(1)} %pad_add_fusion.1.where, bf16[2,4,128,640]{3,2,1,0:T(8,128)(2,1)S(1)} %get-tuple-element.59.keep, bf16[2,4,128,640]{3,2,1,0:T(8,128)(2,1)S(1)} %collective-permute-done.10.other, bf16[640,256]{1,0:T(8,128)(2,1)S(1)} %get-tuple-element.48.own, ...), custom_call_target="tpu_custom_call" | custom-call | flops 1024 | bytes 1024 | tf_op jit(solution)/shard_map/project/pallas_call | solution.py:117
  58.6 1.6 %collective-permute-start.13 = (f32[2,128,256]{2,1,0:T(8,128)S(1)}, f32[2,128,256]{2,1,0:T(8,128)S(1)}, u32[]{:S(2)}, u32[]{:S(2)}) collective-permute-start(f32[2,128,256]{2,1,0:T(8,128)S(1)} %get-tuple-element.70), channel_id=1, source_target_pairs={{0,4},{4,0},{1,5},{5,1},{2,6},{6,2},{3,7},{7,3},{8,12},{12,8},{9,1... | collective-permute-start | bytes 786440 | tf_op jit(solution)/shard_map/ppermute | solution.py:284
  60.3 1.2 %collective-permute-done.14.there = f32[1,128,256]{2,1,0:T(8,128)S(1)} collective-permute-done((f32[1,128,256]{2,1,0:T(8,128)S(1)}, f32[1,128,256]{2,1,0:T(8,128)S(1)}, u32[]{:S(2)}, u32[]{:S(2)}) %collective-permute-start.14) | collective-permute-done | bytes 131104 | tf_op jit(solution)/shard_map/ppermute | solution.py:284
  61.6 2.3 %final_attention.2.refs_0_ = bf16[128,4096]{1,0:T(8,128)(2,1)} custom-call(s32[3]{0:T(128)S(1)} %pad_add_fusion.info, f32[1,128]{1,0:T(1,128)S(1)} %bitcast.26, bf16[128,4096]{1,0:T(8,128)(2,1)S(1)} %bitcast.20, f32[128,4096]{1,0:T(8,128)S(1)} %get-tuple-element.57.acc_ref, f32[8,4096]{1,0:T(8,128)S(1)} %get-tuple-element.58.ml_ref, ...), custom_call_target="tpu_custom_call" | custom-call | flops 1024 | bytes 1024 | tf_op jit(solution)/shard_map/final_attention/pallas_call | solution.py:270
  63.9 1.1 %collective-permute-done.13.theirs = f32[2,128,256]{2,1,0:T(8,128)S(1)} collective-permute-done((f32[2,128,256]{2,1,0:T(8,128)S(1)}, f32[2,128,256]{2,1,0:T(8,128)S(1)}, u32[]{:S(2)}, u32[]{:S(2)}) %collective-permute-start.13) | collective-permute-done | bytes 262176 | tf_op jit(solution)/shard_map/ppermute | solution.py:284
  65.2 1.3 %collective-permute-done.15.there = f32[1,128,256]{2,1,0:T(8,128)S(1)} collective-permute-done((f32[1,128,256]{2,1,0:T(8,128)S(1)}, f32[1,128,256]{2,1,0:T(8,128)S(1)}, u32[]{:S(2)}, u32[]{:S(2)}) %collective-permute-start.15) | collective-permute-done | bytes 131104 | tf_op jit(solution)/shard_map/ppermute | solution.py:284
  66.5 2.3 %final_attention.3 = bf16[128,4096]{1,0:T(8,128)(2,1)} custom-call(s32[3]{0:T(128)S(1)} %pad_add_fusion.info, f32[1,128]{1,0:T(1,128)S(1)} %bitcast.27, bf16[128,4096]{1,0:T(8,128)(2,1)S(1)} %bitcast.21, f32[128,4096]{1,0:T(8,128)S(1)} %get-tuple-element.57.acc_ref, f32[8,4096]{1,0:T(8,128)S(1)} %get-tuple-element.58.ml_ref, ...), custom_call_target="tpu_custom_call", output_to_operand_aliasing={{}: (8, {})} | custom-call | flops 1024 | bytes 1024 | tf_op jit(solution)/shard_map/final_attention/pallas_call | solution.py:270
  (38 shorter events, 4.6 us)
Async XLA Ops:
  0.0 11.6 %copy-start.1 = (bf16[1,128,5120]{2,1,0:T(8,128)(2,1)S(1)}, bf16[1,128,5120]{2,1,0:T(8,128)(2,1)}, u32[]{:S(2)}) copy-start(bf16[1,128,5120]{2,1,0:T(8,128)(2,1)} %param.8) | copy-start | bytes 3932164
  0.0 11.6 %collective-permute-start.1 = (bf16[128,5120]{1,0:T(8,128)(2,1)}, bf16[128,5120]{1,0:T(8,128)(2,1)S(1)}, u32[]{:S(2)}, u32[]{:S(2)}) collective-permute-start(bf16[128,5120]{1,0:T(8,128)(2,1)} %bitcast.22), channel_id=1, source_target_pairs={{0,2},{2,0},{1,3},{3,1},{4,6},{6,4},{5,7},{7,5},{8,10},{10,8},{9,1... | collective-permute-start | bytes 3932168 | tf_op jit(solution)/shard_map/ppermute | solution.py:284
  0.5 4.8 %collective-permute-start = (bf16[320,1024]{1,0:T(8,128)(2,1)}, bf16[320,1024]{1,0:T(8,128)(2,1)S(1)}, u32[]{:S(2)}, u32[]{:S(2)}) collective-permute-start(bf16[320,1024]{1,0:T(8,128)(2,1)} %own_ref.1), channel_id=1, source_target_pairs={{0,2},{2,0},{1,3},{3,1},{4,6},{6,4},{5,7},{7,5},{8,10},{10,8},{9,1... | collective-permute-start | bytes 1966088 | tf_op jit(solution)/shard_map/ppermute | solution.py:284
  0.5 27.3 %collective-permute-start.5 = (bf16[512,1024]{1,0:T(8,128)(2,1)}, bf16[512,1024]{1,0:T(8,128)(2,1)}, u32[]{:S(2)}, u32[]{:S(2)}) collective-permute-start(bf16[512,1024]{1,0:T(8,128)(2,1)} %bitcast.28), channel_id=1, source_target_pairs={{0,1},{1,0},{2,3},{3,2},{4,5},{5,4},{6,7},{7,6},{8,9},{9,8},{10,11... | collective-permute-start | bytes 3145736 | tf_op jit(solution)/shard_map/ppermute | solution.py:303
  5.3 1.1 %copy-start.2 = (bf16[320,1024]{1,0:T(8,128)(2,1)S(1)}, bf16[320,1024]{1,0:T(8,128)(2,1)}, u32[]{:S(2)}) copy-start(bf16[320,1024]{1,0:T(8,128)(2,1)} %own_ref.1) | copy-start | bytes 1966084
  7.0 17.2 %collective-permute-start.3 = (bf16[384,256]{1,0:T(8,128)(2,1)S(1)}, bf16[384,256]{1,0:T(8,128)(2,1)S(1)}, u32[]{:S(2)}, u32[]{:S(2)}) collective-permute-start(bf16[384,256]{1,0:T(8,128)(2,1)S(1)} %get-tuple-element.43), channel_id=1, source_target_pairs={{0,16},{8,24},{16,0},{24,8},{1,17},{9,25},{17,1},{25,9},{2,18},{10... | collective-permute-start | bytes 589832 | tf_op jit(solution)/shard_map/ppermute | solution.py:284
  10.0 14.2 %collective-permute-start.4 = (bf16[384,256]{1,0:T(8,128)(2,1)S(1)}, bf16[384,256]{1,0:T(8,128)(2,1)S(1)}, u32[]{:S(2)}, u32[]{:S(2)}) collective-permute-start(bf16[384,256]{1,0:T(8,128)(2,1)S(1)} %get-tuple-element.43), channel_id=1, source_target_pairs={{0,24},{8,16},{16,8},{24,0},{1,25},{9,17},{17,9},{25,1},{2,26},{10... | collective-permute-start | bytes 589832 | tf_op jit(solution)/shard_map/ppermute | solution.py:284
  11.3 2.6 %copy-start = (bf16[1,128,4096]{2,1,0:T(8,128)(2,1)S(1)}, bf16[1,128,4096]{2,1,0:T(8,128)(2,1)}, u32[]{:S(2)}) copy-start(bf16[1,128,4096]{2,1,0:T(8,128)(2,1)} %param.9) | copy-start | bytes 3145732
  11.3 2.6 %copy-start.4 = (bf16[1,512,1024]{2,1,0:T(8,128)(2,1)S(1)}, bf16[1,512,1024]{2,1,0:T(8,128)(2,1)}, u32[]{:S(2)}) copy-start(bf16[1,512,1024]{2,1,0:T(8,128)(2,1)} %param.10) | copy-start | bytes 3145732
  11.3 16.5 %collective-permute-start.2 = (bf16[640,256]{1,0:T(8,128)(2,1)S(1)}, bf16[640,256]{1,0:T(8,128)(2,1)S(1)}, u32[]{:S(2)}, u32[]{:S(2)}) collective-permute-start(bf16[640,256]{1,0:T(8,128)(2,1)S(1)} %get-tuple-element.40.own), channel_id=1, source_target_pairs={{0,8},{8,0},{16,24},{24,16},{1,9},{9,1},{17,25},{25,17},{2,10},{10... | collective-permute-start | bytes 983048 | tf_op jit(solution)/shard_map/ppermute | solution.py:284
  12.3 36.5 %collective-permute-start.10 = (bf16[2,4,128,640]{3,2,1,0:T(8,128)(2,1)S(1)}, bf16[2,4,128,640]{3,2,1,0:T(8,128)(2,1)S(1)}, u32[]{:S(2)}, u32[]{:S(2)}) collective-permute-start(bf16[2,4,128,640]{3,2,1,0:T(8,128)(2,1)S(1)} %get-tuple-element.41), channel_id=1, source_target_pairs={{0,4},{4,0},{1,5},{5,1},{2,6},{6,2},{3,7},{7,3},{8,12},{12,8},{9,1... | collective-permute-start | bytes 3932168 | tf_op jit(solution)/shard_map/ppermute | solution.py:284
  27.8 14.4 %collective-permute-start.7 = (bf16[320,256]{1,0:T(8,128)(2,1)S(1)}, bf16[320,256]{1,0:T(8,128)(2,1)S(1)}, u32[]{:S(2)}, u32[]{:S(2)}) collective-permute-start(bf16[320,256]{1,0:T(8,128)(2,1)S(1)} %get-tuple-element.49), channel_id=1, source_target_pairs={{0,16},{8,24},{16,0},{24,8},{1,17},{9,25},{17,1},{25,9},{2,18},{10... | collective-permute-start | bytes 491528 | tf_op jit(solution)/shard_map/ppermute | solution.py:284
  30.5 11.7 %collective-permute-start.8 = (bf16[320,256]{1,0:T(8,128)(2,1)S(1)}, bf16[320,256]{1,0:T(8,128)(2,1)S(1)}, u32[]{:S(2)}, u32[]{:S(2)}) collective-permute-start(bf16[320,256]{1,0:T(8,128)(2,1)S(1)} %get-tuple-element.49), channel_id=1, source_target_pairs={{0,24},{8,16},{16,8},{24,0},{1,25},{9,17},{17,9},{25,1},{2,26},{10... | collective-permute-start | bytes 491528 | tf_op jit(solution)/shard_map/ppermute | solution.py:284
  31.4 10.8 %collective-permute-start.9 = (bf16[2,256,256]{2,1,0:T(8,128)(2,1)S(1)}, bf16[2,256,256]{2,1,0:T(8,128)(2,1)S(1)}, u32[]{:S(2)}, u32[]{:S(2)}) collective-permute-start(bf16[2,256,256]{2,1,0:T(8,128)(2,1)S(1)} %pad_maximum_fusion.1), channel_id=1, source_target_pairs={{0,1},{1,0},{2,3},{3,2},{4,5},{5,4},{6,7},{7,6},{8,9},{9,8},{10,11... | collective-permute-start | bytes 786440 | tf_op jit(solution)/shard_map/ppermute | solution.py:284
  33.0 15.2 %collective-permute-start.6 = (bf16[640,256]{1,0:T(8,128)(2,1)S(1)}, bf16[640,256]{1,0:T(8,128)(2,1)S(1)}, u32[]{:S(2)}, u32[]{:S(2)}) collective-permute-start(bf16[640,256]{1,0:T(8,128)(2,1)S(1)} %get-tuple-element.48.own), channel_id=1, source_target_pairs={{0,8},{8,0},{16,24},{24,16},{1,9},{9,1},{17,25},{25,17},{2,10},{10... | collective-permute-start | bytes 983048 | tf_op jit(solution)/shard_map/ppermute | solution.py:284
  48.2 8.8 %collective-permute-start.11 = (bf16[2,320,256]{2,1,0:T(8,128)(2,1)S(1)}, bf16[2,320,256]{2,1,0:T(8,128)(2,1)S(1)}, u32[]{:S(2)}, u32[]{:S(2)}) collective-permute-start(bf16[2,320,256]{2,1,0:T(8,128)(2,1)S(1)} %pad_maximum_fusion), channel_id=1, source_target_pairs={{0,1},{1,0},{2,3},{3,2},{4,5},{5,4},{6,7},{7,6},{8,9},{9,8},{10,11... | collective-permute-start | bytes 983048 | tf_op jit(solution)/shard_map/ppermute | solution.py:284
  50.3 8.2 %collective-permute-start.12 = (f32[2,128,256]{2,1,0:T(8,128)S(1)}, f32[2,128,256]{2,1,0:T(8,128)S(1)}, u32[]{:S(2)}, u32[]{:S(2)}) collective-permute-start(f32[2,128,256]{2,1,0:T(8,128)S(1)} %get-tuple-element.68), channel_id=1, source_target_pairs={{0,4},{4,0},{1,5},{5,1},{2,6},{6,2},{3,7},{7,3},{8,12},{12,8},{9,1... | collective-permute-start | bytes 786440 | tf_op jit(solution)/shard_map/ppermute | solution.py:284
  57.0 3.2 %copy-start.5 = (s32[1,2]{1,0:T(1,128)S(1)}, s32[1,2]{1,0:T(1,128)}, u32[]{:S(2)}) copy-start(s32[1,2]{1,0:T(1,128)} %param.15) | copy-start | bytes 28
  57.0 4.5 %copy-start.3 = (f32[128]{0:T(128)S(1)}, f32[128]{0:T(128)}, u32[]{:S(2)}) copy-start(f32[128]{0:T(128)} %param.12) | copy-start | bytes 1540
  58.6 6.5 %collective-permute-start.13 = (f32[2,128,256]{2,1,0:T(8,128)S(1)}, f32[2,128,256]{2,1,0:T(8,128)S(1)}, u32[]{:S(2)}, u32[]{:S(2)}) collective-permute-start(f32[2,128,256]{2,1,0:T(8,128)S(1)} %get-tuple-element.70), channel_id=1, source_target_pairs={{0,4},{4,0},{1,5},{5,1},{2,6},{6,2},{3,7},{7,3},{8,12},{12,8},{9,1... | collective-permute-start | bytes 786440 | tf_op jit(solution)/shard_map/ppermute | solution.py:284
  60.2 1.4 %collective-permute-start.14 = (f32[1,128,256]{2,1,0:T(8,128)S(1)}, f32[1,128,256]{2,1,0:T(8,128)S(1)}, u32[]{:S(2)}, u32[]{:S(2)}) collective-permute-start(f32[1,128,256]{2,1,0:T(8,128)S(1)} %slice_add_fusion.1), channel_id=1, source_target_pairs={{0,2},{2,0},{1,3},{3,1},{4,6},{6,4},{5,7},{7,5},{8,10},{10,8},{9,1... | collective-permute-start | bytes 393224 | tf_op jit(solution)/shard_map/ppermute | solution.py:284
  65.1 1.4 %collective-permute-start.15 = (f32[1,128,256]{2,1,0:T(8,128)S(1)}, f32[1,128,256]{2,1,0:T(8,128)S(1)}, u32[]{:S(2)}, u32[]{:S(2)}) collective-permute-start(f32[1,128,256]{2,1,0:T(8,128)S(1)} %slice_add_fusion), channel_id=1, source_target_pairs={{0,2},{2,0},{1,3},{3,1},{4,6},{6,4},{5,7},{7,5},{8,10},{10,8},{9,1... | collective-permute-start | bytes 393224 | tf_op jit(solution)/shard_map/ppermute | solution.py:284

commit v6 on v5

--- a/solution.py
+++ b/solution.py
@@ -154,38 +154,47 @@
     return slice(chunk[0] * HD, (chunk[0] + chunk[1]) * HD)
 
 
-def pack_weight_kernel(where, own_ref, got_ref, *outs):
-    rows = own_ref.shape[0]
+def pack_weight_kernel(where, got_ref, own_ref, whole, *refs):
+    far, sem = refs[:-1], refs[-1]
+    rows = got_ref.shape[0]
     core, plane = where[2], where[3]
     half = pl.ds(pl.multiple_of(core * KVH * HD, 128), KVH * HD)
-    own, got = own_ref[:, half], got_ref[:, half]
-    for whole, far, chunk in zip(outs[0::2], outs[1::2], CHUNKS):
-        whole[pl.ds(pl.multiple_of(core * rows, 16), rows), :] = own[:, columns_of(chunk)]
-        whole[pl.ds(pl.multiple_of((1 - core) * rows, 16), rows), :] = got[:, columns_of(chunk)]
-        direct = far.shape[0]
-        far[...] = whole[pl.ds(pl.multiple_of(plane * (2 * rows - direct), 16), direct), :]
+    own_place = pl.ds(pl.multiple_of(core * rows, 16), rows)
+    copy = pltpu.make_async_copy(own_ref.at[:, half], whole.at[own_place, :], sem)
+    copy.start()
+    whole[pl.ds(pl.multiple_of((1 - core) * rows, 16), rows), :] = got_ref[:, half]
+    copy.wait()
+    for out, chunk in zip(far, CHUNKS):
+        direct = out.shape[0]
+        out[...] = whole[pl.ds(pl.multiple_of(plane * (2 * rows - direct), 16), direct), columns_of(chunk)]
 
 
 def pack_weight(where, own, got):
     rows = 2 * own.shape[0]
-    shapes = []
-    for i, (_, heads) in enumerate(CHUNKS):
-        shapes += [(rows, heads * HD), (row_split(rows, i)[1], heads * HD)]
-    outs = [jax.ShapeDtypeStruct(shape, own.dtype) for shape in shapes]
-    outs = on_chip(pack_weight_kernel, "pack_weight", outs, where, own, got)
-    return list(outs[0::2]), list(outs[1::2])
-
-
-def project_kernel(where, keep, other, own, near, forwarded, *refs):
+    shapes = [(rows, KVH * HD)] + [(row_split(rows, i)[1], heads * HD) for i, (_, heads) in enumerate(CHUNKS)]
+    whole, *far = pl.pallas_call(
+        pack_weight_kernel,
+        in_specs=[SMEM, VMEM, pl.BlockSpec(memory_space=pltpu.HBM)],
+        out_specs=[VMEM] * len(shapes),
+        out_shape=[jax.ShapeDtypeStruct(shape, own.dtype) for shape in shapes],
+        scratch_shapes=[pltpu.SemaphoreType.DMA],
+        compiler_params=PARAMS,
+        cost_estimate=HINT,
+        name="pack_weight",
+    )(where, got, own)
+    return whole, far
+
+
+def project_kernel(columns, where, keep, other, own, near, forwarded, *refs):
     direct, mine, theirs, whole = refs[:-3], refs[-3], refs[-2], refs[-1]
     plane = where[3]
     count, extra = direct[0].shape[0], forwarded.shape[1]
     total = None
     for j in range(2 + len(direct)):
         if j == 0:
-            weight = own[...]
+            weight = own[:, columns]
         elif j == 1:
-            weight = near[...]
+            weight = near[:, columns]
         else:
             far = whole.at[j - 2]
             far[pl.ds(pl.multiple_of(plane * extra, 16), count), :] = direct[j - 2][...]
@@ -200,11 +209,11 @@
         theirs[i] = total[(2 + i) * ROWS : (3 + i) * ROWS]
 
 
-def project(where, keep, other, own, near, direct, forwarded):
-    width = own.shape[1]
+def project(where, keep, other, chunk, own, near, direct, forwarded):
+    width = chunk[1] * HD
     out = jax.ShapeDtypeStruct((2, ROWS, width), jnp.float32)
     return on_chip(
-        project_kernel,
+        functools.partial(project_kernel, columns_of(chunk)),
         "project",
         [out, out],
         where,
@@ -304,18 +313,20 @@
 
     whole, far = pack_weight(where, kv_weight, got_weight)
 
-    def send(whole, far):
-        return xor_swap(whole, "z", 1), [xor_swap(far, "z", j) for j in range(2, steps)]
+    def send(far):
+        return [xor_swap(far, "z", j) for j in range(2, steps)]
 
     def forward(i):
-        helped, direct = row_split(whole[0].shape[0], i)
-        parts = [lax.dynamic_slice_in_dim(p, plane * (direct - helped), helped, axis=0) for p in sent[i][1]]
+        helped, direct = row_split(whole.shape[0], i)
+        parts = [lax.dynamic_slice_in_dim(p, plane * (direct - helped), helped, axis=0) for p in sent[i]]
         return xor_swap(jnp.stack(parts), "blk", 1)
 
-    sent = [send(whole[0], far[0])]
+    sent = [send(far[0])]
+    near = xor_swap(whole, "z", 1)
     keep, given = pack_rows(where, x, got_x, y, steps)
     other = xor_swap(given, "y", 1)
 
+    block_table, _ = tie((block_table, whole))
     infos = []
     for stride in range(cycle):
         owner = lax.rem(holder + cycle - stride, cycle)
@@ -323,11 +334,11 @@
         listed = lax.dynamic_index_in_dim(block_table[0], place // BLOCK, axis=1, keepdims=False)
         infos.append(jnp.concatenate([place[None], prompt_lengths, listed]).astype(jnp.int32))
 
-    query, _, _ = tie((query, whole[0], given))
+    query, _, _ = tie((query, whole, given))
     state = prompt_attention(infos[0], query, caches[0], None, 0, KVH)
 
-    sent[0], caches, state, second = tie((sent[0], caches, state, (whole[1], far[1])))
-    sent.append(send(*second))
+    sent[0], caches, state, far[1] = tie((sent[0], caches, state, far[1]))
+    sent.append(send(far[1]))
     forwarded = [forward(0)]
     for stride in range(1, cycle):
         state = prompt_attention(infos[stride], query, caches[stride], state, 0, KVH)
@@ -335,7 +346,7 @@
     forwarded.append(forward(1))
 
     def sums(i):
-        return project(where, keep, other, whole[i], *sent[i], forwarded[i])
+        return project(where, keep, other, CHUNKS[i], whole, near, sent[i], forwarded[i])
 
     info = jnp.concatenate([resp_lengths[0], core[None]]).astype(jnp.int32)
     gain = key_gain[None]

time: 69.1 us -> 64.9 us (0.939)
  the two profiles are of different devices: /device:TPU:0 before, /device:TPU:9 now
where the time goes in v6:
time: 64.9 us; the launch traced here: 64.8 us
  waiting for transfers between devices  23.1 us (36%)
  Pallas kernels  20.8 us (32%)
  starting transfers between devices  18.4 us (28%)
  local copies, waits for them, and re-layouts  1.35 us (2%)
  between operations  0.82 us (1%)
    ppermute x14, waiting for transfers between devices, xor_swap(): lax.ppermute(array, axis, [(i, i ^ by) for i in range(lax.axis_size(axis))])  23.1 us
    ppermute x14, starting transfers between devices, xor_swap(): lax.ppermute(array, axis, [(i, i ^ by) for i in range(lax.axis_size(axis))])  17.2 us
    pallas_call x2, Pallas kernels, prompt_attention(): pl.pallas_call(functools.partial(prompt_kernel, first), grid_spec=pltpu.P...  11.7 us
    pallas_call x2, Pallas kernels, final_attention(): pl.pallas_call(functools.partial(final_kernel, chunk, offset), in_specs=s...  4.67 us
    pallas_call x3, Pallas kernels, on_chip(): pl.pallas_call(kernel, in_specs=[SMEM] + [VMEM] * len(operands), out_spec...  3.76 us
  transfers between devices with their start and end apart: 15, of which 7 were waited for; matrix products, arithmetic and copies ran while one was open for 1% of the time, Pallas kernels for 28%

profile of v6, /device:TPU:9, one launch (start us, length us, event | category | flops | bytes accessed | tf_op | source)
XLA Modules:
  0.0 64.8 jit_solution(2906592148634062790)
XLA Ops:
  0.7 1.2 %collective-permute-start.4 = (bf16[512,1024]{1,0:T(8,128)(2,1)}, bf16[512,1024]{1,0:T(8,128)(2,1)}, u32[]{:S(2)}, u32[]{:S(2)}) collective-permute-start(bf16[512,1024]{1,0:T(8,128)(2,1)} %bitcast.28), channel_id=1, source_target_pairs={{0,1},{1,0},{2,3},{3,2},{4,5},{5,4},{6,7},{7,6},{8,9},{9,8},{10,11... | collective-permute-start | bytes 3145736 | tf_op jit(solution)/shard_map/ppermute | solution.py:312
  2.7 1.8 %collective-permute-done.got_ref = bf16[320,1024]{1,0:T(8,128)(2,1)S(1)} collective-permute-done((bf16[320,1024]{1,0:T(8,128)(2,1)}, bf16[320,1024]{1,0:T(8,128)(2,1)S(1)}, u32[]{:S(2)}, u32[]{:S(2)}) %collective-permute-start) | collective-permute-done | bytes 655392 | tf_op jit(solution)/shard_map/ppermute | solution.py:293
  4.5 1.1 %copy-done.2 = bf16[320,1024]{1,0:T(8,128)(2,1)S(1)} copy-done((bf16[320,1024]{1,0:T(8,128)(2,1)S(1)}, bf16[320,1024]{1,0:T(8,128)(2,1)}, u32[]{:S(2)}) %copy-start.2) | copy-done | bytes 655384
  6.2 2.4 %collective-permute-start.2 = (bf16[384,256]{1,0:T(8,128)(2,1)S(1)}, bf16[384,256]{1,0:T(8,128)(2,1)S(1)}, u32[]{:S(2)}, u32[]{:S(2)}) collective-permute-start(bf16[384,256]{1,0:T(8,128)(2,1)S(1)} %get-tuple-element.40), channel_id=1, source_target_pairs={{0,16},{8,24},{16,0},{24,8},{1,17},{9,25},{17,1},{25,9},{2,18},{10... | collective-permute-start | bytes 589832 | tf_op jit(solution)/shard_map/ppermute | solution.py:293
  8.6 1.3 %collective-permute-start.9 = (bf16[640,512]{1,0:T(8,128)(2,1)S(1)}, bf16[640,512]{1,0:T(8,128)(2,1)S(1)}, u32[]{:S(2)}, u32[]{:S(2)}) collective-permute-start(bf16[640,512]{1,0:T(8,128)(2,1)S(1)} %get-tuple-element.37.own), channel_id=1, source_target_pairs={{0,8},{8,0},{16,24},{24,16},{1,9},{9,1},{17,25},{25,17},{2,10},{10... | collective-permute-start | bytes 1966088 | tf_op jit(solution)/shard_map/ppermute | solution.py:293
  10.9 1.3 %collective-permute-start.8 = (bf16[2,4,128,640]{3,2,1,0:T(8,128)(2,1)S(1)}, bf16[2,4,128,640]{3,2,1,0:T(8,128)(2,1)S(1)}, u32[]{:S(2)}, u32[]{:S(2)}) collective-permute-start(bf16[2,4,128,640]{3,2,1,0:T(8,128)(2,1)S(1)} %get-tuple-element.38), channel_id=1, source_target_pairs={{0,4},{4,0},{1,5},{5,1},{2,6},{6,2},{3,7},{7,3},{8,12},{12,8},{9,1... | collective-permute-start | bytes 3932168 | tf_op jit(solution)/shard_map/ppermute | solution.py:293
  12.2 5.4 %prompt_attention.2 = (f32[128,4096]{1,0:T(8,128)S(1)}, f32[8,4096]{1,0:T(8,128)S(1)}) custom-call(s32[4]{0:T(128)S(1)} %get-tuple-element.71.info, bf16[128,4096]{1,0:T(8,128)(2,1)S(1)} %bitcast.18, bf16[512,1024]{1,0:T(8,128)(2,1)S(1)} %bitcast.29, bf16[512,1024]{1,0:T(8,128)(2,1)S(1)} %bitcast.30), custom_call_target="tpu_custom_call" | custom-call | flops 4294967296 | bytes 1024 | tf_op jit(solution)/shard_map/prompt_attention/pallas_call | solution.py:96
  17.7 3.9 %collective-permute-done.2.refs_0_ = bf16[384,256]{1,0:T(8,128)(2,1)S(1)} collective-permute-done((bf16[384,256]{1,0:T(8,128)(2,1)S(1)}, bf16[384,256]{1,0:T(8,128)(2,1)S(1)}, u32[]{:S(2)}, u32[]{:S(2)}) %collective-permute-start.2) | collective-permute-done | bytes 196640 | tf_op jit(solution)/shard_map/ppermute | solution.py:293
  21.6 4.2 %collective-permute-done.3.refs_1_ = bf16[384,256]{1,0:T(8,128)(2,1)S(1)} collective-permute-done((bf16[384,256]{1,0:T(8,128)(2,1)S(1)}, bf16[384,256]{1,0:T(8,128)(2,1)S(1)}, u32[]{:S(2)}, u32[]{:S(2)}) %collective-permute-start.3) | collective-permute-done | bytes 196640 | tf_op jit(solution)/shard_map/ppermute | solution.py:293
  25.8 1.9 %collective-permute-start.5 = (bf16[320,256]{1,0:T(8,128)(2,1)S(1)}, bf16[320,256]{1,0:T(8,128)(2,1)S(1)}, u32[]{:S(2)}, u32[]{:S(2)}) collective-permute-start(bf16[320,256]{1,0:T(8,128)(2,1)S(1)} %get-tuple-element.45), channel_id=1, source_target_pairs={{0,16},{8,24},{16,0},{24,8},{1,17},{9,25},{17,1},{25,9},{2,18},{10... | collective-permute-start | bytes 491528 | tf_op jit(solution)/shard_map/ppermute | solution.py:293
  28.1 1.3 %collective-permute-start.7 = (bf16[2,256,256]{2,1,0:T(8,128)(2,1)S(1)}, bf16[2,256,256]{2,1,0:T(8,128)(2,1)S(1)}, u32[]{:S(2)}, u32[]{:S(2)}) collective-permute-start(bf16[2,256,256]{2,1,0:T(8,128)(2,1)S(1)} %pad_maximum_fusion.1), channel_id=1, source_target_pairs={{0,1},{1,0},{2,3},{3,2},{4,5},{5,4},{6,7},{7,6},{8,9},{9,8},{10,11... | collective-permute-start | bytes 786440 | tf_op jit(solution)/shard_map/ppermute | solution.py:293
  29.4 6.3 %prompt_attention.3 = (f32[128,4096]{1,0:T(8,128)S(1)}, f32[8,4096]{1,0:T(8,128)S(1)}) custom-call(s32[4]{0:T(128)S(1)} %get-tuple-element.72.info, bf16[128,4096]{1,0:T(8,128)(2,1)S(1)} %bitcast.19, bf16[512,1024]{1,0:T(8,128)(2,1)} %collective-permute-done.4.k_ref.v_ref, bf16[512,1024]{1,0:T(8,128)(2,1)} %collective-permute-done.4.k_ref.v_ref, ...), custom_call_target="tpu_custom_call" | custom-call | flops 4294967296 | bytes 1024 | tf_op jit(solution)/shard_map/prompt_attention/pallas_call | solution.py:96
  35.7 7.1 %collective-permute-done.6.refs_1_ = bf16[320,256]{1,0:T(8,128)(2,1)S(1)} collective-permute-done((bf16[320,256]{1,0:T(8,128)(2,1)S(1)}, bf16[320,256]{1,0:T(8,128)(2,1)S(1)}, u32[]{:S(2)}, u32[]{:S(2)}) %collective-permute-start.6) | collective-permute-done | bytes 163872 | tf_op jit(solution)/shard_map/ppermute | solution.py:293
  42.8 1.3 %collective-permute-start.10 = (bf16[2,320,256]{2,1,0:T(8,128)(2,1)S(1)}, bf16[2,320,256]{2,1,0:T(8,128)(2,1)S(1)}, u32[]{:S(2)}, u32[]{:S(2)}) collective-permute-start(bf16[2,320,256]{2,1,0:T(8,128)(2,1)S(1)} %pad_maximum_fusion), channel_id=1, source_target_pairs={{0,1},{1,0},{2,3},{3,2},{4,5},{5,4},{6,7},{7,6},{8,9},{9,8},{10,11... | collective-permute-start | bytes 983048 | tf_op jit(solution)/shard_map/ppermute | solution.py:293
  44.1 1.5 %project.2 = (f32[2,128,256]{2,1,0:T(8,128)S(1)}, f32[2,128,256]{2,1,0:T(8,128)S(1)}) custom-call(s32[4]{0:T(128)S(1)} %pad_add_fusion.1.where, bf16[2,4,128,640]{3,2,1,0:T(8,128)(2,1)S(1)} %get-tuple-element.55.keep, bf16[2,4,128,640]{3,2,1,0:T(8,128)(2,1)S(1)} %collective-permute-done.8.other, bf16[640,512]{1,0:T(8,128)(2,1)S(1)} %get-tuple-element.37.own, ...), custom_call_target="tpu_custom_call" | custom-call | flops 1024 | bytes 1024 | tf_op jit(solution)/shard_map/project/pallas_call | solution.py:117
  45.6 1.3 %collective-permute-start.11 = (f32[2,128,256]{2,1,0:T(8,128)S(1)}, f32[2,128,256]{2,1,0:T(8,128)S(1)}, u32[]{:S(2)}, u32[]{:S(2)}) collective-permute-start(f32[2,128,256]{2,1,0:T(8,128)S(1)} %get-tuple-element.62), channel_id=1, source_target_pairs={{0,4},{4,0},{1,5},{5,1},{2,6},{6,2},{3,7},{7,3},{8,12},{12,8},{9,1... | collective-permute-start | bytes 786440 | tf_op jit(solution)/shard_map/ppermute | solution.py:293
  46.9 4.2 %collective-permute-done.10.forwarded = bf16[2,320,256]{2,1,0:T(8,128)(2,1)S(1)} collective-permute-done((bf16[2,320,256]{2,1,0:T(8,128)(2,1)S(1)}, bf16[2,320,256]{2,1,0:T(8,128)(2,1)S(1)}, u32[]{:S(2)}, u32[]{:S(2)}) %collective-permute-start.10) | collective-permute-done | bytes 327712 | tf_op jit(solution)/shard_map/ppermute | solution.py:293
  51.0 1.5 %project.3 = (f32[2,128,256]{2,1,0:T(8,128)S(1)}, f32[2,128,256]{2,1,0:T(8,128)S(1)}) custom-call(s32[4]{0:T(128)S(1)} %pad_add_fusion.1.where, bf16[2,4,128,640]{3,2,1,0:T(8,128)(2,1)S(1)} %get-tuple-element.55.keep, bf16[2,4,128,640]{3,2,1,0:T(8,128)(2,1)S(1)} %collective-permute-done.8.other, bf16[640,512]{1,0:T(8,128)(2,1)S(1)} %get-tuple-element.37.own, ...), custom_call_target="tpu_custom_call" | custom-call | flops 1024 | bytes 1024 | tf_op jit(solution)/shard_map/project/pallas_call | solution.py:117
  52.6 1.3 %collective-permute-start.12 = (f32[2,128,256]{2,1,0:T(8,128)S(1)}, f32[2,128,256]{2,1,0:T(8,128)S(1)}, u32[]{:S(2)}, u32[]{:S(2)}) collective-permute-start(f32[2,128,256]{2,1,0:T(8,128)S(1)} %get-tuple-element.64), channel_id=1, source_target_pairs={{0,4},{4,0},{1,5},{5,1},{2,6},{6,2},{3,7},{7,3},{8,12},{12,8},{9,1... | collective-permute-start | bytes 786440 | tf_op jit(solution)/shard_map/ppermute | solution.py:293
  53.9 2.3 %collective-permute-start.13 = (f32[1,128,256]{2,1,0:T(8,128)S(1)}, f32[1,128,256]{2,1,0:T(8,128)S(1)}, u32[]{:S(2)}, u32[]{:S(2)}) collective-permute-start(f32[1,128,256]{2,1,0:T(8,128)S(1)} %slice_add_fusion.1), channel_id=1, source_target_pairs={{0,2},{2,0},{1,3},{3,1},{4,6},{6,4},{5,7},{7,5},{8,10},{10,8},{9,1... | collective-permute-start | bytes 393224 | tf_op jit(solution)/shard_map/ppermute | solution.py:293
  57.2 2.3 %final_attention.2.refs_0_ = bf16[128,4096]{1,0:T(8,128)(2,1)} custom-call(s32[3]{0:T(128)S(1)} %pad_add_fusion.info, f32[1,128]{1,0:T(1,128)S(1)} %bitcast.26, bf16[128,4096]{1,0:T(8,128)(2,1)S(1)} %bitcast.20, f32[128,4096]{1,0:T(8,128)S(1)} %get-tuple-element.53.acc_ref, f32[8,4096]{1,0:T(8,128)S(1)} %get-tuple-element.54.ml_ref, ...), custom_call_target="tpu_custom_call" | custom-call | flops 1024 | bytes 1024 | tf_op jit(solution)/shard_map/final_attention/pallas_call | solution.py:279
  59.5 1.9 %collective-permute-start.14 = (f32[1,128,256]{2,1,0:T(8,128)S(1)}, f32[1,128,256]{2,1,0:T(8,128)S(1)}, u32[]{:S(2)}, u32[]{:S(2)}) collective-permute-start(f32[1,128,256]{2,1,0:T(8,128)S(1)} %slice_add_fusion), channel_id=1, source_target_pairs={{0,2},{2,0},{1,3},{3,1},{4,6},{6,4},{5,7},{7,5},{8,10},{10,8},{9,1... | collective-permute-start | bytes 393224 | tf_op jit(solution)/shard_map/ppermute | solution.py:293
  61.4 1.0 %collective-permute-done.14.there = f32[1,128,256]{2,1,0:T(8,128)S(1)} collective-permute-done((f32[1,128,256]{2,1,0:T(8,128)S(1)}, f32[1,128,256]{2,1,0:T(8,128)S(1)}, u32[]{:S(2)}, u32[]{:S(2)}) %collective-permute-start.14) | collective-permute-done | bytes 131104 | tf_op jit(solution)/shard_map/ppermute | solution.py:293
  62.4 2.3 %final_attention.3 = bf16[128,4096]{1,0:T(8,128)(2,1)} custom-call(s32[3]{0:T(128)S(1)} %pad_add_fusion.info, f32[1,128]{1,0:T(1,128)S(1)} %bitcast.27, bf16[128,4096]{1,0:T(8,128)(2,1)S(1)} %bitcast.21, f32[128,4096]{1,0:T(8,128)S(1)} %get-tuple-element.53.acc_ref, f32[8,4096]{1,0:T(8,128)S(1)} %get-tuple-element.54.ml_ref, ...), custom_call_target="tpu_custom_call", output_to_operand_aliasing={{}: (8, {})} | custom-call | flops 1024 | bytes 1024 | tf_op jit(solution)/shard_map/final_attention/pallas_call | solution.py:279
  (38 shorter events, 4.0 us)
Async XLA Ops:
  0.0 10.2 %copy-start.1 = (bf16[1,128,5120]{2,1,0:T(8,128)(2,1)S(1)}, bf16[1,128,5120]{2,1,0:T(8,128)(2,1)}, u32[]{:S(2)}) copy-start(bf16[1,128,5120]{2,1,0:T(8,128)(2,1)} %param.8) | copy-start | bytes 3932164
  0.0 10.2 %collective-permute-start.1 = (bf16[128,5120]{1,0:T(8,128)(2,1)}, bf16[128,5120]{1,0:T(8,128)(2,1)S(1)}, u32[]{:S(2)}, u32[]{:S(2)}) collective-permute-start(bf16[128,5120]{1,0:T(8,128)(2,1)} %bitcast.22), channel_id=1, source_target_pairs={{0,2},{2,0},{1,3},{3,1},{4,6},{6,4},{5,7},{7,5},{8,10},{10,8},{9,1... | collective-permute-start | bytes 3932168 | tf_op jit(solution)/shard_map/ppermute | solution.py:293
  0.7 3.8 %collective-permute-start = (bf16[320,1024]{1,0:T(8,128)(2,1)}, bf16[320,1024]{1,0:T(8,128)(2,1)S(1)}, u32[]{:S(2)}, u32[]{:S(2)}) collective-permute-start(bf16[320,1024]{1,0:T(8,128)(2,1)} %own_ref.1), channel_id=1, source_target_pairs={{0,2},{2,0},{1,3},{3,1},{4,6},{6,4},{5,7},{7,5},{8,10},{10,8},{9,1... | collective-permute-start | bytes 1966088 | tf_op jit(solution)/shard_map/ppermute | solution.py:293
  0.7 25.1 %collective-permute-start.4 = (bf16[512,1024]{1,0:T(8,128)(2,1)}, bf16[512,1024]{1,0:T(8,128)(2,1)}, u32[]{:S(2)}, u32[]{:S(2)}) collective-permute-start(bf16[512,1024]{1,0:T(8,128)(2,1)} %bitcast.28), channel_id=1, source_target_pairs={{0,1},{1,0},{2,3},{3,2},{4,5},{5,4},{6,7},{7,6},{8,9},{9,8},{10,11... | collective-permute-start | bytes 3145736 | tf_op jit(solution)/shard_map/ppermute | solution.py:312
  4.5 1.1 %copy-start.2 = (bf16[320,1024]{1,0:T(8,128)(2,1)S(1)}, bf16[320,1024]{1,0:T(8,128)(2,1)}, u32[]{:S(2)}) copy-start(bf16[320,1024]{1,0:T(8,128)(2,1)} %own_ref.1) | copy-start | bytes 1966084
  5.6 4.3 %copy-start.5 = (s32[1,2,2]{2,1,0:T(2,128)S(1)}, s32[1,2,2]{2,1,0:T(2,128)}, u32[]{:S(2)}) copy-start(s32[1,2,2]{2,1,0:T(2,128)} %param.14) | copy-start | bytes 52
  6.2 15.4 %collective-permute-start.2 = (bf16[384,256]{1,0:T(8,128)(2,1)S(1)}, bf16[384,256]{1,0:T(8,128)(2,1)S(1)}, u32[]{:S(2)}, u32[]{:S(2)}) collective-permute-start(bf16[384,256]{1,0:T(8,128)(2,1)S(1)} %get-tuple-element.40), channel_id=1, source_target_pairs={{0,16},{8,24},{16,0},{24,8},{1,17},{9,25},{17,1},{25,9},{2,18},{10... | collective-permute-start | bytes 589832 | tf_op jit(solution)/shard_map/ppermute | solution.py:293
  8.6 17.2 %collective-permute-start.3 = (bf16[384,256]{1,0:T(8,128)(2,1)S(1)}, bf16[384,256]{1,0:T(8,128)(2,1)S(1)}, u32[]{:S(2)}, u32[]{:S(2)}) collective-permute-start(bf16[384,256]{1,0:T(8,128)(2,1)S(1)} %get-tuple-element.40), channel_id=1, source_target_pairs={{0,24},{8,16},{16,8},{24,0},{1,25},{9,17},{17,9},{25,1},{2,26},{10... | collective-permute-start | bytes 589832 | tf_op jit(solution)/shard_map/ppermute | solution.py:293
  8.6 35.5 %collective-permute-start.9 = (bf16[640,512]{1,0:T(8,128)(2,1)S(1)}, bf16[640,512]{1,0:T(8,128)(2,1)S(1)}, u32[]{:S(2)}, u32[]{:S(2)}) collective-permute-start(bf16[640,512]{1,0:T(8,128)(2,1)S(1)} %get-tuple-element.37.own), channel_id=1, source_target_pairs={{0,8},{8,0},{16,24},{24,16},{1,9},{9,1},{17,25},{25,17},{2,10},{10... | collective-permute-start | bytes 1966088 | tf_op jit(solution)/shard_map/ppermute | solution.py:293
  10.1 2.1 %copy-start = (bf16[1,128,4096]{2,1,0:T(8,128)(2,1)S(1)}, bf16[1,128,4096]{2,1,0:T(8,128)(2,1)}, u32[]{:S(2)}) copy-start(bf16[1,128,4096]{2,1,0:T(8,128)(2,1)} %param.9) | copy-start | bytes 3145732
  10.1 2.1 %copy-start.4 = (bf16[1,512,1024]{2,1,0:T(8,128)(2,1)S(1)}, bf16[1,512,1024]{2,1,0:T(8,128)(2,1)}, u32[]{:S(2)}) copy-start(bf16[1,512,1024]{2,1,0:T(8,128)(2,1)} %param.10) | copy-start | bytes 3145732
  10.9 33.1 %collective-permute-start.8 = (bf16[2,4,128,640]{3,2,1,0:T(8,128)(2,1)S(1)}, bf16[2,4,128,640]{3,2,1,0:T(8,128)(2,1)S(1)}, u32[]{:S(2)}, u32[]{:S(2)}) collective-permute-start(bf16[2,4,128,640]{3,2,1,0:T(8,128)(2,1)S(1)} %get-tuple-element.38), channel_id=1, source_target_pairs={{0,4},{4,0},{1,5},{5,1},{2,6},{6,2},{3,7},{7,3},{8,12},{12,8},{9,1... | collective-permute-start | bytes 3932168 | tf_op jit(solution)/shard_map/ppermute | solution.py:293
  25.8 9.9 %collective-permute-start.5 = (bf16[320,256]{1,0:T(8,128)(2,1)S(1)}, bf16[320,256]{1,0:T(8,128)(2,1)S(1)}, u32[]{:S(2)}, u32[]{:S(2)}) collective-permute-start(bf16[320,256]{1,0:T(8,128)(2,1)S(1)} %get-tuple-element.45), channel_id=1, source_target_pairs={{0,16},{8,24},{16,0},{24,8},{1,17},{9,25},{17,1},{25,9},{2,18},{10... | collective-permute-start | bytes 491528 | tf_op jit(solution)/shard_map/ppermute | solution.py:293
  27.7 15.1 %collective-permute-start.6 = (bf16[320,256]{1,0:T(8,128)(2,1)S(1)}, bf16[320,256]{1,0:T(8,128)(2,1)S(1)}, u32[]{:S(2)}, u32[]{:S(2)}) collective-permute-start(bf16[320,256]{1,0:T(8,128)(2,1)S(1)} %get-tuple-element.45), channel_id=1, source_target_pairs={{0,24},{8,16},{16,8},{24,0},{1,25},{9,17},{17,9},{25,1},{2,26},{10... | collective-permute-start | bytes 491528 | tf_op jit(solution)/shard_map/ppermute | solution.py:293
  28.1 14.7 %collective-permute-start.7 = (bf16[2,256,256]{2,1,0:T(8,128)(2,1)S(1)}, bf16[2,256,256]{2,1,0:T(8,128)(2,1)S(1)}, u32[]{:S(2)}, u32[]{:S(2)}) collective-permute-start(bf16[2,256,256]{2,1,0:T(8,128)(2,1)S(1)} %pad_maximum_fusion.1), channel_id=1, source_target_pairs={{0,1},{1,0},{2,3},{3,2},{4,5},{5,4},{6,7},{7,6},{8,9},{9,8},{10,11... | collective-permute-start | bytes 786440 | tf_op jit(solution)/shard_map/ppermute | solution.py:293
  42.8 8.3 %collective-permute-start.10 = (bf16[2,320,256]{2,1,0:T(8,128)(2,1)S(1)}, bf16[2,320,256]{2,1,0:T(8,128)(2,1)S(1)}, u32[]{:S(2)}, u32[]{:S(2)}) collective-permute-start(bf16[2,320,256]{2,1,0:T(8,128)(2,1)S(1)} %pad_maximum_fusion), channel_id=1, source_target_pairs={{0,1},{1,0},{2,3},{3,2},{4,5},{5,4},{6,7},{7,6},{8,9},{9,8},{10,11... | collective-permute-start | bytes 983048 | tf_op jit(solution)/shard_map/ppermute | solution.py:293
  45.6 7.0 %collective-permute-start.11 = (f32[2,128,256]{2,1,0:T(8,128)S(1)}, f32[2,128,256]{2,1,0:T(8,128)S(1)}, u32[]{:S(2)}, u32[]{:S(2)}) collective-permute-start(f32[2,128,256]{2,1,0:T(8,128)S(1)} %get-tuple-element.62), channel_id=1, source_target_pairs={{0,4},{4,0},{1,5},{5,1},{2,6},{6,2},{3,7},{7,3},{8,12},{12,8},{9,1... | collective-permute-start | bytes 786440 | tf_op jit(solution)/shard_map/ppermute | solution.py:293
  51.0 5.1 %copy-start.6 = (s32[1,2]{1,0:T(1,128)S(1)}, s32[1,2]{1,0:T(1,128)}, u32[]{:S(2)}) copy-start(s32[1,2]{1,0:T(1,128)} %param.15) | copy-start | bytes 28
  51.0 6.1 %copy-start.3 = (f32[128]{0:T(128)S(1)}, f32[128]{0:T(128)}, u32[]{:S(2)}) copy-start(f32[128]{0:T(128)} %param.12) | copy-start | bytes 1540
  52.6 6.9 %collective-permute-start.12 = (f32[2,128,256]{2,1,0:T(8,128)S(1)}, f32[2,128,256]{2,1,0:T(8,128)S(1)}, u32[]{:S(2)}, u32[]{:S(2)}) collective-permute-start(f32[2,128,256]{2,1,0:T(8,128)S(1)} %get-tuple-element.64), channel_id=1, source_target_pairs={{0,4},{4,0},{1,5},{5,1},{2,6},{6,2},{3,7},{7,3},{8,12},{12,8},{9,1... | collective-permute-start | bytes 786440 | tf_op jit(solution)/shard_map/ppermute | solution.py:293
  53.9 3.3 %collective-permute-start.13 = (f32[1,128,256]{2,1,0:T(8,128)S(1)}, f32[1,128,256]{2,1,0:T(8,128)S(1)}, u32[]{:S(2)}, u32[]{:S(2)}) collective-permute-start(f32[1,128,256]{2,1,0:T(8,128)S(1)} %slice_add_fusion.1), channel_id=1, source_target_pairs={{0,2},{2,0},{1,3},{3,1},{4,6},{6,4},{5,7},{7,5},{8,10},{10,8},{9,1... | collective-permute-start | bytes 393224 | tf_op jit(solution)/shard_map/ppermute | solution.py:293
  59.5 2.9 %collective-permute-start.14 = (f32[1,128,256]{2,1,0:T(8,128)S(1)}, f32[1,128,256]{2,1,0:T(8,128)S(1)}, u32[]{:S(2)}, u32[]{:S(2)}) collective-permute-start(f32[1,128,256]{2,1,0:T(8,128)S(1)} %slice_add_fusion), channel_id=1, source_target_pairs={{0,2},{2,0},{1,3},{3,1},{4,6},{6,4},{5,7},{7,5},{8,10},{10,8},{9,1... | collective-permute-start | bytes 393224 | tf_op jit(solution)/shard_map/ppermute | solution.py:293

commit v7 on v5

--- a/solution.py
+++ b/solution.py
@@ -25,7 +25,7 @@
 LONG = pl.CostEstimate(flops=2**32, bytes_accessed=1024, transcendentals=0)
 
 CHUNKS = ((0, 2), (2, 2))
-HELP = (4, 5)
+HELP = (5, 5)
 
 
 def pair_queries(q_ref, g, extra=None):
@@ -126,23 +126,20 @@
     )(scalars, *operands)
 
 
-def pack_rows_kernel(where, own_ref, got_ref, keep, send):
-    steps, part = keep.shape[1], keep.shape[3]
+def pack_rows_kernel(where, x_ref, keep, send):
+    steps, _, part = keep.shape
     for z in range(steps):
         for out, y in ((keep, where[1]), (send, 1 - where[1])):
-            columns = pl.ds(pl.multiple_of((2 * z + y) * part, 128), part)
-            out[0, z] = own_ref[:, columns]
-            out[1, z] = got_ref[:, columns]
-
-
-def pack_rows(where, own, got, y, steps):
-    part = own.shape[1] // (2 * steps)
+            out[z] = x_ref[:, pl.ds(pl.multiple_of((2 * z + y) * part, 128), part)]
+
+
+def pack_rows(where, x, y, steps):
+    part = x.shape[1] // (2 * steps)
     if part % 128:
-        halves = jnp.stack([own, got]).reshape(2, ROWS, steps, 2, part)
-        halves = jnp.transpose(halves, (3, 0, 2, 1, 4))
+        halves = jnp.transpose(x.reshape(ROWS, steps, 2, part), (2, 1, 0, 3))
         return [lax.dynamic_index_in_dim(halves, i, axis=0, keepdims=False) for i in (y, 1 - y)]
-    outs = [jax.ShapeDtypeStruct((2, steps, ROWS, part), own.dtype)] * 2
-    return on_chip(pack_rows_kernel, "pack_rows", outs, where, own, got)
+    outs = [jax.ShapeDtypeStruct((steps, ROWS, part), x.dtype)] * 2
+    return on_chip(pack_rows_kernel, "pack_rows", outs, where, x)
 
 
 def row_split(rows, i):
@@ -150,18 +147,20 @@
     return helped, rows - helped
 
 
-def columns_of(chunk):
-    return slice(chunk[0] * HD, (chunk[0] + chunk[1]) * HD)
-
-
-def pack_weight_kernel(where, own_ref, got_ref, *outs):
-    rows = own_ref.shape[0]
+def pack_weight_kernel(where, got_ref, own_ref, *refs):
+    outs, sems = refs[:-1], refs[-1]
+    rows = got_ref.shape[0]
     core, plane = where[2], where[3]
-    half = pl.ds(pl.multiple_of(core * KVH * HD, 128), KVH * HD)
-    own, got = own_ref[:, half], got_ref[:, half]
-    for whole, far, chunk in zip(outs[0::2], outs[1::2], CHUNKS):
-        whole[pl.ds(pl.multiple_of(core * rows, 16), rows), :] = own[:, columns_of(chunk)]
-        whole[pl.ds(pl.multiple_of((1 - core) * rows, 16), rows), :] = got[:, columns_of(chunk)]
+    own_place = pl.ds(pl.multiple_of(core * rows, 16), rows)
+    got_place = pl.ds(pl.multiple_of((1 - core) * rows, 16), rows)
+    copies = []
+    for i, (head, heads) in enumerate(CHUNKS):
+        columns = pl.ds(pl.multiple_of((core * KVH + head) * HD, 128), heads * HD)
+        copies.append(pltpu.make_async_copy(own_ref.at[:, columns], outs[2 * i].at[own_place, :], sems.at[i]))
+        copies[-1].start()
+        outs[2 * i][got_place, :] = got_ref[:, columns]
+    for copy, whole, far in zip(copies, outs[0::2], outs[1::2]):
+        copy.wait()
         direct = far.shape[0]
         far[...] = whole[pl.ds(pl.multiple_of(plane * (2 * rows - direct), 16), direct), :]
 
@@ -171,12 +170,20 @@
     shapes = []
     for i, (_, heads) in enumerate(CHUNKS):
         shapes += [(rows, heads * HD), (row_split(rows, i)[1], heads * HD)]
-    outs = [jax.ShapeDtypeStruct(shape, own.dtype) for shape in shapes]
-    outs = on_chip(pack_weight_kernel, "pack_weight", outs, where, own, got)
+    outs = pl.pallas_call(
+        pack_weight_kernel,
+        in_specs=[SMEM, VMEM, pl.BlockSpec(memory_space=pltpu.HBM)],
+        out_specs=[VMEM] * len(shapes),
+        out_shape=[jax.ShapeDtypeStruct(shape, own.dtype) for shape in shapes],
+        scratch_shapes=[pltpu.SemaphoreType.DMA((len(CHUNKS),))],
+        compiler_params=PARAMS,
+        cost_estimate=HINT,
+        name="pack_weight",
+    )(where, got, own)
     return list(outs[0::2]), list(outs[1::2])
 
 
-def project_kernel(where, keep, other, own, near, forwarded, *refs):
+def project_kernel(where, keep, other, others, own, near, forwarded, *refs):
     direct, mine, theirs, whole = refs[:-3], refs[-3], refs[-2], refs[-1]
     plane = where[3]
     count, extra = direct[0].shape[0], forwarded.shape[1]
@@ -192,7 +199,7 @@
             far[pl.ds(pl.multiple_of((1 - plane) * count, 16), extra), :] = forwarded[j - 2]
             weight = far[...]
         place = where[0] ^ j
-        left = jnp.concatenate([x[core, place] for x in (keep, other) for core in range(2)], axis=0)
+        left = jnp.concatenate([keep[place], others[0, place], other[place], others[1, place]], axis=0)
         product = jnp.dot(left, weight, preferred_element_type=jnp.float32)
         total = product if total is None else total + product
     for i in range(2):
@@ -200,7 +207,7 @@
         theirs[i] = total[(2 + i) * ROWS : (3 + i) * ROWS]
 
 
-def project(where, keep, other, own, near, direct, forwarded):
+def project(where, rows_of_x, own, near, direct, forwarded):
     width = own.shape[1]
     out = jax.ShapeDtypeStruct((2, ROWS, width), jnp.float32)
     return on_chip(
@@ -208,8 +215,7 @@
         "project",
         [out, out],
         where,
-        keep,
-        other,
+        *rows_of_x,
         own,
         near,
         forwarded,
@@ -297,25 +303,26 @@
     tie = lax.optimization_barrier
 
     got_weight = xor_swap(kv_weight, "core", 1)
-    got_x = xor_swap(x, "core", 1)
     caches = [prompt_cache[0]]
     for _ in range(cycle - 1):
         caches.append(lax.ppermute(caches[-1], "blk", [(i, (i + 1) % cycle) for i in range(cycle)]))
 
+    keep, given = pack_rows(where, x, y, steps)
+    other = xor_swap(given, "y", 1)
+    got_weight, given = tie((got_weight, given))
     whole, far = pack_weight(where, kv_weight, got_weight)
 
-    def send(whole, far):
-        return xor_swap(whole, "z", 1), [xor_swap(far, "z", j) for j in range(2, steps)]
+    def send(far):
+        return [xor_swap(far, "z", j) for j in range(2, steps)]
 
     def forward(i):
         helped, direct = row_split(whole[0].shape[0], i)
-        parts = [lax.dynamic_slice_in_dim(p, plane * (direct - helped), helped, axis=0) for p in sent[i][1]]
+        parts = [lax.dynamic_slice_in_dim(p, plane * (direct - helped), helped, axis=0) for p in sent[i]]
         return xor_swap(jnp.stack(parts), "blk", 1)
 
-    sent = [send(whole[0], far[0])]
-    keep, given = pack_rows(where, x, got_x, y, steps)
-    other = xor_swap(given, "y", 1)
-
+    sent = [send(far[0])]
+    near = [xor_swap(whole[0], "z", 1)]
+    block_table, _ = tie((block_table, whole[0]))
     infos = []
     for stride in range(cycle):
         owner = lax.rem(holder + cycle - stride, cycle)
@@ -323,24 +330,29 @@
         listed = lax.dynamic_index_in_dim(block_table[0], place // BLOCK, axis=1, keepdims=False)
         infos.append(jnp.concatenate([place[None], prompt_lengths, listed]).astype(jnp.int32))
 
-    query, _, _ = tie((query, whole[0], given))
+    query, _ = tie((query, whole[0]))
     state = prompt_attention(infos[0], query, caches[0], None, 0, KVH)
 
-    sent[0], caches, state, second = tie((sent[0], caches, state, (whole[1], far[1])))
-    sent.append(send(*second))
+    sent[0], near[0], state, second, other = tie((sent[0], near[0], state, (far[1], whole[1]), other))
+    sent.append(send(second[0]))
+    near.append(xor_swap(second[1], "z", 1))
+    rows_of_x = [keep, other, xor_swap(jnp.stack([keep, other]), "core", 1)]
+    sent[0], caches = tie((sent[0], caches))
     forwarded = [forward(0)]
     for stride in range(1, cycle):
         state = prompt_attention(infos[stride], query, caches[stride], state, 0, KVH)
-    sent[1], forwarded[0], state = tie((sent[1], forwarded[0], state))
+
+    def sums(i):
+        return project(where, rows_of_x, whole[i], near[i], sent[i], forwarded[i])
+
+    forwarded[0], state = tie((forwarded[0], state))
+    mine_0, theirs_0 = sums(0)
+    theirs_0 = xor_swap(theirs_0, "y", 1)
+    sent[1], near[1], mine_0 = tie((sent[1], near[1], mine_0))
     forwarded.append(forward(1))
-
-    def sums(i):
-        return project(where, keep, other, whole[i], *sent[i], forwarded[i])
 
     info = jnp.concatenate([resp_lengths[0], core[None]]).astype(jnp.int32)
     gain = key_gain[None]
-    mine_0, theirs_0 = sums(0)
-    theirs_0 = xor_swap(theirs_0, "y", 1)
     forwarded[1], mine_0 = tie((forwarded[1], mine_0))
     mine_1, theirs_1 = sums(1)
     theirs_0, theirs_1 = tie((theirs_0, theirs_1))

time: 69.1 us -> 70.4 us (1.019)
  starting transfers between devices: 19.2 us -> 15.9 us
  waiting for transfers between devices: 25.7 us -> 28.7 us
  Pallas kernels: 20.8 us -> 21.6 us
    ppermute x15, waiting for transfers between devices: 25.7 us -> 28.7 us  [xor_swap(): lax.ppermute(array, axis, [(i, i ^ by) for i in range(lax.axis_size(axis))])]
    ppermute x15, starting transfers between devices: 16.3 us -> 14.4 us  [xor_swap(): lax.ppermute(array, axis, [(i, i ^ by) for i in range(lax.axis_size(axis))])]
    ppermute x1, starting transfers between devices: 2.93 us -> 1.49 us  [per_device(): lax.ppermute(caches[-1], 'blk', [(i, (i + 1) % cycle) for i in range(cycl...]
    unnamed x12 -> x14, local copies, waits for them, and re-layouts: 1.12 us -> 2.42 us
    dynamic_slice x1, local copies, waits for them, and re-layouts: 0.97 us -> 0.21 us  [per_device(): lax.dynamic_index_in_dim(block_table[0], place // BLOCK, axis=1, keepdims...]
    pallas_call x4 -> x3, Pallas kernels: 4.38 us -> 4.53 us  [on_chip(): pl.pallas_call(kernel, in_specs=[SMEM] + [VMEM] * len(operands), out_spec...]
  transfers between devices with their start and end apart: 16 -> 16, of which waited for: 8 -> 10; matrix products, arithmetic and copies ran while one was open for 2% -> 1% of each run, Pallas kernels for 27% -> 27%
where the time goes in v7:
time: 70.4 us; the launch traced here: 70.2 us
  waiting for transfers between devices  28.7 us (41%)
  Pallas kernels  21.6 us (31%)
  starting transfers between devices  15.9 us (23%)
  local copies, waits for them, and re-layouts  2.63 us (4%)
  between operations  0.8 us (1%)
    ppermute x15, waiting for transfers between devices, xor_swap(): lax.ppermute(array, axis, [(i, i ^ by) for i in range(lax.axis_size(axis))])  28.7 us
    ppermute x15, starting transfers between devices, xor_swap(): lax.ppermute(array, axis, [(i, i ^ by) for i in range(lax.axis_size(axis))])  14.4 us
    pallas_call x2, Pallas kernels, prompt_attention(): pl.pallas_call(functools.partial(prompt_kernel, first), grid_spec=pltpu.P...  11.7 us
    pallas_call x2, Pallas kernels, final_attention(): pl.pallas_call(functools.partial(final_kernel, chunk, offset), in_specs=s...  4.68 us
    pallas_call x3, Pallas kernels, on_chip(): pl.pallas_call(kernel, in_specs=[SMEM] + [VMEM] * len(operands), out_spec...  4.53 us
    unnamed x14, local copies, waits for them, and re-layouts  2.42 us
    ppermute x1, starting transfers between devices, per_device(): lax.ppermute(caches[-1], 'blk', [(i, (i + 1) % cycle) for i in range(cycl...  1.49 us
  transfers between devices with their start and end apart: 16, of which 10 were waited for; matrix products, arithmetic and copies ran while one was open for 1% of the time, Pallas kernels for 27%

profile of v7, /device:TPU:0, one launch (start us, length us, event | category | flops | bytes accessed | tf_op | source)
XLA Modules:
  0.0 70.2 jit_solution(1580352146051244849)
XLA Ops:
  0.5 1.3 %copy-done.1 = bf16[1,128,5120]{2,1,0:T(8,128)(2,1)S(1)} copy-done((bf16[1,128,5120]{2,1,0:T(8,128)(2,1)S(1)}, bf16[1,128,5120]{2,1,0:T(8,128)(2,1)}, u32[]{:S(2)}) %copy-start.1) | copy-done | bytes 1310744
  1.9 1.5 %pack_rows.1 = (bf16[4,128,640]{2,1,0:T(8,128)(2,1)S(1)}, bf16[4,128,640]{2,1,0:T(8,128)(2,1)}) custom-call(s32[4]{0:T(128)S(1)} %pad_add_fusion.1.where, bf16[128,5120]{1,0:T(8,128)(2,1)S(1)} %bitcast.24), custom_call_target="tpu_custom_call" | custom-call | flops 1024 | bytes 1024 | tf_op jit(solution)/shard_map/pack_rows/pallas_call | solution.py:117
  3.3 2.5 %collective-permute-start.4 = (bf16[4,128,640]{2,1,0:T(8,128)(2,1)}, bf16[4,128,640]{2,1,0:T(8,128)(2,1)S(1)}, u32[]{:S(2)}, u32[]{:S(2)}) collective-permute-start(bf16[4,128,640]{2,1,0:T(8,128)(2,1)} %get-tuple-element.46), channel_id=1, source_target_pairs={{0,4},{4,0},{1,5},{5,1},{2,6},{6,2},{3,7},{7,3},{8,12},{12,8},{9,1... | collective-permute-start | bytes 1966088 | tf_op jit(solution)/shard_map/ppermute | solution.py:290
  5.9 1.5 %collective-permute-start.5 = (bf16[512,1024]{1,0:T(8,128)(2,1)}, bf16[512,1024]{1,0:T(8,128)(2,1)}, u32[]{:S(2)}, u32[]{:S(2)}) collective-permute-start(bf16[512,1024]{1,0:T(8,128)(2,1)} %bitcast.31), channel_id=1, source_target_pairs={{0,1},{1,0},{2,3},{3,2},{4,5},{5,4},{6,7},{7,6},{8,9},{9,8},{10,11... | collective-permute-start | bytes 3145736 | tf_op jit(solution)/shard_map/ppermute | solution.py:308
  8.0 1.1 %copy-done.2 = bf16[320,1024]{1,0:T(8,128)(2,1)S(1)} copy-done((bf16[320,1024]{1,0:T(8,128)(2,1)S(1)}, bf16[320,1024]{1,0:T(8,128)(2,1)}, u32[]{:S(2)}) %copy-start.2) | copy-done | bytes 655384
  9.8 3.7 %collective-permute-start.2 = (bf16[320,256]{1,0:T(8,128)(2,1)S(1)}, bf16[320,256]{1,0:T(8,128)(2,1)S(1)}, u32[]{:S(2)}, u32[]{:S(2)}) collective-permute-start(bf16[320,256]{1,0:T(8,128)(2,1)S(1)} %get-tuple-element.50), channel_id=1, source_target_pairs={{0,24},{8,16},{16,8},{24,0},{1,25},{9,17},{17,9},{25,1},{2,26},{10... | collective-permute-start | bytes 491528 | tf_op jit(solution)/shard_map/ppermute | solution.py:290
  13.5 0.8 %collective-permute-start.3 = (bf16[640,256]{1,0:T(8,128)(2,1)S(1)}, bf16[640,256]{1,0:T(8,128)(2,1)S(1)}, u32[]{:S(2)}, u32[]{:S(2)}) collective-permute-start(bf16[640,256]{1,0:T(8,128)(2,1)S(1)} %get-tuple-element.48.own), channel_id=1, source_target_pairs={{0,8},{8,0},{16,24},{24,16},{1,9},{9,1},{17,25},{25,17},{2,10},{10... | collective-permute-start | bytes 983048 | tf_op jit(solution)/shard_map/ppermute | solution.py:290
  14.5 5.4 %prompt_attention.2 = (f32[128,4096]{1,0:T(8,128)S(1)}, f32[8,4096]{1,0:T(8,128)S(1)}) custom-call(s32[4]{0:T(128)S(1)} %get-tuple-element.89.info, bf16[128,4096]{1,0:T(8,128)(2,1)S(1)} %bitcast.20, bf16[512,1024]{1,0:T(8,128)(2,1)S(1)} %bitcast.32, bf16[512,1024]{1,0:T(8,128)(2,1)S(1)} %bitcast.33), custom_call_target="tpu_custom_call" | custom-call | flops 4294967296 | bytes 1024 | tf_op jit(solution)/shard_map/prompt_attention/pallas_call | solution.py:96
  20.0 1.5 %collective-permute-done.4.other = bf16[4,128,640]{2,1,0:T(8,128)(2,1)S(1)} collective-permute-done((bf16[4,128,640]{2,1,0:T(8,128)(2,1)}, bf16[4,128,640]{2,1,0:T(8,128)(2,1)S(1)}, u32[]{:S(2)}, u32[]{:S(2)}) %collective-permute-start.4) | collective-permute-done | bytes 655392 | tf_op jit(solution)/shard_map/ppermute | solution.py:290
  21.5 6.1 %collective-permute-done.1.refs_0_ = bf16[320,256]{1,0:T(8,128)(2,1)S(1)} collective-permute-done((bf16[320,256]{1,0:T(8,128)(2,1)S(1)}, bf16[320,256]{1,0:T(8,128)(2,1)S(1)}, u32[]{:S(2)}, u32[]{:S(2)}) %collective-permute-start.1) | collective-permute-done | bytes 163872 | tf_op jit(solution)/shard_map/ppermute | solution.py:290
  27.6 0.8 %collective-permute-done.3.near = bf16[640,256]{1,0:T(8,128)(2,1)S(1)} collective-permute-done((bf16[640,256]{1,0:T(8,128)(2,1)S(1)}, bf16[640,256]{1,0:T(8,128)(2,1)S(1)}, u32[]{:S(2)}, u32[]{:S(2)}) %collective-permute-start.3) | collective-permute-done | bytes 327712 | tf_op jit(solution)/shard_map/ppermute | solution.py:290
  28.7 3.6 %collective-permute-start.9 = (bf16[320,256]{1,0:T(8,128)(2,1)S(1)}, bf16[320,256]{1,0:T(8,128)(2,1)S(1)}, u32[]{:S(2)}, u32[]{:S(2)}) collective-permute-start(bf16[320,256]{1,0:T(8,128)(2,1)S(1)} %get-tuple-element.69), channel_id=1, source_target_pairs={{0,24},{8,16},{16,8},{24,0},{1,25},{9,17},{17,9},{25,1},{2,26},{10... | collective-permute-start | bytes 491528 | tf_op jit(solution)/shard_map/ppermute | solution.py:290
  32.3 0.8 %collective-permute-start.10 = (bf16[640,256]{1,0:T(8,128)(2,1)S(1)}, bf16[640,256]{1,0:T(8,128)(2,1)S(1)}, u32[]{:S(2)}, u32[]{:S(2)}) collective-permute-start(bf16[640,256]{1,0:T(8,128)(2,1)S(1)} %get-tuple-element.70.own), channel_id=1, source_target_pairs={{0,8},{8,0},{16,24},{24,16},{1,9},{9,1},{17,25},{25,17},{2,10},{10... | collective-permute-start | bytes 983048 | tf_op jit(solution)/shard_map/ppermute | solution.py:290
  33.8 6.3 %prompt_attention.3 = (f32[128,4096]{1,0:T(8,128)S(1)}, f32[8,4096]{1,0:T(8,128)S(1)}) custom-call(s32[4]{0:T(128)S(1)} %get-tuple-element.90.info, bf16[128,4096]{1,0:T(8,128)(2,1)S(1)} %bitcast.21, bf16[512,1024]{1,0:T(8,128)(2,1)} %collective-permute-done.5.k_ref.v_ref, bf16[512,1024]{1,0:T(8,128)(2,1)} %collective-permute-done.5.k_ref.v_ref, ...), custom_call_target="tpu_custom_call" | custom-call | flops 4294967296 | bytes 1024 | tf_op jit(solution)/shard_map/prompt_attention/pallas_call | solution.py:96
  40.1 2.3 %collective-permute-done.6.forwarded = bf16[2,320,256]{2,1,0:T(8,128)(2,1)S(1)} collective-permute-done((bf16[2,320,256]{2,1,0:T(8,128)(2,1)S(1)}, bf16[2,320,256]{2,1,0:T(8,128)(2,1)S(1)}, u32[]{:S(2)}, u32[]{:S(2)}) %collective-permute-start.6) | collective-permute-done | bytes 327712 | tf_op jit(solution)/shard_map/ppermute | solution.py:290
  42.4 1.5 %project.2 = (f32[2,128,256]{2,1,0:T(8,128)S(1)}, f32[2,128,256]{2,1,0:T(8,128)S(1)}) custom-call(s32[4]{0:T(128)S(1)} %pad_add_fusion.1.where, bf16[4,128,640]{2,1,0:T(8,128)(2,1)S(1)} %get-tuple-element.67.keep, bf16[4,128,640]{2,1,0:T(8,128)(2,1)S(1)} %collective-permute-done.4.other, bf16[2,4,128,640]{3,2,1,0:T(8,128)(2,1)S(1)} %collective-permute-done.7.others, ...), custom_call_target="tpu_custom_call" | custom-call | flops 1024 | bytes 1024 | tf_op jit(solution)/shard_map/project/pallas_call | solution.py:117
  43.9 3.1 %collective-permute-done.8.refs_0_ = bf16[320,256]{1,0:T(8,128)(2,1)S(1)} collective-permute-done((bf16[320,256]{1,0:T(8,128)(2,1)S(1)}, bf16[320,256]{1,0:T(8,128)(2,1)S(1)}, u32[]{:S(2)}, u32[]{:S(2)}) %collective-permute-start.8) | collective-permute-done | bytes 163872 | tf_op jit(solution)/shard_map/ppermute | solution.py:290
  48.8 8.6 %collective-permute-done.11.forwarded = bf16[2,320,256]{2,1,0:T(8,128)(2,1)S(1)} collective-permute-done((bf16[2,320,256]{2,1,0:T(8,128)(2,1)S(1)}, bf16[2,320,256]{2,1,0:T(8,128)(2,1)S(1)}, u32[]{:S(2)}, u32[]{:S(2)}) %collective-permute-start.11) | collective-permute-done | bytes 327712 | tf_op jit(solution)/shard_map/ppermute | solution.py:290
  57.4 1.5 %project.3 = (f32[2,128,256]{2,1,0:T(8,128)S(1)}, f32[2,128,256]{2,1,0:T(8,128)S(1)}) custom-call(s32[4]{0:T(128)S(1)} %pad_add_fusion.1.where, bf16[4,128,640]{2,1,0:T(8,128)(2,1)S(1)} %get-tuple-element.67.keep, bf16[4,128,640]{2,1,0:T(8,128)(2,1)S(1)} %collective-permute-done.4.other, bf16[2,4,128,640]{3,2,1,0:T(8,128)(2,1)S(1)} %collective-permute-done.7.others, ...), custom_call_target="tpu_custom_call" | custom-call | flops 1024 | bytes 1024 | tf_op jit(solution)/shard_map/project/pallas_call | solution.py:117
  59.7 1.2 %collective-permute-done.14.there = f32[1,128,256]{2,1,0:T(8,128)S(1)} collective-permute-done((f32[1,128,256]{2,1,0:T(8,128)S(1)}, f32[1,128,256]{2,1,0:T(8,128)S(1)}, u32[]{:S(2)}, u32[]{:S(2)}) %collective-permute-start.14) | collective-permute-done | bytes 131104 | tf_op jit(solution)/shard_map/ppermute | solution.py:290
  61.0 2.3 %final_attention.2.refs_0_ = bf16[128,4096]{1,0:T(8,128)(2,1)} custom-call(s32[3]{0:T(128)S(1)} %pad_add_fusion.info, f32[1,128]{1,0:T(1,128)S(1)} %bitcast.29, bf16[128,4096]{1,0:T(8,128)(2,1)S(1)} %bitcast.22, f32[128,4096]{1,0:T(8,128)S(1)} %get-tuple-element.65.acc_ref, f32[8,4096]{1,0:T(8,128)S(1)} %get-tuple-element.66.ml_ref, ...), custom_call_target="tpu_custom_call" | custom-call | flops 1024 | bytes 1024 | tf_op jit(solution)/shard_map/final_attention/pallas_call | solution.py:276
  63.3 3.1 %collective-permute-done.13.theirs = f32[2,128,256]{2,1,0:T(8,128)S(1)} collective-permute-done((f32[2,128,256]{2,1,0:T(8,128)S(1)}, f32[2,128,256]{2,1,0:T(8,128)S(1)}, u32[]{:S(2)}, u32[]{:S(2)}) %collective-permute-start.13) | collective-permute-done | bytes 262176 | tf_op jit(solution)/shard_map/ppermute | solution.py:290
  66.5 1.3 %collective-permute-done.15.there = f32[1,128,256]{2,1,0:T(8,128)S(1)} collective-permute-done((f32[1,128,256]{2,1,0:T(8,128)S(1)}, f32[1,128,256]{2,1,0:T(8,128)S(1)}, u32[]{:S(2)}, u32[]{:S(2)}) %collective-permute-start.15) | collective-permute-done | bytes 131104 | tf_op jit(solution)/shard_map/ppermute | solution.py:290
  67.8 2.3 %final_attention.3 = bf16[128,4096]{1,0:T(8,128)(2,1)} custom-call(s32[3]{0:T(128)S(1)} %pad_add_fusion.info, f32[1,128]{1,0:T(1,128)S(1)} %bitcast.30, bf16[128,4096]{1,0:T(8,128)(2,1)S(1)} %bitcast.23, f32[128,4096]{1,0:T(8,128)S(1)} %get-tuple-element.65.acc_ref, f32[8,4096]{1,0:T(8,128)S(1)} %get-tuple-element.66.ml_ref, ...), custom_call_target="tpu_custom_call", output_to_operand_aliasing={{}: (8, {})} | custom-call | flops 1024 | bytes 1024 | tf_op jit(solution)/shard_map/final_attention/pallas_call | solution.py:276
  (39 shorter events, 5.1 us)
Async XLA Ops:
  0.0 8.0 %collective-permute-start = (bf16[320,1024]{1,0:T(8,128)(2,1)}, bf16[320,1024]{1,0:T(8,128)(2,1)S(1)}, u32[]{:S(2)}, u32[]{:S(2)}) collective-permute-start(bf16[320,1024]{1,0:T(8,128)(2,1)} %own_ref.1), channel_id=1, source_target_pairs={{0,2},{2,0},{1,3},{3,1},{4,6},{6,4},{5,7},{7,5},{8,10},{10,8},{9,1... | collective-permute-start | bytes 1966088 | tf_op jit(solution)/shard_map/ppermute | solution.py:290
  0.5 1.3 %copy-start.1 = (bf16[1,128,5120]{2,1,0:T(8,128)(2,1)S(1)}, bf16[1,128,5120]{2,1,0:T(8,128)(2,1)}, u32[]{:S(2)}) copy-start(bf16[1,128,5120]{2,1,0:T(8,128)(2,1)} %param.8) | copy-start | bytes 3932164
  1.8 12.4 %copy-start.5 = (s32[1,2,2]{2,1,0:T(2,128)S(1)}, s32[1,2,2]{2,1,0:T(2,128)}, u32[]{:S(2)}) copy-start(s32[1,2,2]{2,1,0:T(2,128)} %param.14) | copy-start | bytes 52
  1.9 12.7 %copy-start = (bf16[1,128,4096]{2,1,0:T(8,128)(2,1)S(1)}, bf16[1,128,4096]{2,1,0:T(8,128)(2,1)}, u32[]{:S(2)}) copy-start(bf16[1,128,4096]{2,1,0:T(8,128)(2,1)} %param.9) | copy-start | bytes 3145732
  3.3 18.1 %collective-permute-start.4 = (bf16[4,128,640]{2,1,0:T(8,128)(2,1)}, bf16[4,128,640]{2,1,0:T(8,128)(2,1)S(1)}, u32[]{:S(2)}, u32[]{:S(2)}) collective-permute-start(bf16[4,128,640]{2,1,0:T(8,128)(2,1)} %get-tuple-element.46), channel_id=1, source_target_pairs={{0,4},{4,0},{1,5},{5,1},{2,6},{6,2},{3,7},{7,3},{8,12},{12,8},{9,1... | collective-permute-start | bytes 1966088 | tf_op jit(solution)/shard_map/ppermute | solution.py:290
  5.9 27.3 %collective-permute-start.5 = (bf16[512,1024]{1,0:T(8,128)(2,1)}, bf16[512,1024]{1,0:T(8,128)(2,1)}, u32[]{:S(2)}, u32[]{:S(2)}) collective-permute-start(bf16[512,1024]{1,0:T(8,128)(2,1)} %bitcast.31), channel_id=1, source_target_pairs={{0,1},{1,0},{2,3},{3,2},{4,5},{5,4},{6,7},{7,6},{8,9},{9,8},{10,11... | collective-permute-start | bytes 3145736 | tf_op jit(solution)/shard_map/ppermute | solution.py:308
  8.0 1.1 %copy-start.2 = (bf16[320,1024]{1,0:T(8,128)(2,1)S(1)}, bf16[320,1024]{1,0:T(8,128)(2,1)}, u32[]{:S(2)}) copy-start(bf16[320,1024]{1,0:T(8,128)(2,1)} %own_ref.1) | copy-start | bytes 1966084
  9.1 5.4 %copy-start.4 = (bf16[1,512,1024]{2,1,0:T(8,128)(2,1)S(1)}, bf16[1,512,1024]{2,1,0:T(8,128)(2,1)}, u32[]{:S(2)}) copy-start(bf16[1,512,1024]{2,1,0:T(8,128)(2,1)} %param.10) | copy-start | bytes 3145732
  9.8 11.7 %collective-permute-start.2 = (bf16[320,256]{1,0:T(8,128)(2,1)S(1)}, bf16[320,256]{1,0:T(8,128)(2,1)S(1)}, u32[]{:S(2)}, u32[]{:S(2)}) collective-permute-start(bf16[320,256]{1,0:T(8,128)(2,1)S(1)} %get-tuple-element.50), channel_id=1, source_target_pairs={{0,24},{8,16},{16,8},{24,0},{1,25},{9,17},{17,9},{25,1},{2,26},{10... | collective-permute-start | bytes 491528 | tf_op jit(solution)/shard_map/ppermute | solution.py:290
  13.5 14.1 %collective-permute-start.1 = (bf16[320,256]{1,0:T(8,128)(2,1)S(1)}, bf16[320,256]{1,0:T(8,128)(2,1)S(1)}, u32[]{:S(2)}, u32[]{:S(2)}) collective-permute-start(bf16[320,256]{1,0:T(8,128)(2,1)S(1)} %get-tuple-element.50), channel_id=1, source_target_pairs={{0,16},{8,24},{16,0},{24,8},{1,17},{9,25},{17,1},{25,9},{2,18},{10... | collective-permute-start | bytes 491528 | tf_op jit(solution)/shard_map/ppermute | solution.py:290
  13.5 14.9 %collective-permute-start.3 = (bf16[640,256]{1,0:T(8,128)(2,1)S(1)}, bf16[640,256]{1,0:T(8,128)(2,1)S(1)}, u32[]{:S(2)}, u32[]{:S(2)}) collective-permute-start(bf16[640,256]{1,0:T(8,128)(2,1)S(1)} %get-tuple-element.48.own), channel_id=1, source_target_pairs={{0,8},{8,0},{16,24},{24,16},{1,9},{9,1},{17,25},{25,17},{2,10},{10... | collective-permute-start | bytes 983048 | tf_op jit(solution)/shard_map/ppermute | solution.py:290
  28.5 13.8 %collective-permute-start.7 = (bf16[2,4,128,640]{3,2,1,0:T(8,128)(2,1)S(1)}, bf16[2,4,128,640]{3,2,1,0:T(8,128)(2,1)S(1)}, u32[]{:S(2)}, u32[]{:S(2)}) collective-permute-start(bf16[2,4,128,640]{3,2,1,0:T(8,128)(2,1)S(1)} %pad_maximum_fusion), channel_id=1, source_target_pairs={{0,2},{2,0},{1,3},{3,1},{4,6},{6,4},{5,7},{7,5},{8,10},{10,8},{9,1... | collective-permute-start | bytes 3932168 | tf_op jit(solution)/shard_map/ppermute | solution.py:290
  28.7 15.2 %collective-permute-start.9 = (bf16[320,256]{1,0:T(8,128)(2,1)S(1)}, bf16[320,256]{1,0:T(8,128)(2,1)S(1)}, u32[]{:S(2)}, u32[]{:S(2)}) collective-permute-start(bf16[320,256]{1,0:T(8,128)(2,1)S(1)} %get-tuple-element.69), channel_id=1, source_target_pairs={{0,24},{8,16},{16,8},{24,0},{1,25},{9,17},{17,9},{25,1},{2,26},{10... | collective-permute-start | bytes 491528 | tf_op jit(solution)/shard_map/ppermute | solution.py:290
  32.3 14.7 %collective-permute-start.8 = (bf16[320,256]{1,0:T(8,128)(2,1)S(1)}, bf16[320,256]{1,0:T(8,128)(2,1)S(1)}, u32[]{:S(2)}, u32[]{:S(2)}) collective-permute-start(bf16[320,256]{1,0:T(8,128)(2,1)S(1)} %get-tuple-element.69), channel_id=1, source_target_pairs={{0,16},{8,24},{16,0},{24,8},{1,17},{9,25},{17,1},{25,9},{2,18},{10... | collective-permute-start | bytes 491528 | tf_op jit(solution)/shard_map/ppermute | solution.py:290
  32.3 15.4 %collective-permute-start.10 = (bf16[640,256]{1,0:T(8,128)(2,1)S(1)}, bf16[640,256]{1,0:T(8,128)(2,1)S(1)}, u32[]{:S(2)}, u32[]{:S(2)}) collective-permute-start(bf16[640,256]{1,0:T(8,128)(2,1)S(1)} %get-tuple-element.70.own), channel_id=1, source_target_pairs={{0,8},{8,0},{16,24},{24,16},{1,9},{9,1},{17,25},{25,17},{2,10},{10... | collective-permute-start | bytes 983048 | tf_op jit(solution)/shard_map/ppermute | solution.py:290
  33.2 9.2 %collective-permute-start.6 = (bf16[2,320,256]{2,1,0:T(8,128)(2,1)S(1)}, bf16[2,320,256]{2,1,0:T(8,128)(2,1)S(1)}, u32[]{:S(2)}, u32[]{:S(2)}) collective-permute-start(bf16[2,320,256]{2,1,0:T(8,128)(2,1)S(1)} %pad_maximum_fusion.1), channel_id=1, source_target_pairs={{0,1},{1,0},{2,3},{3,2},{4,5},{5,4},{6,7},{7,6},{8,9},{9,8},{10,11... | collective-permute-start | bytes 983048 | tf_op jit(solution)/shard_map/ppermute | solution.py:290
  47.7 9.7 %collective-permute-start.11 = (bf16[2,320,256]{2,1,0:T(8,128)(2,1)S(1)}, bf16[2,320,256]{2,1,0:T(8,128)(2,1)S(1)}, u32[]{:S(2)}, u32[]{:S(2)}) collective-permute-start(bf16[2,320,256]{2,1,0:T(8,128)(2,1)S(1)} %pad_maximum_fusion.2), channel_id=1, source_target_pairs={{0,1},{1,0},{2,3},{3,2},{4,5},{5,4},{6,7},{7,6},{8,9},{9,8},{10,11... | collective-permute-start | bytes 983048 | tf_op jit(solution)/shard_map/ppermute | solution.py:290
  48.3 11.3 %copy-start.6 = (s32[1,2]{1,0:T(1,128)S(1)}, s32[1,2]{1,0:T(1,128)}, u32[]{:S(2)}) copy-start(s32[1,2]{1,0:T(1,128)} %param.15) | copy-start | bytes 28
  48.3 12.7 %copy-start.3 = (f32[128]{0:T(128)S(1)}, f32[128]{0:T(128)}, u32[]{:S(2)}) copy-start(f32[128]{0:T(128)} %param.12) | copy-start | bytes 1540
  48.3 10.6 %collective-permute-start.12 = (f32[2,128,256]{2,1,0:T(8,128)S(1)}, f32[2,128,256]{2,1,0:T(8,128)S(1)}, u32[]{:S(2)}, u32[]{:S(2)}) collective-permute-start(f32[2,128,256]{2,1,0:T(8,128)S(1)} %get-tuple-element.80), channel_id=1, source_target_pairs={{0,4},{4,0},{1,5},{5,1},{2,6},{6,2},{3,7},{7,3},{8,12},{12,8},{9,1... | collective-permute-start | bytes 786440 | tf_op jit(solution)/shard_map/ppermute | solution.py:290
  58.9 7.5 %collective-permute-start.13 = (f32[2,128,256]{2,1,0:T(8,128)S(1)}, f32[2,128,256]{2,1,0:T(8,128)S(1)}, u32[]{:S(2)}, u32[]{:S(2)}) collective-permute-start(f32[2,128,256]{2,1,0:T(8,128)S(1)} %get-tuple-element.82), channel_id=1, source_target_pairs={{0,4},{4,0},{1,5},{5,1},{2,6},{6,2},{3,7},{7,3},{8,12},{12,8},{9,1... | collective-permute-start | bytes 786440 | tf_op jit(solution)/shard_map/ppermute | solution.py:290
  59.5 1.4 %collective-permute-start.14 = (f32[1,128,256]{2,1,0:T(8,128)S(1)}, f32[1,128,256]{2,1,0:T(8,128)S(1)}, u32[]{:S(2)}, u32[]{:S(2)}) collective-permute-start(f32[1,128,256]{2,1,0:T(8,128)S(1)} %slice_add_fusion.1), channel_id=1, source_target_pairs={{0,2},{2,0},{1,3},{3,1},{4,6},{6,4},{5,7},{7,5},{8,10},{10,8},{9,1... | collective-permute-start | bytes 393224 | tf_op jit(solution)/shard_map/ppermute | solution.py:290
  66.4 1.4 %collective-permute-start.15 = (f32[1,128,256]{2,1,0:T(8,128)S(1)}, f32[1,128,256]{2,1,0:T(8,128)S(1)}, u32[]{:S(2)}, u32[]{:S(2)}) collective-permute-start(f32[1,128,256]{2,1,0:T(8,128)S(1)} %slice_add_fusion), channel_id=1, source_target_pairs={{0,2},{2,0},{1,3},{3,1},{4,6},{6,4},{5,7},{7,5},{8,10},{10,8},{9,1... | collective-permute-start | bytes 393224 | tf_op jit(solution)/shard_map/ppermute | solution.py:290

commit v8 on v6

--- a/solution.py
+++ b/solution.py
@@ -22,10 +22,9 @@
 HIDDEN = -1e30
 NT = (((1,), (1,)), ((), ()))
 HINT = pl.CostEstimate(flops=1024, bytes_accessed=1024, transcendentals=0)
-LONG = pl.CostEstimate(flops=2**32, bytes_accessed=1024, transcendentals=0)
 
 CHUNKS = ((0, 2), (2, 2))
-HELP = (4, 5)
+HELP = (5, 5)
 
 
 def pair_queries(q_ref, g, extra=None):
@@ -103,7 +102,9 @@
             jax.ShapeDtypeStruct((8, heads * SHARED * ROWS), jnp.float32),
         ],
         compiler_params=pltpu.CompilerParams(vmem_limit_bytes=32 * 2**20),
-        cost_estimate=LONG,
+        cost_estimate=pl.CostEstimate(
+            flops=2**33 if first else 2**32, bytes_accessed=1024, transcendentals=0
+        ),
         name="prompt_attention",
     )(info, *operands)
 
@@ -323,6 +324,7 @@
 
     sent = [send(far[0])]
     near = xor_swap(whole, "z", 1)
+    got_x, whole = tie((got_x, whole))
     keep, given = pack_rows(where, x, got_x, y, steps)
     other = xor_swap(given, "y", 1)
 
@@ -337,8 +339,9 @@
     query, _, _ = tie((query, whole, given))
     state = prompt_attention(infos[0], query, caches[0], None, 0, KVH)
 
-    sent[0], caches, state, far[1] = tie((sent[0], caches, state, far[1]))
+    sent[0], state, far[1] = tie((sent[0], state, far[1]))
     sent.append(send(far[1]))
+    sent[0], caches = tie((sent[0], caches))
     forwarded = [forward(0)]
     for stride in range(1, cycle):
         state = prompt_attention(infos[stride], query, caches[stride], state, 0, KVH)
@@ -354,13 +357,14 @@
     theirs_0 = xor_swap(theirs_0, "y", 1)
     forwarded[1], mine_0 = tie((forwarded[1], mine_0))
     mine_1, theirs_1 = sums(1)
-    theirs_0, theirs_1 = tie((theirs_0, theirs_1))
-    theirs_1 = xor_swap(theirs_1, "y", 1)
+    theirs_0, theirs_1, mine_1 = tie((theirs_0, theirs_1, mine_1))
     there_0 = xor_swap(mine_0[1:] + theirs_0[1:], "core", 1)
+    there_1 = [xor_swap(theirs_1[1:], ("y", "core"), 3), xor_swap(mine_1[1:], "core", 1)]
+    theirs_1 = xor_swap(theirs_1[:1], "y", 1)
     result = final_attention(info, gain, query, state, 0, CHUNKS[0], mine_0, theirs_0, there_0, None)
-    theirs_1, result = tie((theirs_1, result))
-    there_1 = xor_swap(mine_1[1:] + theirs_1[1:], "core", 1)
-    result = final_attention(info, gain, query, state, 2, CHUNKS[1], mine_1, theirs_1, there_1, result)
+    result = final_attention(
+        info, gain, query, state, 2, CHUNKS[1], mine_1, theirs_1, jnp.concatenate(there_1), result
+    )
     return result[None]
 
 

time: 64.9 us -> 62.6 us (0.965)
  the two profiles are of different devices: /device:TPU:9 before, /device:TPU:0 now
where the time goes in v8:
time: 62.6 us; the launch traced here: 62.3 us
  starting transfers between devices  23.9 us (38%)
  Pallas kernels  20.8 us (33%)
  waiting for transfers between devices  15.2 us (24%)
  local copies, waits for them, and re-layouts  1.35 us (2%)
  between operations  0.78 us (1%)
    ppermute x15, starting transfers between devices, xor_swap(): lax.ppermute(array, axis, [(i, i ^ by) for i in range(lax.axis_size(axis))])  21 us
    ppermute x15, waiting for transfers between devices, xor_swap(): lax.ppermute(array, axis, [(i, i ^ by) for i in range(lax.axis_size(axis))])  15.2 us
    pallas_call x2, Pallas kernels, prompt_attention(): pl.pallas_call(functools.partial(prompt_kernel, first), grid_spec=pltpu.P...  11.7 us
    pallas_call x2, Pallas kernels, final_attention(): pl.pallas_call(functools.partial(final_kernel, chunk, offset), in_specs=s...  4.67 us
    pallas_call x3, Pallas kernels, on_chip(): pl.pallas_call(kernel, in_specs=[SMEM] + [VMEM] * len(operands), out_spec...  3.76 us
    ppermute x1, starting transfers between devices, per_device(): lax.ppermute(caches[-1], 'blk', [(i, (i + 1) % cycle) for i in range(cycl...  2.93 us
  transfers between devices with their start and end apart: 16, of which 8 were waited for; matrix products, arithmetic and copies ran while one was open for 1% of the time, Pallas kernels for 30%

profile of v8, /device:TPU:0, one launch (start us, length us, event | category | flops | bytes accessed | tf_op | source)
XLA Modules:
  0.0 62.3 jit_solution(16612933789029202716)
XLA Ops:
  0.5 2.9 %collective-permute-start.6 = (bf16[512,1024]{1,0:T(8,128)(2,1)}, bf16[512,1024]{1,0:T(8,128)(2,1)}, u32[]{:S(2)}, u32[]{:S(2)}) collective-permute-start(bf16[512,1024]{1,0:T(8,128)(2,1)} %bitcast.28), channel_id=1, source_target_pairs={{0,1},{1,0},{2,3},{3,2},{4,5},{5,4},{6,7},{7,6},{8,9},{9,8},{10,11... | collective-permute-start | bytes 3145736 | tf_op jit(solution)/shard_map/ppermute | solution.py:313
  4.3 1.1 %copy-done.2 = bf16[320,1024]{1,0:T(8,128)(2,1)S(1)} copy-done((bf16[320,1024]{1,0:T(8,128)(2,1)S(1)}, bf16[320,1024]{1,0:T(8,128)(2,1)}, u32[]{:S(2)}) %copy-start.2) | copy-done | bytes 655384
  5.4 0.6 %pack_weight.1 = (bf16[640,512]{1,0:T(8,128)(2,1)S(1)}, bf16[320,256]{1,0:T(8,128)(2,1)S(1)}, bf16[320,256]{1,0:T(8,128)(2,1)S(1)}) custom-call(s32[4]{0:T(128)S(1)} %pad_add_fusion.1.where, bf16[320,1024]{1,0:T(8,128)(2,1)S(1)} %collective-permute-done.1.got_ref, bf16[320,1024]{1,0:T(8,128)(2,1)S(1)} %copy-done.2), custom_call_target="tpu_custom_call" | custom-call | flops 1024 | bytes 1024 | tf_op jit(solution)/shard_map/pack_weight/pallas_call | solution.py:176
  6.0 4.0 %collective-permute-start.2 = (bf16[320,256]{1,0:T(8,128)(2,1)S(1)}, bf16[320,256]{1,0:T(8,128)(2,1)S(1)}, u32[]{:S(2)}, u32[]{:S(2)}) collective-permute-start(bf16[320,256]{1,0:T(8,128)(2,1)S(1)} %get-tuple-element.45), channel_id=1, source_target_pairs={{0,16},{8,24},{16,0},{24,8},{1,17},{9,25},{17,1},{25,9},{2,18},{10... | collective-permute-start | bytes 491528 | tf_op jit(solution)/shard_map/ppermute | solution.py:294
  10.0 1.3 %collective-permute-start.3 = (bf16[320,256]{1,0:T(8,128)(2,1)S(1)}, bf16[320,256]{1,0:T(8,128)(2,1)S(1)}, u32[]{:S(2)}, u32[]{:S(2)}) collective-permute-start(bf16[320,256]{1,0:T(8,128)(2,1)S(1)} %get-tuple-element.45), channel_id=1, source_target_pairs={{0,24},{8,16},{16,8},{24,0},{1,25},{9,17},{17,9},{25,1},{2,26},{10... | collective-permute-start | bytes 491528 | tf_op jit(solution)/shard_map/ppermute | solution.py:294
  11.7 0.7 %pack_rows.1 = (bf16[2,4,128,640]{3,2,1,0:T(8,128)(2,1)S(1)}, bf16[2,4,128,640]{3,2,1,0:T(8,128)(2,1)S(1)}) custom-call(s32[4]{0:T(128)S(1)} %pad_add_fusion.1.where, bf16[128,5120]{1,0:T(8,128)(2,1)S(1)} %bitcast.21, bf16[128,5120]{1,0:T(8,128)(2,1)S(1)} %collective-permute-done.got_ref), custom_call_target="tpu_custom_call" | custom-call | flops 1024 | bytes 1024 | tf_op jit(solution)/shard_map/pack_rows/pallas_call | solution.py:118
  12.4 1.6 %collective-permute-start.8 = (bf16[2,4,128,640]{3,2,1,0:T(8,128)(2,1)S(1)}, bf16[2,4,128,640]{3,2,1,0:T(8,128)(2,1)S(1)}, u32[]{:S(2)}, u32[]{:S(2)}) collective-permute-start(bf16[2,4,128,640]{3,2,1,0:T(8,128)(2,1)S(1)} %get-tuple-element.43), channel_id=1, source_target_pairs={{0,4},{4,0},{1,5},{5,1},{2,6},{6,2},{3,7},{7,3},{8,12},{12,8},{9,1... | collective-permute-start | bytes 3932168 | tf_op jit(solution)/shard_map/ppermute | solution.py:294
  14.3 5.4 %prompt_attention.2 = (f32[128,4096]{1,0:T(8,128)S(1)}, f32[8,4096]{1,0:T(8,128)S(1)}) custom-call(s32[4]{0:T(128)S(1)} %get-tuple-element.79.info, bf16[128,4096]{1,0:T(8,128)(2,1)S(1)} %bitcast.16, bf16[512,1024]{1,0:T(8,128)(2,1)S(1)} %bitcast.29, bf16[512,1024]{1,0:T(8,128)(2,1)S(1)} %bitcast.30), custom_call_target="tpu_custom_call" | custom-call | flops 8589934592 | bytes 1024 | tf_op jit(solution)/shard_map/prompt_attention/pallas_call | solution.py:95
  19.8 2.3 %collective-permute-done.2.refs_0_ = bf16[320,256]{1,0:T(8,128)(2,1)S(1)} collective-permute-done((bf16[320,256]{1,0:T(8,128)(2,1)S(1)}, bf16[320,256]{1,0:T(8,128)(2,1)S(1)}, u32[]{:S(2)}, u32[]{:S(2)}) %collective-permute-start.2) | collective-permute-done | bytes 163872 | tf_op jit(solution)/shard_map/ppermute | solution.py:294
  22.1 5.7 %collective-permute-start.4 = (bf16[320,256]{1,0:T(8,128)(2,1)S(1)}, bf16[320,256]{1,0:T(8,128)(2,1)S(1)}, u32[]{:S(2)}, u32[]{:S(2)}) collective-permute-start(bf16[320,256]{1,0:T(8,128)(2,1)S(1)} %get-tuple-element.50), channel_id=1, source_target_pairs={{0,16},{8,24},{16,0},{24,8},{1,17},{9,25},{17,1},{25,9},{2,18},{10... | collective-permute-start | bytes 491528 | tf_op jit(solution)/shard_map/ppermute | solution.py:294
  28.2 1.6 %collective-permute-start.7 = (bf16[2,320,256]{2,1,0:T(8,128)(2,1)S(1)}, bf16[2,320,256]{2,1,0:T(8,128)(2,1)S(1)}, u32[]{:S(2)}, u32[]{:S(2)}) collective-permute-start(bf16[2,320,256]{2,1,0:T(8,128)(2,1)S(1)} %pad_maximum_fusion), channel_id=1, source_target_pairs={{0,1},{1,0},{2,3},{3,2},{4,5},{5,4},{6,7},{7,6},{8,9},{9,8},{10,11... | collective-permute-start | bytes 983048 | tf_op jit(solution)/shard_map/ppermute | solution.py:294
  29.8 6.3 %prompt_attention.3 = (f32[128,4096]{1,0:T(8,128)S(1)}, f32[8,4096]{1,0:T(8,128)S(1)}) custom-call(s32[4]{0:T(128)S(1)} %get-tuple-element.80.info, bf16[128,4096]{1,0:T(8,128)(2,1)S(1)} %bitcast.17, bf16[512,1024]{1,0:T(8,128)(2,1)} %collective-permute-done.6.k_ref.v_ref, bf16[512,1024]{1,0:T(8,128)(2,1)} %collective-permute-done.6.k_ref.v_ref, ...), custom_call_target="tpu_custom_call" | custom-call | flops 4294967296 | bytes 1024 | tf_op jit(solution)/shard_map/prompt_attention/pallas_call | solution.py:95
  36.1 4.4 %collective-permute-done.5.refs_1_ = bf16[320,256]{1,0:T(8,128)(2,1)S(1)} collective-permute-done((bf16[320,256]{1,0:T(8,128)(2,1)S(1)}, bf16[320,256]{1,0:T(8,128)(2,1)S(1)}, u32[]{:S(2)}, u32[]{:S(2)}) %collective-permute-start.5) | collective-permute-done | bytes 163872 | tf_op jit(solution)/shard_map/ppermute | solution.py:294
  40.5 1.6 %collective-permute-start.11 = (bf16[2,320,256]{2,1,0:T(8,128)(2,1)S(1)}, bf16[2,320,256]{2,1,0:T(8,128)(2,1)S(1)}, u32[]{:S(2)}, u32[]{:S(2)}) collective-permute-start(bf16[2,320,256]{2,1,0:T(8,128)(2,1)S(1)} %pad_maximum_fusion.1), channel_id=1, source_target_pairs={{0,1},{1,0},{2,3},{3,2},{4,5},{5,4},{6,7},{7,6},{8,9},{9,8},{10,11... | collective-permute-start | bytes 983048 | tf_op jit(solution)/shard_map/ppermute | solution.py:294
  42.0 0.7 %collective-permute-done.8.other = bf16[2,4,128,640]{3,2,1,0:T(8,128)(2,1)S(1)} collective-permute-done((bf16[2,4,128,640]{3,2,1,0:T(8,128)(2,1)S(1)}, bf16[2,4,128,640]{3,2,1,0:T(8,128)(2,1)S(1)}, u32[]{:S(2)}, u32[]{:S(2)}) %collective-permute-start.8) | collective-permute-done | bytes 1310752 | tf_op jit(solution)/shard_map/ppermute | solution.py:294
  42.8 1.5 %project.2 = (f32[2,128,256]{2,1,0:T(8,128)S(1)}, f32[2,128,256]{2,1,0:T(8,128)S(1)}) custom-call(s32[4]{0:T(128)S(1)} %pad_add_fusion.1.where, bf16[2,4,128,640]{3,2,1,0:T(8,128)(2,1)S(1)} %get-tuple-element.62.keep, bf16[2,4,128,640]{3,2,1,0:T(8,128)(2,1)S(1)} %collective-permute-done.8.other, bf16[640,512]{1,0:T(8,128)(2,1)S(1)} %get-tuple-element.41.own, ...), custom_call_target="tpu_custom_call" | custom-call | flops 1024 | bytes 1024 | tf_op jit(solution)/shard_map/project/pallas_call | solution.py:118
  44.3 1.6 %collective-permute-start.10 = (f32[2,128,256]{2,1,0:T(8,128)S(1)}, f32[2,128,256]{2,1,0:T(8,128)S(1)}, u32[]{:S(2)}, u32[]{:S(2)}) collective-permute-start(f32[2,128,256]{2,1,0:T(8,128)S(1)} %get-tuple-element.64), channel_id=1, source_target_pairs={{0,4},{4,0},{1,5},{5,1},{2,6},{6,2},{3,7},{7,3},{8,12},{12,8},{9,1... | collective-permute-start | bytes 786440 | tf_op jit(solution)/shard_map/ppermute | solution.py:294
  45.8 3.4 %collective-permute-done.11.forwarded = bf16[2,320,256]{2,1,0:T(8,128)(2,1)S(1)} collective-permute-done((bf16[2,320,256]{2,1,0:T(8,128)(2,1)S(1)}, bf16[2,320,256]{2,1,0:T(8,128)(2,1)S(1)}, u32[]{:S(2)}, u32[]{:S(2)}) %collective-permute-start.11) | collective-permute-done | bytes 327712 | tf_op jit(solution)/shard_map/ppermute | solution.py:294
  49.3 1.5 %project.3 = (f32[2,128,256]{2,1,0:T(8,128)S(1)}, f32[2,128,256]{2,1,0:T(8,128)S(1)}) custom-call(s32[4]{0:T(128)S(1)} %pad_add_fusion.1.where, bf16[2,4,128,640]{3,2,1,0:T(8,128)(2,1)S(1)} %get-tuple-element.62.keep, bf16[2,4,128,640]{3,2,1,0:T(8,128)(2,1)S(1)} %collective-permute-done.8.other, bf16[640,512]{1,0:T(8,128)(2,1)S(1)} %get-tuple-element.41.own, ...), custom_call_target="tpu_custom_call" | custom-call | flops 1024 | bytes 1024 | tf_op jit(solution)/shard_map/project/pallas_call | solution.py:118
  51.3 1.7 %collective-permute-start.13 = (f32[1,128,256]{2,1,0:T(8,128)S(1)}, f32[1,128,256]{2,1,0:T(8,128)S(1)}, u32[]{:S(2)}, u32[]{:S(2)}) collective-permute-start(f32[1,128,256]{2,1,0:T(8,128)S(1)} %get-tuple-element.77), channel_id=1, source_target_pairs={{0,6},{2,4},{4,2},{6,0},{1,7},{3,5},{5,3},{7,1},{8,14},{10,12},{12... | collective-permute-start | bytes 393224 | tf_op jit(solution)/shard_map/ppermute | solution.py:294
  53.8 2.3 %final_attention.2.refs_0_ = bf16[128,4096]{1,0:T(8,128)(2,1)} custom-call(s32[3]{0:T(128)S(1)} %pad_add_fusion.info, f32[1,128]{1,0:T(1,128)S(1)} %bitcast.26, bf16[128,4096]{1,0:T(8,128)(2,1)S(1)} %bitcast.18, f32[128,4096]{1,0:T(8,128)S(1)} %get-tuple-element.60.acc_ref, f32[8,4096]{1,0:T(8,128)S(1)} %get-tuple-element.61.ml_ref, ...), custom_call_target="tpu_custom_call" | custom-call | flops 1024 | bytes 1024 | tf_op jit(solution)/shard_map/final_attention/pallas_call | solution.py:280
  56.1 0.8 %collective-permute-done.13 = f32[1,128,256]{2,1,0:T(8,128)S(1)} collective-permute-done((f32[1,128,256]{2,1,0:T(8,128)S(1)}, f32[1,128,256]{2,1,0:T(8,128)S(1)}, u32[]{:S(2)}, u32[]{:S(2)}) %collective-permute-start.13) | collective-permute-done | bytes 131104 | tf_op jit(solution)/shard_map/ppermute | solution.py:294
  56.9 3.1 %collective-permute-done.12.theirs = f32[1,128,256]{2,1,0:T(8,128)S(1)} collective-permute-done((f32[1,128,256]{2,1,0:T(8,128)S(1)}, f32[1,128,256]{2,1,0:T(8,128)S(1)}, u32[]{:S(2)}, u32[]{:S(2)}) %collective-permute-start.12) | collective-permute-done | bytes 131104 | tf_op jit(solution)/shard_map/ppermute | solution.py:294
  60.0 2.3 %final_attention.3 = bf16[128,4096]{1,0:T(8,128)(2,1)} custom-call(s32[3]{0:T(128)S(1)} %pad_add_fusion.info, f32[1,128]{1,0:T(1,128)S(1)} %bitcast.27, bf16[128,4096]{1,0:T(8,128)(2,1)S(1)} %bitcast.19, f32[128,4096]{1,0:T(8,128)S(1)} %get-tuple-element.60.acc_ref, f32[8,4096]{1,0:T(8,128)S(1)} %get-tuple-element.61.ml_ref, ...), custom_call_target="tpu_custom_call", output_to_operand_aliasing={{}: (8, {})} | custom-call | flops 1024 | bytes 1024 | tf_op jit(solution)/shard_map/final_attention/pallas_call | solution.py:280
  (40 shorter events, 3.1 us)
Async XLA Ops:
  0.0 11.7 %copy-start.1 = (bf16[1,128,5120]{2,1,0:T(8,128)(2,1)S(1)}, bf16[1,128,5120]{2,1,0:T(8,128)(2,1)}, u32[]{:S(2)}) copy-start(bf16[1,128,5120]{2,1,0:T(8,128)(2,1)} %param.8) | copy-start | bytes 3932164
  0.0 11.7 %collective-permute-start = (bf16[128,5120]{1,0:T(8,128)(2,1)}, bf16[128,5120]{1,0:T(8,128)(2,1)S(1)}, u32[]{:S(2)}, u32[]{:S(2)}) collective-permute-start(bf16[128,5120]{1,0:T(8,128)(2,1)} %bitcast.20), channel_id=1, source_target_pairs={{0,2},{2,0},{1,3},{3,1},{4,6},{6,4},{5,7},{7,5},{8,10},{10,8},{9,1... | collective-permute-start | bytes 3932168 | tf_op jit(solution)/shard_map/ppermute | solution.py:294
  0.5 3.8 %collective-permute-start.1 = (bf16[320,1024]{1,0:T(8,128)(2,1)}, bf16[320,1024]{1,0:T(8,128)(2,1)S(1)}, u32[]{:S(2)}, u32[]{:S(2)}) collective-permute-start(bf16[320,1024]{1,0:T(8,128)(2,1)} %own_ref.1), channel_id=1, source_target_pairs={{0,2},{2,0},{1,3},{3,1},{4,6},{6,4},{5,7},{7,5},{8,10},{10,8},{9,1... | collective-permute-start | bytes 1966088 | tf_op jit(solution)/shard_map/ppermute | solution.py:294
  0.5 27.7 %collective-permute-start.6 = (bf16[512,1024]{1,0:T(8,128)(2,1)}, bf16[512,1024]{1,0:T(8,128)(2,1)}, u32[]{:S(2)}, u32[]{:S(2)}) collective-permute-start(bf16[512,1024]{1,0:T(8,128)(2,1)} %bitcast.28), channel_id=1, source_target_pairs={{0,1},{1,0},{2,3},{3,2},{4,5},{5,4},{6,7},{7,6},{8,9},{9,8},{10,11... | collective-permute-start | bytes 3145736 | tf_op jit(solution)/shard_map/ppermute | solution.py:313
  4.3 1.1 %copy-start.2 = (bf16[320,1024]{1,0:T(8,128)(2,1)S(1)}, bf16[320,1024]{1,0:T(8,128)(2,1)}, u32[]{:S(2)}) copy-start(bf16[320,1024]{1,0:T(8,128)(2,1)} %own_ref.1) | copy-start | bytes 1966084
  6.0 16.1 %collective-permute-start.2 = (bf16[320,256]{1,0:T(8,128)(2,1)S(1)}, bf16[320,256]{1,0:T(8,128)(2,1)S(1)}, u32[]{:S(2)}, u32[]{:S(2)}) collective-permute-start(bf16[320,256]{1,0:T(8,128)(2,1)S(1)} %get-tuple-element.45), channel_id=1, source_target_pairs={{0,16},{8,24},{16,0},{24,8},{1,17},{9,25},{17,1},{25,9},{2,18},{10... | collective-permute-start | bytes 491528 | tf_op jit(solution)/shard_map/ppermute | solution.py:294
  10.0 12.1 %collective-permute-start.3 = (bf16[320,256]{1,0:T(8,128)(2,1)S(1)}, bf16[320,256]{1,0:T(8,128)(2,1)S(1)}, u32[]{:S(2)}, u32[]{:S(2)}) collective-permute-start(bf16[320,256]{1,0:T(8,128)(2,1)S(1)} %get-tuple-element.45), channel_id=1, source_target_pairs={{0,24},{8,16},{16,8},{24,0},{1,25},{9,17},{17,9},{25,1},{2,26},{10... | collective-permute-start | bytes 491528 | tf_op jit(solution)/shard_map/ppermute | solution.py:294
  11.4 2.7 %copy-start.5 = (s32[1,2,2]{2,1,0:T(2,128)S(1)}, s32[1,2,2]{2,1,0:T(2,128)}, u32[]{:S(2)}) copy-start(s32[1,2,2]{2,1,0:T(2,128)} %param.14) | copy-start | bytes 52
  11.4 3.0 %copy-start = (bf16[1,128,4096]{2,1,0:T(8,128)(2,1)S(1)}, bf16[1,128,4096]{2,1,0:T(8,128)(2,1)}, u32[]{:S(2)}) copy-start(bf16[1,128,4096]{2,1,0:T(8,128)(2,1)} %param.9) | copy-start | bytes 3145732
  11.4 3.0 %copy-start.4 = (bf16[1,512,1024]{2,1,0:T(8,128)(2,1)S(1)}, bf16[1,512,1024]{2,1,0:T(8,128)(2,1)}, u32[]{:S(2)}) copy-start(bf16[1,512,1024]{2,1,0:T(8,128)(2,1)} %param.10) | copy-start | bytes 3145732
  11.4 30.7 %collective-permute-start.9 = (bf16[640,512]{1,0:T(8,128)(2,1)S(1)}, bf16[640,512]{1,0:T(8,128)(2,1)S(1)}, u32[]{:S(2)}, u32[]{:S(2)}) collective-permute-start(bf16[640,512]{1,0:T(8,128)(2,1)S(1)} %get-tuple-element.41.own), channel_id=1, source_target_pairs={{0,8},{8,0},{16,24},{24,16},{1,9},{9,1},{17,25},{25,17},{2,10},{10... | collective-permute-start | bytes 1966088 | tf_op jit(solution)/shard_map/ppermute | solution.py:294
  12.4 30.3 %collective-permute-start.8 = (bf16[2,4,128,640]{3,2,1,0:T(8,128)(2,1)S(1)}, bf16[2,4,128,640]{3,2,1,0:T(8,128)(2,1)S(1)}, u32[]{:S(2)}, u32[]{:S(2)}) collective-permute-start(bf16[2,4,128,640]{3,2,1,0:T(8,128)(2,1)S(1)} %get-tuple-element.43), channel_id=1, source_target_pairs={{0,4},{4,0},{1,5},{5,1},{2,6},{6,2},{3,7},{7,3},{8,12},{12,8},{9,1... | collective-permute-start | bytes 3932168 | tf_op jit(solution)/shard_map/ppermute | solution.py:294
  22.1 14.0 %collective-permute-start.4 = (bf16[320,256]{1,0:T(8,128)(2,1)S(1)}, bf16[320,256]{1,0:T(8,128)(2,1)S(1)}, u32[]{:S(2)}, u32[]{:S(2)}) collective-permute-start(bf16[320,256]{1,0:T(8,128)(2,1)S(1)} %get-tuple-element.50), channel_id=1, source_target_pairs={{0,16},{8,24},{16,0},{24,8},{1,17},{9,25},{17,1},{25,9},{2,18},{10... | collective-permute-start | bytes 491528 | tf_op jit(solution)/shard_map/ppermute | solution.py:294
  27.7 12.7 %collective-permute-start.5 = (bf16[320,256]{1,0:T(8,128)(2,1)S(1)}, bf16[320,256]{1,0:T(8,128)(2,1)S(1)}, u32[]{:S(2)}, u32[]{:S(2)}) collective-permute-start(bf16[320,256]{1,0:T(8,128)(2,1)S(1)} %get-tuple-element.50), channel_id=1, source_target_pairs={{0,24},{8,16},{16,8},{24,0},{1,25},{9,17},{17,9},{25,1},{2,26},{10... | collective-permute-start | bytes 491528 | tf_op jit(solution)/shard_map/ppermute | solution.py:294
  28.2 12.2 %collective-permute-start.7 = (bf16[2,320,256]{2,1,0:T(8,128)(2,1)S(1)}, bf16[2,320,256]{2,1,0:T(8,128)(2,1)S(1)}, u32[]{:S(2)}, u32[]{:S(2)}) collective-permute-start(bf16[2,320,256]{2,1,0:T(8,128)(2,1)S(1)} %pad_maximum_fusion), channel_id=1, source_target_pairs={{0,1},{1,0},{2,3},{3,2},{4,5},{5,4},{6,7},{7,6},{8,9},{9,8},{10,11... | collective-permute-start | bytes 983048 | tf_op jit(solution)/shard_map/ppermute | solution.py:294
  40.5 8.8 %collective-permute-start.11 = (bf16[2,320,256]{2,1,0:T(8,128)(2,1)S(1)}, bf16[2,320,256]{2,1,0:T(8,128)(2,1)S(1)}, u32[]{:S(2)}, u32[]{:S(2)}) collective-permute-start(bf16[2,320,256]{2,1,0:T(8,128)(2,1)S(1)} %pad_maximum_fusion.1), channel_id=1, source_target_pairs={{0,1},{1,0},{2,3},{3,2},{4,5},{5,4},{6,7},{7,6},{8,9},{9,8},{10,11... | collective-permute-start | bytes 983048 | tf_op jit(solution)/shard_map/ppermute | solution.py:294
  44.3 6.9 %collective-permute-start.10 = (f32[2,128,256]{2,1,0:T(8,128)S(1)}, f32[2,128,256]{2,1,0:T(8,128)S(1)}, u32[]{:S(2)}, u32[]{:S(2)}) collective-permute-start(f32[2,128,256]{2,1,0:T(8,128)S(1)} %get-tuple-element.64), channel_id=1, source_target_pairs={{0,4},{4,0},{1,5},{5,1},{2,6},{6,2},{3,7},{7,3},{8,12},{12,8},{9,1... | collective-permute-start | bytes 786440 | tf_op jit(solution)/shard_map/ppermute | solution.py:294
  49.3 4.4 %copy-start.6 = (s32[1,2]{1,0:T(1,128)S(1)}, s32[1,2]{1,0:T(1,128)}, u32[]{:S(2)}) copy-start(s32[1,2]{1,0:T(1,128)} %param.15) | copy-start | bytes 28
  49.3 4.5 %copy-start.3 = (f32[128]{0:T(128)S(1)}, f32[128]{0:T(128)}, u32[]{:S(2)}) copy-start(f32[128]{0:T(128)} %param.12) | copy-start | bytes 1540
  51.2 2.5 %collective-permute-start.15 = (f32[1,128,256]{2,1,0:T(8,128)S(1)}, f32[1,128,256]{2,1,0:T(8,128)S(1)}, u32[]{:S(2)}, u32[]{:S(2)}) collective-permute-start(f32[1,128,256]{2,1,0:T(8,128)S(1)} %slice_add_fusion), channel_id=1, source_target_pairs={{0,2},{2,0},{1,3},{3,1},{4,6},{6,4},{5,7},{7,5},{8,10},{10,8},{9,1... | collective-permute-start | bytes 393224 | tf_op jit(solution)/shard_map/ppermute | solution.py:294
  51.3 5.5 %collective-permute-start.13 = (f32[1,128,256]{2,1,0:T(8,128)S(1)}, f32[1,128,256]{2,1,0:T(8,128)S(1)}, u32[]{:S(2)}, u32[]{:S(2)}) collective-permute-start(f32[1,128,256]{2,1,0:T(8,128)S(1)} %get-tuple-element.77), channel_id=1, source_target_pairs={{0,6},{2,4},{4,2},{6,0},{1,7},{3,5},{5,3},{7,1},{8,14},{10,12},{12... | collective-permute-start | bytes 393224 | tf_op jit(solution)/shard_map/ppermute | solution.py:294
  53.0 3.8 %collective-permute-start.14 = (f32[1,128,256]{2,1,0:T(8,128)S(1)}, f32[1,128,256]{2,1,0:T(8,128)S(1)}, u32[]{:S(2)}, u32[]{:S(2)}) collective-permute-start(f32[1,128,256]{2,1,0:T(8,128)S(1)} %slice.17), channel_id=1, source_target_pairs={{0,2},{2,0},{1,3},{3,1},{4,6},{6,4},{5,7},{7,5},{8,10},{10,8},{9,1... | collective-permute-start | bytes 393224 | tf_op jit(solution)/shard_map/ppermute | solution.py:294
  53.1 6.9 %collective-permute-start.12 = (f32[1,128,256]{2,1,0:T(8,128)S(1)}, f32[1,128,256]{2,1,0:T(8,128)S(1)}, u32[]{:S(2)}, u32[]{:S(2)}) collective-permute-start(f32[1,128,256]{2,1,0:T(8,128)S(1)} %get-tuple-element.78), channel_id=1, source_target_pairs={{0,4},{4,0},{1,5},{5,1},{2,6},{6,2},{3,7},{7,3},{8,12},{12,8},{9,1... | collective-permute-start | bytes 393224 | tf_op jit(solution)/shard_map/ppermute | solution.py:294

commit v9 on v8

--- a/solution.py
+++ b/solution.py
@@ -103,7 +103,7 @@
         ],
         compiler_params=pltpu.CompilerParams(vmem_limit_bytes=32 * 2**20),
         cost_estimate=pl.CostEstimate(
-            flops=2**33 if first else 2**32, bytes_accessed=1024, transcendentals=0
+            flops=2**34 if first else 2**33, bytes_accessed=1024, transcendentals=0
         ),
         name="prompt_attention",
     )(info, *operands)
@@ -128,12 +128,12 @@
 
 
 def pack_rows_kernel(where, own_ref, got_ref, keep, send):
-    steps, part = keep.shape[1], keep.shape[3]
+    _, steps, _, part = keep.shape
     for z in range(steps):
-        for out, y in ((keep, where[1]), (send, 1 - where[1])):
-            columns = pl.ds(pl.multiple_of((2 * z + y) * part, 128), part)
-            out[0, z] = own_ref[:, columns]
-            out[1, z] = got_ref[:, columns]
+        columns = [pl.ds(pl.multiple_of((2 * z + y) * part, 128), part) for y in (where[1], 1 - where[1])]
+        keep[0, z] = own_ref[:, columns[0]]
+        keep[1, z] = got_ref[:, columns[0]]
+        send[z] = own_ref[:, columns[1]]
 
 
 def pack_rows(where, own, got, y, steps):
@@ -141,8 +141,10 @@
     if part % 128:
         halves = jnp.stack([own, got]).reshape(2, ROWS, steps, 2, part)
         halves = jnp.transpose(halves, (3, 0, 2, 1, 4))
-        return [lax.dynamic_index_in_dim(halves, i, axis=0, keepdims=False) for i in (y, 1 - y)]
-    outs = [jax.ShapeDtypeStruct((2, steps, ROWS, part), own.dtype)] * 2
+        keep, send = [lax.dynamic_index_in_dim(halves, i, axis=0, keepdims=False) for i in (y, 1 - y)]
+        return keep, send[0]
+    shapes = [(2, steps, ROWS, part), (steps, ROWS, part)]
+    outs = [jax.ShapeDtypeStruct(shape, own.dtype) for shape in shapes]
     return on_chip(pack_rows_kernel, "pack_rows", outs, where, own, got)
 
 
@@ -155,16 +157,21 @@
     return slice(chunk[0] * HD, (chunk[0] + chunk[1]) * HD)
 
 
-def pack_weight_kernel(where, got_ref, own_ref, whole, *refs):
-    far, sem = refs[:-1], refs[-1]
+def own_half_kernel(where, weight_ref, out):
+    out[...] = weight_ref[:, pl.ds(pl.multiple_of(where[2] * KVH * HD, 128), KVH * HD)]
+
+
+def own_half(where, weight):
+    out = jax.ShapeDtypeStruct((weight.shape[0], KVH * HD), weight.dtype)
+    return on_chip(own_half_kernel, "own_half", [out], where, weight)[0]
+
+
+def pack_weight_kernel(where, own_ref, got_ref, whole, *far):
     rows = got_ref.shape[0]
     core, plane = where[2], where[3]
     half = pl.ds(pl.multiple_of(core * KVH * HD, 128), KVH * HD)
-    own_place = pl.ds(pl.multiple_of(core * rows, 16), rows)
-    copy = pltpu.make_async_copy(own_ref.at[:, half], whole.at[own_place, :], sem)
-    copy.start()
+    whole[pl.ds(pl.multiple_of(core * rows, 16), rows), :] = own_ref[...]
     whole[pl.ds(pl.multiple_of((1 - core) * rows, 16), rows), :] = got_ref[:, half]
-    copy.wait()
     for out, chunk in zip(far, CHUNKS):
         direct = out.shape[0]
         out[...] = whole[pl.ds(pl.multiple_of(plane * (2 * rows - direct), 16), direct), columns_of(chunk)]
@@ -173,20 +180,12 @@
 def pack_weight(where, own, got):
     rows = 2 * own.shape[0]
     shapes = [(rows, KVH * HD)] + [(row_split(rows, i)[1], heads * HD) for i, (_, heads) in enumerate(CHUNKS)]
-    whole, *far = pl.pallas_call(
-        pack_weight_kernel,
-        in_specs=[SMEM, VMEM, pl.BlockSpec(memory_space=pltpu.HBM)],
-        out_specs=[VMEM] * len(shapes),
-        out_shape=[jax.ShapeDtypeStruct(shape, own.dtype) for shape in shapes],
-        scratch_shapes=[pltpu.SemaphoreType.DMA],
-        compiler_params=PARAMS,
-        cost_estimate=HINT,
-        name="pack_weight",
-    )(where, got, own)
+    outs = [jax.ShapeDtypeStruct(shape, own.dtype) for shape in shapes]
+    whole, *far = on_chip(pack_weight_kernel, "pack_weight", outs, where, own, got)
     return whole, far
 
 
-def project_kernel(columns, where, keep, other, own, near, forwarded, *refs):
+def project_kernel(columns, where, keep, other, other_2, own, near, forwarded, *refs):
     direct, mine, theirs, whole = refs[:-3], refs[-3], refs[-2], refs[-1]
     plane = where[3]
     count, extra = direct[0].shape[0], forwarded.shape[1]
@@ -202,7 +201,7 @@
             far[pl.ds(pl.multiple_of((1 - plane) * count, 16), extra), :] = forwarded[j - 2]
             weight = far[...]
         place = where[0] ^ j
-        left = jnp.concatenate([x[core, place] for x in (keep, other) for core in range(2)], axis=0)
+        left = jnp.concatenate([keep[0, place], keep[1, place], other[place], other_2[place]], axis=0)
         product = jnp.dot(left, weight, preferred_element_type=jnp.float32)
         total = product if total is None else total + product
     for i in range(2):
@@ -210,7 +209,7 @@
         theirs[i] = total[(2 + i) * ROWS : (3 + i) * ROWS]
 
 
-def project(where, keep, other, chunk, own, near, direct, forwarded):
+def project(where, rows_of_x, chunk, own, near, direct, forwarded):
     width = chunk[1] * HD
     out = jax.ShapeDtypeStruct((2, ROWS, width), jnp.float32)
     return on_chip(
@@ -218,8 +217,7 @@
         "project",
         [out, out],
         where,
-        keep,
-        other,
+        *rows_of_x,
         own,
         near,
         forwarded,
@@ -228,7 +226,7 @@
     )
 
 
-def final_kernel(chunk, offset, info, gain_ref, q_ref, acc_ref, ml_ref, mine, theirs, there, *refs):
+def final_kernel(chunk, offset, info, gain_ref, q_ref, acc_ref, ml_ref, mine, theirs, there, there_2, *refs):
     result, built, sem = refs[-3:]
     head, heads = chunk
     slot = lax.broadcasted_iota(jnp.int32, (ROWS, PAIR), 0)
@@ -241,7 +239,7 @@
     for k in range(heads):
         part = slice(k * HD, (k + 1) * HD)
         here = mine[0, :, part] + theirs[0, :, part]
-        away = there[0, :, part] if there.shape[0] == 1 else there[0, :, part] + there[1, :, part]
+        away = there[0, :, part] + there_2[0, :, part]
         first_core = jnp.full(here.shape, info[2]) == 0
         raw = jnp.where(first_core, here, away)
         mean = jnp.mean(raw * raw, axis=1, keepdims=True)
@@ -270,7 +268,7 @@
 
 def final_attention(info, gain, query, state, offset, chunk, mine, theirs, there, result):
     heads = chunk[1]
-    operands = [gain, query, *state, mine, theirs, there]
+    operands = [gain, query, *state, mine, theirs, *there]
     specs = [SMEM] + [VMEM] * len(operands)
     aliases = {}
     if result is not None:
@@ -312,7 +310,8 @@
     for _ in range(cycle - 1):
         caches.append(lax.ppermute(caches[-1], "blk", [(i, (i + 1) % cycle) for i in range(cycle)]))
 
-    whole, far = pack_weight(where, kv_weight, got_weight)
+    own, got_weight = tie((own_half(where, kv_weight), got_weight))
+    whole, far = pack_weight(where, own, got_weight)
 
     def send(far):
         return [xor_swap(far, "z", j) for j in range(2, steps)]
@@ -342,29 +341,32 @@
     sent[0], state, far[1] = tie((sent[0], state, far[1]))
     sent.append(send(far[1]))
     sent[0], caches = tie((sent[0], caches))
+    state, other = tie((state, other))
+    rows_of_x = [keep, other, xor_swap(other, "core", 1)]
     forwarded = [forward(0)]
     for stride in range(1, cycle):
         state = prompt_attention(infos[stride], query, caches[stride], state, 0, KVH)
-    sent[1], forwarded[0], state = tie((sent[1], forwarded[0], state))
+    forwarded[0], state = tie((forwarded[0], state))
+
+    def sums(i):
+        return project(where, rows_of_x, CHUNKS[i], whole, near, sent[i], forwarded[i])
+
+    def owners(mine, theirs):
+        there = [xor_swap(theirs[1:], ("y", "core"), 3), xor_swap(mine[1:], "core", 1)]
+        return xor_swap(theirs[:1], "y", 1), there
+
+    mine_0, theirs_0 = sums(0)
+    sent[1], mine_0 = tie((sent[1], mine_0))
     forwarded.append(forward(1))
-
-    def sums(i):
-        return project(where, keep, other, CHUNKS[i], whole, near, sent[i], forwarded[i])
-
+    here_0, there_0 = owners(mine_0, theirs_0)
+    forwarded[1], mine_0 = tie((forwarded[1], mine_0))
+    mine_1, theirs_1 = sums(1)
+    here_0, there_0, mine_1, theirs_1 = tie((here_0, there_0, mine_1, theirs_1))
+    here_1, there_1 = owners(mine_1, theirs_1)
     info = jnp.concatenate([resp_lengths[0], core[None]]).astype(jnp.int32)
     gain = key_gain[None]
-    mine_0, theirs_0 = sums(0)
-    theirs_0 = xor_swap(theirs_0, "y", 1)
-    forwarded[1], mine_0 = tie((forwarded[1], mine_0))
-    mine_1, theirs_1 = sums(1)
-    theirs_0, theirs_1, mine_1 = tie((theirs_0, theirs_1, mine_1))
-    there_0 = xor_swap(mine_0[1:] + theirs_0[1:], "core", 1)
-    there_1 = [xor_swap(theirs_1[1:], ("y", "core"), 3), xor_swap(mine_1[1:], "core", 1)]
-    theirs_1 = xor_swap(theirs_1[:1], "y", 1)
-    result = final_attention(info, gain, query, state, 0, CHUNKS[0], mine_0, theirs_0, there_0, None)
-    result = final_attention(
-        info, gain, query, state, 2, CHUNKS[1], mine_1, theirs_1, jnp.concatenate(there_1), result
-    )
+    result = final_attention(info, gain, query, state, 0, CHUNKS[0], mine_0, here_0, there_0, None)
+    result = final_attention(info, gain, query, state, 2, CHUNKS[1], mine_1, here_1, there_1, result)
     return result[None]
 
 

time: 62.6 us -> 61.9 us (0.989)
  starting transfers between devices: 23.9 us -> 22.5 us
  Pallas kernels: 20.8 us -> 21.9 us
    pallas_call x3 -> x5, Pallas kernels: 3.76 us -> 5.44 us  [on_chip(): pl.pallas_call(kernel, in_specs=[SMEM] + [VMEM] * len(operands), out_spec...]
    ppermute x15 -> x17, starting transfers between devices: 21 us -> 19.5 us  [xor_swap(): lax.ppermute(array, axis, [(i, i ^ by) for i in range(lax.axis_size(axis))])]
    ppermute x15 -> x17, waiting for transfers between devices: 15.2 us -> 14.8 us  [xor_swap(): lax.ppermute(array, axis, [(i, i ^ by) for i in range(lax.axis_size(axis))])]
  transfers between devices with their start and end apart: 16 -> 18, of which waited for: 8 -> 7; matrix products, arithmetic and copies ran while one was open for 1% -> 1% of each run, Pallas kernels for 30% -> 32%
where the time goes in v9:
time: 61.9 us; the launch traced here: 61.6 us
  starting transfers between devices  22.5 us (36%)
  Pallas kernels  21.9 us (35%)
  waiting for transfers between devices  14.8 us (24%)
  local copies, waits for them, and re-layouts  1.38 us (2%)
  between operations  0.87 us (1%)
    ppermute x17, starting transfers between devices, xor_swap(): lax.ppermute(array, axis, [(i, i ^ by) for i in range(lax.axis_size(axis))])  19.5 us
    ppermute x17, waiting for transfers between devices, xor_swap(): lax.ppermute(array, axis, [(i, i ^ by) for i in range(lax.axis_size(axis))])  14.8 us
    pallas_call x2, Pallas kernels, prompt_attention(): pl.pallas_call(functools.partial(prompt_kernel, first), grid_spec=pltpu.P...  11.7 us
    pallas_call x5, Pallas kernels, on_chip(): pl.pallas_call(kernel, in_specs=[SMEM] + [VMEM] * len(operands), out_spec...  5.44 us
    pallas_call x2, Pallas kernels, final_attention(): pl.pallas_call(functools.partial(final_kernel, chunk, offset), in_specs=s...  4.68 us
    ppermute x1, starting transfers between devices, per_device(): lax.ppermute(caches[-1], 'blk', [(i, (i + 1) % cycle) for i in range(cycl...  2.93 us
  transfers between devices with their start and end apart: 18, of which 7 were waited for; matrix products, arithmetic and copies ran while one was open for 1% of the time, Pallas kernels for 32%

profile of v9, /device:TPU:0, one launch (start us, length us, event | category | flops | bytes accessed | tf_op | source)
XLA Modules:
  0.0 61.6 jit_solution(15607574323003712417)
XLA Ops:
  0.6 2.9 %collective-permute-start.4 = (bf16[512,1024]{1,0:T(8,128)(2,1)}, bf16[512,1024]{1,0:T(8,128)(2,1)}, u32[]{:S(2)}, u32[]{:S(2)}) collective-permute-start(bf16[512,1024]{1,0:T(8,128)(2,1)} %bitcast.28), channel_id=1, source_target_pairs={{0,1},{1,0},{2,3},{3,2},{4,5},{5,4},{6,7},{7,6},{8,9},{9,8},{10,11... | collective-permute-start | bytes 3145736 | tf_op jit(solution)/shard_map/ppermute | solution.py:311
  3.5 1.1 %copy-done.2 = bf16[320,1024]{1,0:T(8,128)(2,1)S(1)} copy-done((bf16[320,1024]{1,0:T(8,128)(2,1)S(1)}, bf16[320,1024]{1,0:T(8,128)(2,1)}, u32[]{:S(2)}) %copy-start.2) | copy-done | bytes 655384
  5.9 1.2 %pack_weight.1 = (bf16[640,512]{1,0:T(8,128)(2,1)S(1)}, bf16[320,256]{1,0:T(8,128)(2,1)S(1)}, bf16[320,256]{1,0:T(8,128)(2,1)S(1)}) custom-call(s32[4]{0:T(128)S(1)} %pad_add_fusion.1.where, bf16[320,512]{1,0:T(8,128)(2,1)S(1)} %own_half.1.own_ref, bf16[320,1024]{1,0:T(8,128)(2,1)} %collective-permute-done.1.got_ref), custom_call_target="tpu_custom_call" | custom-call | flops 1024 | bytes 1024 | tf_op jit(solution)/shard_map/pack_weight/pallas_call | solution.py:118
  7.1 2.7 %collective-permute-start.2 = (bf16[320,256]{1,0:T(8,128)(2,1)S(1)}, bf16[320,256]{1,0:T(8,128)(2,1)S(1)}, u32[]{:S(2)}, u32[]{:S(2)}) collective-permute-start(bf16[320,256]{1,0:T(8,128)(2,1)S(1)} %get-tuple-element.55), channel_id=1, source_target_pairs={{0,16},{8,24},{16,0},{24,8},{1,17},{9,25},{17,1},{25,9},{2,18},{10... | collective-permute-start | bytes 491528 | tf_op jit(solution)/shard_map/ppermute | solution.py:292
  9.7 1.3 %collective-permute-start.3 = (bf16[320,256]{1,0:T(8,128)(2,1)S(1)}, bf16[320,256]{1,0:T(8,128)(2,1)S(1)}, u32[]{:S(2)}, u32[]{:S(2)}) collective-permute-start(bf16[320,256]{1,0:T(8,128)(2,1)S(1)} %get-tuple-element.55), channel_id=1, source_target_pairs={{0,24},{8,16},{16,8},{24,0},{1,25},{9,17},{17,9},{25,1},{2,26},{10... | collective-permute-start | bytes 491528 | tf_op jit(solution)/shard_map/ppermute | solution.py:292
  12.1 1.6 %collective-permute-start.6 = (bf16[4,128,640]{2,1,0:T(8,128)(2,1)S(1)}, bf16[4,128,640]{2,1,0:T(8,128)(2,1)S(1)}, u32[]{:S(2)}, u32[]{:S(2)}) collective-permute-start(bf16[4,128,640]{2,1,0:T(8,128)(2,1)S(1)} %get-tuple-element.53), channel_id=1, source_target_pairs={{0,4},{4,0},{1,5},{5,1},{2,6},{6,2},{3,7},{7,3},{8,12},{12,8},{9,1... | collective-permute-start | bytes 1966088 | tf_op jit(solution)/shard_map/ppermute | solution.py:292
  14.0 5.4 %prompt_attention.2 = (f32[128,4096]{1,0:T(8,128)S(1)}, f32[8,4096]{1,0:T(8,128)S(1)}) custom-call(s32[4]{0:T(128)S(1)} %get-tuple-element.97.info, bf16[128,4096]{1,0:T(8,128)(2,1)S(1)} %bitcast.16, bf16[512,1024]{1,0:T(8,128)(2,1)S(1)} %bitcast.29, bf16[512,1024]{1,0:T(8,128)(2,1)S(1)} %bitcast.30), custom_call_target="tpu_custom_call" | custom-call | flops 17179869184 | bytes 1024 | tf_op jit(solution)/shard_map/prompt_attention/pallas_call | solution.py:95
  19.4 2.7 %collective-permute-done.2.refs_0_ = bf16[320,256]{1,0:T(8,128)(2,1)S(1)} collective-permute-done((bf16[320,256]{1,0:T(8,128)(2,1)S(1)}, bf16[320,256]{1,0:T(8,128)(2,1)S(1)}, u32[]{:S(2)}, u32[]{:S(2)}) %collective-permute-start.2) | collective-permute-done | bytes 163872 | tf_op jit(solution)/shard_map/ppermute | solution.py:292
  22.2 5.0 %collective-permute-start.11 = (bf16[320,256]{1,0:T(8,128)(2,1)S(1)}, bf16[320,256]{1,0:T(8,128)(2,1)S(1)}, u32[]{:S(2)}, u32[]{:S(2)}) collective-permute-start(bf16[320,256]{1,0:T(8,128)(2,1)S(1)} %get-tuple-element.77), channel_id=1, source_target_pairs={{0,16},{8,24},{16,0},{24,8},{1,17},{9,25},{17,1},{25,9},{2,18},{10... | collective-permute-start | bytes 491528 | tf_op jit(solution)/shard_map/ppermute | solution.py:292
  27.7 1.6 %collective-permute-start.5 = (bf16[2,320,256]{2,1,0:T(8,128)(2,1)S(1)}, bf16[2,320,256]{2,1,0:T(8,128)(2,1)S(1)}, u32[]{:S(2)}, u32[]{:S(2)}) collective-permute-start(bf16[2,320,256]{2,1,0:T(8,128)(2,1)S(1)} %pad_maximum_fusion), channel_id=1, source_target_pairs={{0,1},{1,0},{2,3},{3,2},{4,5},{5,4},{6,7},{7,6},{8,9},{9,8},{10,11... | collective-permute-start | bytes 983048 | tf_op jit(solution)/shard_map/ppermute | solution.py:292
  29.2 6.3 %prompt_attention.3 = (f32[128,4096]{1,0:T(8,128)S(1)}, f32[8,4096]{1,0:T(8,128)S(1)}) custom-call(s32[4]{0:T(128)S(1)} %get-tuple-element.98.info, bf16[128,4096]{1,0:T(8,128)(2,1)S(1)} %bitcast.17, bf16[512,1024]{1,0:T(8,128)(2,1)} %collective-permute-done.4.k_ref.v_ref, bf16[512,1024]{1,0:T(8,128)(2,1)} %collective-permute-done.4.k_ref.v_ref, ...), custom_call_target="tpu_custom_call" | custom-call | flops 8589934592 | bytes 1024 | tf_op jit(solution)/shard_map/prompt_attention/pallas_call | solution.py:95
  35.5 1.3 %collective-permute-done.5.forwarded = bf16[2,320,256]{2,1,0:T(8,128)(2,1)S(1)} collective-permute-done((bf16[2,320,256]{2,1,0:T(8,128)(2,1)S(1)}, bf16[2,320,256]{2,1,0:T(8,128)(2,1)S(1)}, u32[]{:S(2)}, u32[]{:S(2)}) %collective-permute-start.5) | collective-permute-done | bytes 327712 | tf_op jit(solution)/shard_map/ppermute | solution.py:292
  36.8 3.1 %collective-permute-done.8.near = bf16[640,512]{1,0:T(8,128)(2,1)S(1)} collective-permute-done((bf16[640,512]{1,0:T(8,128)(2,1)S(1)}, bf16[640,512]{1,0:T(8,128)(2,1)S(1)}, u32[]{:S(2)}, u32[]{:S(2)}) %collective-permute-start.8) | collective-permute-done | bytes 655392 | tf_op jit(solution)/shard_map/ppermute | solution.py:292
  39.9 1.5 %project.2 = (f32[2,128,256]{2,1,0:T(8,128)S(1)}, f32[2,128,256]{2,1,0:T(8,128)S(1)}) custom-call(s32[4]{0:T(128)S(1)} %pad_add_fusion.1.where, bf16[2,4,128,640]{3,2,1,0:T(8,128)(2,1)S(1)} %get-tuple-element.73.keep, bf16[4,128,640]{2,1,0:T(8,128)(2,1)S(1)} %collective-permute-done.6.other, bf16[4,128,640]{2,1,0:T(8,128)(2,1)S(1)} %collective-permute-done.7.other_2, ...), custom_call_target="tpu_custom_call" | custom-call | flops 1024 | bytes 1024 | tf_op jit(solution)/shard_map/project/pallas_call | solution.py:118
  41.5 1.6 %collective-permute-start.14 = (bf16[2,320,256]{2,1,0:T(8,128)(2,1)S(1)}, bf16[2,320,256]{2,1,0:T(8,128)(2,1)S(1)}, u32[]{:S(2)}, u32[]{:S(2)}) collective-permute-start(bf16[2,320,256]{2,1,0:T(8,128)(2,1)S(1)} %pad_maximum_fusion.1), channel_id=1, source_target_pairs={{0,1},{1,0},{2,3},{3,2},{4,5},{5,4},{6,7},{7,6},{8,9},{9,8},{10,11... | collective-permute-start | bytes 983048 | tf_op jit(solution)/shard_map/ppermute | solution.py:292
  43.2 1.7 %collective-permute-start.10 = (f32[1,128,256]{2,1,0:T(8,128)S(1)}, f32[1,128,256]{2,1,0:T(8,128)S(1)}, u32[]{:S(2)}, u32[]{:S(2)}) collective-permute-start(f32[1,128,256]{2,1,0:T(8,128)S(1)} %get-tuple-element.95), channel_id=1, source_target_pairs={{0,6},{2,4},{4,2},{6,0},{1,7},{3,5},{5,3},{7,1},{8,14},{10,12},{12... | collective-permute-start | bytes 393224 | tf_op jit(solution)/shard_map/ppermute | solution.py:292
  45.4 3.3 %collective-permute-done.14.forwarded = bf16[2,320,256]{2,1,0:T(8,128)(2,1)S(1)} collective-permute-done((bf16[2,320,256]{2,1,0:T(8,128)(2,1)S(1)}, bf16[2,320,256]{2,1,0:T(8,128)(2,1)S(1)}, u32[]{:S(2)}, u32[]{:S(2)}) %collective-permute-start.14) | collective-permute-done | bytes 327712 | tf_op jit(solution)/shard_map/ppermute | solution.py:292
  48.7 1.5 %project.3 = (f32[2,128,256]{2,1,0:T(8,128)S(1)}, f32[2,128,256]{2,1,0:T(8,128)S(1)}) custom-call(s32[4]{0:T(128)S(1)} %pad_add_fusion.1.where, bf16[2,4,128,640]{3,2,1,0:T(8,128)(2,1)S(1)} %get-tuple-element.73.keep, bf16[4,128,640]{2,1,0:T(8,128)(2,1)S(1)} %collective-permute-done.6.other, bf16[4,128,640]{2,1,0:T(8,128)(2,1)S(1)} %collective-permute-done.7.other_2, ...), custom_call_target="tpu_custom_call" | custom-call | flops 1024 | bytes 1024 | tf_op jit(solution)/shard_map/project/pallas_call | solution.py:118
  50.3 1.6 %collective-permute-done.9.theirs = f32[1,128,256]{2,1,0:T(8,128)S(1)} collective-permute-done((f32[1,128,256]{2,1,0:T(8,128)S(1)}, f32[1,128,256]{2,1,0:T(8,128)S(1)}, u32[]{:S(2)}, u32[]{:S(2)}) %collective-permute-start.9) | collective-permute-done | bytes 131104 | tf_op jit(solution)/shard_map/ppermute | solution.py:292
  51.9 1.6 %collective-permute-start.15 = (f32[1,128,256]{2,1,0:T(8,128)S(1)}, f32[1,128,256]{2,1,0:T(8,128)S(1)}, u32[]{:S(2)}, u32[]{:S(2)}) collective-permute-start(f32[1,128,256]{2,1,0:T(8,128)S(1)} %get-tuple-element.94), channel_id=1, source_target_pairs={{0,4},{4,0},{1,5},{5,1},{2,6},{6,2},{3,7},{7,3},{8,12},{12,8},{9,1... | collective-permute-start | bytes 393224 | tf_op jit(solution)/shard_map/ppermute | solution.py:292
  54.3 2.3 %final_attention.2.refs_0_ = bf16[128,4096]{1,0:T(8,128)(2,1)} custom-call(s32[3]{0:T(128)S(1)} %pad_add_fusion.info, f32[1,128]{1,0:T(1,128)S(1)} %bitcast.26, bf16[128,4096]{1,0:T(8,128)(2,1)S(1)} %bitcast.18, f32[128,4096]{1,0:T(8,128)S(1)} %get-tuple-element.71.acc_ref, f32[8,4096]{1,0:T(8,128)S(1)} %get-tuple-element.72.ml_ref, ...), custom_call_target="tpu_custom_call" | custom-call | flops 1024 | bytes 1024 | tf_op jit(solution)/shard_map/final_attention/pallas_call | solution.py:278
  56.6 0.8 %collective-permute-done.15.theirs = f32[1,128,256]{2,1,0:T(8,128)S(1)} collective-permute-done((f32[1,128,256]{2,1,0:T(8,128)S(1)}, f32[1,128,256]{2,1,0:T(8,128)S(1)}, u32[]{:S(2)}, u32[]{:S(2)}) %collective-permute-start.15) | collective-permute-done | bytes 131104 | tf_op jit(solution)/shard_map/ppermute | solution.py:292
  57.4 1.9 %collective-permute-done.16.there = f32[1,128,256]{2,1,0:T(8,128)S(1)} collective-permute-done((f32[1,128,256]{2,1,0:T(8,128)S(1)}, f32[1,128,256]{2,1,0:T(8,128)S(1)}, u32[]{:S(2)}, u32[]{:S(2)}) %collective-permute-start.16) | collective-permute-done | bytes 131104 | tf_op jit(solution)/shard_map/ppermute | solution.py:292
  59.3 2.3 %final_attention.3 = bf16[128,4096]{1,0:T(8,128)(2,1)} custom-call(s32[3]{0:T(128)S(1)} %pad_add_fusion.info, f32[1,128]{1,0:T(1,128)S(1)} %bitcast.27, bf16[128,4096]{1,0:T(8,128)(2,1)S(1)} %bitcast.19, f32[128,4096]{1,0:T(8,128)S(1)} %get-tuple-element.71.acc_ref, f32[8,4096]{1,0:T(8,128)S(1)} %get-tuple-element.72.ml_ref, ...), custom_call_target="tpu_custom_call", output_to_operand_aliasing={{}: (9, {})} | custom-call | flops 1024 | bytes 1024 | tf_op jit(solution)/shard_map/final_attention/pallas_call | solution.py:278
  (45 shorter events, 4.4 us)
Async XLA Ops:
  0.0 11.4 %copy-start.1 = (bf16[1,128,5120]{2,1,0:T(8,128)(2,1)S(1)}, bf16[1,128,5120]{2,1,0:T(8,128)(2,1)}, u32[]{:S(2)}) copy-start(bf16[1,128,5120]{2,1,0:T(8,128)(2,1)} %param.8) | copy-start | bytes 3932164
  0.0 11.4 %collective-permute-start = (bf16[128,5120]{1,0:T(8,128)(2,1)}, bf16[128,5120]{1,0:T(8,128)(2,1)S(1)}, u32[]{:S(2)}, u32[]{:S(2)}) collective-permute-start(bf16[128,5120]{1,0:T(8,128)(2,1)} %bitcast.20), channel_id=1, source_target_pairs={{0,2},{2,0},{1,3},{3,1},{4,6},{6,4},{5,7},{7,5},{8,10},{10,8},{9,1... | collective-permute-start | bytes 3932168 | tf_op jit(solution)/shard_map/ppermute | solution.py:292
  0.5 5.4 %collective-permute-start.1 = (bf16[320,1024]{1,0:T(8,128)(2,1)}, bf16[320,1024]{1,0:T(8,128)(2,1)}, u32[]{:S(2)}, u32[]{:S(2)}) collective-permute-start(bf16[320,1024]{1,0:T(8,128)(2,1)} %weight_ref.1), channel_id=1, source_target_pairs={{0,2},{2,0},{1,3},{3,1},{4,6},{6,4},{5,7},{7,5},{8,10},{10,8},{9,1... | collective-permute-start | bytes 1966088 | tf_op jit(solution)/shard_map/ppermute | solution.py:292
  0.6 27.0 %collective-permute-start.4 = (bf16[512,1024]{1,0:T(8,128)(2,1)}, bf16[512,1024]{1,0:T(8,128)(2,1)}, u32[]{:S(2)}, u32[]{:S(2)}) collective-permute-start(bf16[512,1024]{1,0:T(8,128)(2,1)} %bitcast.28), channel_id=1, source_target_pairs={{0,1},{1,0},{2,3},{3,2},{4,5},{5,4},{6,7},{7,6},{8,9},{9,8},{10,11... | collective-permute-start | bytes 3145736 | tf_op jit(solution)/shard_map/ppermute | solution.py:311
  7.1 15.1 %collective-permute-start.2 = (bf16[320,256]{1,0:T(8,128)(2,1)S(1)}, bf16[320,256]{1,0:T(8,128)(2,1)S(1)}, u32[]{:S(2)}, u32[]{:S(2)}) collective-permute-start(bf16[320,256]{1,0:T(8,128)(2,1)S(1)} %get-tuple-element.55), channel_id=1, source_target_pairs={{0,16},{8,24},{16,0},{24,8},{1,17},{9,25},{17,1},{25,9},{2,18},{10... | collective-permute-start | bytes 491528 | tf_op jit(solution)/shard_map/ppermute | solution.py:292
  9.7 12.5 %collective-permute-start.3 = (bf16[320,256]{1,0:T(8,128)(2,1)S(1)}, bf16[320,256]{1,0:T(8,128)(2,1)S(1)}, u32[]{:S(2)}, u32[]{:S(2)}) collective-permute-start(bf16[320,256]{1,0:T(8,128)(2,1)S(1)} %get-tuple-element.55), channel_id=1, source_target_pairs={{0,24},{8,16},{16,8},{24,0},{1,25},{9,17},{17,9},{25,1},{2,26},{10... | collective-permute-start | bytes 491528 | tf_op jit(solution)/shard_map/ppermute | solution.py:292
  11.1 2.6 %copy-start.5 = (s32[1,2,2]{2,1,0:T(2,128)S(1)}, s32[1,2,2]{2,1,0:T(2,128)}, u32[]{:S(2)}) copy-start(s32[1,2,2]{2,1,0:T(2,128)} %param.14) | copy-start | bytes 52
  11.1 2.9 %copy-start = (bf16[1,128,4096]{2,1,0:T(8,128)(2,1)S(1)}, bf16[1,128,4096]{2,1,0:T(8,128)(2,1)}, u32[]{:S(2)}) copy-start(bf16[1,128,4096]{2,1,0:T(8,128)(2,1)} %param.9) | copy-start | bytes 3145732
  11.1 2.9 %copy-start.4 = (bf16[1,512,1024]{2,1,0:T(8,128)(2,1)S(1)}, bf16[1,512,1024]{2,1,0:T(8,128)(2,1)}, u32[]{:S(2)}) copy-start(bf16[1,512,1024]{2,1,0:T(8,128)(2,1)} %param.10) | copy-start | bytes 3145732
  11.1 28.8 %collective-permute-start.8 = (bf16[640,512]{1,0:T(8,128)(2,1)S(1)}, bf16[640,512]{1,0:T(8,128)(2,1)S(1)}, u32[]{:S(2)}, u32[]{:S(2)}) collective-permute-start(bf16[640,512]{1,0:T(8,128)(2,1)S(1)} %get-tuple-element.51.own), channel_id=1, source_target_pairs={{0,8},{8,0},{16,24},{24,16},{1,9},{9,1},{17,25},{25,17},{2,10},{10... | collective-permute-start | bytes 1966088 | tf_op jit(solution)/shard_map/ppermute | solution.py:292
  12.1 17.1 %collective-permute-start.6 = (bf16[4,128,640]{2,1,0:T(8,128)(2,1)S(1)}, bf16[4,128,640]{2,1,0:T(8,128)(2,1)S(1)}, u32[]{:S(2)}, u32[]{:S(2)}) collective-permute-start(bf16[4,128,640]{2,1,0:T(8,128)(2,1)S(1)} %get-tuple-element.53), channel_id=1, source_target_pairs={{0,4},{4,0},{1,5},{5,1},{2,6},{6,2},{3,7},{7,3},{8,12},{12,8},{9,1... | collective-permute-start | bytes 1966088 | tf_op jit(solution)/shard_map/ppermute | solution.py:292
  22.2 19.3 %collective-permute-start.11 = (bf16[320,256]{1,0:T(8,128)(2,1)S(1)}, bf16[320,256]{1,0:T(8,128)(2,1)S(1)}, u32[]{:S(2)}, u32[]{:S(2)}) collective-permute-start(bf16[320,256]{1,0:T(8,128)(2,1)S(1)} %get-tuple-element.77), channel_id=1, source_target_pairs={{0,16},{8,24},{16,0},{24,8},{1,17},{9,25},{17,1},{25,9},{2,18},{10... | collective-permute-start | bytes 491528 | tf_op jit(solution)/shard_map/ppermute | solution.py:292
  27.2 14.3 %collective-permute-start.12 = (bf16[320,256]{1,0:T(8,128)(2,1)S(1)}, bf16[320,256]{1,0:T(8,128)(2,1)S(1)}, u32[]{:S(2)}, u32[]{:S(2)}) collective-permute-start(bf16[320,256]{1,0:T(8,128)(2,1)S(1)} %get-tuple-element.77), channel_id=1, source_target_pairs={{0,24},{8,16},{16,8},{24,0},{1,25},{9,17},{17,9},{25,1},{2,26},{10... | collective-permute-start | bytes 491528 | tf_op jit(solution)/shard_map/ppermute | solution.py:292
  27.7 9.1 %collective-permute-start.5 = (bf16[2,320,256]{2,1,0:T(8,128)(2,1)S(1)}, bf16[2,320,256]{2,1,0:T(8,128)(2,1)S(1)}, u32[]{:S(2)}, u32[]{:S(2)}) collective-permute-start(bf16[2,320,256]{2,1,0:T(8,128)(2,1)S(1)} %pad_maximum_fusion), channel_id=1, source_target_pairs={{0,1},{1,0},{2,3},{3,2},{4,5},{5,4},{6,7},{7,6},{8,9},{9,8},{10,11... | collective-permute-start | bytes 983048 | tf_op jit(solution)/shard_map/ppermute | solution.py:292
  29.2 10.7 %collective-permute-start.7 = (bf16[4,128,640]{2,1,0:T(8,128)(2,1)S(1)}, bf16[4,128,640]{2,1,0:T(8,128)(2,1)S(1)}, u32[]{:S(2)}, u32[]{:S(2)}) collective-permute-start(bf16[4,128,640]{2,1,0:T(8,128)(2,1)S(1)} %collective-permute-done.6.other), channel_id=1, source_target_pairs={{0,2},{2,0},{1,3},{3,1},{4,6},{6,4},{5,7},{7,5},{8,10},{10,8},{9,1... | collective-permute-start | bytes 1966088 | tf_op jit(solution)/shard_map/ppermute | solution.py:292
  41.5 7.2 %collective-permute-start.14 = (bf16[2,320,256]{2,1,0:T(8,128)(2,1)S(1)}, bf16[2,320,256]{2,1,0:T(8,128)(2,1)S(1)}, u32[]{:S(2)}, u32[]{:S(2)}) collective-permute-start(bf16[2,320,256]{2,1,0:T(8,128)(2,1)S(1)} %pad_maximum_fusion.1), channel_id=1, source_target_pairs={{0,1},{1,0},{2,3},{3,2},{4,5},{5,4},{6,7},{7,6},{8,9},{9,8},{10,11... | collective-permute-start | bytes 983048 | tf_op jit(solution)/shard_map/ppermute | solution.py:292
  43.1 7.1 %collective-permute-start.13 = (f32[1,128,256]{2,1,0:T(8,128)S(1)}, f32[1,128,256]{2,1,0:T(8,128)S(1)}, u32[]{:S(2)}, u32[]{:S(2)}) collective-permute-start(f32[1,128,256]{2,1,0:T(8,128)S(1)} %slice.20), channel_id=1, source_target_pairs={{0,2},{2,0},{1,3},{3,1},{4,6},{6,4},{5,7},{7,5},{8,10},{10,8},{9,1... | collective-permute-start | bytes 393224 | tf_op jit(solution)/shard_map/ppermute | solution.py:292
  43.2 7.0 %collective-permute-start.10 = (f32[1,128,256]{2,1,0:T(8,128)S(1)}, f32[1,128,256]{2,1,0:T(8,128)S(1)}, u32[]{:S(2)}, u32[]{:S(2)}) collective-permute-start(f32[1,128,256]{2,1,0:T(8,128)S(1)} %get-tuple-element.95), channel_id=1, source_target_pairs={{0,6},{2,4},{4,2},{6,0},{1,7},{3,5},{5,3},{7,1},{8,14},{10,12},{12... | collective-permute-start | bytes 393224 | tf_op jit(solution)/shard_map/ppermute | solution.py:292
  44.9 9.3 %copy-start.6 = (s32[1,2]{1,0:T(1,128)S(1)}, s32[1,2]{1,0:T(1,128)}, u32[]{:S(2)}) copy-start(s32[1,2]{1,0:T(1,128)} %param.15) | copy-start | bytes 28
  44.9 9.4 %copy-start.3 = (f32[128]{0:T(128)S(1)}, f32[128]{0:T(128)}, u32[]{:S(2)}) copy-start(f32[128]{0:T(128)} %param.12) | copy-start | bytes 1540
  44.9 7.0 %collective-permute-start.9 = (f32[1,128,256]{2,1,0:T(8,128)S(1)}, f32[1,128,256]{2,1,0:T(8,128)S(1)}, u32[]{:S(2)}, u32[]{:S(2)}) collective-permute-start(f32[1,128,256]{2,1,0:T(8,128)S(1)} %get-tuple-element.96), channel_id=1, source_target_pairs={{0,4},{4,0},{1,5},{5,1},{2,6},{6,2},{3,7},{7,3},{8,12},{12,8},{9,1... | collective-permute-start | bytes 393224 | tf_op jit(solution)/shard_map/ppermute | solution.py:292
  51.9 5.5 %collective-permute-start.15 = (f32[1,128,256]{2,1,0:T(8,128)S(1)}, f32[1,128,256]{2,1,0:T(8,128)S(1)}, u32[]{:S(2)}, u32[]{:S(2)}) collective-permute-start(f32[1,128,256]{2,1,0:T(8,128)S(1)} %get-tuple-element.94), channel_id=1, source_target_pairs={{0,4},{4,0},{1,5},{5,1},{2,6},{6,2},{3,7},{7,3},{8,12},{12,8},{9,1... | collective-permute-start | bytes 393224 | tf_op jit(solution)/shard_map/ppermute | solution.py:292
  53.5 5.8 %collective-permute-start.16 = (f32[1,128,256]{2,1,0:T(8,128)S(1)}, f32[1,128,256]{2,1,0:T(8,128)S(1)}, u32[]{:S(2)}, u32[]{:S(2)}) collective-permute-start(f32[1,128,256]{2,1,0:T(8,128)S(1)} %get-tuple-element.93), channel_id=1, source_target_pairs={{0,6},{2,4},{4,2},{6,0},{1,7},{3,5},{5,3},{7,1},{8,14},{10,12},{12... | collective-permute-start | bytes 393224 | tf_op jit(solution)/shard_map/ppermute | solution.py:292
  53.5 5.8 %collective-permute-start.17 = (f32[1,128,256]{2,1,0:T(8,128)S(1)}, f32[1,128,256]{2,1,0:T(8,128)S(1)}, u32[]{:S(2)}, u32[]{:S(2)}) collective-permute-start(f32[1,128,256]{2,1,0:T(8,128)S(1)} %slice.23), channel_id=1, source_target_pairs={{0,2},{2,0},{1,3},{3,1},{4,6},{6,4},{5,7},{7,5},{8,10},{10,8},{9,1... | collective-permute-start | bytes 393224 | tf_op jit(solution)/shard_map/ppermute | solution.py:292
  (1 other events, 1.1 us)

commit v10 on v9

--- a/solution.py
+++ b/solution.py
@@ -153,53 +153,66 @@
     return helped, rows - helped
 
 
-def columns_of(chunk):
-    return slice(chunk[0] * HD, (chunk[0] + chunk[1]) * HD)
-
-
-def own_half_kernel(where, weight_ref, out):
-    out[...] = weight_ref[:, pl.ds(pl.multiple_of(where[2] * KVH * HD, 128), KVH * HD)]
-
-
-def own_half(where, weight):
-    out = jax.ShapeDtypeStruct((weight.shape[0], KVH * HD), weight.dtype)
-    return on_chip(own_half_kernel, "own_half", [out], where, weight)[0]
-
-
-def pack_weight_kernel(where, own_ref, got_ref, whole, *far):
+def own_rows_kernel(where, weight_ref, *outs):
+    rows = weight_ref.shape[0]
+    for out, (head, heads) in zip(outs, CHUNKS):
+        columns = pl.ds(pl.multiple_of((where[2] * KVH + head) * HD, 128), heads * HD)
+        out[pl.ds(pl.multiple_of(where[2] * rows, 16), rows), :] = weight_ref[:, columns]
+
+
+def own_rows(where, weight):
+    outs = [jax.ShapeDtypeStruct((2 * weight.shape[0], heads * HD), weight.dtype) for _, heads in CHUNKS]
+    return on_chip(own_rows_kernel, "own_rows", outs, where, weight)
+
+
+def pack_weight_kernel(where, got_ref, *refs):
+    count = len(CHUNKS)
+    wholes, fars = refs[count : 2 * count], refs[2 * count :]
     rows = got_ref.shape[0]
     core, plane = where[2], where[3]
-    half = pl.ds(pl.multiple_of(core * KVH * HD, 128), KVH * HD)
-    whole[pl.ds(pl.multiple_of(core * rows, 16), rows), :] = own_ref[...]
-    whole[pl.ds(pl.multiple_of((1 - core) * rows, 16), rows), :] = got_ref[:, half]
-    for out, chunk in zip(far, CHUNKS):
-        direct = out.shape[0]
-        out[...] = whole[pl.ds(pl.multiple_of(plane * (2 * rows - direct), 16), direct), columns_of(chunk)]
-
-
-def pack_weight(where, own, got):
-    rows = 2 * own.shape[0]
-    shapes = [(rows, KVH * HD)] + [(row_split(rows, i)[1], heads * HD) for i, (_, heads) in enumerate(CHUNKS)]
-    outs = [jax.ShapeDtypeStruct(shape, own.dtype) for shape in shapes]
-    whole, *far = on_chip(pack_weight_kernel, "pack_weight", outs, where, own, got)
-    return whole, far
-
-
-def project_kernel(columns, where, keep, other, other_2, own, near, forwarded, *refs):
-    direct, mine, theirs, whole = refs[:-3], refs[-3], refs[-2], refs[-1]
+    for whole, far, (head, heads) in zip(wholes, fars, CHUNKS):
+        columns = pl.ds(pl.multiple_of((core * KVH + head) * HD, 128), heads * HD)
+        whole[pl.ds(pl.multiple_of((1 - core) * rows, 16), rows), :] = got_ref[:, columns]
+        direct = far.shape[0]
+        far[...] = whole[pl.ds(pl.multiple_of(plane * (2 * rows - direct), 16), direct), :]
+
+
+def pack_weight(where, got, wholes):
+    count = len(CHUNKS)
+    outs = [jax.ShapeDtypeStruct(whole.shape, whole.dtype) for whole in wholes]
+    for i, whole in enumerate(wholes):
+        outs.append(jax.ShapeDtypeStruct((row_split(whole.shape[0], i)[1], whole.shape[1]), whole.dtype))
+    outs = pl.pallas_call(
+        pack_weight_kernel,
+        in_specs=[SMEM] + [VMEM] * (1 + count),
+        out_specs=[VMEM] * len(outs),
+        out_shape=outs,
+        input_output_aliases={2 + i: i for i in range(count)},
+        compiler_params=PARAMS,
+        cost_estimate=HINT,
+        name="pack_weight",
+    )(where, got, *wholes)
+    return list(outs[:count]), list(outs[count:])
+
+
+def project_kernel(where, keep, other, other_2, own, near, *refs):
+    mine, theirs, whole = refs[-3:]
+    far = whole.shape[0]
+    direct, forwarded = refs[:far], refs[far:-3]
     plane = where[3]
-    count, extra = direct[0].shape[0], forwarded.shape[1]
+    count, extra = direct[0].shape[0], whole.shape[1] - direct[0].shape[0]
     total = None
-    for j in range(2 + len(direct)):
+    for j in range(2 + far):
         if j == 0:
-            weight = own[:, columns]
+            weight = own[...]
         elif j == 1:
-            weight = near[:, columns]
+            weight = near[...]
         else:
-            far = whole.at[j - 2]
-            far[pl.ds(pl.multiple_of(plane * extra, 16), count), :] = direct[j - 2][...]
-            far[pl.ds(pl.multiple_of((1 - plane) * count, 16), extra), :] = forwarded[j - 2]
-            weight = far[...]
+            piece = whole.at[j - 2]
+            piece[pl.ds(pl.multiple_of(plane * extra, 16), count), :] = direct[j - 2][...]
+            rest = forwarded[0][j - 2] if len(forwarded) == 1 else forwarded[j - 2][...]
+            piece[pl.ds(pl.multiple_of((1 - plane) * count, 16), extra), :] = rest
+            weight = piece[...]
         place = where[0] ^ j
         left = jnp.concatenate([keep[0, place], keep[1, place], other[place], other_2[place]], axis=0)
         product = jnp.dot(left, weight, preferred_element_type=jnp.float32)
@@ -209,19 +222,19 @@
         theirs[i] = total[(2 + i) * ROWS : (3 + i) * ROWS]
 
 
-def project(where, rows_of_x, chunk, own, near, direct, forwarded):
-    width = chunk[1] * HD
+def project(where, rows_of_x, own, near, direct, forwarded):
+    width = own.shape[1]
     out = jax.ShapeDtypeStruct((2, ROWS, width), jnp.float32)
     return on_chip(
-        functools.partial(project_kernel, columns_of(chunk)),
+        project_kernel,
         "project",
         [out, out],
         where,
         *rows_of_x,
         own,
         near,
-        forwarded,
         *direct,
+        *forwarded,
         scratch=[pltpu.VMEM((len(direct), own.shape[0], width), jnp.bfloat16)],
     )
 
@@ -310,24 +323,24 @@
     for _ in range(cycle - 1):
         caches.append(lax.ppermute(caches[-1], "blk", [(i, (i + 1) % cycle) for i in range(cycle)]))
 
-    own, got_weight = tie((own_half(where, kv_weight), got_weight))
-    whole, far = pack_weight(where, own, got_weight)
+    wholes, got_weight = tie((own_rows(where, kv_weight), got_weight))
+    whole, far = pack_weight(where, got_weight, wholes)
 
     def send(far):
         return [xor_swap(far, "z", j) for j in range(2, steps)]
 
-    def forward(i):
-        helped, direct = row_split(whole.shape[0], i)
+    def forward(i, stacked):
+        helped, direct = row_split(whole[0].shape[0], i)
         parts = [lax.dynamic_slice_in_dim(p, plane * (direct - helped), helped, axis=0) for p in sent[i]]
-        return xor_swap(jnp.stack(parts), "blk", 1)
+        return [xor_swap(part, "blk", 1) for part in ([jnp.stack(parts)] if stacked else parts)]
 
     sent = [send(far[0])]
-    near = xor_swap(whole, "z", 1)
-    got_x, whole = tie((got_x, whole))
+    near = [xor_swap(whole[0], "z", 1)]
+    got_x, whole[1] = tie((got_x, whole[1]))
     keep, given = pack_rows(where, x, got_x, y, steps)
     other = xor_swap(given, "y", 1)
 
-    block_table, _ = tie((block_table, whole))
+    block_table, _ = tie((block_table, whole[0]))
     infos = []
     for stride in range(cycle):
         owner = lax.rem(holder + cycle - stride, cycle)
@@ -335,29 +348,30 @@
         listed = lax.dynamic_index_in_dim(block_table[0], place // BLOCK, axis=1, keepdims=False)
         infos.append(jnp.concatenate([place[None], prompt_lengths, listed]).astype(jnp.int32))
 
-    query, _, _ = tie((query, whole, given))
+    query, _, _ = tie((query, whole[0], given))
     state = prompt_attention(infos[0], query, caches[0], None, 0, KVH)
 
-    sent[0], state, far[1] = tie((sent[0], state, far[1]))
+    sent[0], state, far[1], whole[1] = tie((sent[0], state, far[1], whole[1]))
     sent.append(send(far[1]))
+    near.append(xor_swap(whole[1], "z", 1))
     sent[0], caches = tie((sent[0], caches))
+    forwarded = [forward(0, True)]
     state, other = tie((state, other))
     rows_of_x = [keep, other, xor_swap(other, "core", 1)]
-    forwarded = [forward(0)]
     for stride in range(1, cycle):
         state = prompt_attention(infos[stride], query, caches[stride], state, 0, KVH)
-    forwarded[0], state = tie((forwarded[0], state))
 
     def sums(i):
-        return project(where, rows_of_x, CHUNKS[i], whole, near, sent[i], forwarded[i])
+        return project(where, rows_of_x, whole[i], near[i], sent[i], forwarded[i])
 
     def owners(mine, theirs):
         there = [xor_swap(theirs[1:], ("y", "core"), 3), xor_swap(mine[1:], "core", 1)]
         return xor_swap(theirs[:1], "y", 1), there
 
+    forwarded[0], state = tie((forwarded[0], state))
     mine_0, theirs_0 = sums(0)
     sent[1], mine_0 = tie((sent[1], mine_0))
-    forwarded.append(forward(1))
+    forwarded.append(forward(1, True))
     here_0, there_0 = owners(mine_0, theirs_0)
     forwarded[1], mine_0 = tie((forwarded[1], mine_0))
     mine_1, theirs_1 = sums(1)

time: 61.9 us -> 61.4 us (level)
  the two profiles are of different devices: /device:TPU:0 before, /device:TPU:11 now
where the time goes in v10:
time: 61.4 us; the launch traced here: 61.2 us
  Pallas kernels  21.9 us (36%)
  waiting for transfers between devices  20.2 us (33%)
  starting transfers between devices  16.6 us (27%)
  local copies, waits for them, and re-layouts  1.39 us (2%)
  between operations  0.89 us (1%)
    ppermute x18, waiting for transfers between devices, xor_swap(): lax.ppermute(array, axis, [(i, i ^ by) for i in range(lax.axis_size(axis))])  19.5 us
    ppermute x18, starting transfers between devices, xor_swap(): lax.ppermute(array, axis, [(i, i ^ by) for i in range(lax.axis_size(axis))])  16.3 us
    pallas_call x2, Pallas kernels, prompt_attention(): pl.pallas_call(functools.partial(prompt_kernel, first), grid_spec=pltpu.P...  11.7 us
    pallas_call x2, Pallas kernels, final_attention(): pl.pallas_call(functools.partial(final_kernel, chunk, offset), in_specs=s...  4.68 us
    pallas_call x4, Pallas kernels, on_chip(): pl.pallas_call(kernel, in_specs=[SMEM] + [VMEM] * len(operands), out_spec...  4.3 us
  transfers between devices with their start and end apart: 19, of which 7 were waited for; matrix products, arithmetic and copies ran while one was open for 1% of the time, Pallas kernels for 32%

profile of v10, /device:TPU:11, one launch (start us, length us, event | category | flops | bytes accessed | tf_op | source)
XLA Modules:
  0.0 61.2 jit_solution(4920793314788676627)
XLA Ops:
  1.1 1.1 %copy-done.2 = bf16[320,1024]{1,0:T(8,128)(2,1)S(1)} copy-done((bf16[320,1024]{1,0:T(8,128)(2,1)S(1)}, bf16[320,1024]{1,0:T(8,128)(2,1)}, u32[]{:S(2)}) %copy-start.2) | copy-done | bytes 655384
  3.5 1.0 %collective-permute-done.got_ref = bf16[320,1024]{1,0:T(8,128)(2,1)} collective-permute-done((bf16[320,1024]{1,0:T(8,128)(2,1)}, bf16[320,1024]{1,0:T(8,128)(2,1)}, u32[]{:S(2)}, u32[]{:S(2)}) %collective-permute-start) | collective-permute-done | bytes 655392 | tf_op jit(solution)/shard_map/ppermute | solution.py:305
  4.5 1.2 %pack_weight.1 = (bf16[640,256]{1,0:T(8,128)(2,1)S(1)}, bf16[640,256]{1,0:T(8,128)(2,1)S(1)}, bf16[320,256]{1,0:T(8,128)(2,1)S(1)}, bf16[320,256]{1,0:T(8,128)(2,1)S(1)}) custom-call(s32[4]{0:T(128)S(1)} %pad_add_fusion.1.where, bf16[320,1024]{1,0:T(8,128)(2,1)} %collective-permute-done.got_ref, ...), custom_call_target="tpu_custom_call", output_to_operand_aliasing={{0}: (2, {}), {1}: (3, {})} | custom-call | flops 1024 | bytes 1024 | tf_op jit(solution)/shard_map/pack_weight/pallas_call | solution.py:185
  5.7 2.4 %collective-permute-start.2 = (bf16[320,256]{1,0:T(8,128)(2,1)S(1)}, bf16[320,256]{1,0:T(8,128)(2,1)S(1)}, u32[]{:S(2)}, u32[]{:S(2)}) collective-permute-start(bf16[320,256]{1,0:T(8,128)(2,1)S(1)} %get-tuple-element.63), channel_id=1, source_target_pairs={{0,16},{8,24},{16,0},{24,8},{1,17},{9,25},{17,1},{25,9},{2,18},{10... | collective-permute-start | bytes 491528 | tf_op jit(solution)/shard_map/ppermute | solution.py:305
  8.0 1.3 %collective-permute-start.8 = (bf16[640,256]{1,0:T(8,128)(2,1)S(1)}, bf16[640,256]{1,0:T(8,128)(2,1)S(1)}, u32[]{:S(2)}, u32[]{:S(2)}) collective-permute-start(bf16[640,256]{1,0:T(8,128)(2,1)S(1)} %get-tuple-element.58.own), channel_id=1, source_target_pairs={{0,8},{8,0},{16,24},{24,16},{1,9},{9,1},{17,25},{25,17},{2,10},{10... | collective-permute-start | bytes 983048 | tf_op jit(solution)/shard_map/ppermute | solution.py:305
  9.6 0.7 %pack_rows.1 = (bf16[2,4,128,640]{3,2,1,0:T(8,128)(2,1)S(1)}, bf16[4,128,640]{2,1,0:T(8,128)(2,1)S(1)}) custom-call(s32[4]{0:T(128)S(1)} %pad_add_fusion.1.where, bf16[128,5120]{1,0:T(8,128)(2,1)S(1)} %bitcast.21, bf16[128,5120]{1,0:T(8,128)(2,1)S(1)} %collective-permute-done.1.got_ref), custom_call_target="tpu_custom_call" | custom-call | flops 1024 | bytes 1024 | tf_op jit(solution)/shard_map/pack_rows/pallas_call | solution.py:118
  10.3 1.3 %collective-permute-start.6 = (bf16[4,128,640]{2,1,0:T(8,128)(2,1)S(1)}, bf16[4,128,640]{2,1,0:T(8,128)(2,1)S(1)}, u32[]{:S(2)}, u32[]{:S(2)}) collective-permute-start(bf16[4,128,640]{2,1,0:T(8,128)(2,1)S(1)} %get-tuple-element.61), channel_id=1, source_target_pairs={{0,4},{4,0},{1,5},{5,1},{2,6},{6,2},{3,7},{7,3},{8,12},{12,8},{9,1... | collective-permute-start | bytes 1966088 | tf_op jit(solution)/shard_map/ppermute | solution.py:305
  11.6 5.4 %prompt_attention.2 = (f32[128,4096]{1,0:T(8,128)S(1)}, f32[8,4096]{1,0:T(8,128)S(1)}) custom-call(s32[4]{0:T(128)S(1)} %get-tuple-element.107.info, bf16[128,4096]{1,0:T(8,128)(2,1)S(1)} %bitcast.16, bf16[512,1024]{1,0:T(8,128)(2,1)S(1)} %bitcast.29, bf16[512,1024]{1,0:T(8,128)(2,1)S(1)} %bitcast.30), custom_call_target="tpu_custom_call" | custom-call | flops 17179869184 | bytes 1024 | tf_op jit(solution)/shard_map/prompt_attention/pallas_call | solution.py:95
  17.1 1.9 %collective-permute-done.2.refs_0_ = bf16[320,256]{1,0:T(8,128)(2,1)S(1)} collective-permute-done((bf16[320,256]{1,0:T(8,128)(2,1)S(1)}, bf16[320,256]{1,0:T(8,128)(2,1)S(1)}, u32[]{:S(2)}, u32[]{:S(2)}) %collective-permute-start.2) | collective-permute-done | bytes 163872 | tf_op jit(solution)/shard_map/ppermute | solution.py:305
  18.9 3.5 %collective-permute-done.3.refs_1_ = bf16[320,256]{1,0:T(8,128)(2,1)S(1)} collective-permute-done((bf16[320,256]{1,0:T(8,128)(2,1)S(1)}, bf16[320,256]{1,0:T(8,128)(2,1)S(1)}, u32[]{:S(2)}, u32[]{:S(2)}) %collective-permute-start.3) | collective-permute-done | bytes 163872 | tf_op jit(solution)/shard_map/ppermute | solution.py:305
  22.5 2.3 %collective-permute-start.12 = (bf16[320,256]{1,0:T(8,128)(2,1)S(1)}, bf16[320,256]{1,0:T(8,128)(2,1)S(1)}, u32[]{:S(2)}, u32[]{:S(2)}) collective-permute-start(bf16[320,256]{1,0:T(8,128)(2,1)S(1)} %get-tuple-element.86), channel_id=1, source_target_pairs={{0,24},{8,16},{16,8},{24,0},{1,25},{9,17},{17,9},{25,1},{2,26},{10... | collective-permute-start | bytes 491528 | tf_op jit(solution)/shard_map/ppermute | solution.py:305
  25.8 1.8 %collective-permute-start.7 = (bf16[4,128,640]{2,1,0:T(8,128)(2,1)S(1)}, bf16[4,128,640]{2,1,0:T(8,128)(2,1)S(1)}, u32[]{:S(2)}, u32[]{:S(2)}) collective-permute-start(bf16[4,128,640]{2,1,0:T(8,128)(2,1)S(1)} %collective-permute-done.6.other), channel_id=1, source_target_pairs={{0,2},{2,0},{1,3},{3,1},{4,6},{6,4},{5,7},{7,5},{8,10},{10,8},{9,1... | collective-permute-start | bytes 1966088 | tf_op jit(solution)/shard_map/ppermute | solution.py:305
  27.5 6.3 %prompt_attention.3 = (f32[128,4096]{1,0:T(8,128)S(1)}, f32[8,4096]{1,0:T(8,128)S(1)}) custom-call(s32[4]{0:T(128)S(1)} %get-tuple-element.108.info, bf16[128,4096]{1,0:T(8,128)(2,1)S(1)} %bitcast.17, bf16[512,1024]{1,0:T(8,128)(2,1)} %collective-permute-done.4.k_ref.v_ref, bf16[512,1024]{1,0:T(8,128)(2,1)} %collective-permute-done.4.k_ref.v_ref, ...), custom_call_target="tpu_custom_call" | custom-call | flops 8589934592 | bytes 1024 | tf_op jit(solution)/shard_map/prompt_attention/pallas_call | solution.py:95
  34.3 1.5 %project.2 = (f32[2,128,256]{2,1,0:T(8,128)S(1)}, f32[2,128,256]{2,1,0:T(8,128)S(1)}) custom-call(s32[4]{0:T(128)S(1)} %pad_add_fusion.1.where, bf16[2,4,128,640]{3,2,1,0:T(8,128)(2,1)S(1)} %get-tuple-element.82.keep, bf16[4,128,640]{2,1,0:T(8,128)(2,1)S(1)} %collective-permute-done.6.other, bf16[4,128,640]{2,1,0:T(8,128)(2,1)S(1)} %collective-permute-done.7.other_2, ...), custom_call_target="tpu_custom_call" | custom-call | flops 1024 | bytes 1024 | tf_op jit(solution)/shard_map/project/pallas_call | solution.py:118
  35.8 4.1 %collective-permute-done.12.refs_1_ = bf16[320,256]{1,0:T(8,128)(2,1)S(1)} collective-permute-done((bf16[320,256]{1,0:T(8,128)(2,1)S(1)}, bf16[320,256]{1,0:T(8,128)(2,1)S(1)}, u32[]{:S(2)}, u32[]{:S(2)}) %collective-permute-start.12) | collective-permute-done | bytes 163872 | tf_op jit(solution)/shard_map/ppermute | solution.py:305
  40.2 0.9 %collective-permute-start.13 = (f32[1,128,256]{2,1,0:T(8,128)S(1)}, f32[1,128,256]{2,1,0:T(8,128)S(1)}, u32[]{:S(2)}, u32[]{:S(2)}) collective-permute-start(f32[1,128,256]{2,1,0:T(8,128)S(1)} %slice.20), channel_id=1, source_target_pairs={{0,2},{2,0},{1,3},{3,1},{4,6},{6,4},{5,7},{7,5},{8,10},{10,8},{9,1... | collective-permute-start | bytes 393224 | tf_op jit(solution)/shard_map/ppermute | solution.py:305
  41.1 1.2 %collective-permute-start.10 = (f32[1,128,256]{2,1,0:T(8,128)S(1)}, f32[1,128,256]{2,1,0:T(8,128)S(1)}, u32[]{:S(2)}, u32[]{:S(2)}) collective-permute-start(f32[1,128,256]{2,1,0:T(8,128)S(1)} %get-tuple-element.105), channel_id=1, source_target_pairs={{0,6},{2,4},{4,2},{6,0},{1,7},{3,5},{5,3},{7,1},{8,14},{10,12},{12... | collective-permute-start | bytes 393224 | tf_op jit(solution)/shard_map/ppermute | solution.py:305
  42.6 6.1 %collective-permute-done.15.refs_2_ = bf16[2,320,256]{2,1,0:T(8,128)(2,1)S(1)} collective-permute-done((bf16[2,320,256]{2,1,0:T(8,128)(2,1)S(1)}, bf16[2,320,256]{2,1,0:T(8,128)(2,1)S(1)}, u32[]{:S(2)}, u32[]{:S(2)}) %collective-permute-start.15) | collective-permute-done | bytes 327712 | tf_op jit(solution)/shard_map/ppermute | solution.py:305
  48.7 1.5 %project.3 = (f32[2,128,256]{2,1,0:T(8,128)S(1)}, f32[2,128,256]{2,1,0:T(8,128)S(1)}) custom-call(s32[4]{0:T(128)S(1)} %pad_add_fusion.1.where, bf16[2,4,128,640]{3,2,1,0:T(8,128)(2,1)S(1)} %get-tuple-element.82.keep, bf16[4,128,640]{2,1,0:T(8,128)(2,1)S(1)} %collective-permute-done.6.other, bf16[4,128,640]{2,1,0:T(8,128)(2,1)S(1)} %collective-permute-done.7.other_2, ...), custom_call_target="tpu_custom_call" | custom-call | flops 1024 | bytes 1024 | tf_op jit(solution)/shard_map/project/pallas_call | solution.py:118
  50.3 1.3 %collective-permute-start.16 = (f32[1,128,256]{2,1,0:T(8,128)S(1)}, f32[1,128,256]{2,1,0:T(8,128)S(1)}, u32[]{:S(2)}, u32[]{:S(2)}) collective-permute-start(f32[1,128,256]{2,1,0:T(8,128)S(1)} %get-tuple-element.104), channel_id=1, source_target_pairs={{0,4},{4,0},{1,5},{5,1},{2,6},{6,2},{3,7},{7,3},{8,12},{12,8},{9,1... | collective-permute-start | bytes 393224 | tf_op jit(solution)/shard_map/ppermute | solution.py:305
  51.6 1.8 %collective-permute-start.17 = (f32[1,128,256]{2,1,0:T(8,128)S(1)}, f32[1,128,256]{2,1,0:T(8,128)S(1)}, u32[]{:S(2)}, u32[]{:S(2)}) collective-permute-start(f32[1,128,256]{2,1,0:T(8,128)S(1)} %get-tuple-element.103), channel_id=1, source_target_pairs={{0,6},{2,4},{4,2},{6,0},{1,7},{3,5},{5,3},{7,1},{8,14},{10,12},{12... | collective-permute-start | bytes 393224 | tf_op jit(solution)/shard_map/ppermute | solution.py:305
  53.6 2.3 %final_attention.2.refs_0_ = bf16[128,4096]{1,0:T(8,128)(2,1)} custom-call(s32[3]{0:T(128)S(1)} %pad_add_fusion.info, f32[1,128]{1,0:T(1,128)S(1)} %bitcast.26, bf16[128,4096]{1,0:T(8,128)(2,1)S(1)} %bitcast.18, f32[128,4096]{1,0:T(8,128)S(1)} %get-tuple-element.80.acc_ref, f32[8,4096]{1,0:T(8,128)S(1)} %get-tuple-element.81.ml_ref, ...), custom_call_target="tpu_custom_call" | custom-call | flops 1024 | bytes 1024 | tf_op jit(solution)/shard_map/final_attention/pallas_call | solution.py:291
  55.9 2.9 %collective-permute-done.17.there = f32[1,128,256]{2,1,0:T(8,128)S(1)} collective-permute-done((f32[1,128,256]{2,1,0:T(8,128)S(1)}, f32[1,128,256]{2,1,0:T(8,128)S(1)}, u32[]{:S(2)}, u32[]{:S(2)}) %collective-permute-start.17) | collective-permute-done | bytes 131104 | tf_op jit(solution)/shard_map/ppermute | solution.py:305
  58.8 2.3 %final_attention.3 = bf16[128,4096]{1,0:T(8,128)(2,1)} custom-call(s32[3]{0:T(128)S(1)} %pad_add_fusion.info, f32[1,128]{1,0:T(1,128)S(1)} %bitcast.27, bf16[128,4096]{1,0:T(8,128)(2,1)S(1)} %bitcast.19, f32[128,4096]{1,0:T(8,128)S(1)} %get-tuple-element.80.acc_ref, f32[8,4096]{1,0:T(8,128)S(1)} %get-tuple-element.81.ml_ref, ...), custom_call_target="tpu_custom_call", output_to_operand_aliasing={{}: (9, {})} | custom-call | flops 1024 | bytes 1024 | tf_op jit(solution)/shard_map/final_attention/pallas_call | solution.py:291
  (47 shorter events, 4.2 us)
Async XLA Ops:
  0.0 9.6 %copy-start.1 = (bf16[1,128,5120]{2,1,0:T(8,128)(2,1)S(1)}, bf16[1,128,5120]{2,1,0:T(8,128)(2,1)}, u32[]{:S(2)}) copy-start(bf16[1,128,5120]{2,1,0:T(8,128)(2,1)} %param.8) | copy-start | bytes 3932164
  0.0 9.6 %collective-permute-start.1 = (bf16[128,5120]{1,0:T(8,128)(2,1)}, bf16[128,5120]{1,0:T(8,128)(2,1)S(1)}, u32[]{:S(2)}, u32[]{:S(2)}) collective-permute-start(bf16[128,5120]{1,0:T(8,128)(2,1)} %bitcast.20), channel_id=1, source_target_pairs={{0,2},{2,0},{1,3},{3,1},{4,6},{6,4},{5,7},{7,5},{8,10},{10,8},{9,1... | collective-permute-start | bytes 3932168 | tf_op jit(solution)/shard_map/ppermute | solution.py:305
  0.7 3.8 %collective-permute-start = (bf16[320,1024]{1,0:T(8,128)(2,1)}, bf16[320,1024]{1,0:T(8,128)(2,1)}, u32[]{:S(2)}, u32[]{:S(2)}) collective-permute-start(bf16[320,1024]{1,0:T(8,128)(2,1)} %weight_ref.1), channel_id=1, source_target_pairs={{0,2},{2,0},{1,3},{3,1},{4,6},{6,4},{5,7},{7,5},{8,10},{10,8},{9,1... | collective-permute-start | bytes 1966088 | tf_op jit(solution)/shard_map/ppermute | solution.py:305
  0.8 24.6 %collective-permute-start.4 = (bf16[512,1024]{1,0:T(8,128)(2,1)}, bf16[512,1024]{1,0:T(8,128)(2,1)}, u32[]{:S(2)}, u32[]{:S(2)}) collective-permute-start(bf16[512,1024]{1,0:T(8,128)(2,1)} %bitcast.28), channel_id=1, source_target_pairs={{0,1},{1,0},{2,3},{3,2},{4,5},{5,4},{6,7},{7,6},{8,9},{9,8},{10,11... | collective-permute-start | bytes 3145736 | tf_op jit(solution)/shard_map/ppermute | solution.py:324
  2.2 7.1 %copy-start.5 = (s32[1,2,2]{2,1,0:T(2,128)S(1)}, s32[1,2,2]{2,1,0:T(2,128)}, u32[]{:S(2)}) copy-start(s32[1,2,2]{2,1,0:T(2,128)} %param.14) | copy-start | bytes 52
  5.7 13.3 %collective-permute-start.2 = (bf16[320,256]{1,0:T(8,128)(2,1)S(1)}, bf16[320,256]{1,0:T(8,128)(2,1)S(1)}, u32[]{:S(2)}, u32[]{:S(2)}) collective-permute-start(bf16[320,256]{1,0:T(8,128)(2,1)S(1)} %get-tuple-element.63), channel_id=1, source_target_pairs={{0,16},{8,24},{16,0},{24,8},{1,17},{9,25},{17,1},{25,9},{2,18},{10... | collective-permute-start | bytes 491528 | tf_op jit(solution)/shard_map/ppermute | solution.py:305
  8.0 14.4 %collective-permute-start.3 = (bf16[320,256]{1,0:T(8,128)(2,1)S(1)}, bf16[320,256]{1,0:T(8,128)(2,1)S(1)}, u32[]{:S(2)}, u32[]{:S(2)}) collective-permute-start(bf16[320,256]{1,0:T(8,128)(2,1)S(1)} %get-tuple-element.63), channel_id=1, source_target_pairs={{0,24},{8,16},{16,8},{24,0},{1,25},{9,17},{17,9},{25,1},{2,26},{10... | collective-permute-start | bytes 491528 | tf_op jit(solution)/shard_map/ppermute | solution.py:305
  8.0 26.2 %collective-permute-start.8 = (bf16[640,256]{1,0:T(8,128)(2,1)S(1)}, bf16[640,256]{1,0:T(8,128)(2,1)S(1)}, u32[]{:S(2)}, u32[]{:S(2)}) collective-permute-start(bf16[640,256]{1,0:T(8,128)(2,1)S(1)} %get-tuple-element.58.own), channel_id=1, source_target_pairs={{0,8},{8,0},{16,24},{24,16},{1,9},{9,1},{17,25},{25,17},{2,10},{10... | collective-permute-start | bytes 983048 | tf_op jit(solution)/shard_map/ppermute | solution.py:305
  9.6 2.0 %copy-start = (bf16[1,128,4096]{2,1,0:T(8,128)(2,1)S(1)}, bf16[1,128,4096]{2,1,0:T(8,128)(2,1)}, u32[]{:S(2)}) copy-start(bf16[1,128,4096]{2,1,0:T(8,128)(2,1)} %param.9) | copy-start | bytes 3145732
  10.3 15.5 %collective-permute-start.6 = (bf16[4,128,640]{2,1,0:T(8,128)(2,1)S(1)}, bf16[4,128,640]{2,1,0:T(8,128)(2,1)S(1)}, u32[]{:S(2)}, u32[]{:S(2)}) collective-permute-start(bf16[4,128,640]{2,1,0:T(8,128)(2,1)S(1)} %get-tuple-element.61), channel_id=1, source_target_pairs={{0,4},{4,0},{1,5},{5,1},{2,6},{6,2},{3,7},{7,3},{8,12},{12,8},{9,1... | collective-permute-start | bytes 1966088 | tf_op jit(solution)/shard_map/ppermute | solution.py:305
  22.4 13.3 %collective-permute-start.11 = (bf16[320,256]{1,0:T(8,128)(2,1)S(1)}, bf16[320,256]{1,0:T(8,128)(2,1)S(1)}, u32[]{:S(2)}, u32[]{:S(2)}) collective-permute-start(bf16[320,256]{1,0:T(8,128)(2,1)S(1)} %get-tuple-element.86), channel_id=1, source_target_pairs={{0,16},{8,24},{16,0},{24,8},{1,17},{9,25},{17,1},{25,9},{2,18},{10... | collective-permute-start | bytes 491528 | tf_op jit(solution)/shard_map/ppermute | solution.py:305
  22.5 17.4 %collective-permute-start.12 = (bf16[320,256]{1,0:T(8,128)(2,1)S(1)}, bf16[320,256]{1,0:T(8,128)(2,1)S(1)}, u32[]{:S(2)}, u32[]{:S(2)}) collective-permute-start(bf16[320,256]{1,0:T(8,128)(2,1)S(1)} %get-tuple-element.86), channel_id=1, source_target_pairs={{0,24},{8,16},{16,8},{24,0},{1,25},{9,17},{17,9},{25,1},{2,26},{10... | collective-permute-start | bytes 491528 | tf_op jit(solution)/shard_map/ppermute | solution.py:305
  25.5 8.4 %collective-permute-start.5 = (bf16[2,320,256]{2,1,0:T(8,128)(2,1)S(1)}, bf16[2,320,256]{2,1,0:T(8,128)(2,1)S(1)}, u32[]{:S(2)}, u32[]{:S(2)}) collective-permute-start(bf16[2,320,256]{2,1,0:T(8,128)(2,1)S(1)} %pad_maximum_fusion), channel_id=1, source_target_pairs={{0,1},{1,0},{2,3},{3,2},{4,5},{5,4},{6,7},{7,6},{8,9},{9,8},{10,11... | collective-permute-start | bytes 983048 | tf_op jit(solution)/shard_map/ppermute | solution.py:305
  25.8 8.5 %collective-permute-start.7 = (bf16[4,128,640]{2,1,0:T(8,128)(2,1)S(1)}, bf16[4,128,640]{2,1,0:T(8,128)(2,1)S(1)}, u32[]{:S(2)}, u32[]{:S(2)}) collective-permute-start(bf16[4,128,640]{2,1,0:T(8,128)(2,1)S(1)} %collective-permute-done.6.other), channel_id=1, source_target_pairs={{0,2},{2,0},{1,3},{3,1},{4,6},{6,4},{5,7},{7,5},{8,10},{10,8},{9,1... | collective-permute-start | bytes 1966088 | tf_op jit(solution)/shard_map/ppermute | solution.py:305
  33.8 14.9 %collective-permute-start.14 = (bf16[640,256]{1,0:T(8,128)(2,1)S(1)}, bf16[640,256]{1,0:T(8,128)(2,1)S(1)}, u32[]{:S(2)}, u32[]{:S(2)}) collective-permute-start(bf16[640,256]{1,0:T(8,128)(2,1)S(1)} %get-tuple-element.89.own), channel_id=1, source_target_pairs={{0,8},{8,0},{16,24},{24,16},{1,9},{9,1},{17,25},{25,17},{2,10},{10... | collective-permute-start | bytes 983048 | tf_op jit(solution)/shard_map/ppermute | solution.py:305
  39.9 8.8 %collective-permute-start.15 = (bf16[2,320,256]{2,1,0:T(8,128)(2,1)S(1)}, bf16[2,320,256]{2,1,0:T(8,128)(2,1)S(1)}, u32[]{:S(2)}, u32[]{:S(2)}) collective-permute-start(bf16[2,320,256]{2,1,0:T(8,128)(2,1)S(1)} %pad_maximum_fusion.1), channel_id=1, source_target_pairs={{0,1},{1,0},{2,3},{3,2},{4,5},{5,4},{6,7},{7,6},{8,9},{9,8},{10,11... | collective-permute-start | bytes 983048 | tf_op jit(solution)/shard_map/ppermute | solution.py:305
  40.2 10.0 %collective-permute-start.13 = (f32[1,128,256]{2,1,0:T(8,128)S(1)}, f32[1,128,256]{2,1,0:T(8,128)S(1)}, u32[]{:S(2)}, u32[]{:S(2)}) collective-permute-start(f32[1,128,256]{2,1,0:T(8,128)S(1)} %slice.20), channel_id=1, source_target_pairs={{0,2},{2,0},{1,3},{3,1},{4,6},{6,4},{5,7},{7,5},{8,10},{10,8},{9,1... | collective-permute-start | bytes 393224 | tf_op jit(solution)/shard_map/ppermute | solution.py:305
  41.1 9.1 %collective-permute-start.10 = (f32[1,128,256]{2,1,0:T(8,128)S(1)}, f32[1,128,256]{2,1,0:T(8,128)S(1)}, u32[]{:S(2)}, u32[]{:S(2)}) collective-permute-start(f32[1,128,256]{2,1,0:T(8,128)S(1)} %get-tuple-element.105), channel_id=1, source_target_pairs={{0,6},{2,4},{4,2},{6,0},{1,7},{3,5},{5,3},{7,1},{8,14},{10,12},{12... | collective-permute-start | bytes 393224 | tf_op jit(solution)/shard_map/ppermute | solution.py:305
  42.4 11.1 %copy-start.6 = (s32[1,2]{1,0:T(1,128)S(1)}, s32[1,2]{1,0:T(1,128)}, u32[]{:S(2)}) copy-start(s32[1,2]{1,0:T(1,128)} %param.15) | copy-start | bytes 28
  42.4 11.2 %copy-start.3 = (f32[128]{0:T(128)S(1)}, f32[128]{0:T(128)}, u32[]{:S(2)}) copy-start(f32[128]{0:T(128)} %param.12) | copy-start | bytes 1540
  42.4 7.9 %collective-permute-start.9 = (f32[1,128,256]{2,1,0:T(8,128)S(1)}, f32[1,128,256]{2,1,0:T(8,128)S(1)}, u32[]{:S(2)}, u32[]{:S(2)}) collective-permute-start(f32[1,128,256]{2,1,0:T(8,128)S(1)} %get-tuple-element.106), channel_id=1, source_target_pairs={{0,4},{4,0},{1,5},{5,1},{2,6},{6,2},{3,7},{7,3},{8,12},{12,8},{9,1... | collective-permute-start | bytes 393224 | tf_op jit(solution)/shard_map/ppermute | solution.py:305
  50.3 5.6 %collective-permute-start.16 = (f32[1,128,256]{2,1,0:T(8,128)S(1)}, f32[1,128,256]{2,1,0:T(8,128)S(1)}, u32[]{:S(2)}, u32[]{:S(2)}) collective-permute-start(f32[1,128,256]{2,1,0:T(8,128)S(1)} %get-tuple-element.104), channel_id=1, source_target_pairs={{0,4},{4,0},{1,5},{5,1},{2,6},{6,2},{3,7},{7,3},{8,12},{12,8},{9,1... | collective-permute-start | bytes 393224 | tf_op jit(solution)/shard_map/ppermute | solution.py:305
  51.6 7.3 %collective-permute-start.17 = (f32[1,128,256]{2,1,0:T(8,128)S(1)}, f32[1,128,256]{2,1,0:T(8,128)S(1)}, u32[]{:S(2)}, u32[]{:S(2)}) collective-permute-start(f32[1,128,256]{2,1,0:T(8,128)S(1)} %get-tuple-element.103), channel_id=1, source_target_pairs={{0,6},{2,4},{4,2},{6,0},{1,7},{3,5},{5,3},{7,1},{8,14},{10,12},{12... | collective-permute-start | bytes 393224 | tf_op jit(solution)/shard_map/ppermute | solution.py:305
  53.4 5.4 %collective-permute-start.18 = (f32[1,128,256]{2,1,0:T(8,128)S(1)}, f32[1,128,256]{2,1,0:T(8,128)S(1)}, u32[]{:S(2)}, u32[]{:S(2)}) collective-permute-start(f32[1,128,256]{2,1,0:T(8,128)S(1)} %slice.23), channel_id=1, source_target_pairs={{0,2},{2,0},{1,3},{3,1},{4,6},{6,4},{5,7},{7,5},{8,10},{10,8},{9,1... | collective-permute-start | bytes 393224 | tf_op jit(solution)/shard_map/ppermute | solution.py:305
  (2 other events, 3.1 us)

commit v11 on v9

--- a/solution.py
+++ b/solution.py
@@ -153,76 +153,101 @@
     return helped, rows - helped
 
 
-def columns_of(chunk):
-    return slice(chunk[0] * HD, (chunk[0] + chunk[1]) * HD)
-
-
-def own_half_kernel(where, weight_ref, out):
-    out[...] = weight_ref[:, pl.ds(pl.multiple_of(where[2] * KVH * HD, 128), KVH * HD)]
-
-
-def own_half(where, weight):
-    out = jax.ShapeDtypeStruct((weight.shape[0], KVH * HD), weight.dtype)
-    return on_chip(own_half_kernel, "own_half", [out], where, weight)[0]
-
-
-def pack_weight_kernel(where, own_ref, got_ref, whole, *far):
-    rows = got_ref.shape[0]
-    core, plane = where[2], where[3]
-    half = pl.ds(pl.multiple_of(core * KVH * HD, 128), KVH * HD)
-    whole[pl.ds(pl.multiple_of(core * rows, 16), rows), :] = own_ref[...]
-    whole[pl.ds(pl.multiple_of((1 - core) * rows, 16), rows), :] = got_ref[:, half]
-    for out, chunk in zip(far, CHUNKS):
-        direct = out.shape[0]
-        out[...] = whole[pl.ds(pl.multiple_of(plane * (2 * rows - direct), 16), direct), columns_of(chunk)]
-
-
-def pack_weight(where, own, got):
-    rows = 2 * own.shape[0]
-    shapes = [(rows, KVH * HD)] + [(row_split(rows, i)[1], heads * HD) for i, (_, heads) in enumerate(CHUNKS)]
-    outs = [jax.ShapeDtypeStruct(shape, own.dtype) for shape in shapes]
-    whole, *far = on_chip(pack_weight_kernel, "pack_weight", outs, where, own, got)
-    return whole, far
-
-
-def project_kernel(columns, where, keep, other, other_2, own, near, forwarded, *refs):
-    direct, mine, theirs, whole = refs[:-3], refs[-3], refs[-2], refs[-1]
+def weight_columns(core, chunk):
+    head, heads = chunk
+    return pl.ds(pl.multiple_of((core * KVH + head) * HD, 128), heads * HD)
+
+
+def far_rows_kernel(chunk, where, own_ref, got_ref, far):
+    rows, count = own_ref.shape[0], far.shape[0]
+    core, place = where[2], where[3] * (2 * rows - count)
+    columns = weight_columns(core, chunk)
+    if count == rows:
+        @pl.when(core == where[3])
+        def _():
+            far[...] = own_ref[:, columns]
+
+        @pl.when(core != where[3])
+        def _():
+            far[...] = got_ref[:, columns]
+    else:
+        for z in range(0, count, 16):
+            row = place + z
+            from_own = row // rows == core
+            inside = pl.ds(pl.multiple_of(lax.rem(row, rows), 16), 16)
+
+            @pl.when(from_own)
+            def _():
+                far[z : z + 16, :] = own_ref[inside, columns]
+
+            @pl.when(jnp.logical_not(from_own))
+            def _():
+                far[z : z + 16, :] = got_ref[inside, columns]
+
+
+def far_rows(where, own, got, i):
+    count = row_split(2 * own.shape[0], i)[1]
+    out = jax.ShapeDtypeStruct((count, CHUNKS[i][1] * HD), own.dtype)
+    return on_chip(functools.partial(far_rows_kernel, CHUNKS[i]), "far_rows", [out], where, own, got)[0]
+
+
+def whole_rows_kernel(where, own_ref, got_ref, *outs):
+    rows, core = own_ref.shape[0], where[2]
+    for out, chunk in zip(outs, CHUNKS):
+        columns = weight_columns(core, chunk)
+        out[pl.ds(pl.multiple_of(core * rows, 16), rows), :] = own_ref[:, columns]
+        out[pl.ds(pl.multiple_of((1 - core) * rows, 16), rows), :] = got_ref[:, columns]
+
+
+def whole_rows(where, own, got):
+    outs = [jax.ShapeDtypeStruct((2 * own.shape[0], heads * HD), own.dtype) for _, heads in CHUNKS]
+    return list(on_chip(whole_rows_kernel, "whole_rows", outs, where, own, got))
+
+
+def project_kernel(counts, where, keep, other, other_2, *refs):
+    parts = []
+    for count in counts:
+        parts.append(refs[:count])
+        refs = refs[count:]
+    near, direct, forwarded, before = parts
+    mine, theirs = refs[:2]
     plane = where[3]
-    count, extra = direct[0].shape[0], forwarded.shape[1]
+    weights = list(enumerate(near))
+    for i, piece in enumerate(direct):
+        count, rows = piece.shape[0], refs[2].shape[1]
+        whole = refs[2].at[i]
+        whole[pl.ds(pl.multiple_of(plane * (rows - count), 16), count), :] = piece[...]
+        whole[pl.ds(pl.multiple_of((1 - plane) * count, 16), rows - count), :] = forwarded[0][i]
+        weights.append((2 + i, whole))
     total = None
-    for j in range(2 + len(direct)):
-        if j == 0:
-            weight = own[:, columns]
-        elif j == 1:
-            weight = near[:, columns]
-        else:
-            far = whole.at[j - 2]
-            far[pl.ds(pl.multiple_of(plane * extra, 16), count), :] = direct[j - 2][...]
-            far[pl.ds(pl.multiple_of((1 - plane) * count, 16), extra), :] = forwarded[j - 2]
-            weight = far[...]
+    if before:
+        total = jnp.concatenate([ref[i] for ref in before for i in range(2)], axis=0)
+    for j, weight in weights:
         place = where[0] ^ j
         left = jnp.concatenate([keep[0, place], keep[1, place], other[place], other_2[place]], axis=0)
-        product = jnp.dot(left, weight, preferred_element_type=jnp.float32)
+        product = jnp.dot(left, weight[...], preferred_element_type=jnp.float32)
         total = product if total is None else total + product
     for i in range(2):
         mine[i] = total[i * ROWS : (i + 1) * ROWS]
         theirs[i] = total[(2 + i) * ROWS : (3 + i) * ROWS]
 
 
-def project(where, rows_of_x, chunk, own, near, direct, forwarded):
-    width = chunk[1] * HD
+def project(where, rows_of_x, near=(), direct=(), forwarded=(), before=()):
+    width = (near or direct)[0].shape[1]
     out = jax.ShapeDtypeStruct((2, ROWS, width), jnp.float32)
+    scratch = []
+    if direct:
+        rows = direct[0].shape[0] + forwarded[0].shape[1]
+        scratch.append(pltpu.VMEM((len(direct), rows, width), jnp.bfloat16))
+    operands = [near, direct, forwarded, before]
     return on_chip(
-        functools.partial(project_kernel, columns_of(chunk)),
+        functools.partial(project_kernel, [len(part) for part in operands]),
         "project",
         [out, out],
         where,
         *rows_of_x,
-        own,
-        near,
-        forwarded,
-        *direct,
-        scratch=[pltpu.VMEM((len(direct), own.shape[0], width), jnp.bfloat16)],
+        *[array for part in operands for array in part],
+        scratch=scratch,
     )
 
 
@@ -244,7 +269,7 @@
         raw = jnp.where(first_core, here, away)
         mean = jnp.mean(raw * raw, axis=1, keepdims=True)
         keys = (raw * lax.rsqrt(mean + 1e-06) * gain_ref[...]).astype(jnp.bfloat16)
-        values = jnp.where(first_core, away, here).T.astype(jnp.bfloat16)
+        values = jnp.where(first_core, away, here).astype(jnp.bfloat16).T
         pairs = range(0, SHARED, 2)
         products = [scores_of(keys, pair_queries(q_ref, (head + k) * SHARED + g)) for g in pairs]
         for g, scores in zip(pairs, products):
@@ -257,8 +282,9 @@
             total = jnp.sum(weights, axis=0, keepdims=True) + faded * ml_ref[1:2, cols]
             acc = jnp.dot(values, weights.astype(jnp.bfloat16), preferred_element_type=jnp.float32)
             acc = (acc + faded * acc_ref[:, cols]) * (live / total)
-            built[k, :, g * HD : (g + 1) * HD] = acc[:, :ROWS].T.astype(jnp.bfloat16)
-            built[k, :, (g + 1) * HD : (g + 2) * HD] = acc[:, ROWS:].T.astype(jnp.bfloat16)
+            acc = acc.astype(jnp.bfloat16)
+            built[k, :, g * HD : (g + 1) * HD] = acc[:, :ROWS].T
+            built[k, :, (g + 1) * HD : (g + 2) * HD] = acc[:, ROWS:].T
         place = result.at[:, pl.ds((head + k) * GROUP, GROUP)]
         copies.append(pltpu.make_async_copy(built.at[k], place, sem.at[k]))
         copies[-1].start()
@@ -310,24 +336,25 @@
     for _ in range(cycle - 1):
         caches.append(lax.ppermute(caches[-1], "blk", [(i, (i + 1) % cycle) for i in range(cycle)]))
 
-    own, got_weight = tie((own_half(where, kv_weight), got_weight))
-    whole, far = pack_weight(where, own, got_weight)
+    far = [far_rows(where, kv_weight, got_weight, 0)]
+    whole = whole_rows(where, kv_weight, got_weight)
+    far.append(far_rows(where, kv_weight, got_weight, 1))
 
     def send(far):
         return [xor_swap(far, "z", j) for j in range(2, steps)]
 
     def forward(i):
-        helped, direct = row_split(whole.shape[0], i)
+        helped, direct = row_split(whole[0].shape[0], i)
         parts = [lax.dynamic_slice_in_dim(p, plane * (direct - helped), helped, axis=0) for p in sent[i]]
-        return xor_swap(jnp.stack(parts), "blk", 1)
+        return [xor_swap(jnp.stack(parts), "blk", 1)]
 
     sent = [send(far[0])]
-    near = xor_swap(whole, "z", 1)
-    got_x, whole = tie((got_x, whole))
+    near = [xor_swap(whole[0], "z", 1)]
+    got_x, whole[1] = tie((got_x, whole[1]))
     keep, given = pack_rows(where, x, got_x, y, steps)
     other = xor_swap(given, "y", 1)
 
-    block_table, _ = tie((block_table, whole))
+    block_table, _ = tie((block_table, whole[0]))
     infos = []
     for stride in range(cycle):
         owner = lax.rem(holder + cycle - stride, cycle)
@@ -335,32 +362,34 @@
         listed = lax.dynamic_index_in_dim(block_table[0], place // BLOCK, axis=1, keepdims=False)
         infos.append(jnp.concatenate([place[None], prompt_lengths, listed]).astype(jnp.int32))
 
-    query, _, _ = tie((query, whole, given))
+    query, _, _ = tie((query, whole[0], given))
     state = prompt_attention(infos[0], query, caches[0], None, 0, KVH)
 
-    sent[0], state, far[1] = tie((sent[0], state, far[1]))
-    sent.append(send(far[1]))
-    sent[0], caches = tie((sent[0], caches))
+    sent.append([])
+    for j, piece in enumerate(sent[0], 2):
+        piece, far[1], state = tie((piece, far[1], state))
+        sent[0][j - 2] = piece
+        sent[1].append(xor_swap(far[1], "z", j))
+    sent[0], caches, whole[1] = tie((sent[0], caches, whole[1]))
+    near.append(xor_swap(whole[1], "z", 1))
+    forwarded = [forward(0)]
     state, other = tie((state, other))
     rows_of_x = [keep, other, xor_swap(other, "core", 1)]
-    forwarded = [forward(0)]
     for stride in range(1, cycle):
         state = prompt_attention(infos[stride], query, caches[stride], state, 0, KVH)
-    forwarded[0], state = tie((forwarded[0], state))
-
-    def sums(i):
-        return project(where, rows_of_x, CHUNKS[i], whole, near, sent[i], forwarded[i])
 
     def owners(mine, theirs):
         there = [xor_swap(theirs[1:], ("y", "core"), 3), xor_swap(mine[1:], "core", 1)]
         return xor_swap(theirs[:1], "y", 1), there
 
-    mine_0, theirs_0 = sums(0)
-    sent[1], mine_0 = tie((sent[1], mine_0))
+    forwarded[0], state = tie((forwarded[0], state))
+    mine_0, theirs_0 = project(where, rows_of_x, [whole[0], near[0]], sent[0], forwarded[0])
+    sent[1], mine_0, theirs_0 = tie((sent[1], mine_0, theirs_0))
     forwarded.append(forward(1))
     here_0, there_0 = owners(mine_0, theirs_0)
-    forwarded[1], mine_0 = tie((forwarded[1], mine_0))
-    mine_1, theirs_1 = sums(1)
+    early = project(where, rows_of_x, [whole[1], near[1]])
+    forwarded[1], early = tie((forwarded[1], early))
+    mine_1, theirs_1 = project(where, rows_of_x, (), sent[1], forwarded[1], early)
     here_0, there_0, mine_1, theirs_1 = tie((here_0, there_0, mine_1, theirs_1))
     here_1, there_1 = owners(mine_1, theirs_1)
     info = jnp.concatenate([resp_lengths[0], core[None]]).astype(jnp.int32)

time: 61.9 us -> 63.8 us (1.031)
  waiting for transfers between devices: 14.8 us -> 17 us
    ppermute x1, waiting for transfers between devices: 0.01 us -> 1.69 us  [per_device(): lax.ppermute(caches[-1], 'blk', [(i, (i + 1) % cycle) for i in range(cycl...]
    pallas_call x5 -> x7, Pallas kernels: 5.44 us -> 6.26 us  [on_chip(): pl.pallas_call(kernel, in_specs=[SMEM] + [VMEM] * len(operands), out_spec...]
    pallas_call x2, Pallas kernels: 11.7 us -> 11.1 us  [prompt_attention(): pl.pallas_call(functools.partial(prompt_kernel, first), grid_spec=pltpu.P...]
    ppermute x17 -> x18, waiting for transfers between devices: 14.8 us -> 15.3 us  [xor_swap(): lax.ppermute(array, axis, [(i, i ^ by) for i in range(lax.axis_size(axis))])]
    ppermute x17 -> x18, starting transfers between devices: 19.5 us -> 19.1 us  [xor_swap(): lax.ppermute(array, axis, [(i, i ^ by) for i in range(lax.axis_size(axis))])]
  transfers between devices with their start and end apart: 18 -> 19, of which waited for: 7 -> 8; matrix products, arithmetic and copies ran while one was open for 1% -> 1% of each run, Pallas kernels for 32% -> 31%
where the time goes in v11:
time: 63.8 us; the launch traced here: 63.6 us
  starting transfers between devices  22.1 us (35%)
  Pallas kernels  21.9 us (34%)
  waiting for transfers between devices  17 us (27%)
  local copies, waits for them, and re-layouts  1.4 us (2%)
  between operations  0.9 us (1%)
    ppermute x18, starting transfers between devices, xor_swap(): lax.ppermute(array, axis, [(i, i ^ by) for i in range(lax.axis_size(axis))])  19.1 us
    ppermute x18, waiting for transfers between devices, xor_swap(): lax.ppermute(array, axis, [(i, i ^ by) for i in range(lax.axis_size(axis))])  15.3 us
    pallas_call x2, Pallas kernels, prompt_attention(): pl.pallas_call(functools.partial(prompt_kernel, first), grid_spec=pltpu.P...  11.1 us
    pallas_call x7, Pallas kernels, on_chip(): pl.pallas_call(kernel, in_specs=[SMEM] + [VMEM] * len(operands), out_spec...  6.26 us
    pallas_call x2, Pallas kernels, final_attention(): pl.pallas_call(functools.partial(final_kernel, chunk, offset), in_specs=s...  4.61 us
    ppermute x1, starting transfers between devices, per_device(): lax.ppermute(caches[-1], 'blk', [(i, (i + 1) % cycle) for i in range(cycl...  2.94 us
    ppermute x1, waiting for transfers between devices, per_device(): lax.ppermute(caches[-1], 'blk', [(i, (i + 1) % cycle) for i in range(cycl...  1.69 us
  transfers between devices with their start and end apart: 19, of which 8 were waited for; matrix products, arithmetic and copies ran while one was open for 1% of the time, Pallas kernels for 31%

profile of v11, /device:TPU:0, one launch (start us, length us, event | category | flops | bytes accessed | tf_op | source)
XLA Modules:
  0.0 63.6 jit_solution(11008927269425784178)
XLA Ops:
  0.5 2.9 %collective-permute-start.4 = (bf16[512,1024]{1,0:T(8,128)(2,1)}, bf16[512,1024]{1,0:T(8,128)(2,1)S(1)}, u32[]{:S(2)}, u32[]{:S(2)}) collective-permute-start(bf16[512,1024]{1,0:T(8,128)(2,1)} %bitcast.28), channel_id=1, source_target_pairs={{0,1},{1,0},{2,3},{3,2},{4,5},{5,4},{6,7},{7,6},{8,9},{9,8},{10,11... | collective-permute-start | bytes 3145736 | tf_op jit(solution)/shard_map/ppermute | solution.py:337
  4.3 1.1 %copy-done = bf16[320,1024]{1,0:T(8,128)(2,1)S(1)} copy-done((bf16[320,1024]{1,0:T(8,128)(2,1)S(1)}, bf16[320,1024]{1,0:T(8,128)(2,1)}, u32[]{:S(2)}) %copy-start) | copy-done | bytes 655384
  6.0 5.0 %collective-permute-start.3 = (bf16[320,256]{1,0:T(8,128)(2,1)S(1)}, bf16[320,256]{1,0:T(8,128)(2,1)S(1)}, u32[]{:S(2)}, u32[]{:S(2)}) collective-permute-start(bf16[320,256]{1,0:T(8,128)(2,1)S(1)} %far_rows.2), channel_id=1, source_target_pairs={{0,24},{8,16},{16,8},{24,0},{1,25},{9,17},{17,9},{25,1},{2,26},{10... | collective-permute-start | bytes 491528 | tf_op jit(solution)/shard_map/ppermute | solution.py:318
  11.6 0.7 %collective-permute-start.10 = (bf16[640,256]{1,0:T(8,128)(2,1)S(1)}, bf16[640,256]{1,0:T(8,128)(2,1)S(1)}, u32[]{:S(2)}, u32[]{:S(2)}) collective-permute-start(bf16[640,256]{1,0:T(8,128)(2,1)S(1)} %get-tuple-element.53.refs_0_), channel_id=1, source_target_pairs={{0,8},{8,0},{16,24},{24,16},{1,9},{9,1},{17,25},{25,17},{2,10},{10... | collective-permute-start | bytes 983048 | tf_op jit(solution)/shard_map/ppermute | solution.py:318
  14.0 1.7 %collective-permute-start.6 = (bf16[4,128,640]{2,1,0:T(8,128)(2,1)S(1)}, bf16[4,128,640]{2,1,0:T(8,128)(2,1)S(1)}, u32[]{:S(2)}, u32[]{:S(2)}) collective-permute-start(bf16[4,128,640]{2,1,0:T(8,128)(2,1)S(1)} %get-tuple-element.56), channel_id=1, source_target_pairs={{0,4},{4,0},{1,5},{5,1},{2,6},{6,2},{3,7},{7,3},{8,12},{12,8},{9,1... | collective-permute-start | bytes 1966088 | tf_op jit(solution)/shard_map/ppermute | solution.py:318
  15.7 5.4 %prompt_attention.2 = (f32[128,4096]{1,0:T(8,128)S(1)}, f32[8,4096]{1,0:T(8,128)S(1)}) custom-call(s32[4]{0:T(128)S(1)} %get-tuple-element.107.info, bf16[128,4096]{1,0:T(8,128)(2,1)S(1)} %bitcast.16, bf16[512,1024]{1,0:T(8,128)(2,1)S(1)} %bitcast.29, bf16[512,1024]{1,0:T(8,128)(2,1)S(1)} %bitcast.30), custom_call_target="tpu_custom_call" | custom-call | flops 17179869184 | bytes 1024 | tf_op jit(solution)/shard_map/prompt_attention/pallas_call | solution.py:95
  21.1 4.1 %collective-permute-done.2.refs_2_ = bf16[320,256]{1,0:T(8,128)(2,1)S(1)} collective-permute-done((bf16[320,256]{1,0:T(8,128)(2,1)S(1)}, bf16[320,256]{1,0:T(8,128)(2,1)S(1)}, u32[]{:S(2)}, u32[]{:S(2)}) %collective-permute-start.2) | collective-permute-done | bytes 163872 | tf_op jit(solution)/shard_map/ppermute | solution.py:318
  25.3 1.7 %collective-permute-done.4.k_ref.v_ref = bf16[512,1024]{1,0:T(8,128)(2,1)S(1)} collective-permute-done((bf16[512,1024]{1,0:T(8,128)(2,1)}, bf16[512,1024]{1,0:T(8,128)(2,1)S(1)}, u32[]{:S(2)}, u32[]{:S(2)}) %collective-permute-start.4) | collective-permute-done | bytes 1048608 | tf_op jit(solution)/shard_map/ppermute | solution.py:337
  27.0 3.9 %collective-permute-start.8 = (bf16[320,256]{1,0:T(8,128)(2,1)S(1)}, bf16[320,256]{1,0:T(8,128)(2,1)S(1)}, u32[]{:S(2)}, u32[]{:S(2)}) collective-permute-start(bf16[320,256]{1,0:T(8,128)(2,1)S(1)} %far_rows.3), channel_id=1, source_target_pairs={{0,24},{8,16},{16,8},{24,0},{1,25},{9,17},{17,9},{25,1},{2,26},{10... | collective-permute-start | bytes 491528 | tf_op jit(solution)/shard_map/ppermute | solution.py:318
  30.9 1.6 %collective-permute-start.5 = (bf16[2,320,256]{2,1,0:T(8,128)(2,1)S(1)}, bf16[2,320,256]{2,1,0:T(8,128)(2,1)S(1)}, u32[]{:S(2)}, u32[]{:S(2)}) collective-permute-start(bf16[2,320,256]{2,1,0:T(8,128)(2,1)S(1)} %pad_maximum_fusion), channel_id=1, source_target_pairs={{0,1},{1,0},{2,3},{3,2},{4,5},{5,4},{6,7},{7,6},{8,9},{9,8},{10,11... | collective-permute-start | bytes 983048 | tf_op jit(solution)/shard_map/ppermute | solution.py:318
  32.4 5.6 %prompt_attention.3 = (f32[128,4096]{1,0:T(8,128)S(1)}, f32[8,4096]{1,0:T(8,128)S(1)}) custom-call(s32[4]{0:T(128)S(1)} %get-tuple-element.108.info, bf16[128,4096]{1,0:T(8,128)(2,1)S(1)} %bitcast.17, bf16[512,1024]{1,0:T(8,128)(2,1)S(1)} %collective-permute-done.4.k_ref.v_ref, bf16[512,1024]{1,0:T(8,128)(2,1)S(1)} %collective-permute-done.4.k_ref.v_ref, ...), custom_call_target="tpu_custom_call" | custom-call | flops 8589934592 | bytes 1024 | tf_op jit(solution)/shard_map/prompt_attention/pallas_call | solution.py:95
  38.1 1.3 %collective-permute-done.5.refs_4_ = bf16[2,320,256]{2,1,0:T(8,128)(2,1)S(1)} collective-permute-done((bf16[2,320,256]{2,1,0:T(8,128)(2,1)S(1)}, bf16[2,320,256]{2,1,0:T(8,128)(2,1)S(1)}, u32[]{:S(2)}, u32[]{:S(2)}) %collective-permute-start.5) | collective-permute-done | bytes 327712 | tf_op jit(solution)/shard_map/ppermute | solution.py:318
  39.4 1.5 %project.3 = (f32[2,128,256]{2,1,0:T(8,128)S(1)}, f32[2,128,256]{2,1,0:T(8,128)S(1)}) custom-call(s32[4]{0:T(128)S(1)} %pad_add_fusion.1.where, bf16[2,4,128,640]{3,2,1,0:T(8,128)(2,1)S(1)} %get-tuple-element.79.keep, bf16[4,128,640]{2,1,0:T(8,128)(2,1)S(1)} %collective-permute-done.6.other, bf16[4,128,640]{2,1,0:T(8,128)(2,1)S(1)} %collective-permute-done.9.other_2, ...), custom_call_target="tpu_custom_call" | custom-call | flops 1024 | bytes 1024 | tf_op jit(solution)/shard_map/project/pallas_call | solution.py:118
  41.1 1.6 %collective-permute-start.14 = (bf16[2,320,256]{2,1,0:T(8,128)(2,1)S(1)}, bf16[2,320,256]{2,1,0:T(8,128)(2,1)S(1)}, u32[]{:S(2)}, u32[]{:S(2)}) collective-permute-start(bf16[2,320,256]{2,1,0:T(8,128)(2,1)S(1)} %pad_maximum_fusion.1), channel_id=1, source_target_pairs={{0,1},{1,0},{2,3},{3,2},{4,5},{5,4},{6,7},{7,6},{8,9},{9,8},{10,11... | collective-permute-start | bytes 983048 | tf_op jit(solution)/shard_map/ppermute | solution.py:318
  42.7 1.4 %collective-permute-start.12 = (f32[1,128,256]{2,1,0:T(8,128)S(1)}, f32[1,128,256]{2,1,0:T(8,128)S(1)}, u32[]{:S(2)}, u32[]{:S(2)}) collective-permute-start(f32[1,128,256]{2,1,0:T(8,128)S(1)} %get-tuple-element.105), channel_id=1, source_target_pairs={{0,6},{2,4},{4,2},{6,0},{1,7},{3,5},{5,3},{7,1},{8,14},{10,12},{12... | collective-permute-start | bytes 393224 | tf_op jit(solution)/shard_map/ppermute | solution.py:318
  44.6 3.7 %collective-permute-done.15.refs_1_ = bf16[640,256]{1,0:T(8,128)(2,1)S(1)} collective-permute-done((bf16[640,256]{1,0:T(8,128)(2,1)S(1)}, bf16[640,256]{1,0:T(8,128)(2,1)S(1)}, u32[]{:S(2)}, u32[]{:S(2)}) %collective-permute-start.15) | collective-permute-done | bytes 327712 | tf_op jit(solution)/shard_map/ppermute | solution.py:318
  48.3 1.1 %project.4 = (f32[2,128,256]{2,1,0:T(8,128)S(1)}, f32[2,128,256]{2,1,0:T(8,128)S(1)}) custom-call(s32[4]{0:T(128)S(1)} %pad_add_fusion.1.where, bf16[2,4,128,640]{3,2,1,0:T(8,128)(2,1)S(1)} %get-tuple-element.79.keep, bf16[4,128,640]{2,1,0:T(8,128)(2,1)S(1)} %collective-permute-done.6.other, bf16[4,128,640]{2,1,0:T(8,128)(2,1)S(1)} %collective-permute-done.9.other_2, ...), custom_call_target="tpu_custom_call" | custom-call | flops 1024 | bytes 1024 | tf_op jit(solution)/shard_map/project/pallas_call | solution.py:118
  49.4 1.9 %collective-permute-done.14.refs_2_ = bf16[2,320,256]{2,1,0:T(8,128)(2,1)S(1)} collective-permute-done((bf16[2,320,256]{2,1,0:T(8,128)(2,1)S(1)}, bf16[2,320,256]{2,1,0:T(8,128)(2,1)S(1)}, u32[]{:S(2)}, u32[]{:S(2)}) %collective-permute-start.14) | collective-permute-done | bytes 327712 | tf_op jit(solution)/shard_map/ppermute | solution.py:318
  51.3 1.1 %project.5 = (f32[2,128,256]{2,1,0:T(8,128)S(1)}, f32[2,128,256]{2,1,0:T(8,128)S(1)}) custom-call(s32[4]{0:T(128)S(1)} %pad_add_fusion.1.where, bf16[2,4,128,640]{3,2,1,0:T(8,128)(2,1)S(1)} %get-tuple-element.79.keep, bf16[4,128,640]{2,1,0:T(8,128)(2,1)S(1)} %collective-permute-done.6.other, bf16[4,128,640]{2,1,0:T(8,128)(2,1)S(1)} %collective-permute-done.9.other_2, ...), custom_call_target="tpu_custom_call" | custom-call | flops 1024 | bytes 1024 | tf_op jit(solution)/shard_map/project/pallas_call | solution.py:118
  52.6 1.6 %collective-permute-start.17 = (f32[1,128,256]{2,1,0:T(8,128)S(1)}, f32[1,128,256]{2,1,0:T(8,128)S(1)}, u32[]{:S(2)}, u32[]{:S(2)}) collective-permute-start(f32[1,128,256]{2,1,0:T(8,128)S(1)} %get-tuple-element.103), channel_id=1, source_target_pairs={{0,6},{2,4},{4,2},{6,0},{1,7},{3,5},{5,3},{7,1},{8,14},{10,12},{12... | collective-permute-start | bytes 393224 | tf_op jit(solution)/shard_map/ppermute | solution.py:318
  54.8 2.3 %final_attention.2.refs_0_ = bf16[128,4096]{1,0:T(8,128)(2,1)} custom-call(s32[3]{0:T(128)S(1)} %pad_add_fusion.info, f32[1,128]{1,0:T(1,128)S(1)} %bitcast.26, bf16[128,4096]{1,0:T(8,128)(2,1)S(1)} %bitcast.18, f32[128,4096]{1,0:T(8,128)S(1)} %get-tuple-element.76.acc_ref, f32[8,4096]{1,0:T(8,128)S(1)} %get-tuple-element.77.ml_ref, ...), custom_call_target="tpu_custom_call" | custom-call | flops 1024 | bytes 1024 | tf_op jit(solution)/shard_map/final_attention/pallas_call | solution.py:304
  57.2 0.9 %collective-permute-done.17.there = f32[1,128,256]{2,1,0:T(8,128)S(1)} collective-permute-done((f32[1,128,256]{2,1,0:T(8,128)S(1)}, f32[1,128,256]{2,1,0:T(8,128)S(1)}, u32[]{:S(2)}, u32[]{:S(2)}) %collective-permute-start.17) | collective-permute-done | bytes 131104 | tf_op jit(solution)/shard_map/ppermute | solution.py:318
  58.1 3.2 %collective-permute-done.16.theirs = f32[1,128,256]{2,1,0:T(8,128)S(1)} collective-permute-done((f32[1,128,256]{2,1,0:T(8,128)S(1)}, f32[1,128,256]{2,1,0:T(8,128)S(1)}, u32[]{:S(2)}, u32[]{:S(2)}) %collective-permute-start.16) | collective-permute-done | bytes 131104 | tf_op jit(solution)/shard_map/ppermute | solution.py:318
  61.3 2.3 %final_attention.3 = bf16[128,4096]{1,0:T(8,128)(2,1)} custom-call(s32[3]{0:T(128)S(1)} %pad_add_fusion.info, f32[1,128]{1,0:T(1,128)S(1)} %bitcast.27, bf16[128,4096]{1,0:T(8,128)(2,1)S(1)} %bitcast.19, f32[128,4096]{1,0:T(8,128)S(1)} %get-tuple-element.76.acc_ref, f32[8,4096]{1,0:T(8,128)S(1)} %get-tuple-element.77.ml_ref, ...), custom_call_target="tpu_custom_call", output_to_operand_aliasing={{}: (9, {})} | custom-call | flops 1024 | bytes 1024 | tf_op jit(solution)/shard_map/final_attention/pallas_call | solution.py:304
  (49 shorter events, 4.9 us)
Async XLA Ops:
  0.0 13.2 %collective-permute-start.1 = (bf16[128,5120]{1,0:T(8,128)(2,1)}, bf16[128,5120]{1,0:T(8,128)(2,1)S(1)}, u32[]{:S(2)}, u32[]{:S(2)}) collective-permute-start(bf16[128,5120]{1,0:T(8,128)(2,1)} %bitcast.20), channel_id=1, source_target_pairs={{0,2},{2,0},{1,3},{3,1},{4,6},{6,4},{5,7},{7,5},{8,10},{10,8},{9,1... | collective-permute-start | bytes 3932168 | tf_op jit(solution)/shard_map/ppermute | solution.py:318
  0.5 3.8 %collective-permute-start = (bf16[320,1024]{1,0:T(8,128)(2,1)}, bf16[320,1024]{1,0:T(8,128)(2,1)S(1)}, u32[]{:S(2)}, u32[]{:S(2)}) collective-permute-start(bf16[320,1024]{1,0:T(8,128)(2,1)} %own_ref.5), channel_id=1, source_target_pairs={{0,2},{2,0},{1,3},{3,1},{4,6},{6,4},{5,7},{7,5},{8,10},{10,8},{9,1... | collective-permute-start | bytes 1966088 | tf_op jit(solution)/shard_map/ppermute | solution.py:318
  0.5 26.5 %collective-permute-start.4 = (bf16[512,1024]{1,0:T(8,128)(2,1)}, bf16[512,1024]{1,0:T(8,128)(2,1)S(1)}, u32[]{:S(2)}, u32[]{:S(2)}) collective-permute-start(bf16[512,1024]{1,0:T(8,128)(2,1)} %bitcast.28), channel_id=1, source_target_pairs={{0,1},{1,0},{2,3},{3,2},{4,5},{5,4},{6,7},{7,6},{8,9},{9,8},{10,11... | collective-permute-start | bytes 3145736 | tf_op jit(solution)/shard_map/ppermute | solution.py:337
  5.9 7.0 %copy-start.5 = (s32[1,2,2]{2,1,0:T(2,128)S(1)}, s32[1,2,2]{2,1,0:T(2,128)}, u32[]{:S(2)}) copy-start(s32[1,2,2]{2,1,0:T(2,128)} %param.14) | copy-start | bytes 52
  5.9 7.3 %copy-start.2 = (bf16[1,128,5120]{2,1,0:T(8,128)(2,1)S(1)}, bf16[1,128,5120]{2,1,0:T(8,128)(2,1)}, u32[]{:S(2)}) copy-start(bf16[1,128,5120]{2,1,0:T(8,128)(2,1)} %param.8) | copy-start | bytes 3932164
  6.0 19.3 %collective-permute-start.3 = (bf16[320,256]{1,0:T(8,128)(2,1)S(1)}, bf16[320,256]{1,0:T(8,128)(2,1)S(1)}, u32[]{:S(2)}, u32[]{:S(2)}) collective-permute-start(bf16[320,256]{1,0:T(8,128)(2,1)S(1)} %far_rows.2), channel_id=1, source_target_pairs={{0,24},{8,16},{16,8},{24,0},{1,25},{9,17},{17,9},{25,1},{2,26},{10... | collective-permute-start | bytes 491528 | tf_op jit(solution)/shard_map/ppermute | solution.py:318
  11.0 14.3 %collective-permute-start.2 = (bf16[320,256]{1,0:T(8,128)(2,1)S(1)}, bf16[320,256]{1,0:T(8,128)(2,1)S(1)}, u32[]{:S(2)}, u32[]{:S(2)}) collective-permute-start(bf16[320,256]{1,0:T(8,128)(2,1)S(1)} %far_rows.2), channel_id=1, source_target_pairs={{0,16},{8,24},{16,0},{24,8},{1,17},{9,25},{17,1},{25,9},{2,18},{10... | collective-permute-start | bytes 491528 | tf_op jit(solution)/shard_map/ppermute | solution.py:318
  11.6 27.8 %collective-permute-start.10 = (bf16[640,256]{1,0:T(8,128)(2,1)S(1)}, bf16[640,256]{1,0:T(8,128)(2,1)S(1)}, u32[]{:S(2)}, u32[]{:S(2)}) collective-permute-start(bf16[640,256]{1,0:T(8,128)(2,1)S(1)} %get-tuple-element.53.refs_0_), channel_id=1, source_target_pairs={{0,8},{8,0},{16,24},{24,16},{1,9},{9,1},{17,25},{25,17},{2,10},{10... | collective-permute-start | bytes 983048 | tf_op jit(solution)/shard_map/ppermute | solution.py:318
  13.2 2.5 %copy-start.1 = (bf16[1,128,4096]{2,1,0:T(8,128)(2,1)S(1)}, bf16[1,128,4096]{2,1,0:T(8,128)(2,1)}, u32[]{:S(2)}) copy-start(bf16[1,128,4096]{2,1,0:T(8,128)(2,1)} %param.9) | copy-start | bytes 3145732
  14.0 18.5 %collective-permute-start.6 = (bf16[4,128,640]{2,1,0:T(8,128)(2,1)S(1)}, bf16[4,128,640]{2,1,0:T(8,128)(2,1)S(1)}, u32[]{:S(2)}, u32[]{:S(2)}) collective-permute-start(bf16[4,128,640]{2,1,0:T(8,128)(2,1)S(1)} %get-tuple-element.56), channel_id=1, source_target_pairs={{0,4},{4,0},{1,5},{5,1},{2,6},{6,2},{3,7},{7,3},{8,12},{12,8},{9,1... | collective-permute-start | bytes 1966088 | tf_op jit(solution)/shard_map/ppermute | solution.py:318
  25.3 15.7 %collective-permute-start.7 = (bf16[320,256]{1,0:T(8,128)(2,1)S(1)}, bf16[320,256]{1,0:T(8,128)(2,1)S(1)}, u32[]{:S(2)}, u32[]{:S(2)}) collective-permute-start(bf16[320,256]{1,0:T(8,128)(2,1)S(1)} %far_rows.3), channel_id=1, source_target_pairs={{0,16},{8,24},{16,0},{24,8},{1,17},{9,25},{17,1},{25,9},{2,18},{10... | collective-permute-start | bytes 491528 | tf_op jit(solution)/shard_map/ppermute | solution.py:318
  27.0 14.0 %collective-permute-start.8 = (bf16[320,256]{1,0:T(8,128)(2,1)S(1)}, bf16[320,256]{1,0:T(8,128)(2,1)S(1)}, u32[]{:S(2)}, u32[]{:S(2)}) collective-permute-start(bf16[320,256]{1,0:T(8,128)(2,1)S(1)} %far_rows.3), channel_id=1, source_target_pairs={{0,24},{8,16},{16,8},{24,0},{1,25},{9,17},{17,9},{25,1},{2,26},{10... | collective-permute-start | bytes 491528 | tf_op jit(solution)/shard_map/ppermute | solution.py:318
  30.9 8.6 %collective-permute-start.5 = (bf16[2,320,256]{2,1,0:T(8,128)(2,1)S(1)}, bf16[2,320,256]{2,1,0:T(8,128)(2,1)S(1)}, u32[]{:S(2)}, u32[]{:S(2)}) collective-permute-start(bf16[2,320,256]{2,1,0:T(8,128)(2,1)S(1)} %pad_maximum_fusion), channel_id=1, source_target_pairs={{0,1},{1,0},{2,3},{3,2},{4,5},{5,4},{6,7},{7,6},{8,9},{9,8},{10,11... | collective-permute-start | bytes 983048 | tf_op jit(solution)/shard_map/ppermute | solution.py:318
  32.4 7.0 %collective-permute-start.9 = (bf16[4,128,640]{2,1,0:T(8,128)(2,1)S(1)}, bf16[4,128,640]{2,1,0:T(8,128)(2,1)S(1)}, u32[]{:S(2)}, u32[]{:S(2)}) collective-permute-start(bf16[4,128,640]{2,1,0:T(8,128)(2,1)S(1)} %collective-permute-done.6.other), channel_id=1, source_target_pairs={{0,2},{2,0},{1,3},{3,1},{4,6},{6,4},{5,7},{7,5},{8,10},{10,8},{9,1... | collective-permute-start | bytes 1966088 | tf_op jit(solution)/shard_map/ppermute | solution.py:318
  39.4 8.9 %collective-permute-start.15 = (bf16[640,256]{1,0:T(8,128)(2,1)S(1)}, bf16[640,256]{1,0:T(8,128)(2,1)S(1)}, u32[]{:S(2)}, u32[]{:S(2)}) collective-permute-start(bf16[640,256]{1,0:T(8,128)(2,1)S(1)} %get-tuple-element.88.refs_0_), channel_id=1, source_target_pairs={{0,8},{8,0},{16,24},{24,16},{1,9},{9,1},{17,25},{25,17},{2,10},{10... | collective-permute-start | bytes 983048 | tf_op jit(solution)/shard_map/ppermute | solution.py:318
  41.0 11.5 %collective-permute-start.13 = (f32[1,128,256]{2,1,0:T(8,128)S(1)}, f32[1,128,256]{2,1,0:T(8,128)S(1)}, u32[]{:S(2)}, u32[]{:S(2)}) collective-permute-start(f32[1,128,256]{2,1,0:T(8,128)S(1)} %slice.20), channel_id=1, source_target_pairs={{0,2},{2,0},{1,3},{3,1},{4,6},{6,4},{5,7},{7,5},{8,10},{10,8},{9,1... | collective-permute-start | bytes 393224 | tf_op jit(solution)/shard_map/ppermute | solution.py:318
  41.1 10.2 %collective-permute-start.14 = (bf16[2,320,256]{2,1,0:T(8,128)(2,1)S(1)}, bf16[2,320,256]{2,1,0:T(8,128)(2,1)S(1)}, u32[]{:S(2)}, u32[]{:S(2)}) collective-permute-start(bf16[2,320,256]{2,1,0:T(8,128)(2,1)S(1)} %pad_maximum_fusion.1), channel_id=1, source_target_pairs={{0,1},{1,0},{2,3},{3,2},{4,5},{5,4},{6,7},{7,6},{8,9},{9,8},{10,11... | collective-permute-start | bytes 983048 | tf_op jit(solution)/shard_map/ppermute | solution.py:318
  42.7 9.8 %collective-permute-start.12 = (f32[1,128,256]{2,1,0:T(8,128)S(1)}, f32[1,128,256]{2,1,0:T(8,128)S(1)}, u32[]{:S(2)}, u32[]{:S(2)}) collective-permute-start(f32[1,128,256]{2,1,0:T(8,128)S(1)} %get-tuple-element.105), channel_id=1, source_target_pairs={{0,6},{2,4},{4,2},{6,0},{1,7},{3,5},{5,3},{7,1},{8,14},{10,12},{12... | collective-permute-start | bytes 393224 | tf_op jit(solution)/shard_map/ppermute | solution.py:318
  44.1 8.4 %collective-permute-start.11 = (f32[1,128,256]{2,1,0:T(8,128)S(1)}, f32[1,128,256]{2,1,0:T(8,128)S(1)}, u32[]{:S(2)}, u32[]{:S(2)}) collective-permute-start(f32[1,128,256]{2,1,0:T(8,128)S(1)} %get-tuple-element.106), channel_id=1, source_target_pairs={{0,4},{4,0},{1,5},{5,1},{2,6},{6,2},{3,7},{7,3},{8,12},{12,8},{9,1... | collective-permute-start | bytes 393224 | tf_op jit(solution)/shard_map/ppermute | solution.py:318
  51.3 3.5 %copy-start.6 = (s32[1,2]{1,0:T(1,128)S(1)}, s32[1,2]{1,0:T(1,128)}, u32[]{:S(2)}) copy-start(s32[1,2]{1,0:T(1,128)} %param.15) | copy-start | bytes 28
  51.3 3.5 %copy-start.3 = (f32[128]{0:T(128)S(1)}, f32[128]{0:T(128)}, u32[]{:S(2)}) copy-start(f32[128]{0:T(128)} %param.12) | copy-start | bytes 1540
  52.5 4.6 %collective-permute-start.18 = (f32[1,128,256]{2,1,0:T(8,128)S(1)}, f32[1,128,256]{2,1,0:T(8,128)S(1)}, u32[]{:S(2)}, u32[]{:S(2)}) collective-permute-start(f32[1,128,256]{2,1,0:T(8,128)S(1)} %slice.23), channel_id=1, source_target_pairs={{0,2},{2,0},{1,3},{3,1},{4,6},{6,4},{5,7},{7,5},{8,10},{10,8},{9,1... | collective-permute-start | bytes 393224 | tf_op jit(solution)/shard_map/ppermute | solution.py:318
  52.6 5.5 %collective-permute-start.17 = (f32[1,128,256]{2,1,0:T(8,128)S(1)}, f32[1,128,256]{2,1,0:T(8,128)S(1)}, u32[]{:S(2)}, u32[]{:S(2)}) collective-permute-start(f32[1,128,256]{2,1,0:T(8,128)S(1)} %get-tuple-element.103), channel_id=1, source_target_pairs={{0,6},{2,4},{4,2},{6,0},{1,7},{3,5},{5,3},{7,1},{8,14},{10,12},{12... | collective-permute-start | bytes 393224 | tf_op jit(solution)/shard_map/ppermute | solution.py:318
  54.3 7.0 %collective-permute-start.16 = (f32[1,128,256]{2,1,0:T(8,128)S(1)}, f32[1,128,256]{2,1,0:T(8,128)S(1)}, u32[]{:S(2)}, u32[]{:S(2)}) collective-permute-start(f32[1,128,256]{2,1,0:T(8,128)S(1)} %get-tuple-element.104), channel_id=1, source_target_pairs={{0,4},{4,0},{1,5},{5,1},{2,6},{6,2},{3,7},{7,3},{8,12},{12,8},{9,1... | collective-permute-start | bytes 393224 | tf_op jit(solution)/shard_map/ppermute | solution.py:318
  (2 other events, 3.5 us)

commit v12 on v10

--- a/solution.py
+++ b/solution.py
@@ -23,8 +23,8 @@
 NT = (((1,), (1,)), ((), ()))
 HINT = pl.CostEstimate(flops=1024, bytes_accessed=1024, transcendentals=0)
 
-CHUNKS = ((0, 2), (2, 2))
-HELP = (5, 5)
+CHUNKS = ((0, 2), (2, 1), (3, 1))
+HELP = (5, 5, 5)
 
 
 def pair_queries(q_ref, g, extra=None):
@@ -239,9 +239,14 @@
     )
 
 
-def final_kernel(chunk, offset, info, gain_ref, q_ref, acc_ref, ml_ref, mine, theirs, there, there_2, *refs):
+def final_kernel(counts, head, info, gain_ref, q_ref, acc_ref, ml_ref, *refs):
     result, built, sem = refs[-3:]
-    head, heads = chunk
+    parts = []
+    for count in counts:
+        mine, here, *away = refs[:count]
+        refs = refs[count:]
+        for column in range(0, mine.shape[2], HD):
+            parts.append((mine, here, away, slice(column, column + HD)))
     slot = lax.broadcasted_iota(jnp.int32, (ROWS, PAIR), 0)
     row = lax.broadcasted_iota(jnp.int32, (ROWS, PAIR), 1) % ROWS
     length = jnp.where(row < RLEN, info[0], info[1])
@@ -249,10 +254,9 @@
     seen = (slot >= base) & (slot <= row) & (slot - base < length)
     live = jnp.where(row - base < length, 1.0, 0.0)[0:1]
     copies = []
-    for k in range(heads):
-        part = slice(k * HD, (k + 1) * HD)
-        here = mine[0, :, part] + theirs[0, :, part]
-        away = there[0, :, part] + there_2[0, :, part]
+    for k, (mine, here, away, part) in enumerate(parts):
+        here = mine[0, :, part] + here[0, :, part]
+        away = sum(ref[0, :, part] for ref in away)
         first_core = jnp.full(here.shape, info[2]) == 0
         raw = jnp.where(first_core, here, away)
         mean = jnp.mean(raw * raw, axis=1, keepdims=True)
@@ -261,7 +265,7 @@
         pairs = range(0, SHARED, 2)
         products = [scores_of(keys, pair_queries(q_ref, (head + k) * SHARED + g)) for g in pairs]
         for g, scores in zip(pairs, products):
-            cols = slice(((offset + k) * SHARED + g) * HD, ((offset + k) * SHARED + g + 2) * HD)
+            cols = slice((k * SHARED + g) * HD, (k * SHARED + g + 2) * HD)
             scores = jnp.where(seen, scores, HIDDEN)
             before = ml_ref[0:1, cols]
             largest = jnp.maximum(jnp.max(scores, axis=0, keepdims=True), before)
@@ -279,9 +283,9 @@
         copy.wait()
 
 
-def final_attention(info, gain, query, state, offset, chunk, mine, theirs, there, result):
-    heads = chunk[1]
-    operands = [gain, query, *state, mine, theirs, *there]
+def final_attention(info, gain, query, state, head, chunks, result):
+    heads = sum(chunk[0].shape[2] for chunk in chunks) // HD
+    operands = [gain, query, *state, *[array for chunk in chunks for array in chunk]]
     specs = [SMEM] + [VMEM] * len(operands)
     aliases = {}
     if result is not None:
@@ -289,7 +293,7 @@
         specs.append(pl.BlockSpec(memory_space=pl.ANY))
         aliases = {len(operands): 0}
     return pl.pallas_call(
-        functools.partial(final_kernel, chunk, offset),
+        functools.partial(final_kernel, [len(chunk) for chunk in chunks], head),
         in_specs=specs,
         out_specs=pl.BlockSpec(memory_space=pl.ANY),
         out_shape=jax.ShapeDtypeStruct((ROWS, HQ * HD), jnp.bfloat16),
@@ -351,6 +355,16 @@
     query, _, _ = tie((query, whole[0], given))
     state = prompt_attention(infos[0], query, caches[0], None, 0, KVH)
 
+    def rest(head, state):
+        offset = head
+        for stride in range(1, cycle):
+            state = prompt_attention(infos[stride], query, caches[stride], state, head, 2, offset)
+            offset = 0
+        return state
+
+    def sums(i):
+        return project(where, rows_of_x, whole[i], near[i], sent[i], forwarded[i])
+
     sent[0], state, far[1], whole[1] = tie((sent[0], state, far[1], whole[1]))
     sent.append(send(far[1]))
     near.append(xor_swap(whole[1], "z", 1))
@@ -358,30 +372,36 @@
     forwarded = [forward(0, True)]
     state, other = tie((state, other))
     rows_of_x = [keep, other, xor_swap(other, "core", 1)]
-    for stride in range(1, cycle):
-        state = prompt_attention(infos[stride], query, caches[stride], state, 0, KVH)
-
-    def sums(i):
-        return project(where, rows_of_x, whole[i], near[i], sent[i], forwarded[i])
+    halves = [rest(0, state)]
+    sent[1], near[0], far[2], halves[0], state, rows_of_x[2] = tie((sent[1], near[0], far[2], halves[0], state, rows_of_x[2]))
+    sent.append(send(far[2]))
+    forwarded[0], sent[1], whole[2] = tie((forwarded[0], sent[1], whole[2]))
+    forwarded.append(forward(1, True))
+    near.append(xor_swap(whole[2], "z", 1))
 
     def owners(mine, theirs):
         there = [xor_swap(theirs[1:], ("y", "core"), 3), xor_swap(mine[1:], "core", 1)]
-        return xor_swap(theirs[:1], "y", 1), there
-
-    forwarded[0], state = tie((forwarded[0], state))
+        return [mine, xor_swap(theirs[:1], "y", 1), *there]
+
     mine_0, theirs_0 = sums(0)
-    sent[1], mine_0 = tie((sent[1], mine_0))
-    forwarded.append(forward(1, True))
-    here_0, there_0 = owners(mine_0, theirs_0)
+    state, mine_0 = tie((state, mine_0))
+    halves.append(rest(2, state))
+    sent[2], mine_0, halves[1] = tie((sent[2], mine_0, halves[1]))
+    forwarded.append(forward(2, True))
+    here_0 = xor_swap(theirs_0, "y", 1)
     forwarded[1], mine_0 = tie((forwarded[1], mine_0))
     mine_1, theirs_1 = sums(1)
-    here_0, there_0, mine_1, theirs_1 = tie((here_0, there_0, mine_1, theirs_1))
-    here_1, there_1 = owners(mine_1, theirs_1)
+    here_0, mine_1, theirs_1 = tie((here_0, mine_1, theirs_1))
+    first = [mine_0, here_0, xor_swap(mine_0[1:] + here_0[1:], "core", 1)]
+    here_1 = xor_swap(theirs_1, "y", 1)
+    forwarded[2], mine_1 = tie((forwarded[2], mine_1))
+    mine_2, theirs_2 = sums(2)
+    third = owners(mine_2, theirs_2)
+    second = [mine_1, here_1, xor_swap(mine_1[1:] + here_1[1:], "core", 1)]
     info = jnp.concatenate([resp_lengths[0], core[None]]).astype(jnp.int32)
     gain = key_gain[None]
-    result = final_attention(info, gain, query, state, 0, CHUNKS[0], mine_0, here_0, there_0, None)
-    result = final_attention(info, gain, query, state, 2, CHUNKS[1], mine_1, here_1, there_1, result)
-    return result[None]
+    result = final_attention(info, gain, query, halves[0], 0, [first], None)
+    return final_attention(info, gain, query, halves[1], 2, [second, third], result)[None]
 
 
 def solution(mesh):

time: 61.4 us -> 62.7 us (1.021)
  the two profiles are of different devices: /device:TPU:11 before, /device:TPU:0 now
where the time goes in v12:
time: 62.7 us; the launch traced here: 62.5 us
  starting transfers between devices  27.9 us (44%)
  Pallas kernels  24.6 us (39%)
  waiting for transfers between devices  7.3 us (12%)
  local copies, waits for them, and re-layouts  1.35 us (2%)
  between operations  0.96 us (2%)
    ppermute x23, starting transfers between devices, xor_swap(): lax.ppermute(array, axis, [(i, i ^ by) for i in range(lax.axis_size(axis))])  24.9 us
    pallas_call x3, Pallas kernels, prompt_attention(): pl.pallas_call(functools.partial(prompt_kernel, first), grid_spec=pltpu.P...  13.2 us
    ppermute x23, waiting for transfers between devices, xor_swap(): lax.ppermute(array, axis, [(i, i ^ by) for i in range(lax.axis_size(axis))])  7.3 us
    pallas_call x5, Pallas kernels, on_chip(): pl.pallas_call(kernel, in_specs=[SMEM] + [VMEM] * len(operands), out_spec...  5.63 us
    pallas_call x2, Pallas kernels, final_attention(): pl.pallas_call(functools.partial(final_kernel, [len(chunk) for chunk in c...  4.67 us
    ppermute x1, starting transfers between devices, per_device(): lax.ppermute(caches[-1], 'blk', [(i, (i + 1) % cycle) for i in range(cycl...  2.93 us
  transfers between devices with their start and end apart: 24, of which 4 were waited for; matrix products, arithmetic and copies ran while one was open for 1% of the time, Pallas kernels for 36%

profile of v12, /device:TPU:0, one launch (start us, length us, event | category | flops | bytes accessed | tf_op | source)
XLA Modules:
  0.0 62.5 jit_solution(2112131408479560814)
XLA Ops:
  0.6 2.9 %collective-permute-start.7 = (bf16[512,1024]{1,0:T(8,128)(2,1)}, bf16[512,1024]{1,0:T(8,128)(2,1)}, u32[]{:S(2)}, u32[]{:S(2)}) collective-permute-start(bf16[512,1024]{1,0:T(8,128)(2,1)} %bitcast.33), channel_id=1, source_target_pairs={{0,1},{1,0},{2,3},{3,2},{4,5},{5,4},{6,7},{7,6},{8,9},{9,8},{10,11... | collective-permute-start | bytes 3145736 | tf_op jit(solution)/shard_map/ppermute | solution.py:328
  3.5 1.1 %copy-done.2 = bf16[320,1024]{1,0:T(8,128)(2,1)S(1)} copy-done((bf16[320,1024]{1,0:T(8,128)(2,1)S(1)}, bf16[320,1024]{1,0:T(8,128)(2,1)}, u32[]{:S(2)}) %copy-start.2) | copy-done | bytes 655384
  6.0 1.2 %pack_weight.1 = (bf16[640,256]{1,0:T(8,128)(2,1)S(1)}, bf16[640,128]{1,0:T(8,128)(2,1)S(1)}, bf16[640,128]{1,0:T(8,128)(2,1)S(1)}, bf16[320,256]{1,0:T(8,128)(2...) custom-call(s32[4]{0:T(128)S(1)} %pad_add_fusion.1.where, ...), custom_call_target="tpu_custom_call", output_to_operand_aliasing={{0}: (2, {}), {1}: (3, {}), {2}: (4, {})} | custom-call | flops 1024 | bytes 1024 | tf_op jit(solution)/shard_map/pack_weight/pallas_call | solution.py:185
  7.1 2.7 %collective-permute-start.2 = (bf16[320,256]{1,0:T(8,128)(2,1)S(1)}, bf16[320,256]{1,0:T(8,128)(2,1)S(1)}, u32[]{:S(2)}, u32[]{:S(2)}) collective-permute-start(bf16[320,256]{1,0:T(8,128)(2,1)S(1)} %get-tuple-element.88), channel_id=1, source_target_pairs={{0,16},{8,24},{16,0},{24,8},{1,17},{9,25},{17,1},{25,9},{2,18},{10... | collective-permute-start | bytes 491528 | tf_op jit(solution)/shard_map/ppermute | solution.py:309
  9.8 1.3 %collective-permute-start.3 = (bf16[320,256]{1,0:T(8,128)(2,1)S(1)}, bf16[320,256]{1,0:T(8,128)(2,1)S(1)}, u32[]{:S(2)}, u32[]{:S(2)}) collective-permute-start(bf16[320,256]{1,0:T(8,128)(2,1)S(1)} %get-tuple-element.88), channel_id=1, source_target_pairs={{0,24},{8,16},{16,8},{24,0},{1,25},{9,17},{17,9},{25,1},{2,26},{10... | collective-permute-start | bytes 491528 | tf_op jit(solution)/shard_map/ppermute | solution.py:309
  12.4 1.6 %collective-permute-start.8 = (bf16[4,128,640]{2,1,0:T(8,128)(2,1)S(1)}, bf16[4,128,640]{2,1,0:T(8,128)(2,1)S(1)}, u32[]{:S(2)}, u32[]{:S(2)}) collective-permute-start(bf16[4,128,640]{2,1,0:T(8,128)(2,1)S(1)} %get-tuple-element.86), channel_id=1, source_target_pairs={{0,4},{4,0},{1,5},{5,1},{2,6},{6,2},{3,7},{7,3},{8,12},{12,8},{9,1... | collective-permute-start | bytes 1966088 | tf_op jit(solution)/shard_map/ppermute | solution.py:309
  14.0 5.4 %prompt_attention.3 = (f32[128,4096]{1,0:T(8,128)S(1)}, f32[8,4096]{1,0:T(8,128)S(1)}) custom-call(s32[4]{0:T(128)S(1)} %get-tuple-element.151.info, bf16[128,4096]{1,0:T(8,128)(2,1)S(1)} %bitcast.18, bf16[512,1024]{1,0:T(8,128)(2,1)S(1)} %bitcast.34, bf16[512,1024]{1,0:T(8,128)(2,1)S(1)} %bitcast.35), custom_call_target="tpu_custom_call" | custom-call | flops 17179869184 | bytes 1024 | tf_op jit(solution)/shard_map/prompt_attention/pallas_call | solution.py:95
  19.5 2.8 %collective-permute-done.2.refs_0_ = bf16[320,256]{1,0:T(8,128)(2,1)S(1)} collective-permute-done((bf16[320,256]{1,0:T(8,128)(2,1)S(1)}, bf16[320,256]{1,0:T(8,128)(2,1)S(1)}, u32[]{:S(2)}, u32[]{:S(2)}) %collective-permute-start.2) | collective-permute-done | bytes 163872 | tf_op jit(solution)/shard_map/ppermute | solution.py:309
  22.2 5.0 %collective-permute-start.4 = (bf16[320,128]{1,0:T(8,128)(2,1)S(1)}, bf16[320,128]{1,0:T(8,128)(2,1)S(1)}, u32[]{:S(2)}, u32[]{:S(2)}) collective-permute-start(bf16[320,128]{1,0:T(8,128)(2,1)S(1)} %get-tuple-element.94), channel_id=1, source_target_pairs={{0,16},{8,24},{16,0},{24,8},{1,17},{9,25},{17,1},{25,9},{2,18},{10... | collective-permute-start | bytes 245768 | tf_op jit(solution)/shard_map/ppermute | solution.py:309
  27.7 1.6 %collective-permute-start.12 = (bf16[2,320,256]{2,1,0:T(8,128)(2,1)S(1)}, bf16[2,320,256]{2,1,0:T(8,128)(2,1)S(1)}, u32[]{:S(2)}, u32[]{:S(2)}) collective-permute-start(bf16[2,320,256]{2,1,0:T(8,128)(2,1)S(1)} %pad_maximum_fusion), channel_id=1, source_target_pairs={{0,1},{1,0},{2,3},{3,2},{4,5},{5,4},{6,7},{7,6},{8,9},{9,8},{10,11... | collective-permute-start | bytes 983048 | tf_op jit(solution)/shard_map/ppermute | solution.py:309
  29.3 3.9 %prompt_attention.4 = (f32[128,2048]{1,0:T(8,128)S(1)}, f32[8,2048]{1,0:T(8,128)S(1)}) custom-call(s32[4]{0:T(128)S(1)} %get-tuple-element.152.info, bf16[128,4096]{1,0:T(8,128)(2,1)S(1)} %bitcast.19, bf16[512,1024]{1,0:T(8,128)(2,1)} %collective-permute-done.7.k_ref.v_ref, bf16[512,1024]{1,0:T(8,128)(2,1)} %collective-permute-done.7.k_ref.v_ref, ...), custom_call_target="tpu_custom_call" | custom-call | flops 8589934592 | bytes 1024 | tf_op jit(solution)/shard_map/prompt_attention/pallas_call | solution.py:95
  33.1 1.5 %collective-permute-start.15 = (bf16[640,128]{1,0:T(8,128)(2,1)S(1)}, bf16[640,128]{1,0:T(8,128)(2,1)S(1)}, u32[]{:S(2)}, u32[]{:S(2)}) collective-permute-start(bf16[640,128]{1,0:T(8,128)(2,1)S(1)} %get-tuple-element.129.own), channel_id=1, source_target_pairs={{0,8},{8,0},{16,24},{24,16},{1,9},{9,1},{17,25},{25,17},{2,10},{10... | collective-permute-start | bytes 491528 | tf_op jit(solution)/shard_map/ppermute | solution.py:309
  34.6 2.7 %collective-permute-start.10 = (bf16[320,128]{1,0:T(8,128)(2,1)S(1)}, bf16[320,128]{1,0:T(8,128)(2,1)S(1)}, u32[]{:S(2)}, u32[]{:S(2)}) collective-permute-start(bf16[320,128]{1,0:T(8,128)(2,1)S(1)} %get-tuple-element.106), channel_id=1, source_target_pairs={{0,16},{8,24},{16,0},{24,8},{1,17},{9,25},{17,1},{25,9},{2,18},{10... | collective-permute-start | bytes 245768 | tf_op jit(solution)/shard_map/ppermute | solution.py:309
  37.3 0.9 %collective-permute-start.11 = (bf16[320,128]{1,0:T(8,128)(2,1)S(1)}, bf16[320,128]{1,0:T(8,128)(2,1)S(1)}, u32[]{:S(2)}, u32[]{:S(2)}) collective-permute-start(bf16[320,128]{1,0:T(8,128)(2,1)S(1)} %get-tuple-element.106), channel_id=1, source_target_pairs={{0,24},{8,16},{16,8},{24,0},{1,25},{9,17},{17,9},{25,1},{2,26},{10... | collective-permute-start | bytes 245768 | tf_op jit(solution)/shard_map/ppermute | solution.py:309
  38.1 1.5 %project.3 = (f32[2,128,256]{2,1,0:T(8,128)S(1)}, f32[2,128,256]{2,1,0:T(8,128)S(1)}) custom-call(s32[4]{0:T(128)S(1)} %pad_add_fusion.1.where, bf16[2,4,128,640]{3,2,1,0:T(8,128)(2,1)S(1)} %get-tuple-element.109.keep, bf16[4,128,640]{2,1,0:T(8,128)(2,1)S(1)} %collective-permute-done.8.other, bf16[4,128,640]{2,1,0:T(8,128)(2,1)S(1)} %collective-permute-done.9.other_2, ...), custom_call_target="tpu_custom_call" | custom-call | flops 1024 | bytes 1024 | tf_op jit(solution)/shard_map/project/pallas_call | solution.py:118
  39.7 1.6 %collective-permute-start.14 = (f32[2,128,256]{2,1,0:T(8,128)S(1)}, f32[2,128,256]{2,1,0:T(8,128)S(1)}, u32[]{:S(2)}, u32[]{:S(2)}) collective-permute-start(f32[2,128,256]{2,1,0:T(8,128)S(1)} %get-tuple-element.128), channel_id=1, source_target_pairs={{0,4},{4,0},{1,5},{5,1},{2,6},{6,2},{3,7},{7,3},{8,12},{12,8},{9,1... | collective-permute-start | bytes 786440 | tf_op jit(solution)/shard_map/ppermute | solution.py:309
  41.3 1.6 %collective-permute-start.16 = (bf16[2,320,128]{2,1,0:T(8,128)(2,1)S(1)}, bf16[2,320,128]{2,1,0:T(8,128)(2,1)S(1)}, u32[]{:S(2)}, u32[]{:S(2)}) collective-permute-start(bf16[2,320,128]{2,1,0:T(8,128)(2,1)S(1)} %pad_maximum_fusion.2), channel_id=1, source_target_pairs={{0,1},{1,0},{2,3},{3,2},{4,5},{5,4},{6,7},{7,6},{8,9},{9,8},{10,11... | collective-permute-start | bytes 491528 | tf_op jit(solution)/shard_map/ppermute | solution.py:309
  42.9 3.9 %prompt_attention.5 = (f32[128,2048]{1,0:T(8,128)S(1)}, f32[8,2048]{1,0:T(8,128)S(1)}) custom-call(s32[4]{0:T(128)S(1)} %get-tuple-element.152.info, bf16[128,4096]{1,0:T(8,128)(2,1)S(1)} %bitcast.20, bf16[512,1024]{1,0:T(8,128)(2,1)} %collective-permute-done.7.k_ref.v_ref, bf16[512,1024]{1,0:T(8,128)(2,1)} %collective-permute-done.7.k_ref.v_ref, ...), custom_call_target="tpu_custom_call" | custom-call | flops 8589934592 | bytes 1024 | tf_op jit(solution)/shard_map/prompt_attention/pallas_call | solution.py:95
  47.4 1.4 %project.4 = (f32[2,128,128]{2,1,0:T(8,128)S(1)}, f32[2,128,128]{2,1,0:T(8,128)S(1)}) custom-call(s32[4]{0:T(128)S(1)} %pad_add_fusion.1.where, bf16[2,4,128,640]{3,2,1,0:T(8,128)(2,1)S(1)} %get-tuple-element.109.keep, bf16[4,128,640]{2,1,0:T(8,128)(2,1)S(1)} %collective-permute-done.8.other, bf16[4,128,640]{2,1,0:T(8,128)(2,1)S(1)} %collective-permute-done.9.other_2, ...), custom_call_target="tpu_custom_call" | custom-call | flops 1024 | bytes 1024 | tf_op jit(solution)/shard_map/project/pallas_call | solution.py:118
  48.8 3.3 %collective-permute-done.13.refs_2_ = bf16[2,320,128]{2,1,0:T(8,128)(2,1)S(1)} collective-permute-done((bf16[2,320,128]{2,1,0:T(8,128)(2,1)S(1)}, bf16[2,320,128]{2,1,0:T(8,128)(2,1)S(1)}, u32[]{:S(2)}, u32[]{:S(2)}) %collective-permute-start.13) | collective-permute-done | bytes 163872 | tf_op jit(solution)/shard_map/ppermute | solution.py:309
  52.7 1.4 %project.5 = (f32[2,128,128]{2,1,0:T(8,128)S(1)}, f32[2,128,128]{2,1,0:T(8,128)S(1)}) custom-call(s32[4]{0:T(128)S(1)} %pad_add_fusion.1.where, bf16[2,4,128,640]{3,2,1,0:T(8,128)(2,1)S(1)} %get-tuple-element.109.keep, bf16[4,128,640]{2,1,0:T(8,128)(2,1)S(1)} %collective-permute-done.8.other, bf16[4,128,640]{2,1,0:T(8,128)(2,1)S(1)} %collective-permute-done.9.other_2, ...), custom_call_target="tpu_custom_call" | custom-call | flops 1024 | bytes 1024 | tf_op jit(solution)/shard_map/project/pallas_call | solution.py:118
  54.1 1.6 %collective-permute-start.20 = (f32[1,128,128]{2,1,0:T(8,128)S(1)}, f32[1,128,128]{2,1,0:T(8,128)S(1)}, u32[]{:S(2)}, u32[]{:S(2)}) collective-permute-start(f32[1,128,128]{2,1,0:T(8,128)S(1)} %get-tuple-element.150), channel_id=1, source_target_pairs={{0,4},{4,0},{1,5},{5,1},{2,6},{6,2},{3,7},{7,3},{8,12},{12,8},{9,1... | collective-permute-start | bytes 196616 | tf_op jit(solution)/shard_map/ppermute | solution.py:309
  57.7 2.3 %final_attention.2.refs_7_ = bf16[128,4096]{1,0:T(8,128)(2,1)} custom-call(s32[3]{0:T(128)S(1)} %pad_add_fusion.info, f32[1,128]{1,0:T(1,128)S(1)} %bitcast.31, bf16[128,4096]{1,0:T(8,128)(2,1)S(1)} %bitcast.21, f32[128,2048]{1,0:T(8,128)S(1)} %get-tuple-element.143.acc_ref, f32[8,2048]{1,0:T(8,128)S(1)} %get-tuple-element.144.ml_ref, ...), custom_call_target="tpu_custom_call" | custom-call | flops 1024 | bytes 1024 | tf_op jit(solution)/shard_map/final_attention/pallas_call | solution.py:295
  60.1 2.3 %final_attention.3 = bf16[128,4096]{1,0:T(8,128)(2,1)} custom-call(s32[3]{0:T(128)S(1)} %pad_add_fusion.info, f32[1,128]{1,0:T(1,128)S(1)} %bitcast.32, bf16[128,4096]{1,0:T(8,128)(2,1)S(1)} %bitcast.22, f32[128,2048]{1,0:T(8,128)S(1)} %get-tuple-element.124.acc_ref, f32[8,2048]{1,0:T(8,128)S(1)} %get-tuple-element.125.ml_ref, ...), custom_call_target="tpu_custom_call", output_to_operand_aliasing={{}: (12, {})} | custom-call | flops 1024 | bytes 1024 | tf_op jit(solution)/shard_map/final_attention/pallas_call | solution.py:295
  (60 shorter events, 6.2 us)
Async XLA Ops:
  0.0 11.7 %collective-permute-start.1 = (bf16[128,5120]{1,0:T(8,128)(2,1)}, bf16[128,5120]{1,0:T(8,128)(2,1)S(1)}, u32[]{:S(2)}, u32[]{:S(2)}) collective-permute-start(bf16[128,5120]{1,0:T(8,128)(2,1)} %bitcast.23), channel_id=1, source_target_pairs={{0,2},{2,0},{1,3},{3,1},{4,6},{6,4},{5,7},{7,5},{8,10},{10,8},{9,1... | collective-permute-start | bytes 3932168 | tf_op jit(solution)/shard_map/ppermute | solution.py:309
  0.5 5.5 %collective-permute-start = (bf16[320,1024]{1,0:T(8,128)(2,1)}, bf16[320,1024]{1,0:T(8,128)(2,1)}, u32[]{:S(2)}, u32[]{:S(2)}) collective-permute-start(bf16[320,1024]{1,0:T(8,128)(2,1)} %weight_ref.1), channel_id=1, source_target_pairs={{0,2},{2,0},{1,3},{3,1},{4,6},{6,4},{5,7},{7,5},{8,10},{10,8},{9,1... | collective-permute-start | bytes 1966088 | tf_op jit(solution)/shard_map/ppermute | solution.py:309
  0.6 27.0 %collective-permute-start.7 = (bf16[512,1024]{1,0:T(8,128)(2,1)}, bf16[512,1024]{1,0:T(8,128)(2,1)}, u32[]{:S(2)}, u32[]{:S(2)}) collective-permute-start(bf16[512,1024]{1,0:T(8,128)(2,1)} %bitcast.33), channel_id=1, source_target_pairs={{0,1},{1,0},{2,3},{3,2},{4,5},{5,4},{6,7},{7,6},{8,9},{9,8},{10,11... | collective-permute-start | bytes 3145736 | tf_op jit(solution)/shard_map/ppermute | solution.py:328
  7.1 15.1 %collective-permute-start.2 = (bf16[320,256]{1,0:T(8,128)(2,1)S(1)}, bf16[320,256]{1,0:T(8,128)(2,1)S(1)}, u32[]{:S(2)}, u32[]{:S(2)}) collective-permute-start(bf16[320,256]{1,0:T(8,128)(2,1)S(1)} %get-tuple-element.88), channel_id=1, source_target_pairs={{0,16},{8,24},{16,0},{24,8},{1,17},{9,25},{17,1},{25,9},{2,18},{10... | collective-permute-start | bytes 491528 | tf_op jit(solution)/shard_map/ppermute | solution.py:309
  9.8 12.4 %collective-permute-start.3 = (bf16[320,256]{1,0:T(8,128)(2,1)S(1)}, bf16[320,256]{1,0:T(8,128)(2,1)S(1)}, u32[]{:S(2)}, u32[]{:S(2)}) collective-permute-start(bf16[320,256]{1,0:T(8,128)(2,1)S(1)} %get-tuple-element.88), channel_id=1, source_target_pairs={{0,24},{8,16},{16,8},{24,0},{1,25},{9,17},{17,9},{25,1},{2,26},{10... | collective-permute-start | bytes 491528 | tf_op jit(solution)/shard_map/ppermute | solution.py:309
  11.1 22.0 %collective-permute-start.6 = (bf16[640,256]{1,0:T(8,128)(2,1)S(1)}, bf16[640,256]{1,0:T(8,128)(2,1)S(1)}, u32[]{:S(2)}, u32[]{:S(2)}) collective-permute-start(bf16[640,256]{1,0:T(8,128)(2,1)S(1)} %get-tuple-element.83.own), channel_id=1, source_target_pairs={{0,8},{8,0},{16,24},{24,16},{1,9},{9,1},{17,25},{25,17},{2,10},{10... | collective-permute-start | bytes 983048 | tf_op jit(solution)/shard_map/ppermute | solution.py:309
  12.4 16.8 %collective-permute-start.8 = (bf16[4,128,640]{2,1,0:T(8,128)(2,1)S(1)}, bf16[4,128,640]{2,1,0:T(8,128)(2,1)S(1)}, u32[]{:S(2)}, u32[]{:S(2)}) collective-permute-start(bf16[4,128,640]{2,1,0:T(8,128)(2,1)S(1)} %get-tuple-element.86), channel_id=1, source_target_pairs={{0,4},{4,0},{1,5},{5,1},{2,6},{6,2},{3,7},{7,3},{8,12},{12,8},{9,1... | collective-permute-start | bytes 1966088 | tf_op jit(solution)/shard_map/ppermute | solution.py:309
  22.2 12.4 %collective-permute-start.4 = (bf16[320,128]{1,0:T(8,128)(2,1)S(1)}, bf16[320,128]{1,0:T(8,128)(2,1)S(1)}, u32[]{:S(2)}, u32[]{:S(2)}) collective-permute-start(bf16[320,128]{1,0:T(8,128)(2,1)S(1)} %get-tuple-element.94), channel_id=1, source_target_pairs={{0,16},{8,24},{16,0},{24,8},{1,17},{9,25},{17,1},{25,9},{2,18},{10... | collective-permute-start | bytes 245768 | tf_op jit(solution)/shard_map/ppermute | solution.py:309
  27.2 7.4 %collective-permute-start.5 = (bf16[320,128]{1,0:T(8,128)(2,1)S(1)}, bf16[320,128]{1,0:T(8,128)(2,1)S(1)}, u32[]{:S(2)}, u32[]{:S(2)}) collective-permute-start(bf16[320,128]{1,0:T(8,128)(2,1)S(1)} %get-tuple-element.94), channel_id=1, source_target_pairs={{0,24},{8,16},{16,8},{24,0},{1,25},{9,17},{17,9},{25,1},{2,26},{10... | collective-permute-start | bytes 245768 | tf_op jit(solution)/shard_map/ppermute | solution.py:309
  27.7 10.4 %collective-permute-start.12 = (bf16[2,320,256]{2,1,0:T(8,128)(2,1)S(1)}, bf16[2,320,256]{2,1,0:T(8,128)(2,1)S(1)}, u32[]{:S(2)}, u32[]{:S(2)}) collective-permute-start(bf16[2,320,256]{2,1,0:T(8,128)(2,1)S(1)} %pad_maximum_fusion), channel_id=1, source_target_pairs={{0,1},{1,0},{2,3},{3,2},{4,5},{5,4},{6,7},{7,6},{8,9},{9,8},{10,11... | collective-permute-start | bytes 983048 | tf_op jit(solution)/shard_map/ppermute | solution.py:309
  29.2 5.4 %collective-permute-start.9 = (bf16[4,128,640]{2,1,0:T(8,128)(2,1)S(1)}, bf16[4,128,640]{2,1,0:T(8,128)(2,1)S(1)}, u32[]{:S(2)}, u32[]{:S(2)}) collective-permute-start(bf16[4,128,640]{2,1,0:T(8,128)(2,1)S(1)} %collective-permute-done.8.other), channel_id=1, source_target_pairs={{0,2},{2,0},{1,3},{3,1},{4,6},{6,4},{5,7},{7,5},{8,10},{10,8},{9,1... | collective-permute-start | bytes 1966088 | tf_op jit(solution)/shard_map/ppermute | solution.py:309
  33.1 14.3 %collective-permute-start.15 = (bf16[640,128]{1,0:T(8,128)(2,1)S(1)}, bf16[640,128]{1,0:T(8,128)(2,1)S(1)}, u32[]{:S(2)}, u32[]{:S(2)}) collective-permute-start(bf16[640,128]{1,0:T(8,128)(2,1)S(1)} %get-tuple-element.129.own), channel_id=1, source_target_pairs={{0,8},{8,0},{16,24},{24,16},{1,9},{9,1},{17,25},{25,17},{2,10},{10... | collective-permute-start | bytes 491528 | tf_op jit(solution)/shard_map/ppermute | solution.py:309
  34.6 12.1 %collective-permute-start.10 = (bf16[320,128]{1,0:T(8,128)(2,1)S(1)}, bf16[320,128]{1,0:T(8,128)(2,1)S(1)}, u32[]{:S(2)}, u32[]{:S(2)}) collective-permute-start(bf16[320,128]{1,0:T(8,128)(2,1)S(1)} %get-tuple-element.106), channel_id=1, source_target_pairs={{0,16},{8,24},{16,0},{24,8},{1,17},{9,25},{17,1},{25,9},{2,18},{10... | collective-permute-start | bytes 245768 | tf_op jit(solution)/shard_map/ppermute | solution.py:309
  37.3 9.5 %collective-permute-start.11 = (bf16[320,128]{1,0:T(8,128)(2,1)S(1)}, bf16[320,128]{1,0:T(8,128)(2,1)S(1)}, u32[]{:S(2)}, u32[]{:S(2)}) collective-permute-start(bf16[320,128]{1,0:T(8,128)(2,1)S(1)} %get-tuple-element.106), channel_id=1, source_target_pairs={{0,24},{8,16},{16,8},{24,0},{1,25},{9,17},{17,9},{25,1},{2,26},{10... | collective-permute-start | bytes 245768 | tf_op jit(solution)/shard_map/ppermute | solution.py:309
  39.7 9.1 %collective-permute-start.14 = (f32[2,128,256]{2,1,0:T(8,128)S(1)}, f32[2,128,256]{2,1,0:T(8,128)S(1)}, u32[]{:S(2)}, u32[]{:S(2)}) collective-permute-start(f32[2,128,256]{2,1,0:T(8,128)S(1)} %get-tuple-element.128), channel_id=1, source_target_pairs={{0,4},{4,0},{1,5},{5,1},{2,6},{6,2},{3,7},{7,3},{8,12},{12,8},{9,1... | collective-permute-start | bytes 786440 | tf_op jit(solution)/shard_map/ppermute | solution.py:309
  41.3 6.1 %collective-permute-start.16 = (bf16[2,320,128]{2,1,0:T(8,128)(2,1)S(1)}, bf16[2,320,128]{2,1,0:T(8,128)(2,1)S(1)}, u32[]{:S(2)}, u32[]{:S(2)}) collective-permute-start(bf16[2,320,128]{2,1,0:T(8,128)(2,1)S(1)} %pad_maximum_fusion.2), channel_id=1, source_target_pairs={{0,1},{1,0},{2,3},{3,2},{4,5},{5,4},{6,7},{7,6},{8,9},{9,8},{10,11... | collective-permute-start | bytes 491528 | tf_op jit(solution)/shard_map/ppermute | solution.py:309
  46.8 5.4 %collective-permute-start.13 = (bf16[2,320,128]{2,1,0:T(8,128)(2,1)S(1)}, bf16[2,320,128]{2,1,0:T(8,128)(2,1)S(1)}, u32[]{:S(2)}, u32[]{:S(2)}) collective-permute-start(bf16[2,320,128]{2,1,0:T(8,128)(2,1)S(1)} %pad_maximum_fusion.1), channel_id=1, source_target_pairs={{0,1},{1,0},{2,3},{3,2},{4,5},{5,4},{6,7},{7,6},{8,9},{9,8},{10,11... | collective-permute-start | bytes 491528 | tf_op jit(solution)/shard_map/ppermute | solution.py:309
  47.3 5.3 %collective-permute-start.19 = (bf16[640,128]{1,0:T(8,128)(2,1)S(1)}, bf16[640,128]{1,0:T(8,128)(2,1)S(1)}, u32[]{:S(2)}, u32[]{:S(2)}) collective-permute-start(bf16[640,128]{1,0:T(8,128)(2,1)S(1)} %get-tuple-element.139.own), channel_id=1, source_target_pairs={{0,8},{8,0},{16,24},{24,16},{1,9},{9,1},{17,25},{25,17},{2,10},{10... | collective-permute-start | bytes 491528 | tf_op jit(solution)/shard_map/ppermute | solution.py:309
  52.2 5.0 %collective-permute-start.17 = (f32[2,128,128]{2,1,0:T(8,128)S(1)}, f32[2,128,128]{2,1,0:T(8,128)S(1)}, u32[]{:S(2)}, u32[]{:S(2)}) collective-permute-start(f32[2,128,128]{2,1,0:T(8,128)S(1)} %get-tuple-element.138), channel_id=1, source_target_pairs={{0,4},{4,0},{1,5},{5,1},{2,6},{6,2},{3,7},{7,3},{8,12},{12,8},{9,1... | collective-permute-start | bytes 393224 | tf_op jit(solution)/shard_map/ppermute | solution.py:309
  54.1 6.0 %collective-permute-start.20 = (f32[1,128,128]{2,1,0:T(8,128)S(1)}, f32[1,128,128]{2,1,0:T(8,128)S(1)}, u32[]{:S(2)}, u32[]{:S(2)}) collective-permute-start(f32[1,128,128]{2,1,0:T(8,128)S(1)} %get-tuple-element.150), channel_id=1, source_target_pairs={{0,4},{4,0},{1,5},{5,1},{2,6},{6,2},{3,7},{7,3},{8,12},{12,8},{9,1... | collective-permute-start | bytes 196616 | tf_op jit(solution)/shard_map/ppermute | solution.py:309
  55.7 4.4 %collective-permute-start.21 = (f32[1,128,128]{2,1,0:T(8,128)S(1)}, f32[1,128,128]{2,1,0:T(8,128)S(1)}, u32[]{:S(2)}, u32[]{:S(2)}) collective-permute-start(f32[1,128,128]{2,1,0:T(8,128)S(1)} %get-tuple-element.149), channel_id=1, source_target_pairs={{0,6},{2,4},{4,2},{6,0},{1,7},{3,5},{5,3},{7,1},{8,14},{10,12},{12... | collective-permute-start | bytes 196616 | tf_op jit(solution)/shard_map/ppermute | solution.py:309
  55.7 4.4 %collective-permute-start.22 = (f32[1,128,128]{2,1,0:T(8,128)S(1)}, f32[1,128,128]{2,1,0:T(8,128)S(1)}, u32[]{:S(2)}, u32[]{:S(2)}) collective-permute-start(f32[1,128,128]{2,1,0:T(8,128)S(1)} %slice.25), channel_id=1, source_target_pairs={{0,2},{2,0},{1,3},{3,1},{4,6},{6,4},{5,7},{7,5},{8,10},{10,8},{9,1... | collective-permute-start | bytes 196616 | tf_op jit(solution)/shard_map/ppermute | solution.py:309
  56.3 1.4 %collective-permute-start.23 = (f32[1,128,256]{2,1,0:T(8,128)S(1)}, f32[1,128,256]{2,1,0:T(8,128)S(1)}, u32[]{:S(2)}, u32[]{:S(2)}) collective-permute-start(f32[1,128,256]{2,1,0:T(8,128)S(1)} %slice_add_fusion), channel_id=1, source_target_pairs={{0,2},{2,0},{1,3},{3,1},{4,6},{6,4},{5,7},{7,5},{8,10},{10,8},{9,1... | collective-permute-start | bytes 393224 | tf_op jit(solution)/shard_map/ppermute | solution.py:309
  57.1 3.0 %collective-permute-start.18 = (f32[1,128,128]{2,1,0:T(8,128)S(1)}, f32[1,128,128]{2,1,0:T(8,128)S(1)}, u32[]{:S(2)}, u32[]{:S(2)}) collective-permute-start(f32[1,128,128]{2,1,0:T(8,128)S(1)} %slice_add_fusion.1), channel_id=1, source_target_pairs={{0,2},{2,0},{1,3},{3,1},{4,6},{6,4},{5,7},{7,5},{8,10},{10,8},{9,1... | collective-permute-start | bytes 196616 | tf_op jit(solution)/shard_map/ppermute | solution.py:309
  (7 other events, 41.5 us)

commit v13 on v12

--- a/solution.py
+++ b/solution.py
@@ -239,8 +239,9 @@
     )
 
 
-def final_kernel(counts, head, info, gain_ref, q_ref, acc_ref, ml_ref, *refs):
+def final_kernel(counts, info, gain_ref, q_ref, *refs):
     result, built, sem = refs[-3:]
+    states, refs = (refs[:2], refs[2:4]), refs[4:]
     parts = []
     for count in counts:
         mine, here, *away = refs[:count]
@@ -255,6 +256,7 @@
     live = jnp.where(row - base < length, 1.0, 0.0)[0:1]
     copies = []
     for k, (mine, here, away, part) in enumerate(parts):
+        acc_ref, ml_ref = states[k // 2]
         here = mine[0, :, part] + here[0, :, part]
         away = sum(ref[0, :, part] for ref in away)
         first_core = jnp.full(here.shape, info[2]) == 0
@@ -263,9 +265,9 @@
         keys = (raw * lax.rsqrt(mean + 1e-06) * gain_ref[...]).astype(jnp.bfloat16)
         values = jnp.where(first_core, away, here).T.astype(jnp.bfloat16)
         pairs = range(0, SHARED, 2)
-        products = [scores_of(keys, pair_queries(q_ref, (head + k) * SHARED + g)) for g in pairs]
+        products = [scores_of(keys, pair_queries(q_ref, k * SHARED + g)) for g in pairs]
         for g, scores in zip(pairs, products):
-            cols = slice((k * SHARED + g) * HD, (k * SHARED + g + 2) * HD)
+            cols = slice((k % 2 * SHARED + g) * HD, (k % 2 * SHARED + g + 2) * HD)
             scores = jnp.where(seen, scores, HIDDEN)
             before = ml_ref[0:1, cols]
             largest = jnp.maximum(jnp.max(scores, axis=0, keepdims=True), before)
@@ -276,29 +278,23 @@
             acc = (acc + faded * acc_ref[:, cols]) * (live / total)
             built[k, :, g * HD : (g + 1) * HD] = acc[:, :ROWS].T.astype(jnp.bfloat16)
             built[k, :, (g + 1) * HD : (g + 2) * HD] = acc[:, ROWS:].T.astype(jnp.bfloat16)
-        place = result.at[:, pl.ds((head + k) * GROUP, GROUP)]
+        place = result.at[:, pl.ds(k * GROUP, GROUP)]
         copies.append(pltpu.make_async_copy(built.at[k], place, sem.at[k]))
         copies[-1].start()
     for copy in copies:
         copy.wait()
 
 
-def final_attention(info, gain, query, state, head, chunks, result):
-    heads = sum(chunk[0].shape[2] for chunk in chunks) // HD
-    operands = [gain, query, *state, *[array for chunk in chunks for array in chunk]]
-    specs = [SMEM] + [VMEM] * len(operands)
-    aliases = {}
-    if result is not None:
-        operands.append(result)
-        specs.append(pl.BlockSpec(memory_space=pl.ANY))
-        aliases = {len(operands): 0}
+def final_attention(info, gain, query, states, chunks):
+    operands = [gain, query]
+    operands += [array for state in states for array in state]
+    operands += [array for chunk in chunks for array in chunk]
     return pl.pallas_call(
-        functools.partial(final_kernel, [len(chunk) for chunk in chunks], head),
-        in_specs=specs,
+        functools.partial(final_kernel, [len(chunk) for chunk in chunks]),
+        in_specs=[SMEM] + [VMEM] * len(operands),
         out_specs=pl.BlockSpec(memory_space=pl.ANY),
         out_shape=jax.ShapeDtypeStruct((ROWS, HQ * HD), jnp.bfloat16),
-        scratch_shapes=[pltpu.VMEM((heads, ROWS, GROUP), jnp.bfloat16), pltpu.SemaphoreType.DMA((heads,))],
-        input_output_aliases=aliases,
+        scratch_shapes=[pltpu.VMEM((KVH, ROWS, GROUP), jnp.bfloat16), pltpu.SemaphoreType.DMA((KVH,))],
         compiler_params=PARAMS,
         cost_estimate=HINT,
         name="final_attention",
@@ -384,24 +380,22 @@
         return [mine, xor_swap(theirs[:1], "y", 1), *there]
 
     mine_0, theirs_0 = sums(0)
-    state, mine_0 = tie((state, mine_0))
-    halves.append(rest(2, state))
-    sent[2], mine_0, halves[1] = tie((sent[2], mine_0, halves[1]))
+    sent[2], mine_0 = tie((sent[2], mine_0))
     forwarded.append(forward(2, True))
     here_0 = xor_swap(theirs_0, "y", 1)
     forwarded[1], mine_0 = tie((forwarded[1], mine_0))
     mine_1, theirs_1 = sums(1)
-    here_0, mine_1, theirs_1 = tie((here_0, mine_1, theirs_1))
+    here_1 = xor_swap(theirs_1, "y", 1)
+    forwarded[2], mine_1, here_0, here_1 = tie((forwarded[2], mine_1, here_0, here_1))
     first = [mine_0, here_0, xor_swap(mine_0[1:] + here_0[1:], "core", 1)]
-    here_1 = xor_swap(theirs_1, "y", 1)
-    forwarded[2], mine_1 = tie((forwarded[2], mine_1))
     mine_2, theirs_2 = sums(2)
     third = owners(mine_2, theirs_2)
+    state, mine_2 = tie((state, mine_2))
+    halves.append(rest(2, state))
     second = [mine_1, here_1, xor_swap(mine_1[1:] + here_1[1:], "core", 1)]
     info = jnp.concatenate([resp_lengths[0], core[None]]).astype(jnp.int32)
     gain = key_gain[None]
-    result = final_attention(info, gain, query, halves[0], 0, [first], None)
-    return final_attention(info, gain, query, halves[1], 2, [second, third], result)[None]
+    return final_attention(info, gain, query, halves, [first, second, third])[None]
 
 
 def solution(mesh):

time: 62.7 us -> 63.2 us (level)
  waiting for transfers between devices: 7.3 us -> 11.1 us
  Pallas kernels: 24.6 us -> 23 us
  starting transfers between devices: 27.9 us -> 26.3 us
    ppermute x23, waiting for transfers between devices: 7.3 us -> 11.1 us  [xor_swap(): lax.ppermute(array, axis, [(i, i ^ by) for i in range(lax.axis_size(axis))])]
    pallas_call x2 -> x1, Pallas kernels: 4.67 us -> 3.01 us  [final_attention(): pl.pallas_call(functools.partial(final_kernel, [len(chunk) for chunk in c...]
    ppermute x23, starting transfers between devices: 24.9 us -> 23.4 us  [xor_swap(): lax.ppermute(array, axis, [(i, i ^ by) for i in range(lax.axis_size(axis))])]
  transfers between devices with their start and end apart: 24 -> 24, of which waited for: 4 -> 6; matrix products, arithmetic and copies ran while one was open for 1% -> 1% of each run, Pallas kernels for 36% -> 29%
where the time goes in v13:
time: 63.2 us; the launch traced here: 63 us
  starting transfers between devices  26.3 us (42%)
  Pallas kernels  23 us (36%)
  waiting for transfers between devices  11.1 us (18%)
  local copies, waits for them, and re-layouts  1.35 us (2%)
  between operations  0.95 us (2%)
    ppermute x23, starting transfers between devices, xor_swap(): lax.ppermute(array, axis, [(i, i ^ by) for i in range(lax.axis_size(axis))])  23.4 us
    pallas_call x3, Pallas kernels, prompt_attention(): pl.pallas_call(functools.partial(prompt_kernel, first), grid_spec=pltpu.P...  13.2 us
    ppermute x23, waiting for transfers between devices, xor_swap(): lax.ppermute(array, axis, [(i, i ^ by) for i in range(lax.axis_size(axis))])  11.1 us
    pallas_call x5, Pallas kernels, on_chip(): pl.pallas_call(kernel, in_specs=[SMEM] + [VMEM] * len(operands), out_spec...  5.61 us
    pallas_call x1, Pallas kernels, final_attention(): pl.pallas_call(functools.partial(final_kernel, [len(chunk) for chunk in c...  3.01 us
    ppermute x1, starting transfers between devices, per_device(): lax.ppermute(caches[-1], 'blk', [(i, (i + 1) % cycle) for i in range(cycl...  2.93 us
  transfers between devices with their start and end apart: 24, of which 6 were waited for; matrix products, arithmetic and copies ran while one was open for 1% of the time, Pallas kernels for 29%

profile of v13, /device:TPU:0, one launch (start us, length us, event | category | flops | bytes accessed | tf_op | source)
XLA Modules:
  0.0 63.0 jit_solution(9610239540848012762)
XLA Ops:
  0.6 2.9 %collective-permute-start.7 = (bf16[512,1024]{1,0:T(8,128)(2,1)}, bf16[512,1024]{1,0:T(8,128)(2,1)}, u32[]{:S(2)}, u32[]{:S(2)}) collective-permute-start(bf16[512,1024]{1,0:T(8,128)(2,1)} %bitcast.31), channel_id=1, source_target_pairs={{0,1},{1,0},{2,3},{3,2},{4,5},{5,4},{6,7},{7,6},{8,9},{9,8},{10,11... | collective-permute-start | bytes 3145736 | tf_op jit(solution)/shard_map/ppermute | solution.py:324
  3.5 1.1 %copy-done.2 = bf16[320,1024]{1,0:T(8,128)(2,1)S(1)} copy-done((bf16[320,1024]{1,0:T(8,128)(2,1)S(1)}, bf16[320,1024]{1,0:T(8,128)(2,1)}, u32[]{:S(2)}) %copy-start.2) | copy-done | bytes 655384
  6.0 1.2 %pack_weight.1 = (bf16[640,256]{1,0:T(8,128)(2,1)S(1)}, bf16[640,128]{1,0:T(8,128)(2,1)S(1)}, bf16[640,128]{1,0:T(8,128)(2,1)S(1)}, bf16[320,256]{1,0:T(8,128)(2...) custom-call(s32[4]{0:T(128)S(1)} %pad_add_fusion.1.where, ...), custom_call_target="tpu_custom_call", output_to_operand_aliasing={{0}: (2, {}), {1}: (3, {}), {2}: (4, {})} | custom-call | flops 1024 | bytes 1024 | tf_op jit(solution)/shard_map/pack_weight/pallas_call | solution.py:185
  7.1 3.7 %collective-permute-start.3 = (bf16[320,256]{1,0:T(8,128)(2,1)S(1)}, bf16[320,256]{1,0:T(8,128)(2,1)S(1)}, u32[]{:S(2)}, u32[]{:S(2)}) collective-permute-start(bf16[320,256]{1,0:T(8,128)(2,1)S(1)} %get-tuple-element.84), channel_id=1, source_target_pairs={{0,24},{8,16},{16,8},{24,0},{1,25},{9,17},{17,9},{25,1},{2,26},{10... | collective-permute-start | bytes 491528 | tf_op jit(solution)/shard_map/ppermute | solution.py:305
  12.6 1.6 %collective-permute-start.8 = (bf16[4,128,640]{2,1,0:T(8,128)(2,1)S(1)}, bf16[4,128,640]{2,1,0:T(8,128)(2,1)S(1)}, u32[]{:S(2)}, u32[]{:S(2)}) collective-permute-start(bf16[4,128,640]{2,1,0:T(8,128)(2,1)S(1)} %get-tuple-element.82), channel_id=1, source_target_pairs={{0,4},{4,0},{1,5},{5,1},{2,6},{6,2},{3,7},{7,3},{8,12},{12,8},{9,1... | collective-permute-start | bytes 1966088 | tf_op jit(solution)/shard_map/ppermute | solution.py:305
  14.2 5.4 %prompt_attention.3 = (f32[128,4096]{1,0:T(8,128)S(1)}, f32[8,4096]{1,0:T(8,128)S(1)}) custom-call(s32[4]{0:T(128)S(1)} %get-tuple-element.143.info, bf16[128,4096]{1,0:T(8,128)(2,1)S(1)} %bitcast.20, bf16[512,1024]{1,0:T(8,128)(2,1)S(1)} %bitcast.32, bf16[512,1024]{1,0:T(8,128)(2,1)S(1)} %bitcast.33), custom_call_target="tpu_custom_call" | custom-call | flops 17179869184 | bytes 1024 | tf_op jit(solution)/shard_map/prompt_attention/pallas_call | solution.py:95
  19.7 5.1 %collective-permute-done.2.refs_0_ = bf16[320,256]{1,0:T(8,128)(2,1)S(1)} collective-permute-done((bf16[320,256]{1,0:T(8,128)(2,1)S(1)}, bf16[320,256]{1,0:T(8,128)(2,1)S(1)}, u32[]{:S(2)}, u32[]{:S(2)}) %collective-permute-start.2) | collective-permute-done | bytes 163872 | tf_op jit(solution)/shard_map/ppermute | solution.py:305
  24.8 2.6 %collective-permute-start.5 = (bf16[320,128]{1,0:T(8,128)(2,1)S(1)}, bf16[320,128]{1,0:T(8,128)(2,1)S(1)}, u32[]{:S(2)}, u32[]{:S(2)}) collective-permute-start(bf16[320,128]{1,0:T(8,128)(2,1)S(1)} %get-tuple-element.90), channel_id=1, source_target_pairs={{0,24},{8,16},{16,8},{24,0},{1,25},{9,17},{17,9},{25,1},{2,26},{10... | collective-permute-start | bytes 245768 | tf_op jit(solution)/shard_map/ppermute | solution.py:305
  27.5 1.6 %collective-permute-start.10 = (bf16[2,320,256]{2,1,0:T(8,128)(2,1)S(1)}, bf16[2,320,256]{2,1,0:T(8,128)(2,1)S(1)}, u32[]{:S(2)}, u32[]{:S(2)}) collective-permute-start(bf16[2,320,256]{2,1,0:T(8,128)(2,1)S(1)} %pad_maximum_fusion), channel_id=1, source_target_pairs={{0,1},{1,0},{2,3},{3,2},{4,5},{5,4},{6,7},{7,6},{8,9},{9,8},{10,11... | collective-permute-start | bytes 983048 | tf_op jit(solution)/shard_map/ppermute | solution.py:305
  29.1 3.9 %prompt_attention.4 = (f32[128,2048]{1,0:T(8,128)S(1)}, f32[8,2048]{1,0:T(8,128)S(1)}) custom-call(s32[4]{0:T(128)S(1)} %get-tuple-element.144.info, bf16[128,4096]{1,0:T(8,128)(2,1)S(1)} %bitcast.21, bf16[512,1024]{1,0:T(8,128)(2,1)} %collective-permute-done.7.k_ref.v_ref, bf16[512,1024]{1,0:T(8,128)(2,1)} %collective-permute-done.7.k_ref.v_ref, ...), custom_call_target="tpu_custom_call" | custom-call | flops 8589934592 | bytes 1024 | tf_op jit(solution)/shard_map/prompt_attention/pallas_call | solution.py:95
  33.7 2.9 %collective-permute-start.13 = (bf16[320,128]{1,0:T(8,128)(2,1)S(1)}, bf16[320,128]{1,0:T(8,128)(2,1)S(1)}, u32[]{:S(2)}, u32[]{:S(2)}) collective-permute-start(bf16[320,128]{1,0:T(8,128)(2,1)S(1)} %get-tuple-element.114), channel_id=1, source_target_pairs={{0,24},{8,16},{16,8},{24,0},{1,25},{9,17},{17,9},{25,1},{2,26},{10... | collective-permute-start | bytes 245768 | tf_op jit(solution)/shard_map/ppermute | solution.py:305
  36.7 1.3 %collective-permute-start.16 = (bf16[2,320,128]{2,1,0:T(8,128)(2,1)S(1)}, bf16[2,320,128]{2,1,0:T(8,128)(2,1)S(1)}, u32[]{:S(2)}, u32[]{:S(2)}) collective-permute-start(bf16[2,320,128]{2,1,0:T(8,128)(2,1)S(1)} %pad_maximum_fusion.2), channel_id=1, source_target_pairs={{0,1},{1,0},{2,3},{3,2},{4,5},{5,4},{6,7},{7,6},{8,9},{9,8},{10,11... | collective-permute-start | bytes 491528 | tf_op jit(solution)/shard_map/ppermute | solution.py:305
  38.0 1.8 %collective-permute-start.15 = (bf16[640,128]{1,0:T(8,128)(2,1)S(1)}, bf16[640,128]{1,0:T(8,128)(2,1)S(1)}, u32[]{:S(2)}, u32[]{:S(2)}) collective-permute-start(bf16[640,128]{1,0:T(8,128)(2,1)S(1)} %get-tuple-element.120.own), channel_id=1, source_target_pairs={{0,8},{8,0},{16,24},{24,16},{1,9},{9,1},{17,25},{25,17},{2,10},{10... | collective-permute-start | bytes 491528 | tf_op jit(solution)/shard_map/ppermute | solution.py:305
  39.8 1.5 %project.3 = (f32[2,128,256]{2,1,0:T(8,128)S(1)}, f32[2,128,256]{2,1,0:T(8,128)S(1)}) custom-call(s32[4]{0:T(128)S(1)} %pad_add_fusion.1.where, bf16[2,4,128,640]{3,2,1,0:T(8,128)(2,1)S(1)} %get-tuple-element.106.keep, bf16[4,128,640]{2,1,0:T(8,128)(2,1)S(1)} %collective-permute-done.8.other, bf16[4,128,640]{2,1,0:T(8,128)(2,1)S(1)} %collective-permute-done.9.other_2, ...), custom_call_target="tpu_custom_call" | custom-call | flops 1024 | bytes 1024 | tf_op jit(solution)/shard_map/project/pallas_call | solution.py:118
  41.4 1.6 %collective-permute-start.17 = (f32[2,128,256]{2,1,0:T(8,128)S(1)}, f32[2,128,256]{2,1,0:T(8,128)S(1)}, u32[]{:S(2)}, u32[]{:S(2)}) collective-permute-start(f32[2,128,256]{2,1,0:T(8,128)S(1)} %get-tuple-element.126), channel_id=1, source_target_pairs={{0,4},{4,0},{1,5},{5,1},{2,6},{6,2},{3,7},{7,3},{8,12},{12,8},{9,1... | collective-permute-start | bytes 786440 | tf_op jit(solution)/shard_map/ppermute | solution.py:305
  43.0 1.4 %collective-permute-done.12.refs_0_ = bf16[320,128]{1,0:T(8,128)(2,1)S(1)} collective-permute-done((bf16[320,128]{1,0:T(8,128)(2,1)S(1)}, bf16[320,128]{1,0:T(8,128)(2,1)S(1)}, u32[]{:S(2)}, u32[]{:S(2)}) %collective-permute-start.12) | collective-permute-done | bytes 81952 | tf_op jit(solution)/shard_map/ppermute | solution.py:305
  45.6 1.4 %project.4 = (f32[2,128,128]{2,1,0:T(8,128)S(1)}, f32[2,128,128]{2,1,0:T(8,128)S(1)}) custom-call(s32[4]{0:T(128)S(1)} %pad_add_fusion.1.where, bf16[2,4,128,640]{3,2,1,0:T(8,128)(2,1)S(1)} %get-tuple-element.106.keep, bf16[4,128,640]{2,1,0:T(8,128)(2,1)S(1)} %collective-permute-done.8.other, bf16[4,128,640]{2,1,0:T(8,128)(2,1)S(1)} %collective-permute-done.9.other_2, ...), custom_call_target="tpu_custom_call" | custom-call | flops 1024 | bytes 1024 | tf_op jit(solution)/shard_map/project/pallas_call | solution.py:118
  47.0 1.6 %collective-permute-start.18 = (f32[2,128,128]{2,1,0:T(8,128)S(1)}, f32[2,128,128]{2,1,0:T(8,128)S(1)}, u32[]{:S(2)}, u32[]{:S(2)}) collective-permute-start(f32[2,128,128]{2,1,0:T(8,128)S(1)} %get-tuple-element.127), channel_id=1, source_target_pairs={{0,4},{4,0},{1,5},{5,1},{2,6},{6,2},{3,7},{7,3},{8,12},{12,8},{9,1... | collective-permute-start | bytes 393224 | tf_op jit(solution)/shard_map/ppermute | solution.py:305
  48.7 1.6 %collective-permute-done.14.refs_2_ = bf16[2,320,128]{2,1,0:T(8,128)(2,1)S(1)} collective-permute-done((bf16[2,320,128]{2,1,0:T(8,128)(2,1)S(1)}, bf16[2,320,128]{2,1,0:T(8,128)(2,1)S(1)}, u32[]{:S(2)}, u32[]{:S(2)}) %collective-permute-start.14) | collective-permute-done | bytes 163872 | tf_op jit(solution)/shard_map/ppermute | solution.py:305
  50.3 1.8 %collective-permute-done.18.refs_8_ = f32[2,128,128]{2,1,0:T(8,128)S(1)} collective-permute-done((f32[2,128,128]{2,1,0:T(8,128)S(1)}, f32[2,128,128]{2,1,0:T(8,128)S(1)}, u32[]{:S(2)}, u32[]{:S(2)}) %collective-permute-start.18) | collective-permute-done | bytes 131104 | tf_op jit(solution)/shard_map/ppermute | solution.py:305
  52.0 1.4 %project.5 = (f32[2,128,128]{2,1,0:T(8,128)S(1)}, f32[2,128,128]{2,1,0:T(8,128)S(1)}) custom-call(s32[4]{0:T(128)S(1)} %pad_add_fusion.1.where, bf16[2,4,128,640]{3,2,1,0:T(8,128)(2,1)S(1)} %get-tuple-element.106.keep, bf16[4,128,640]{2,1,0:T(8,128)(2,1)S(1)} %collective-permute-done.8.other, bf16[4,128,640]{2,1,0:T(8,128)(2,1)S(1)} %collective-permute-done.9.other_2, ...), custom_call_target="tpu_custom_call" | custom-call | flops 1024 | bytes 1024 | tf_op jit(solution)/shard_map/project/pallas_call | solution.py:118
  54.1 1.2 %collective-permute-start.22 = (f32[1,128,128]{2,1,0:T(8,128)S(1)}, f32[1,128,128]{2,1,0:T(8,128)S(1)}, u32[]{:S(2)}, u32[]{:S(2)}) collective-permute-start(f32[1,128,128]{2,1,0:T(8,128)S(1)} %get-tuple-element.141), channel_id=1, source_target_pairs={{0,6},{2,4},{4,2},{6,0},{1,7},{3,5},{5,3},{7,1},{8,14},{10,12},{12... | collective-permute-start | bytes 196616 | tf_op jit(solution)/shard_map/ppermute | solution.py:305
  56.0 3.9 %prompt_attention.5 = (f32[128,2048]{1,0:T(8,128)S(1)}, f32[8,2048]{1,0:T(8,128)S(1)}) custom-call(s32[4]{0:T(128)S(1)} %get-tuple-element.144.info, bf16[128,4096]{1,0:T(8,128)(2,1)S(1)} %bitcast.22, bf16[512,1024]{1,0:T(8,128)(2,1)} %collective-permute-done.7.k_ref.v_ref, bf16[512,1024]{1,0:T(8,128)(2,1)} %collective-permute-done.7.k_ref.v_ref, ...), custom_call_target="tpu_custom_call" | custom-call | flops 8589934592 | bytes 1024 | tf_op jit(solution)/shard_map/prompt_attention/pallas_call | solution.py:95
  60.0 3.0 %final_attention.1 = bf16[128,4096]{1,0:T(8,128)(2,1)} custom-call(s32[3]{0:T(128)S(1)} %pad_add_fusion.info, f32[1,128]{1,0:T(1,128)S(1)} %bitcast.30, bf16[128,4096]{1,0:T(8,128)(2,1)S(1)} %bitcast.23, f32[128,2048]{1,0:T(8,128)S(1)} %get-tuple-element.102.refs_0_, f32[8,2048]{1,0:T(8,128)S(1)} %get-tuple-element.103.refs_1_, ...), custom_call_target="tpu_custom_call" | custom-call | flops 1024 | bytes 1024 | tf_op jit(solution)/shard_map/final_attention/pallas_call | solution.py:292
  (59 shorter events, 6.5 us)
Async XLA Ops:
  0.0 11.9 %collective-permute-start.1 = (bf16[128,5120]{1,0:T(8,128)(2,1)}, bf16[128,5120]{1,0:T(8,128)(2,1)S(1)}, u32[]{:S(2)}, u32[]{:S(2)}) collective-permute-start(bf16[128,5120]{1,0:T(8,128)(2,1)} %bitcast.18), channel_id=1, source_target_pairs={{0,2},{2,0},{1,3},{3,1},{4,6},{6,4},{5,7},{7,5},{8,10},{10,8},{9,1... | collective-permute-start | bytes 3932168 | tf_op jit(solution)/shard_map/ppermute | solution.py:305
  0.5 5.5 %collective-permute-start = (bf16[320,1024]{1,0:T(8,128)(2,1)}, bf16[320,1024]{1,0:T(8,128)(2,1)}, u32[]{:S(2)}, u32[]{:S(2)}) collective-permute-start(bf16[320,1024]{1,0:T(8,128)(2,1)} %weight_ref.1), channel_id=1, source_target_pairs={{0,2},{2,0},{1,3},{3,1},{4,6},{6,4},{5,7},{7,5},{8,10},{10,8},{9,1... | collective-permute-start | bytes 1966088 | tf_op jit(solution)/shard_map/ppermute | solution.py:305
  0.6 26.8 %collective-permute-start.7 = (bf16[512,1024]{1,0:T(8,128)(2,1)}, bf16[512,1024]{1,0:T(8,128)(2,1)}, u32[]{:S(2)}, u32[]{:S(2)}) collective-permute-start(bf16[512,1024]{1,0:T(8,128)(2,1)} %bitcast.31), channel_id=1, source_target_pairs={{0,1},{1,0},{2,3},{3,2},{4,5},{5,4},{6,7},{7,6},{8,9},{9,8},{10,11... | collective-permute-start | bytes 3145736 | tf_op jit(solution)/shard_map/ppermute | solution.py:324
  7.1 12.5 %collective-permute-start.3 = (bf16[320,256]{1,0:T(8,128)(2,1)S(1)}, bf16[320,256]{1,0:T(8,128)(2,1)S(1)}, u32[]{:S(2)}, u32[]{:S(2)}) collective-permute-start(bf16[320,256]{1,0:T(8,128)(2,1)S(1)} %get-tuple-element.84), channel_id=1, source_target_pairs={{0,24},{8,16},{16,8},{24,0},{1,25},{9,17},{17,9},{25,1},{2,26},{10... | collective-permute-start | bytes 491528 | tf_op jit(solution)/shard_map/ppermute | solution.py:305
  10.8 14.0 %collective-permute-start.2 = (bf16[320,256]{1,0:T(8,128)(2,1)S(1)}, bf16[320,256]{1,0:T(8,128)(2,1)S(1)}, u32[]{:S(2)}, u32[]{:S(2)}) collective-permute-start(bf16[320,256]{1,0:T(8,128)(2,1)S(1)} %get-tuple-element.84), channel_id=1, source_target_pairs={{0,16},{8,24},{16,0},{24,8},{1,17},{9,25},{17,1},{25,9},{2,18},{10... | collective-permute-start | bytes 491528 | tf_op jit(solution)/shard_map/ppermute | solution.py:305
  10.8 22.1 %collective-permute-start.6 = (bf16[640,256]{1,0:T(8,128)(2,1)S(1)}, bf16[640,256]{1,0:T(8,128)(2,1)S(1)}, u32[]{:S(2)}, u32[]{:S(2)}) collective-permute-start(bf16[640,256]{1,0:T(8,128)(2,1)S(1)} %get-tuple-element.79.own), channel_id=1, source_target_pairs={{0,8},{8,0},{16,24},{24,16},{1,9},{9,1},{17,25},{25,17},{2,10},{10... | collective-permute-start | bytes 983048 | tf_op jit(solution)/shard_map/ppermute | solution.py:305
  12.6 16.4 %collective-permute-start.8 = (bf16[4,128,640]{2,1,0:T(8,128)(2,1)S(1)}, bf16[4,128,640]{2,1,0:T(8,128)(2,1)S(1)}, u32[]{:S(2)}, u32[]{:S(2)}) collective-permute-start(bf16[4,128,640]{2,1,0:T(8,128)(2,1)S(1)} %get-tuple-element.82), channel_id=1, source_target_pairs={{0,4},{4,0},{1,5},{5,1},{2,6},{6,2},{3,7},{7,3},{8,12},{12,8},{9,1... | collective-permute-start | bytes 1966088 | tf_op jit(solution)/shard_map/ppermute | solution.py:305
  24.8 8.2 %collective-permute-start.5 = (bf16[320,128]{1,0:T(8,128)(2,1)S(1)}, bf16[320,128]{1,0:T(8,128)(2,1)S(1)}, u32[]{:S(2)}, u32[]{:S(2)}) collective-permute-start(bf16[320,128]{1,0:T(8,128)(2,1)S(1)} %get-tuple-element.90), channel_id=1, source_target_pairs={{0,24},{8,16},{16,8},{24,0},{1,25},{9,17},{17,9},{25,1},{2,26},{10... | collective-permute-start | bytes 245768 | tf_op jit(solution)/shard_map/ppermute | solution.py:305
  27.4 6.3 %collective-permute-start.4 = (bf16[320,128]{1,0:T(8,128)(2,1)S(1)}, bf16[320,128]{1,0:T(8,128)(2,1)S(1)}, u32[]{:S(2)}, u32[]{:S(2)}) collective-permute-start(bf16[320,128]{1,0:T(8,128)(2,1)S(1)} %get-tuple-element.90), channel_id=1, source_target_pairs={{0,16},{8,24},{16,0},{24,8},{1,17},{9,25},{17,1},{25,9},{2,18},{10... | collective-permute-start | bytes 245768 | tf_op jit(solution)/shard_map/ppermute | solution.py:305
  27.5 9.2 %collective-permute-start.10 = (bf16[2,320,256]{2,1,0:T(8,128)(2,1)S(1)}, bf16[2,320,256]{2,1,0:T(8,128)(2,1)S(1)}, u32[]{:S(2)}, u32[]{:S(2)}) collective-permute-start(bf16[2,320,256]{2,1,0:T(8,128)(2,1)S(1)} %pad_maximum_fusion), channel_id=1, source_target_pairs={{0,1},{1,0},{2,3},{3,2},{4,5},{5,4},{6,7},{7,6},{8,9},{9,8},{10,11... | collective-permute-start | bytes 983048 | tf_op jit(solution)/shard_map/ppermute | solution.py:305
  29.1 4.7 %collective-permute-start.9 = (bf16[4,128,640]{2,1,0:T(8,128)(2,1)S(1)}, bf16[4,128,640]{2,1,0:T(8,128)(2,1)S(1)}, u32[]{:S(2)}, u32[]{:S(2)}) collective-permute-start(bf16[4,128,640]{2,1,0:T(8,128)(2,1)S(1)} %collective-permute-done.8.other), channel_id=1, source_target_pairs={{0,2},{2,0},{1,3},{3,1},{4,6},{6,4},{5,7},{7,5},{8,10},{10,8},{9,1... | collective-permute-start | bytes 1966088 | tf_op jit(solution)/shard_map/ppermute | solution.py:305
  33.7 9.2 %collective-permute-start.13 = (bf16[320,128]{1,0:T(8,128)(2,1)S(1)}, bf16[320,128]{1,0:T(8,128)(2,1)S(1)}, u32[]{:S(2)}, u32[]{:S(2)}) collective-permute-start(bf16[320,128]{1,0:T(8,128)(2,1)S(1)} %get-tuple-element.114), channel_id=1, source_target_pairs={{0,24},{8,16},{16,8},{24,0},{1,25},{9,17},{17,9},{25,1},{2,26},{10... | collective-permute-start | bytes 245768 | tf_op jit(solution)/shard_map/ppermute | solution.py:305
  36.7 7.7 %collective-permute-start.12 = (bf16[320,128]{1,0:T(8,128)(2,1)S(1)}, bf16[320,128]{1,0:T(8,128)(2,1)S(1)}, u32[]{:S(2)}, u32[]{:S(2)}) collective-permute-start(bf16[320,128]{1,0:T(8,128)(2,1)S(1)} %get-tuple-element.114), channel_id=1, source_target_pairs={{0,16},{8,24},{16,0},{24,8},{1,17},{9,25},{17,1},{25,9},{2,18},{10... | collective-permute-start | bytes 245768 | tf_op jit(solution)/shard_map/ppermute | solution.py:305
  36.7 8.6 %collective-permute-start.16 = (bf16[2,320,128]{2,1,0:T(8,128)(2,1)S(1)}, bf16[2,320,128]{2,1,0:T(8,128)(2,1)S(1)}, u32[]{:S(2)}, u32[]{:S(2)}) collective-permute-start(bf16[2,320,128]{2,1,0:T(8,128)(2,1)S(1)} %pad_maximum_fusion.2), channel_id=1, source_target_pairs={{0,1},{1,0},{2,3},{3,2},{4,5},{5,4},{6,7},{7,6},{8,9},{9,8},{10,11... | collective-permute-start | bytes 491528 | tf_op jit(solution)/shard_map/ppermute | solution.py:305
  38.0 7.6 %collective-permute-start.15 = (bf16[640,128]{1,0:T(8,128)(2,1)S(1)}, bf16[640,128]{1,0:T(8,128)(2,1)S(1)}, u32[]{:S(2)}, u32[]{:S(2)}) collective-permute-start(bf16[640,128]{1,0:T(8,128)(2,1)S(1)} %get-tuple-element.120.own), channel_id=1, source_target_pairs={{0,8},{8,0},{16,24},{24,16},{1,9},{9,1},{17,25},{25,17},{2,10},{10... | collective-permute-start | bytes 491528 | tf_op jit(solution)/shard_map/ppermute | solution.py:305
  41.4 8.9 %collective-permute-start.17 = (f32[2,128,256]{2,1,0:T(8,128)S(1)}, f32[2,128,256]{2,1,0:T(8,128)S(1)}, u32[]{:S(2)}, u32[]{:S(2)}) collective-permute-start(f32[2,128,256]{2,1,0:T(8,128)S(1)} %get-tuple-element.126), channel_id=1, source_target_pairs={{0,4},{4,0},{1,5},{5,1},{2,6},{6,2},{3,7},{7,3},{8,12},{12,8},{9,1... | collective-permute-start | bytes 786440 | tf_op jit(solution)/shard_map/ppermute | solution.py:305
  44.4 5.8 %collective-permute-start.14 = (bf16[2,320,128]{2,1,0:T(8,128)(2,1)S(1)}, bf16[2,320,128]{2,1,0:T(8,128)(2,1)S(1)}, u32[]{:S(2)}, u32[]{:S(2)}) collective-permute-start(bf16[2,320,128]{2,1,0:T(8,128)(2,1)S(1)} %pad_maximum_fusion.1), channel_id=1, source_target_pairs={{0,1},{1,0},{2,3},{3,2},{4,5},{5,4},{6,7},{7,6},{8,9},{9,8},{10,11... | collective-permute-start | bytes 491528 | tf_op jit(solution)/shard_map/ppermute | solution.py:305
  45.2 6.8 %collective-permute-start.11 = (bf16[640,128]{1,0:T(8,128)(2,1)S(1)}, bf16[640,128]{1,0:T(8,128)(2,1)S(1)}, u32[]{:S(2)}, u32[]{:S(2)}) collective-permute-start(bf16[640,128]{1,0:T(8,128)(2,1)S(1)} %get-tuple-element.113.own), channel_id=1, source_target_pairs={{0,8},{8,0},{16,24},{24,16},{1,9},{9,1},{17,25},{25,17},{2,10},{10... | collective-permute-start | bytes 491528 | tf_op jit(solution)/shard_map/ppermute | solution.py:305
  47.0 5.0 %collective-permute-start.18 = (f32[2,128,128]{2,1,0:T(8,128)S(1)}, f32[2,128,128]{2,1,0:T(8,128)S(1)}, u32[]{:S(2)}, u32[]{:S(2)}) collective-permute-start(f32[2,128,128]{2,1,0:T(8,128)S(1)} %get-tuple-element.127), channel_id=1, source_target_pairs={{0,4},{4,0},{1,5},{5,1},{2,6},{6,2},{3,7},{7,3},{8,12},{12,8},{9,1... | collective-permute-start | bytes 393224 | tf_op jit(solution)/shard_map/ppermute | solution.py:305
  53.5 6.4 %collective-permute-start.20 = (f32[1,128,128]{2,1,0:T(8,128)S(1)}, f32[1,128,128]{2,1,0:T(8,128)S(1)}, u32[]{:S(2)}, u32[]{:S(2)}) collective-permute-start(f32[1,128,128]{2,1,0:T(8,128)S(1)} %slice_add_fusion.1), channel_id=1, source_target_pairs={{0,2},{2,0},{1,3},{3,1},{4,6},{6,4},{5,7},{7,5},{8,10},{10,8},{9,1... | collective-permute-start | bytes 196616 | tf_op jit(solution)/shard_map/ppermute | solution.py:305
  53.6 6.4 %collective-permute-start.23 = (f32[1,128,128]{2,1,0:T(8,128)S(1)}, f32[1,128,128]{2,1,0:T(8,128)S(1)}, u32[]{:S(2)}, u32[]{:S(2)}) collective-permute-start(f32[1,128,128]{2,1,0:T(8,128)S(1)} %slice.27), channel_id=1, source_target_pairs={{0,2},{2,0},{1,3},{3,1},{4,6},{6,4},{5,7},{7,5},{8,10},{10,8},{9,1... | collective-permute-start | bytes 196616 | tf_op jit(solution)/shard_map/ppermute | solution.py:305
  54.1 5.9 %collective-permute-start.22 = (f32[1,128,128]{2,1,0:T(8,128)S(1)}, f32[1,128,128]{2,1,0:T(8,128)S(1)}, u32[]{:S(2)}, u32[]{:S(2)}) collective-permute-start(f32[1,128,128]{2,1,0:T(8,128)S(1)} %get-tuple-element.141), channel_id=1, source_target_pairs={{0,6},{2,4},{4,2},{6,0},{1,7},{3,5},{5,3},{7,1},{8,14},{10,12},{12... | collective-permute-start | bytes 196616 | tf_op jit(solution)/shard_map/ppermute | solution.py:305
  55.3 4.7 %collective-permute-start.21 = (f32[1,128,128]{2,1,0:T(8,128)S(1)}, f32[1,128,128]{2,1,0:T(8,128)S(1)}, u32[]{:S(2)}, u32[]{:S(2)}) collective-permute-start(f32[1,128,128]{2,1,0:T(8,128)S(1)} %get-tuple-element.142), channel_id=1, source_target_pairs={{0,4},{4,0},{1,5},{5,1},{2,6},{6,2},{3,7},{7,3},{8,12},{12,8},{9,1... | collective-permute-start | bytes 196616 | tf_op jit(solution)/shard_map/ppermute | solution.py:305
  55.8 4.1 %collective-permute-start.19 = (f32[1,128,256]{2,1,0:T(8,128)S(1)}, f32[1,128,256]{2,1,0:T(8,128)S(1)}, u32[]{:S(2)}, u32[]{:S(2)}) collective-permute-start(f32[1,128,256]{2,1,0:T(8,128)S(1)} %slice_add_fusion), channel_id=1, source_target_pairs={{0,2},{2,0},{1,3},{3,1},{4,6},{6,4},{5,7},{7,5},{8,10},{10,8},{9,1... | collective-permute-start | bytes 393224 | tf_op jit(solution)/shard_map/ppermute | solution.py:305
  (7 other events, 32.9 us)

commit v14 on v13

--- a/solution.py
+++ b/solution.py
@@ -198,7 +198,7 @@
 def project_kernel(where, keep, other, other_2, own, near, *refs):
     mine, theirs, whole = refs[-3:]
     far = whole.shape[0]
-    direct, forwarded = refs[:far], refs[far:-3]
+    direct, forwarded, joined = refs[:far], refs[far], refs[far + 1 : -3]
     plane = where[3]
     count, extra = direct[0].shape[0], whole.shape[1] - direct[0].shape[0]
     total = None
@@ -210,21 +210,24 @@
         else:
             piece = whole.at[j - 2]
             piece[pl.ds(pl.multiple_of(plane * extra, 16), count), :] = direct[j - 2][...]
-            rest = forwarded[0][j - 2] if len(forwarded) == 1 else forwarded[j - 2][...]
-            piece[pl.ds(pl.multiple_of((1 - plane) * count, 16), extra), :] = rest
+            piece[pl.ds(pl.multiple_of((1 - plane) * count, 16), extra), :] = forwarded[j - 2]
             weight = piece[...]
         place = where[0] ^ j
         left = jnp.concatenate([keep[0, place], keep[1, place], other[place], other_2[place]], axis=0)
         product = jnp.dot(left, weight, preferred_element_type=jnp.float32)
         total = product if total is None else total + product
+    begin = mine.shape[2] - total.shape[1]
+    for out, old in zip((mine, theirs), joined):
+        out[:, :, :begin] = old[...]
     for i in range(2):
-        mine[i] = total[i * ROWS : (i + 1) * ROWS]
-        theirs[i] = total[(2 + i) * ROWS : (3 + i) * ROWS]
-
-
-def project(where, rows_of_x, own, near, direct, forwarded):
+        mine[i, :, begin:] = total[i * ROWS : (i + 1) * ROWS]
+        theirs[i, :, begin:] = total[(2 + i) * ROWS : (3 + i) * ROWS]
+
+
+def project(where, rows_of_x, own, near, direct, forwarded, joined=()):
     width = own.shape[1]
-    out = jax.ShapeDtypeStruct((2, ROWS, width), jnp.float32)
+    begin = joined[0].shape[2] if joined else 0
+    out = jax.ShapeDtypeStruct((2, ROWS, begin + width), jnp.float32)
     return on_chip(
         project_kernel,
         "project",
@@ -234,7 +237,8 @@
         own,
         near,
         *direct,
-        *forwarded,
+        forwarded,
+        *joined,
         scratch=[pltpu.VMEM((len(direct), own.shape[0], width), jnp.bfloat16)],
     )
 
@@ -329,10 +333,10 @@
     def send(far):
         return [xor_swap(far, "z", j) for j in range(2, steps)]
 
-    def forward(i, stacked):
+    def forward(i):
         helped, direct = row_split(whole[0].shape[0], i)
         parts = [lax.dynamic_slice_in_dim(p, plane * (direct - helped), helped, axis=0) for p in sent[i]]
-        return [xor_swap(part, "blk", 1) for part in ([jnp.stack(parts)] if stacked else parts)]
+        return xor_swap(jnp.stack(parts), "blk", 1)
 
     sent = [send(far[0])]
     near = [xor_swap(whole[0], "z", 1)]
@@ -358,21 +362,21 @@
             offset = 0
         return state
 
-    def sums(i):
-        return project(where, rows_of_x, whole[i], near[i], sent[i], forwarded[i])
+    def sums(i, joined=()):
+        return project(where, rows_of_x, whole[i], near[i], sent[i], forwarded[i], joined)
 
     sent[0], state, far[1], whole[1] = tie((sent[0], state, far[1], whole[1]))
     sent.append(send(far[1]))
     near.append(xor_swap(whole[1], "z", 1))
     sent[0], caches = tie((sent[0], caches))
-    forwarded = [forward(0, True)]
+    forwarded = [forward(0)]
     state, other = tie((state, other))
     rows_of_x = [keep, other, xor_swap(other, "core", 1)]
     halves = [rest(0, state)]
     sent[1], near[0], far[2], halves[0], state, rows_of_x[2] = tie((sent[1], near[0], far[2], halves[0], state, rows_of_x[2]))
     sent.append(send(far[2]))
     forwarded[0], sent[1], whole[2] = tie((forwarded[0], sent[1], whole[2]))
-    forwarded.append(forward(1, True))
+    forwarded.append(forward(1))
     near.append(xor_swap(whole[2], "z", 1))
 
     def owners(mine, theirs):
@@ -381,21 +385,19 @@
 
     mine_0, theirs_0 = sums(0)
     sent[2], mine_0 = tie((sent[2], mine_0))
-    forwarded.append(forward(2, True))
+    forwarded.append(forward(2))
     here_0 = xor_swap(theirs_0, "y", 1)
     forwarded[1], mine_0 = tie((forwarded[1], mine_0))
     mine_1, theirs_1 = sums(1)
-    here_1 = xor_swap(theirs_1, "y", 1)
-    forwarded[2], mine_1, here_0, here_1 = tie((forwarded[2], mine_1, here_0, here_1))
+    forwarded[2], mine_1, theirs_1, here_0 = tie((forwarded[2], mine_1, theirs_1, here_0))
     first = [mine_0, here_0, xor_swap(mine_0[1:] + here_0[1:], "core", 1)]
-    mine_2, theirs_2 = sums(2)
-    third = owners(mine_2, theirs_2)
+    mine_2, theirs_2 = sums(2, (mine_1, theirs_1))
+    second = owners(mine_2, theirs_2)
     state, mine_2 = tie((state, mine_2))
     halves.append(rest(2, state))
-    second = [mine_1, here_1, xor_swap(mine_1[1:] + here_1[1:], "core", 1)]
     info = jnp.concatenate([resp_lengths[0], core[None]]).astype(jnp.int32)
     gain = key_gain[None]
-    return final_attention(info, gain, query, halves, [first, second, third])[None]
+    return final_attention(info, gain, query, halves, [first, second])[None]
 
 
 def solution(mesh):

time: 63.2 us -> 66 us (1.044)
  waiting for transfers between devices: 11.1 us -> 16.6 us
  starting transfers between devices: 26.3 us -> 23.5 us
    ppermute x23 -> x21, waiting for transfers between devices: 11.1 us -> 16.6 us  [xor_swap(): lax.ppermute(array, axis, [(i, i ^ by) for i in range(lax.axis_size(axis))])]
    ppermute x23 -> x21, starting transfers between devices: 23.4 us -> 20.6 us  [xor_swap(): lax.ppermute(array, axis, [(i, i ^ by) for i in range(lax.axis_size(axis))])]
  transfers between devices with their start and end apart: 24 -> 22, of which waited for: 6 -> 6; matrix products, arithmetic and copies ran while one was open for 1% -> 1% of each run, Pallas kernels for 29% -> 28%
where the time goes in v14:
time: 66 us; the launch traced here: 65.7 us
  starting transfers between devices  23.5 us (36%)
  Pallas kernels  23 us (35%)
  waiting for transfers between devices  16.6 us (25%)
  local copies, waits for them, and re-layouts  1.36 us (2%)
  between operations  0.9 us (1%)
    ppermute x21, starting transfers between devices, xor_swap(): lax.ppermute(array, axis, [(i, i ^ by) for i in range(lax.axis_size(axis))])  20.6 us
    ppermute x21, waiting for transfers between devices, xor_swap(): lax.ppermute(array, axis, [(i, i ^ by) for i in range(lax.axis_size(axis))])  16.6 us
    pallas_call x3, Pallas kernels, prompt_attention(): pl.pallas_call(functools.partial(prompt_kernel, first), grid_spec=pltpu.P...  13.2 us
    pallas_call x5, Pallas kernels, on_chip(): pl.pallas_call(kernel, in_specs=[SMEM] + [VMEM] * len(operands), out_spec...  5.62 us
    pallas_call x1, Pallas kernels, final_attention(): pl.pallas_call(functools.partial(final_kernel, [len(chunk) for chunk in c...  3.01 us
    ppermute x1, starting transfers between devices, per_device(): lax.ppermute(caches[-1], 'blk', [(i, (i + 1) % cycle) for i in range(cycl...  2.93 us
  transfers between devices with their start and end apart: 22, of which 6 were waited for; matrix products, arithmetic and copies ran while one was open for 1% of the time, Pallas kernels for 28%

profile of v14, /device:TPU:0, one launch (start us, length us, event | category | flops | bytes accessed | tf_op | source)
XLA Modules:
  0.0 65.7 jit_solution(16299322178456980521)
XLA Ops:
  0.6 2.9 %collective-permute-start.7 = (bf16[512,1024]{1,0:T(8,128)(2,1)}, bf16[512,1024]{1,0:T(8,128)(2,1)}, u32[]{:S(2)}, u32[]{:S(2)}) collective-permute-start(bf16[512,1024]{1,0:T(8,128)(2,1)} %bitcast.31), channel_id=1, source_target_pairs={{0,1},{1,0},{2,3},{3,2},{4,5},{5,4},{6,7},{7,6},{8,9},{9,8},{10,11... | collective-permute-start | bytes 3145736 | tf_op jit(solution)/shard_map/ppermute | solution.py:328
  3.5 1.1 %copy-done.2 = bf16[320,1024]{1,0:T(8,128)(2,1)S(1)} copy-done((bf16[320,1024]{1,0:T(8,128)(2,1)S(1)}, bf16[320,1024]{1,0:T(8,128)(2,1)}, u32[]{:S(2)}) %copy-start.2) | copy-done | bytes 655384
  6.0 1.2 %pack_weight.1 = (bf16[640,256]{1,0:T(8,128)(2,1)S(1)}, bf16[640,128]{1,0:T(8,128)(2,1)S(1)}, bf16[640,128]{1,0:T(8,128)(2,1)S(1)}, bf16[320,256]{1,0:T(8,128)(2...) custom-call(s32[4]{0:T(128)S(1)} %pad_add_fusion.1.where, ...), custom_call_target="tpu_custom_call", output_to_operand_aliasing={{0}: (2, {}), {1}: (3, {}), {2}: (4, {})} | custom-call | flops 1024 | bytes 1024 | tf_op jit(solution)/shard_map/pack_weight/pallas_call | solution.py:185
  7.1 3.7 %collective-permute-start.3 = (bf16[320,256]{1,0:T(8,128)(2,1)S(1)}, bf16[320,256]{1,0:T(8,128)(2,1)S(1)}, u32[]{:S(2)}, u32[]{:S(2)}) collective-permute-start(bf16[320,256]{1,0:T(8,128)(2,1)S(1)} %get-tuple-element.84), channel_id=1, source_target_pairs={{0,24},{8,16},{16,8},{24,0},{1,25},{9,17},{17,9},{25,1},{2,26},{10... | collective-permute-start | bytes 491528 | tf_op jit(solution)/shard_map/ppermute | solution.py:309
  12.6 1.6 %collective-permute-start.8 = (bf16[4,128,640]{2,1,0:T(8,128)(2,1)S(1)}, bf16[4,128,640]{2,1,0:T(8,128)(2,1)S(1)}, u32[]{:S(2)}, u32[]{:S(2)}) collective-permute-start(bf16[4,128,640]{2,1,0:T(8,128)(2,1)S(1)} %get-tuple-element.82), channel_id=1, source_target_pairs={{0,4},{4,0},{1,5},{5,1},{2,6},{6,2},{3,7},{7,3},{8,12},{12,8},{9,1... | collective-permute-start | bytes 1966088 | tf_op jit(solution)/shard_map/ppermute | solution.py:309
  14.2 5.4 %prompt_attention.3 = (f32[128,4096]{1,0:T(8,128)S(1)}, f32[8,4096]{1,0:T(8,128)S(1)}) custom-call(s32[4]{0:T(128)S(1)} %get-tuple-element.143.info, bf16[128,4096]{1,0:T(8,128)(2,1)S(1)} %bitcast.20, bf16[512,1024]{1,0:T(8,128)(2,1)S(1)} %bitcast.32, bf16[512,1024]{1,0:T(8,128)(2,1)S(1)} %bitcast.33), custom_call_target="tpu_custom_call" | custom-call | flops 17179869184 | bytes 1024 | tf_op jit(solution)/shard_map/prompt_attention/pallas_call | solution.py:95
  19.7 5.1 %collective-permute-done.2.refs_0_ = bf16[320,256]{1,0:T(8,128)(2,1)S(1)} collective-permute-done((bf16[320,256]{1,0:T(8,128)(2,1)S(1)}, bf16[320,256]{1,0:T(8,128)(2,1)S(1)}, u32[]{:S(2)}, u32[]{:S(2)}) %collective-permute-start.2) | collective-permute-done | bytes 163872 | tf_op jit(solution)/shard_map/ppermute | solution.py:309
  24.8 2.6 %collective-permute-start.5 = (bf16[320,128]{1,0:T(8,128)(2,1)S(1)}, bf16[320,128]{1,0:T(8,128)(2,1)S(1)}, u32[]{:S(2)}, u32[]{:S(2)}) collective-permute-start(bf16[320,128]{1,0:T(8,128)(2,1)S(1)} %get-tuple-element.90), channel_id=1, source_target_pairs={{0,24},{8,16},{16,8},{24,0},{1,25},{9,17},{17,9},{25,1},{2,26},{10... | collective-permute-start | bytes 245768 | tf_op jit(solution)/shard_map/ppermute | solution.py:309
  27.5 1.6 %collective-permute-start.10 = (bf16[2,320,256]{2,1,0:T(8,128)(2,1)S(1)}, bf16[2,320,256]{2,1,0:T(8,128)(2,1)S(1)}, u32[]{:S(2)}, u32[]{:S(2)}) collective-permute-start(bf16[2,320,256]{2,1,0:T(8,128)(2,1)S(1)} %pad_maximum_fusion), channel_id=1, source_target_pairs={{0,1},{1,0},{2,3},{3,2},{4,5},{5,4},{6,7},{7,6},{8,9},{9,8},{10,11... | collective-permute-start | bytes 983048 | tf_op jit(solution)/shard_map/ppermute | solution.py:309
  29.1 3.9 %prompt_attention.4 = (f32[128,2048]{1,0:T(8,128)S(1)}, f32[8,2048]{1,0:T(8,128)S(1)}) custom-call(s32[4]{0:T(128)S(1)} %get-tuple-element.144.info, bf16[128,4096]{1,0:T(8,128)(2,1)S(1)} %bitcast.21, bf16[512,1024]{1,0:T(8,128)(2,1)} %collective-permute-done.7.k_ref.v_ref, bf16[512,1024]{1,0:T(8,128)(2,1)} %collective-permute-done.7.k_ref.v_ref, ...), custom_call_target="tpu_custom_call" | custom-call | flops 8589934592 | bytes 1024 | tf_op jit(solution)/shard_map/prompt_attention/pallas_call | solution.py:95
  33.0 1.8 %collective-permute-start.15 = (bf16[640,128]{1,0:T(8,128)(2,1)S(1)}, bf16[640,128]{1,0:T(8,128)(2,1)S(1)}, u32[]{:S(2)}, u32[]{:S(2)}) collective-permute-start(bf16[640,128]{1,0:T(8,128)(2,1)S(1)} %get-tuple-element.120.own), channel_id=1, source_target_pairs={{0,8},{8,0},{16,24},{24,16},{1,9},{9,1},{17,25},{25,17},{2,10},{10... | collective-permute-start | bytes 491528 | tf_op jit(solution)/shard_map/ppermute | solution.py:309
  34.7 2.5 %collective-permute-start.13 = (bf16[320,128]{1,0:T(8,128)(2,1)S(1)}, bf16[320,128]{1,0:T(8,128)(2,1)S(1)}, u32[]{:S(2)}, u32[]{:S(2)}) collective-permute-start(bf16[320,128]{1,0:T(8,128)(2,1)S(1)} %get-tuple-element.114), channel_id=1, source_target_pairs={{0,24},{8,16},{16,8},{24,0},{1,25},{9,17},{17,9},{25,1},{2,26},{10... | collective-permute-start | bytes 245768 | tf_op jit(solution)/shard_map/ppermute | solution.py:309
  37.4 0.8 %collective-permute-start.16 = (bf16[2,320,128]{2,1,0:T(8,128)(2,1)S(1)}, bf16[2,320,128]{2,1,0:T(8,128)(2,1)S(1)}, u32[]{:S(2)}, u32[]{:S(2)}) collective-permute-start(bf16[2,320,128]{2,1,0:T(8,128)(2,1)S(1)} %pad_maximum_fusion.2), channel_id=1, source_target_pairs={{0,1},{1,0},{2,3},{3,2},{4,5},{5,4},{6,7},{7,6},{8,9},{9,8},{10,11... | collective-permute-start | bytes 491528 | tf_op jit(solution)/shard_map/ppermute | solution.py:309
  38.2 1.5 %project.3 = (f32[2,128,256]{2,1,0:T(8,128)S(1)}, f32[2,128,256]{2,1,0:T(8,128)S(1)}) custom-call(s32[4]{0:T(128)S(1)} %pad_add_fusion.1.where, bf16[2,4,128,640]{3,2,1,0:T(8,128)(2,1)S(1)} %get-tuple-element.106.keep, bf16[4,128,640]{2,1,0:T(8,128)(2,1)S(1)} %collective-permute-done.8.other, bf16[4,128,640]{2,1,0:T(8,128)(2,1)S(1)} %collective-permute-done.9.other_2, ...), custom_call_target="tpu_custom_call" | custom-call | flops 1024 | bytes 1024 | tf_op jit(solution)/shard_map/project/pallas_call | solution.py:118
  39.7 1.6 %collective-permute-start.17 = (f32[2,128,256]{2,1,0:T(8,128)S(1)}, f32[2,128,256]{2,1,0:T(8,128)S(1)}, u32[]{:S(2)}, u32[]{:S(2)}) collective-permute-start(f32[2,128,256]{2,1,0:T(8,128)S(1)} %get-tuple-element.127), channel_id=1, source_target_pairs={{0,4},{4,0},{1,5},{5,1},{2,6},{6,2},{3,7},{7,3},{8,12},{12,8},{9,1... | collective-permute-start | bytes 786440 | tf_op jit(solution)/shard_map/ppermute | solution.py:309
  41.3 2.7 %collective-permute-done.13.refs_1_ = bf16[320,128]{1,0:T(8,128)(2,1)S(1)} collective-permute-done((bf16[320,128]{1,0:T(8,128)(2,1)S(1)}, bf16[320,128]{1,0:T(8,128)(2,1)S(1)}, u32[]{:S(2)}, u32[]{:S(2)}) %collective-permute-start.13) | collective-permute-done | bytes 81952 | tf_op jit(solution)/shard_map/ppermute | solution.py:309
  44.0 2.0 %collective-permute-done.12.refs_0_ = bf16[320,128]{1,0:T(8,128)(2,1)S(1)} collective-permute-done((bf16[320,128]{1,0:T(8,128)(2,1)S(1)}, bf16[320,128]{1,0:T(8,128)(2,1)S(1)}, u32[]{:S(2)}, u32[]{:S(2)}) %collective-permute-start.12) | collective-permute-done | bytes 81952 | tf_op jit(solution)/shard_map/ppermute | solution.py:309
  46.8 1.4 %project.4 = (f32[2,128,128]{2,1,0:T(8,128)S(1)}, f32[2,128,128]{2,1,0:T(8,128)S(1)}) custom-call(s32[4]{0:T(128)S(1)} %pad_add_fusion.1.where, bf16[2,4,128,640]{3,2,1,0:T(8,128)(2,1)S(1)} %get-tuple-element.106.keep, bf16[4,128,640]{2,1,0:T(8,128)(2,1)S(1)} %collective-permute-done.8.other, bf16[4,128,640]{2,1,0:T(8,128)(2,1)S(1)} %collective-permute-done.9.other_2, ...), custom_call_target="tpu_custom_call" | custom-call | flops 1024 | bytes 1024 | tf_op jit(solution)/shard_map/project/pallas_call | solution.py:118
  48.2 3.1 %collective-permute-done.14.refs_2_ = bf16[2,320,128]{2,1,0:T(8,128)(2,1)S(1)} collective-permute-done((bf16[2,320,128]{2,1,0:T(8,128)(2,1)S(1)}, bf16[2,320,128]{2,1,0:T(8,128)(2,1)S(1)}, u32[]{:S(2)}, u32[]{:S(2)}) %collective-permute-start.14) | collective-permute-done | bytes 163872 | tf_op jit(solution)/shard_map/ppermute | solution.py:309
  52.1 1.4 %project.5 = (f32[2,128,256]{2,1,0:T(8,128)S(1)}, f32[2,128,256]{2,1,0:T(8,128)S(1)}) custom-call(s32[4]{0:T(128)S(1)} %pad_add_fusion.1.where, bf16[2,4,128,640]{3,2,1,0:T(8,128)(2,1)S(1)} %get-tuple-element.106.keep, bf16[4,128,640]{2,1,0:T(8,128)(2,1)S(1)} %collective-permute-done.8.other, bf16[4,128,640]{2,1,0:T(8,128)(2,1)S(1)} %collective-permute-done.9.other_2, ...), custom_call_target="tpu_custom_call" | custom-call | flops 1024 | bytes 1024 | tf_op jit(solution)/shard_map/project/pallas_call | solution.py:118
  54.1 1.2 %collective-permute-start.20 = (f32[1,128,256]{2,1,0:T(8,128)S(1)}, f32[1,128,256]{2,1,0:T(8,128)S(1)}, u32[]{:S(2)}, u32[]{:S(2)}) collective-permute-start(f32[1,128,256]{2,1,0:T(8,128)S(1)} %get-tuple-element.141), channel_id=1, source_target_pairs={{0,6},{2,4},{4,2},{6,0},{1,7},{3,5},{5,3},{7,1},{8,14},{10,12},{12... | collective-permute-start | bytes 393224 | tf_op jit(solution)/shard_map/ppermute | solution.py:309
  55.8 3.9 %prompt_attention.5 = (f32[128,2048]{1,0:T(8,128)S(1)}, f32[8,2048]{1,0:T(8,128)S(1)}) custom-call(s32[4]{0:T(128)S(1)} %get-tuple-element.144.info, bf16[128,4096]{1,0:T(8,128)(2,1)S(1)} %bitcast.22, bf16[512,1024]{1,0:T(8,128)(2,1)} %collective-permute-done.7.k_ref.v_ref, bf16[512,1024]{1,0:T(8,128)(2,1)} %collective-permute-done.7.k_ref.v_ref, ...), custom_call_target="tpu_custom_call" | custom-call | flops 8589934592 | bytes 1024 | tf_op jit(solution)/shard_map/prompt_attention/pallas_call | solution.py:95
  59.7 3.0 %collective-permute-done.19.refs_8_ = f32[1,128,256]{2,1,0:T(8,128)S(1)} collective-permute-done((f32[1,128,256]{2,1,0:T(8,128)S(1)}, f32[1,128,256]{2,1,0:T(8,128)S(1)}, u32[]{:S(2)}, u32[]{:S(2)}) %collective-permute-start.19) | collective-permute-done | bytes 131104 | tf_op jit(solution)/shard_map/ppermute | solution.py:309
  62.7 3.0 %final_attention.1 = bf16[128,4096]{1,0:T(8,128)(2,1)} custom-call(s32[3]{0:T(128)S(1)} %pad_add_fusion.info, f32[1,128]{1,0:T(1,128)S(1)} %bitcast.30, bf16[128,4096]{1,0:T(8,128)(2,1)S(1)} %bitcast.23, f32[128,2048]{1,0:T(8,128)S(1)} %get-tuple-element.102.refs_0_, f32[8,2048]{1,0:T(8,128)S(1)} %get-tuple-element.103.refs_1_, ...), custom_call_target="tpu_custom_call" | custom-call | flops 1024 | bytes 1024 | tf_op jit(solution)/shard_map/final_attention/pallas_call | solution.py:296
  (54 shorter events, 5.9 us)
Async XLA Ops:
  0.0 11.9 %copy-start = (bf16[1,128,5120]{2,1,0:T(8,128)(2,1)S(1)}, bf16[1,128,5120]{2,1,0:T(8,128)(2,1)}, u32[]{:S(2)}) copy-start(bf16[1,128,5120]{2,1,0:T(8,128)(2,1)} %param.8) | copy-start | bytes 3932164
  0.0 11.9 %collective-permute-start.1 = (bf16[128,5120]{1,0:T(8,128)(2,1)}, bf16[128,5120]{1,0:T(8,128)(2,1)S(1)}, u32[]{:S(2)}, u32[]{:S(2)}) collective-permute-start(bf16[128,5120]{1,0:T(8,128)(2,1)} %bitcast.18), channel_id=1, source_target_pairs={{0,2},{2,0},{1,3},{3,1},{4,6},{6,4},{5,7},{7,5},{8,10},{10,8},{9,1... | collective-permute-start | bytes 3932168 | tf_op jit(solution)/shard_map/ppermute | solution.py:309
  0.5 5.5 %collective-permute-start = (bf16[320,1024]{1,0:T(8,128)(2,1)}, bf16[320,1024]{1,0:T(8,128)(2,1)}, u32[]{:S(2)}, u32[]{:S(2)}) collective-permute-start(bf16[320,1024]{1,0:T(8,128)(2,1)} %weight_ref.1), channel_id=1, source_target_pairs={{0,2},{2,0},{1,3},{3,1},{4,6},{6,4},{5,7},{7,5},{8,10},{10,8},{9,1... | collective-permute-start | bytes 1966088 | tf_op jit(solution)/shard_map/ppermute | solution.py:309
  0.6 26.8 %collective-permute-start.7 = (bf16[512,1024]{1,0:T(8,128)(2,1)}, bf16[512,1024]{1,0:T(8,128)(2,1)}, u32[]{:S(2)}, u32[]{:S(2)}) collective-permute-start(bf16[512,1024]{1,0:T(8,128)(2,1)} %bitcast.31), channel_id=1, source_target_pairs={{0,1},{1,0},{2,3},{3,2},{4,5},{5,4},{6,7},{7,6},{8,9},{9,8},{10,11... | collective-permute-start | bytes 3145736 | tf_op jit(solution)/shard_map/ppermute | solution.py:328
  7.1 12.5 %collective-permute-start.3 = (bf16[320,256]{1,0:T(8,128)(2,1)S(1)}, bf16[320,256]{1,0:T(8,128)(2,1)S(1)}, u32[]{:S(2)}, u32[]{:S(2)}) collective-permute-start(bf16[320,256]{1,0:T(8,128)(2,1)S(1)} %get-tuple-element.84), channel_id=1, source_target_pairs={{0,24},{8,16},{16,8},{24,0},{1,25},{9,17},{17,9},{25,1},{2,26},{10... | collective-permute-start | bytes 491528 | tf_op jit(solution)/shard_map/ppermute | solution.py:309
  10.8 14.0 %collective-permute-start.2 = (bf16[320,256]{1,0:T(8,128)(2,1)S(1)}, bf16[320,256]{1,0:T(8,128)(2,1)S(1)}, u32[]{:S(2)}, u32[]{:S(2)}) collective-permute-start(bf16[320,256]{1,0:T(8,128)(2,1)S(1)} %get-tuple-element.84), channel_id=1, source_target_pairs={{0,16},{8,24},{16,0},{24,8},{1,17},{9,25},{17,1},{25,9},{2,18},{10... | collective-permute-start | bytes 491528 | tf_op jit(solution)/shard_map/ppermute | solution.py:309
  10.8 22.1 %collective-permute-start.6 = (bf16[640,256]{1,0:T(8,128)(2,1)S(1)}, bf16[640,256]{1,0:T(8,128)(2,1)S(1)}, u32[]{:S(2)}, u32[]{:S(2)}) collective-permute-start(bf16[640,256]{1,0:T(8,128)(2,1)S(1)} %get-tuple-element.79.own), channel_id=1, source_target_pairs={{0,8},{8,0},{16,24},{24,16},{1,9},{9,1},{17,25},{25,17},{2,10},{10... | collective-permute-start | bytes 983048 | tf_op jit(solution)/shard_map/ppermute | solution.py:309
  12.6 16.4 %collective-permute-start.8 = (bf16[4,128,640]{2,1,0:T(8,128)(2,1)S(1)}, bf16[4,128,640]{2,1,0:T(8,128)(2,1)S(1)}, u32[]{:S(2)}, u32[]{:S(2)}) collective-permute-start(bf16[4,128,640]{2,1,0:T(8,128)(2,1)S(1)} %get-tuple-element.82), channel_id=1, source_target_pairs={{0,4},{4,0},{1,5},{5,1},{2,6},{6,2},{3,7},{7,3},{8,12},{12,8},{9,1... | collective-permute-start | bytes 1966088 | tf_op jit(solution)/shard_map/ppermute | solution.py:309
  24.8 9.9 %collective-permute-start.5 = (bf16[320,128]{1,0:T(8,128)(2,1)S(1)}, bf16[320,128]{1,0:T(8,128)(2,1)S(1)}, u32[]{:S(2)}, u32[]{:S(2)}) collective-permute-start(bf16[320,128]{1,0:T(8,128)(2,1)S(1)} %get-tuple-element.90), channel_id=1, source_target_pairs={{0,24},{8,16},{16,8},{24,0},{1,25},{9,17},{17,9},{25,1},{2,26},{10... | collective-permute-start | bytes 245768 | tf_op jit(solution)/shard_map/ppermute | solution.py:309
  27.4 7.3 %collective-permute-start.4 = (bf16[320,128]{1,0:T(8,128)(2,1)S(1)}, bf16[320,128]{1,0:T(8,128)(2,1)S(1)}, u32[]{:S(2)}, u32[]{:S(2)}) collective-permute-start(bf16[320,128]{1,0:T(8,128)(2,1)S(1)} %get-tuple-element.90), channel_id=1, source_target_pairs={{0,16},{8,24},{16,0},{24,8},{1,17},{9,25},{17,1},{25,9},{2,18},{10... | collective-permute-start | bytes 245768 | tf_op jit(solution)/shard_map/ppermute | solution.py:309
  27.5 9.9 %collective-permute-start.10 = (bf16[2,320,256]{2,1,0:T(8,128)(2,1)S(1)}, bf16[2,320,256]{2,1,0:T(8,128)(2,1)S(1)}, u32[]{:S(2)}, u32[]{:S(2)}) collective-permute-start(bf16[2,320,256]{2,1,0:T(8,128)(2,1)S(1)} %pad_maximum_fusion), channel_id=1, source_target_pairs={{0,1},{1,0},{2,3},{3,2},{4,5},{5,4},{6,7},{7,6},{8,9},{9,8},{10,11... | collective-permute-start | bytes 983048 | tf_op jit(solution)/shard_map/ppermute | solution.py:309
  29.1 5.6 %collective-permute-start.9 = (bf16[4,128,640]{2,1,0:T(8,128)(2,1)S(1)}, bf16[4,128,640]{2,1,0:T(8,128)(2,1)S(1)}, u32[]{:S(2)}, u32[]{:S(2)}) collective-permute-start(bf16[4,128,640]{2,1,0:T(8,128)(2,1)S(1)} %collective-permute-done.8.other), channel_id=1, source_target_pairs={{0,2},{2,0},{1,3},{3,1},{4,6},{6,4},{5,7},{7,5},{8,10},{10,8},{9,1... | collective-permute-start | bytes 1966088 | tf_op jit(solution)/shard_map/ppermute | solution.py:309
  33.0 13.9 %collective-permute-start.15 = (bf16[640,128]{1,0:T(8,128)(2,1)S(1)}, bf16[640,128]{1,0:T(8,128)(2,1)S(1)}, u32[]{:S(2)}, u32[]{:S(2)}) collective-permute-start(bf16[640,128]{1,0:T(8,128)(2,1)S(1)} %get-tuple-element.120.own), channel_id=1, source_target_pairs={{0,8},{8,0},{16,24},{24,16},{1,9},{9,1},{17,25},{25,17},{2,10},{10... | collective-permute-start | bytes 491528 | tf_op jit(solution)/shard_map/ppermute | solution.py:309
  34.7 9.3 %collective-permute-start.13 = (bf16[320,128]{1,0:T(8,128)(2,1)S(1)}, bf16[320,128]{1,0:T(8,128)(2,1)S(1)}, u32[]{:S(2)}, u32[]{:S(2)}) collective-permute-start(bf16[320,128]{1,0:T(8,128)(2,1)S(1)} %get-tuple-element.114), channel_id=1, source_target_pairs={{0,24},{8,16},{16,8},{24,0},{1,25},{9,17},{17,9},{25,1},{2,26},{10... | collective-permute-start | bytes 245768 | tf_op jit(solution)/shard_map/ppermute | solution.py:309
  37.3 8.7 %collective-permute-start.12 = (bf16[320,128]{1,0:T(8,128)(2,1)S(1)}, bf16[320,128]{1,0:T(8,128)(2,1)S(1)}, u32[]{:S(2)}, u32[]{:S(2)}) collective-permute-start(bf16[320,128]{1,0:T(8,128)(2,1)S(1)} %get-tuple-element.114), channel_id=1, source_target_pairs={{0,16},{8,24},{16,0},{24,8},{1,17},{9,25},{17,1},{25,9},{2,18},{10... | collective-permute-start | bytes 245768 | tf_op jit(solution)/shard_map/ppermute | solution.py:309
  37.4 9.5 %collective-permute-start.16 = (bf16[2,320,128]{2,1,0:T(8,128)(2,1)S(1)}, bf16[2,320,128]{2,1,0:T(8,128)(2,1)S(1)}, u32[]{:S(2)}, u32[]{:S(2)}) collective-permute-start(bf16[2,320,128]{2,1,0:T(8,128)(2,1)S(1)} %pad_maximum_fusion.2), channel_id=1, source_target_pairs={{0,1},{1,0},{2,3},{3,2},{4,5},{5,4},{6,7},{7,6},{8,9},{9,8},{10,11... | collective-permute-start | bytes 491528 | tf_op jit(solution)/shard_map/ppermute | solution.py:309
  38.2 8.6 %copy-start.6 = (s32[1,2]{1,0:T(1,128)S(1)}, s32[1,2]{1,0:T(1,128)}, u32[]{:S(2)}) copy-start(s32[1,2]{1,0:T(1,128)} %param.15) | copy-start | bytes 28
  39.7 11.7 %collective-permute-start.17 = (f32[2,128,256]{2,1,0:T(8,128)S(1)}, f32[2,128,256]{2,1,0:T(8,128)S(1)}, u32[]{:S(2)}, u32[]{:S(2)}) collective-permute-start(f32[2,128,256]{2,1,0:T(8,128)S(1)} %get-tuple-element.127), channel_id=1, source_target_pairs={{0,4},{4,0},{1,5},{5,1},{2,6},{6,2},{3,7},{7,3},{8,12},{12,8},{9,1... | collective-permute-start | bytes 786440 | tf_op jit(solution)/shard_map/ppermute | solution.py:309
  46.0 5.4 %collective-permute-start.14 = (bf16[2,320,128]{2,1,0:T(8,128)(2,1)S(1)}, bf16[2,320,128]{2,1,0:T(8,128)(2,1)S(1)}, u32[]{:S(2)}, u32[]{:S(2)}) collective-permute-start(bf16[2,320,128]{2,1,0:T(8,128)(2,1)S(1)} %pad_maximum_fusion.1), channel_id=1, source_target_pairs={{0,1},{1,0},{2,3},{3,2},{4,5},{5,4},{6,7},{7,6},{8,9},{9,8},{10,11... | collective-permute-start | bytes 491528 | tf_op jit(solution)/shard_map/ppermute | solution.py:309
  46.8 5.3 %collective-permute-start.11 = (bf16[640,128]{1,0:T(8,128)(2,1)S(1)}, bf16[640,128]{1,0:T(8,128)(2,1)S(1)}, u32[]{:S(2)}, u32[]{:S(2)}) collective-permute-start(bf16[640,128]{1,0:T(8,128)(2,1)S(1)} %get-tuple-element.113.own), channel_id=1, source_target_pairs={{0,8},{8,0},{16,24},{24,16},{1,9},{9,1},{17,25},{25,17},{2,10},{10... | collective-permute-start | bytes 491528 | tf_op jit(solution)/shard_map/ppermute | solution.py:309
  53.5 6.2 %collective-permute-start.18 = (f32[1,128,256]{2,1,0:T(8,128)S(1)}, f32[1,128,256]{2,1,0:T(8,128)S(1)}, u32[]{:S(2)}, u32[]{:S(2)}) collective-permute-start(f32[1,128,256]{2,1,0:T(8,128)S(1)} %slice_add_fusion), channel_id=1, source_target_pairs={{0,2},{2,0},{1,3},{3,1},{4,6},{6,4},{5,7},{7,5},{8,10},{10,8},{9,1... | collective-permute-start | bytes 393224 | tf_op jit(solution)/shard_map/ppermute | solution.py:309
  53.6 6.1 %collective-permute-start.21 = (f32[1,128,256]{2,1,0:T(8,128)S(1)}, f32[1,128,256]{2,1,0:T(8,128)S(1)}, u32[]{:S(2)}, u32[]{:S(2)}) collective-permute-start(f32[1,128,256]{2,1,0:T(8,128)S(1)} %slice.19), channel_id=1, source_target_pairs={{0,2},{2,0},{1,3},{3,1},{4,6},{6,4},{5,7},{7,5},{8,10},{10,8},{9,1... | collective-permute-start | bytes 393224 | tf_op jit(solution)/shard_map/ppermute | solution.py:309
  54.1 5.6 %collective-permute-start.20 = (f32[1,128,256]{2,1,0:T(8,128)S(1)}, f32[1,128,256]{2,1,0:T(8,128)S(1)}, u32[]{:S(2)}, u32[]{:S(2)}) collective-permute-start(f32[1,128,256]{2,1,0:T(8,128)S(1)} %get-tuple-element.141), channel_id=1, source_target_pairs={{0,6},{2,4},{4,2},{6,0},{1,7},{3,5},{5,3},{7,1},{8,14},{10,12},{12... | collective-permute-start | bytes 393224 | tf_op jit(solution)/shard_map/ppermute | solution.py:309
  55.3 7.4 %collective-permute-start.19 = (f32[1,128,256]{2,1,0:T(8,128)S(1)}, f32[1,128,256]{2,1,0:T(8,128)S(1)}, u32[]{:S(2)}, u32[]{:S(2)}) collective-permute-start(f32[1,128,256]{2,1,0:T(8,128)S(1)} %get-tuple-element.142), channel_id=1, source_target_pairs={{0,4},{4,0},{1,5},{5,1},{2,6},{6,2},{3,7},{7,3},{8,12},{12,8},{9,1... | collective-permute-start | bytes 393224 | tf_op jit(solution)/shard_map/ppermute | solution.py:309
  (5 other events, 20.1 us)

commit v15 on v10

--- a/solution.py
+++ b/solution.py
@@ -24,7 +24,6 @@
 HINT = pl.CostEstimate(flops=1024, bytes_accessed=1024, transcendentals=0)
 
 CHUNKS = ((0, 2), (2, 2))
-HELP = (5, 5)
 
 
 def pair_queries(q_ref, g, extra=None):
@@ -148,11 +147,6 @@
     return on_chip(pack_rows_kernel, "pack_rows", outs, where, own, got)
 
 
-def row_split(rows, i):
-    helped = rows * HELP[i] // 10
-    return helped, rows - helped
-
-
 def own_rows_kernel(where, weight_ref, *outs):
     rows = weight_ref.shape[0]
     for out, (head, heads) in zip(outs, CHUNKS):
@@ -165,23 +159,40 @@
     return on_chip(own_rows_kernel, "own_rows", outs, where, weight)
 
 
+def far_first_kernel(where, whole_ref, got_ref, far):
+    rows, core, plane = got_ref.shape[0], where[2], where[3]
+    head, heads = CHUNKS[0]
+
+    @pl.when(core == plane)
+    def _():
+        far[...] = whole_ref[pl.ds(pl.multiple_of(core * rows, 16), rows), :]
+
+    @pl.when(core != plane)
+    def _():
+        far[...] = got_ref[:, pl.ds(pl.multiple_of((core * KVH + head) * HD, 128), heads * HD)]
+
+
+def far_first(where, whole, got):
+    out = jax.ShapeDtypeStruct((got.shape[0], whole.shape[1]), whole.dtype)
+    return on_chip(far_first_kernel, "far_first", [out], where, whole, got)[0]
+
+
 def pack_weight_kernel(where, got_ref, *refs):
     count = len(CHUNKS)
     wholes, fars = refs[count : 2 * count], refs[2 * count :]
     rows = got_ref.shape[0]
     core, plane = where[2], where[3]
-    for whole, far, (head, heads) in zip(wholes, fars, CHUNKS):
+    for whole, (head, heads) in zip(wholes, CHUNKS):
         columns = pl.ds(pl.multiple_of((core * KVH + head) * HD, 128), heads * HD)
         whole[pl.ds(pl.multiple_of((1 - core) * rows, 16), rows), :] = got_ref[:, columns]
-        direct = far.shape[0]
-        far[...] = whole[pl.ds(pl.multiple_of(plane * (2 * rows - direct), 16), direct), :]
+    for whole, far in zip(wholes[1:], fars):
+        far[...] = whole[pl.ds(pl.multiple_of(plane * rows, 16), rows), :]
 
 
 def pack_weight(where, got, wholes):
     count = len(CHUNKS)
     outs = [jax.ShapeDtypeStruct(whole.shape, whole.dtype) for whole in wholes]
-    for i, whole in enumerate(wholes):
-        outs.append(jax.ShapeDtypeStruct((row_split(whole.shape[0], i)[1], whole.shape[1]), whole.dtype))
+    outs += [jax.ShapeDtypeStruct((got.shape[0], whole.shape[1]), whole.dtype) for whole in wholes[1:]]
     outs = pl.pallas_call(
         pack_weight_kernel,
         in_specs=[SMEM] + [VMEM] * (1 + count),
@@ -324,15 +335,16 @@
         caches.append(lax.ppermute(caches[-1], "blk", [(i, (i + 1) % cycle) for i in range(cycle)]))
 
     wholes, got_weight = tie((own_rows(where, kv_weight), got_weight))
-    whole, far = pack_weight(where, got_weight, wholes)
+    far = far_first(where, wholes[0], got_weight)
+    got_weight, far = tie((got_weight, far))
+    whole, rest = pack_weight(where, got_weight, wholes)
+    far = [far, *rest]
 
     def send(far):
         return [xor_swap(far, "z", j) for j in range(2, steps)]
 
-    def forward(i, stacked):
-        helped, direct = row_split(whole[0].shape[0], i)
-        parts = [lax.dynamic_slice_in_dim(p, plane * (direct - helped), helped, axis=0) for p in sent[i]]
-        return [xor_swap(part, "blk", 1) for part in ([jnp.stack(parts)] if stacked else parts)]
+    def forward(i):
+        return [xor_swap(jnp.stack(sent[i]), "blk", 1)]
 
     sent = [send(far[0])]
     near = [xor_swap(whole[0], "z", 1)]
@@ -355,7 +367,7 @@
     sent.append(send(far[1]))
     near.append(xor_swap(whole[1], "z", 1))
     sent[0], caches = tie((sent[0], caches))
-    forwarded = [forward(0, True)]
+    forwarded = [forward(0)]
     state, other = tie((state, other))
     rows_of_x = [keep, other, xor_swap(other, "core", 1)]
     for stride in range(1, cycle):
@@ -371,7 +383,7 @@
     forwarded[0], state = tie((forwarded[0], state))
     mine_0, theirs_0 = sums(0)
     sent[1], mine_0 = tie((sent[1], mine_0))
-    forwarded.append(forward(1, True))
+    forwarded.append(forward(1))
     here_0, there_0 = owners(mine_0, theirs_0)
     forwarded[1], mine_0 = tie((forwarded[1], mine_0))
     mine_1, theirs_1 = sums(1)

time: 61.4 us -> 60.8 us (level)
  the two profiles are of different devices: /device:TPU:11 before, /device:TPU:0 now
where the time goes in v15:
time: 60.8 us; the launch traced here: 60.1 us
  starting transfers between devices  24.1 us (40%)
  Pallas kernels  22.8 us (38%)
  waiting for transfers between devices  10.4 us (17%)
  local copies, waits for them, and re-layouts  1.39 us (2%)
  between operations  1.01 us (2%)
    ppermute x18, starting transfers between devices, xor_swap(): lax.ppermute(array, axis, [(i, i ^ by) for i in range(lax.axis_size(axis))])  21.2 us
    pallas_call x2, Pallas kernels, prompt_attention(): pl.pallas_call(functools.partial(prompt_kernel, first), grid_spec=pltpu.P...  11.7 us
    ppermute x18, waiting for transfers between devices, xor_swap(): lax.ppermute(array, axis, [(i, i ^ by) for i in range(lax.axis_size(axis))])  10.3 us
    pallas_call x5, Pallas kernels, on_chip(): pl.pallas_call(kernel, in_specs=[SMEM] + [VMEM] * len(operands), out_spec...  5.81 us
    pallas_call x2, Pallas kernels, final_attention(): pl.pallas_call(functools.partial(final_kernel, chunk, offset), in_specs=s...  4.7 us
    ppermute x1, starting transfers between devices, per_device(): lax.ppermute(caches[-1], 'blk', [(i, (i + 1) % cycle) for i in range(cycl...  2.94 us
  transfers between devices with their start and end apart: 19, of which 7 were waited for; matrix products, arithmetic and copies ran while one was open for 1% of the time, Pallas kernels for 34%

profile of v15, /device:TPU:0, one launch (start us, length us, event | category | flops | bytes accessed | tf_op | source)
XLA Modules:
  0.0 60.1 jit_solution(14877625016320297143)
XLA Ops:
  0.6 2.9 %collective-permute-start.4 = (bf16[512,1024]{1,0:T(8,128)(2,1)}, bf16[512,1024]{1,0:T(8,128)(2,1)}, u32[]{:S(2)}, u32[]{:S(2)}) collective-permute-start(bf16[512,1024]{1,0:T(8,128)(2,1)} %bitcast.28), channel_id=1, source_target_pairs={{0,1},{1,0},{2,3},{3,2},{4,5},{5,4},{6,7},{7,6},{8,9},{9,8},{10,11... | collective-permute-start | bytes 3145736 | tf_op jit(solution)/shard_map/ppermute | solution.py:335
  3.5 1.1 %copy-done.2 = bf16[320,1024]{1,0:T(8,128)(2,1)S(1)} copy-done((bf16[320,1024]{1,0:T(8,128)(2,1)S(1)}, bf16[320,1024]{1,0:T(8,128)(2,1)}, u32[]{:S(2)}) %copy-start.2) | copy-done | bytes 655384
  6.6 2.7 %collective-permute-start.2 = (bf16[320,256]{1,0:T(8,128)(2,1)S(1)}, bf16[320,256]{1,0:T(8,128)(2,1)S(1)}, u32[]{:S(2)}, u32[]{:S(2)}) collective-permute-start(bf16[320,256]{1,0:T(8,128)(2,1)S(1)} %far_first.1), channel_id=1, source_target_pairs={{0,16},{8,24},{16,0},{24,8},{1,17},{9,25},{17,1},{25,9},{2,18},{10... | collective-permute-start | bytes 491528 | tf_op jit(solution)/shard_map/ppermute | solution.py:316
  9.3 1.3 %collective-permute-start.3 = (bf16[320,256]{1,0:T(8,128)(2,1)S(1)}, bf16[320,256]{1,0:T(8,128)(2,1)S(1)}, u32[]{:S(2)}, u32[]{:S(2)}) collective-permute-start(bf16[320,256]{1,0:T(8,128)(2,1)S(1)} %far_first.1), channel_id=1, source_target_pairs={{0,24},{8,16},{16,8},{24,0},{1,25},{9,17},{17,9},{25,1},{2,26},{10... | collective-permute-start | bytes 491528 | tf_op jit(solution)/shard_map/ppermute | solution.py:316
  11.9 1.6 %pack_rows.1 = (bf16[2,4,128,640]{3,2,1,0:T(8,128)(2,1)S(1)}, bf16[4,128,640]{2,1,0:T(8,128)(2,1)S(1)}) custom-call(s32[4]{0:T(128)S(1)} %pad_add_fusion.1.where, bf16[128,5120]{1,0:T(8,128)(2,1)S(1)} %bitcast.21, bf16[128,5120]{1,0:T(8,128)(2,1)} %collective-permute-done.1.got_ref), custom_call_target="tpu_custom_call" | custom-call | flops 1024 | bytes 1024 | tf_op jit(solution)/shard_map/pack_rows/pallas_call | solution.py:117
  13.5 1.6 %collective-permute-start.6 = (bf16[4,128,640]{2,1,0:T(8,128)(2,1)S(1)}, bf16[4,128,640]{2,1,0:T(8,128)(2,1)S(1)}, u32[]{:S(2)}, u32[]{:S(2)}) collective-permute-start(bf16[4,128,640]{2,1,0:T(8,128)(2,1)S(1)} %get-tuple-element.63), channel_id=1, source_target_pairs={{0,4},{4,0},{1,5},{5,1},{2,6},{6,2},{3,7},{7,3},{8,12},{12,8},{9,1... | collective-permute-start | bytes 1966088 | tf_op jit(solution)/shard_map/ppermute | solution.py:316
  15.1 5.4 %prompt_attention.2 = (f32[128,4096]{1,0:T(8,128)S(1)}, f32[8,4096]{1,0:T(8,128)S(1)}) custom-call(s32[4]{0:T(128)S(1)} %get-tuple-element.109.info, bf16[128,4096]{1,0:T(8,128)(2,1)S(1)} %bitcast.16, bf16[512,1024]{1,0:T(8,128)(2,1)S(1)} %bitcast.29, bf16[512,1024]{1,0:T(8,128)(2,1)S(1)} %bitcast.30), custom_call_target="tpu_custom_call" | custom-call | flops 17179869184 | bytes 1024 | tf_op jit(solution)/shard_map/prompt_attention/pallas_call | solution.py:94
  20.5 1.1 %collective-permute-done.2.refs_0_ = bf16[320,256]{1,0:T(8,128)(2,1)S(1)} collective-permute-done((bf16[320,256]{1,0:T(8,128)(2,1)S(1)}, bf16[320,256]{1,0:T(8,128)(2,1)S(1)}, u32[]{:S(2)}, u32[]{:S(2)}) %collective-permute-start.2) | collective-permute-done | bytes 163872 | tf_op jit(solution)/shard_map/ppermute | solution.py:316
  21.6 5.0 %collective-permute-start.11 = (bf16[320,256]{1,0:T(8,128)(2,1)S(1)}, bf16[320,256]{1,0:T(8,128)(2,1)S(1)}, u32[]{:S(2)}, u32[]{:S(2)}) collective-permute-start(bf16[320,256]{1,0:T(8,128)(2,1)S(1)} %get-tuple-element.88), channel_id=1, source_target_pairs={{0,16},{8,24},{16,0},{24,8},{1,17},{9,25},{17,1},{25,9},{2,18},{10... | collective-permute-start | bytes 491528 | tf_op jit(solution)/shard_map/ppermute | solution.py:316
  27.2 1.8 %collective-permute-start.5 = (bf16[2,320,256]{2,1,0:T(8,128)(2,1)S(1)}, bf16[2,320,256]{2,1,0:T(8,128)(2,1)S(1)}, u32[]{:S(2)}, u32[]{:S(2)}) collective-permute-start(bf16[2,320,256]{2,1,0:T(8,128)(2,1)S(1)} %pad_maximum_fusion), channel_id=1, source_target_pairs={{0,1},{1,0},{2,3},{3,2},{4,5},{5,4},{6,7},{7,6},{8,9},{9,8},{10,11... | collective-permute-start | bytes 983048 | tf_op jit(solution)/shard_map/ppermute | solution.py:316
  29.4 6.3 %prompt_attention.3 = (f32[128,4096]{1,0:T(8,128)S(1)}, f32[8,4096]{1,0:T(8,128)S(1)}) custom-call(s32[4]{0:T(128)S(1)} %get-tuple-element.110.info, bf16[128,4096]{1,0:T(8,128)(2,1)S(1)} %bitcast.17, bf16[512,1024]{1,0:T(8,128)(2,1)} %collective-permute-done.4.k_ref.v_ref, bf16[512,1024]{1,0:T(8,128)(2,1)} %collective-permute-done.4.k_ref.v_ref, ...), custom_call_target="tpu_custom_call" | custom-call | flops 8589934592 | bytes 1024 | tf_op jit(solution)/shard_map/prompt_attention/pallas_call | solution.py:94
  35.7 0.7 %collective-permute-done.5.refs_2_ = bf16[2,320,256]{2,1,0:T(8,128)(2,1)S(1)} collective-permute-done((bf16[2,320,256]{2,1,0:T(8,128)(2,1)S(1)}, bf16[2,320,256]{2,1,0:T(8,128)(2,1)S(1)}, u32[]{:S(2)}, u32[]{:S(2)}) %collective-permute-start.5) | collective-permute-done | bytes 327712 | tf_op jit(solution)/shard_map/ppermute | solution.py:316
  36.4 1.5 %collective-permute-start.14 = (bf16[640,256]{1,0:T(8,128)(2,1)S(1)}, bf16[640,256]{1,0:T(8,128)(2,1)S(1)}, u32[]{:S(2)}, u32[]{:S(2)}) collective-permute-start(bf16[640,256]{1,0:T(8,128)(2,1)S(1)} %get-tuple-element.91.own), channel_id=1, source_target_pairs={{0,8},{8,0},{16,24},{24,16},{1,9},{9,1},{17,25},{25,17},{2,10},{10... | collective-permute-start | bytes 983048 | tf_op jit(solution)/shard_map/ppermute | solution.py:316
  37.9 1.5 %project.2 = (f32[2,128,256]{2,1,0:T(8,128)S(1)}, f32[2,128,256]{2,1,0:T(8,128)S(1)}) custom-call(s32[4]{0:T(128)S(1)} %pad_add_fusion.1.where, bf16[2,4,128,640]{3,2,1,0:T(8,128)(2,1)S(1)} %get-tuple-element.84.keep, bf16[4,128,640]{2,1,0:T(8,128)(2,1)S(1)} %collective-permute-done.6.other, bf16[4,128,640]{2,1,0:T(8,128)(2,1)S(1)} %collective-permute-done.7.other_2, ...), custom_call_target="tpu_custom_call" | custom-call | flops 1024 | bytes 1024 | tf_op jit(solution)/shard_map/project/pallas_call | solution.py:117
  39.5 1.6 %collective-permute-start.15 = (bf16[2,320,256]{2,1,0:T(8,128)(2,1)S(1)}, bf16[2,320,256]{2,1,0:T(8,128)(2,1)S(1)}, u32[]{:S(2)}, u32[]{:S(2)}) collective-permute-start(bf16[2,320,256]{2,1,0:T(8,128)(2,1)S(1)} %pad_maximum_fusion.1), channel_id=1, source_target_pairs={{0,1},{1,0},{2,3},{3,2},{4,5},{5,4},{6,7},{7,6},{8,9},{9,8},{10,11... | collective-permute-start | bytes 983048 | tf_op jit(solution)/shard_map/ppermute | solution.py:316
  41.1 1.7 %collective-permute-start.10 = (f32[1,128,256]{2,1,0:T(8,128)S(1)}, f32[1,128,256]{2,1,0:T(8,128)S(1)}, u32[]{:S(2)}, u32[]{:S(2)}) collective-permute-start(f32[1,128,256]{2,1,0:T(8,128)S(1)} %get-tuple-element.107), channel_id=1, source_target_pairs={{0,6},{2,4},{4,2},{6,0},{1,7},{3,5},{5,3},{7,1},{8,14},{10,12},{12... | collective-permute-start | bytes 393224 | tf_op jit(solution)/shard_map/ppermute | solution.py:316
  43.3 5.5 %collective-permute-done.15.refs_2_ = bf16[2,320,256]{2,1,0:T(8,128)(2,1)S(1)} collective-permute-done((bf16[2,320,256]{2,1,0:T(8,128)(2,1)S(1)}, bf16[2,320,256]{2,1,0:T(8,128)(2,1)S(1)}, u32[]{:S(2)}, u32[]{:S(2)}) %collective-permute-start.15) | collective-permute-done | bytes 327712 | tf_op jit(solution)/shard_map/ppermute | solution.py:316
  48.8 1.5 %project.3 = (f32[2,128,256]{2,1,0:T(8,128)S(1)}, f32[2,128,256]{2,1,0:T(8,128)S(1)}) custom-call(s32[4]{0:T(128)S(1)} %pad_add_fusion.1.where, bf16[2,4,128,640]{3,2,1,0:T(8,128)(2,1)S(1)} %get-tuple-element.84.keep, bf16[4,128,640]{2,1,0:T(8,128)(2,1)S(1)} %collective-permute-done.6.other, bf16[4,128,640]{2,1,0:T(8,128)(2,1)S(1)} %collective-permute-done.7.other_2, ...), custom_call_target="tpu_custom_call" | custom-call | flops 1024 | bytes 1024 | tf_op jit(solution)/shard_map/project/pallas_call | solution.py:117
  50.4 1.6 %collective-permute-start.16 = (f32[1,128,256]{2,1,0:T(8,128)S(1)}, f32[1,128,256]{2,1,0:T(8,128)S(1)}, u32[]{:S(2)}, u32[]{:S(2)}) collective-permute-start(f32[1,128,256]{2,1,0:T(8,128)S(1)} %get-tuple-element.106), channel_id=1, source_target_pairs={{0,4},{4,0},{1,5},{5,1},{2,6},{6,2},{3,7},{7,3},{8,12},{12,8},{9,1... | collective-permute-start | bytes 393224 | tf_op jit(solution)/shard_map/ppermute | solution.py:316
  52.0 0.7 %collective-permute-start.18 = (f32[1,128,256]{2,1,0:T(8,128)S(1)}, f32[1,128,256]{2,1,0:T(8,128)S(1)}, u32[]{:S(2)}, u32[]{:S(2)}) collective-permute-start(f32[1,128,256]{2,1,0:T(8,128)S(1)} %slice.23), channel_id=1, source_target_pairs={{0,2},{2,0},{1,3},{3,1},{4,6},{6,4},{5,7},{7,5},{8,10},{10,8},{9,1... | collective-permute-start | bytes 393224 | tf_op jit(solution)/shard_map/ppermute | solution.py:316
  52.7 2.4 %final_attention.2.refs_0_ = bf16[128,4096]{1,0:T(8,128)(2,1)} custom-call(s32[3]{0:T(128)S(1)} %pad_add_fusion.info, f32[1,128]{1,0:T(1,128)S(1)} %bitcast.26, bf16[128,4096]{1,0:T(8,128)(2,1)S(1)} %bitcast.18, f32[128,4096]{1,0:T(8,128)S(1)} %get-tuple-element.82.acc_ref, f32[8,4096]{1,0:T(8,128)S(1)} %get-tuple-element.83.ml_ref, ...), custom_call_target="tpu_custom_call" | custom-call | flops 1024 | bytes 1024 | tf_op jit(solution)/shard_map/final_attention/pallas_call | solution.py:302
  55.1 0.8 %collective-permute-done.16.theirs = f32[1,128,256]{2,1,0:T(8,128)S(1)} collective-permute-done((f32[1,128,256]{2,1,0:T(8,128)S(1)}, f32[1,128,256]{2,1,0:T(8,128)S(1)}, u32[]{:S(2)}, u32[]{:S(2)}) %collective-permute-start.16) | collective-permute-done | bytes 131104 | tf_op jit(solution)/shard_map/ppermute | solution.py:316
  55.9 1.9 %collective-permute-done.17.there = f32[1,128,256]{2,1,0:T(8,128)S(1)} collective-permute-done((f32[1,128,256]{2,1,0:T(8,128)S(1)}, f32[1,128,256]{2,1,0:T(8,128)S(1)}, u32[]{:S(2)}, u32[]{:S(2)}) %collective-permute-start.17) | collective-permute-done | bytes 131104 | tf_op jit(solution)/shard_map/ppermute | solution.py:316
  57.7 2.3 %final_attention.3 = bf16[128,4096]{1,0:T(8,128)(2,1)} custom-call(s32[3]{0:T(128)S(1)} %pad_add_fusion.info, f32[1,128]{1,0:T(1,128)S(1)} %bitcast.27, bf16[128,4096]{1,0:T(8,128)(2,1)S(1)} %bitcast.19, f32[128,4096]{1,0:T(8,128)S(1)} %get-tuple-element.82.acc_ref, f32[8,4096]{1,0:T(8,128)S(1)} %get-tuple-element.83.ml_ref, ...), custom_call_target="tpu_custom_call", output_to_operand_aliasing={{}: (9, {})} | custom-call | flops 1024 | bytes 1024 | tf_op jit(solution)/shard_map/final_attention/pallas_call | solution.py:302
  (48 shorter events, 4.7 us)
Async XLA Ops:
  0.0 11.8 %collective-permute-start.1 = (bf16[128,5120]{1,0:T(8,128)(2,1)}, bf16[128,5120]{1,0:T(8,128)(2,1)}, u32[]{:S(2)}, u32[]{:S(2)}) collective-permute-start(bf16[128,5120]{1,0:T(8,128)(2,1)} %bitcast.20), channel_id=1, source_target_pairs={{0,2},{2,0},{1,3},{3,1},{4,6},{6,4},{5,7},{7,5},{8,10},{10,8},{9,1... | collective-permute-start | bytes 3932168 | tf_op jit(solution)/shard_map/ppermute | solution.py:316
  0.5 5.6 %collective-permute-start = (bf16[320,1024]{1,0:T(8,128)(2,1)}, bf16[320,1024]{1,0:T(8,128)(2,1)S(1)}, u32[]{:S(2)}, u32[]{:S(2)}) collective-permute-start(bf16[320,1024]{1,0:T(8,128)(2,1)} %weight_ref.1), channel_id=1, source_target_pairs={{0,2},{2,0},{1,3},{3,1},{4,6},{6,4},{5,7},{7,5},{8,10},{10,8},{9,1... | collective-permute-start | bytes 1966088 | tf_op jit(solution)/shard_map/ppermute | solution.py:316
  0.6 26.6 %collective-permute-start.4 = (bf16[512,1024]{1,0:T(8,128)(2,1)}, bf16[512,1024]{1,0:T(8,128)(2,1)}, u32[]{:S(2)}, u32[]{:S(2)}) collective-permute-start(bf16[512,1024]{1,0:T(8,128)(2,1)} %bitcast.28), channel_id=1, source_target_pairs={{0,1},{1,0},{2,3},{3,2},{4,5},{5,4},{6,7},{7,6},{8,9},{9,8},{10,11... | collective-permute-start | bytes 3145736 | tf_op jit(solution)/shard_map/ppermute | solution.py:335
  5.2 6.3 %copy-start.5 = (s32[1,2,2]{2,1,0:T(2,128)S(1)}, s32[1,2,2]{2,1,0:T(2,128)}, u32[]{:S(2)}) copy-start(s32[1,2,2]{2,1,0:T(2,128)} %param.14) | copy-start | bytes 52
  5.2 6.6 %copy-start.1 = (bf16[1,128,5120]{2,1,0:T(8,128)(2,1)S(1)}, bf16[1,128,5120]{2,1,0:T(8,128)(2,1)}, u32[]{:S(2)}) copy-start(bf16[1,128,5120]{2,1,0:T(8,128)(2,1)} %param.8) | copy-start | bytes 3932164
  6.6 15.0 %collective-permute-start.2 = (bf16[320,256]{1,0:T(8,128)(2,1)S(1)}, bf16[320,256]{1,0:T(8,128)(2,1)S(1)}, u32[]{:S(2)}, u32[]{:S(2)}) collective-permute-start(bf16[320,256]{1,0:T(8,128)(2,1)S(1)} %far_first.1), channel_id=1, source_target_pairs={{0,16},{8,24},{16,0},{24,8},{1,17},{9,25},{17,1},{25,9},{2,18},{10... | collective-permute-start | bytes 491528 | tf_op jit(solution)/shard_map/ppermute | solution.py:316
  9.3 12.4 %collective-permute-start.3 = (bf16[320,256]{1,0:T(8,128)(2,1)S(1)}, bf16[320,256]{1,0:T(8,128)(2,1)S(1)}, u32[]{:S(2)}, u32[]{:S(2)}) collective-permute-start(bf16[320,256]{1,0:T(8,128)(2,1)S(1)} %far_first.1), channel_id=1, source_target_pairs={{0,24},{8,16},{16,8},{24,0},{1,25},{9,17},{17,9},{25,1},{2,26},{10... | collective-permute-start | bytes 491528 | tf_op jit(solution)/shard_map/ppermute | solution.py:316
  11.2 26.6 %collective-permute-start.8 = (bf16[640,256]{1,0:T(8,128)(2,1)S(1)}, bf16[640,256]{1,0:T(8,128)(2,1)S(1)}, u32[]{:S(2)}, u32[]{:S(2)}) collective-permute-start(bf16[640,256]{1,0:T(8,128)(2,1)S(1)} %get-tuple-element.60.own), channel_id=1, source_target_pairs={{0,8},{8,0},{16,24},{24,16},{1,9},{9,1},{17,25},{25,17},{2,10},{10... | collective-permute-start | bytes 983048 | tf_op jit(solution)/shard_map/ppermute | solution.py:316
  11.8 3.3 %copy-start = (bf16[1,128,4096]{2,1,0:T(8,128)(2,1)S(1)}, bf16[1,128,4096]{2,1,0:T(8,128)(2,1)}, u32[]{:S(2)}) copy-start(bf16[1,128,4096]{2,1,0:T(8,128)(2,1)} %param.9) | copy-start | bytes 3145732
  13.5 15.9 %collective-permute-start.6 = (bf16[4,128,640]{2,1,0:T(8,128)(2,1)S(1)}, bf16[4,128,640]{2,1,0:T(8,128)(2,1)S(1)}, u32[]{:S(2)}, u32[]{:S(2)}) collective-permute-start(bf16[4,128,640]{2,1,0:T(8,128)(2,1)S(1)} %get-tuple-element.63), channel_id=1, source_target_pairs={{0,4},{4,0},{1,5},{5,1},{2,6},{6,2},{3,7},{7,3},{8,12},{12,8},{9,1... | collective-permute-start | bytes 1966088 | tf_op jit(solution)/shard_map/ppermute | solution.py:316
  21.6 17.8 %collective-permute-start.11 = (bf16[320,256]{1,0:T(8,128)(2,1)S(1)}, bf16[320,256]{1,0:T(8,128)(2,1)S(1)}, u32[]{:S(2)}, u32[]{:S(2)}) collective-permute-start(bf16[320,256]{1,0:T(8,128)(2,1)S(1)} %get-tuple-element.88), channel_id=1, source_target_pairs={{0,16},{8,24},{16,0},{24,8},{1,17},{9,25},{17,1},{25,9},{2,18},{10... | collective-permute-start | bytes 491528 | tf_op jit(solution)/shard_map/ppermute | solution.py:316
  26.6 12.8 %collective-permute-start.12 = (bf16[320,256]{1,0:T(8,128)(2,1)S(1)}, bf16[320,256]{1,0:T(8,128)(2,1)S(1)}, u32[]{:S(2)}, u32[]{:S(2)}) collective-permute-start(bf16[320,256]{1,0:T(8,128)(2,1)S(1)} %get-tuple-element.88), channel_id=1, source_target_pairs={{0,24},{8,16},{16,8},{24,0},{1,25},{9,17},{17,9},{25,1},{2,26},{10... | collective-permute-start | bytes 491528 | tf_op jit(solution)/shard_map/ppermute | solution.py:316
  27.2 9.1 %collective-permute-start.5 = (bf16[2,320,256]{2,1,0:T(8,128)(2,1)S(1)}, bf16[2,320,256]{2,1,0:T(8,128)(2,1)S(1)}, u32[]{:S(2)}, u32[]{:S(2)}) collective-permute-start(bf16[2,320,256]{2,1,0:T(8,128)(2,1)S(1)} %pad_maximum_fusion), channel_id=1, source_target_pairs={{0,1},{1,0},{2,3},{3,2},{4,5},{5,4},{6,7},{7,6},{8,9},{9,8},{10,11... | collective-permute-start | bytes 983048 | tf_op jit(solution)/shard_map/ppermute | solution.py:316
  29.4 8.5 %collective-permute-start.7 = (bf16[4,128,640]{2,1,0:T(8,128)(2,1)S(1)}, bf16[4,128,640]{2,1,0:T(8,128)(2,1)S(1)}, u32[]{:S(2)}, u32[]{:S(2)}) collective-permute-start(bf16[4,128,640]{2,1,0:T(8,128)(2,1)S(1)} %collective-permute-done.6.other), channel_id=1, source_target_pairs={{0,2},{2,0},{1,3},{3,1},{4,6},{6,4},{5,7},{7,5},{8,10},{10,8},{9,1... | collective-permute-start | bytes 1966088 | tf_op jit(solution)/shard_map/ppermute | solution.py:316
  36.4 12.4 %collective-permute-start.14 = (bf16[640,256]{1,0:T(8,128)(2,1)S(1)}, bf16[640,256]{1,0:T(8,128)(2,1)S(1)}, u32[]{:S(2)}, u32[]{:S(2)}) collective-permute-start(bf16[640,256]{1,0:T(8,128)(2,1)S(1)} %get-tuple-element.91.own), channel_id=1, source_target_pairs={{0,8},{8,0},{16,24},{24,16},{1,9},{9,1},{17,25},{25,17},{2,10},{10... | collective-permute-start | bytes 983048 | tf_op jit(solution)/shard_map/ppermute | solution.py:316
  39.5 9.3 %collective-permute-start.15 = (bf16[2,320,256]{2,1,0:T(8,128)(2,1)S(1)}, bf16[2,320,256]{2,1,0:T(8,128)(2,1)S(1)}, u32[]{:S(2)}, u32[]{:S(2)}) collective-permute-start(bf16[2,320,256]{2,1,0:T(8,128)(2,1)S(1)} %pad_maximum_fusion.1), channel_id=1, source_target_pairs={{0,1},{1,0},{2,3},{3,2},{4,5},{5,4},{6,7},{7,6},{8,9},{9,8},{10,11... | collective-permute-start | bytes 983048 | tf_op jit(solution)/shard_map/ppermute | solution.py:316
  41.0 9.3 %collective-permute-start.13 = (f32[1,128,256]{2,1,0:T(8,128)S(1)}, f32[1,128,256]{2,1,0:T(8,128)S(1)}, u32[]{:S(2)}, u32[]{:S(2)}) collective-permute-start(f32[1,128,256]{2,1,0:T(8,128)S(1)} %slice.20), channel_id=1, source_target_pairs={{0,2},{2,0},{1,3},{3,1},{4,6},{6,4},{5,7},{7,5},{8,10},{10,8},{9,1... | collective-permute-start | bytes 393224 | tf_op jit(solution)/shard_map/ppermute | solution.py:316
  41.1 9.2 %collective-permute-start.10 = (f32[1,128,256]{2,1,0:T(8,128)S(1)}, f32[1,128,256]{2,1,0:T(8,128)S(1)}, u32[]{:S(2)}, u32[]{:S(2)}) collective-permute-start(f32[1,128,256]{2,1,0:T(8,128)S(1)} %get-tuple-element.107), channel_id=1, source_target_pairs={{0,6},{2,4},{4,2},{6,0},{1,7},{3,5},{5,3},{7,1},{8,14},{10,12},{12... | collective-permute-start | bytes 393224 | tf_op jit(solution)/shard_map/ppermute | solution.py:316
  42.8 9.8 %copy-start.6 = (s32[1,2]{1,0:T(1,128)S(1)}, s32[1,2]{1,0:T(1,128)}, u32[]{:S(2)}) copy-start(s32[1,2]{1,0:T(1,128)} %param.15) | copy-start | bytes 28
  42.8 9.9 %copy-start.3 = (f32[128]{0:T(128)S(1)}, f32[128]{0:T(128)}, u32[]{:S(2)}) copy-start(f32[128]{0:T(128)} %param.12) | copy-start | bytes 1540
  42.8 7.5 %collective-permute-start.9 = (f32[1,128,256]{2,1,0:T(8,128)S(1)}, f32[1,128,256]{2,1,0:T(8,128)S(1)}, u32[]{:S(2)}, u32[]{:S(2)}) collective-permute-start(f32[1,128,256]{2,1,0:T(8,128)S(1)} %get-tuple-element.108), channel_id=1, source_target_pairs={{0,4},{4,0},{1,5},{5,1},{2,6},{6,2},{3,7},{7,3},{8,12},{12,8},{9,1... | collective-permute-start | bytes 393224 | tf_op jit(solution)/shard_map/ppermute | solution.py:316
  50.4 5.5 %collective-permute-start.16 = (f32[1,128,256]{2,1,0:T(8,128)S(1)}, f32[1,128,256]{2,1,0:T(8,128)S(1)}, u32[]{:S(2)}, u32[]{:S(2)}) collective-permute-start(f32[1,128,256]{2,1,0:T(8,128)S(1)} %get-tuple-element.106), channel_id=1, source_target_pairs={{0,4},{4,0},{1,5},{5,1},{2,6},{6,2},{3,7},{7,3},{8,12},{12,8},{9,1... | collective-permute-start | bytes 393224 | tf_op jit(solution)/shard_map/ppermute | solution.py:316
  51.9 5.8 %collective-permute-start.17 = (f32[1,128,256]{2,1,0:T(8,128)S(1)}, f32[1,128,256]{2,1,0:T(8,128)S(1)}, u32[]{:S(2)}, u32[]{:S(2)}) collective-permute-start(f32[1,128,256]{2,1,0:T(8,128)S(1)} %get-tuple-element.105), channel_id=1, source_target_pairs={{0,6},{2,4},{4,2},{6,0},{1,7},{3,5},{5,3},{7,1},{8,14},{10,12},{12... | collective-permute-start | bytes 393224 | tf_op jit(solution)/shard_map/ppermute | solution.py:316
  52.0 5.8 %collective-permute-start.18 = (f32[1,128,256]{2,1,0:T(8,128)S(1)}, f32[1,128,256]{2,1,0:T(8,128)S(1)}, u32[]{:S(2)}, u32[]{:S(2)}) collective-permute-start(f32[1,128,256]{2,1,0:T(8,128)S(1)} %slice.23), channel_id=1, source_target_pairs={{0,2},{2,0},{1,3},{3,1},{4,6},{6,4},{5,7},{7,5},{8,10},{10,8},{9,1... | collective-permute-start | bytes 393224 | tf_op jit(solution)/shard_map/ppermute | solution.py:316
  (2 other events, 4.3 us)

commit v16 on v15

--- a/solution.py
+++ b/solution.py
@@ -259,7 +259,8 @@
     base = jnp.where(row < RLEN, 0, RLEN)
     seen = (slot >= base) & (slot <= row) & (slot - base < length)
     live = jnp.where(row - base < length, 1.0, 0.0)[0:1]
-    copies = []
+    pairs = range(0, SHARED, 2)
+    values, products = [], []
     for k in range(heads):
         part = slice(k * HD, (k + 1) * HD)
         here = mine[0, :, part] + theirs[0, :, part]
@@ -268,10 +269,11 @@
         raw = jnp.where(first_core, here, away)
         mean = jnp.mean(raw * raw, axis=1, keepdims=True)
         keys = (raw * lax.rsqrt(mean + 1e-06) * gain_ref[...]).astype(jnp.bfloat16)
-        values = jnp.where(first_core, away, here).T.astype(jnp.bfloat16)
-        pairs = range(0, SHARED, 2)
-        products = [scores_of(keys, pair_queries(q_ref, (head + k) * SHARED + g)) for g in pairs]
-        for g, scores in zip(pairs, products):
+        values.append(jnp.where(first_core, away, here).T.astype(jnp.bfloat16))
+        products.append([scores_of(keys, pair_queries(q_ref, (head + k) * SHARED + g)) for g in pairs])
+    copies = []
+    for k in range(heads):
+        for g, scores in zip(pairs, products[k]):
             cols = slice(((offset + k) * SHARED + g) * HD, ((offset + k) * SHARED + g + 2) * HD)
             scores = jnp.where(seen, scores, HIDDEN)
             before = ml_ref[0:1, cols]
@@ -279,7 +281,7 @@
             faded = jnp.exp2((before - largest) * SCALE)
             weights = jnp.exp2((scores - largest) * SCALE)
             total = jnp.sum(weights, axis=0, keepdims=True) + faded * ml_ref[1:2, cols]
-            acc = jnp.dot(values, weights.astype(jnp.bfloat16), preferred_element_type=jnp.float32)
+            acc = jnp.dot(values[k], weights.astype(jnp.bfloat16), preferred_element_type=jnp.float32)
             acc = (acc + faded * acc_ref[:, cols]) * (live / total)
             built[k, :, g * HD : (g + 1) * HD] = acc[:, :ROWS].T.astype(jnp.bfloat16)
             built[k, :, (g + 1) * HD : (g + 2) * HD] = acc[:, ROWS:].T.astype(jnp.bfloat16)

time: 60.8 us -> 60.6 us (level)
  no operation moved by 1% of the time
where the time goes in v16:
time: 60.6 us; the launch traced here: 59.9 us
  starting transfers between devices  24.1 us (40%)
  Pallas kernels  22.5 us (37%)
  waiting for transfers between devices  10.6 us (17%)
  local copies, waits for them, and re-layouts  1.39 us (2%)
  between operations  1.01 us (2%)
    ppermute x18, starting transfers between devices, xor_swap(): lax.ppermute(array, axis, [(i, i ^ by) for i in range(lax.axis_size(axis))])  21.2 us
    pallas_call x2, Pallas kernels, prompt_attention(): pl.pallas_call(functools.partial(prompt_kernel, first), grid_spec=pltpu.P...  11.7 us
    ppermute x18, waiting for transfers between devices, xor_swap(): lax.ppermute(array, axis, [(i, i ^ by) for i in range(lax.axis_size(axis))])  10.5 us
    pallas_call x5, Pallas kernels, on_chip(): pl.pallas_call(kernel, in_specs=[SMEM] + [VMEM] * len(operands), out_spec...  5.81 us
    pallas_call x2, Pallas kernels, final_attention(): pl.pallas_call(functools.partial(final_kernel, chunk, offset), in_specs=s...  4.32 us
    ppermute x1, starting transfers between devices, per_device(): lax.ppermute(caches[-1], 'blk', [(i, (i + 1) % cycle) for i in range(cycl...  2.94 us
  transfers between devices with their start and end apart: 19, of which 7 were waited for; matrix products, arithmetic and copies ran while one was open for 1% of the time, Pallas kernels for 34%

profile of v16, /device:TPU:0, one launch (start us, length us, event | category | flops | bytes accessed | tf_op | source)
XLA Modules:
  0.0 59.9 jit_solution(8109100640907356574)
XLA Ops:
  0.6 2.9 %collective-permute-start.4 = (bf16[512,1024]{1,0:T(8,128)(2,1)}, bf16[512,1024]{1,0:T(8,128)(2,1)}, u32[]{:S(2)}, u32[]{:S(2)}) collective-permute-start(bf16[512,1024]{1,0:T(8,128)(2,1)} %bitcast.28), channel_id=1, source_target_pairs={{0,1},{1,0},{2,3},{3,2},{4,5},{5,4},{6,7},{7,6},{8,9},{9,8},{10,11... | collective-permute-start | bytes 3145736 | tf_op jit(solution)/shard_map/ppermute | solution.py:337
  3.5 1.1 %copy-done.2 = bf16[320,1024]{1,0:T(8,128)(2,1)S(1)} copy-done((bf16[320,1024]{1,0:T(8,128)(2,1)S(1)}, bf16[320,1024]{1,0:T(8,128)(2,1)}, u32[]{:S(2)}) %copy-start.2) | copy-done | bytes 655384
  6.6 2.7 %collective-permute-start.2 = (bf16[320,256]{1,0:T(8,128)(2,1)S(1)}, bf16[320,256]{1,0:T(8,128)(2,1)S(1)}, u32[]{:S(2)}, u32[]{:S(2)}) collective-permute-start(bf16[320,256]{1,0:T(8,128)(2,1)S(1)} %far_first.1), channel_id=1, source_target_pairs={{0,16},{8,24},{16,0},{24,8},{1,17},{9,25},{17,1},{25,9},{2,18},{10... | collective-permute-start | bytes 491528 | tf_op jit(solution)/shard_map/ppermute | solution.py:318
  9.3 1.3 %collective-permute-start.3 = (bf16[320,256]{1,0:T(8,128)(2,1)S(1)}, bf16[320,256]{1,0:T(8,128)(2,1)S(1)}, u32[]{:S(2)}, u32[]{:S(2)}) collective-permute-start(bf16[320,256]{1,0:T(8,128)(2,1)S(1)} %far_first.1), channel_id=1, source_target_pairs={{0,24},{8,16},{16,8},{24,0},{1,25},{9,17},{17,9},{25,1},{2,26},{10... | collective-permute-start | bytes 491528 | tf_op jit(solution)/shard_map/ppermute | solution.py:318
  11.9 1.6 %pack_rows.1 = (bf16[2,4,128,640]{3,2,1,0:T(8,128)(2,1)S(1)}, bf16[4,128,640]{2,1,0:T(8,128)(2,1)S(1)}) custom-call(s32[4]{0:T(128)S(1)} %pad_add_fusion.1.where, bf16[128,5120]{1,0:T(8,128)(2,1)S(1)} %bitcast.21, bf16[128,5120]{1,0:T(8,128)(2,1)} %collective-permute-done.1.got_ref), custom_call_target="tpu_custom_call" | custom-call | flops 1024 | bytes 1024 | tf_op jit(solution)/shard_map/pack_rows/pallas_call | solution.py:117
  13.5 1.6 %collective-permute-start.6 = (bf16[4,128,640]{2,1,0:T(8,128)(2,1)S(1)}, bf16[4,128,640]{2,1,0:T(8,128)(2,1)S(1)}, u32[]{:S(2)}, u32[]{:S(2)}) collective-permute-start(bf16[4,128,640]{2,1,0:T(8,128)(2,1)S(1)} %get-tuple-element.63), channel_id=1, source_target_pairs={{0,4},{4,0},{1,5},{5,1},{2,6},{6,2},{3,7},{7,3},{8,12},{12,8},{9,1... | collective-permute-start | bytes 1966088 | tf_op jit(solution)/shard_map/ppermute | solution.py:318
  15.1 5.4 %prompt_attention.2 = (f32[128,4096]{1,0:T(8,128)S(1)}, f32[8,4096]{1,0:T(8,128)S(1)}) custom-call(s32[4]{0:T(128)S(1)} %get-tuple-element.109.info, bf16[128,4096]{1,0:T(8,128)(2,1)S(1)} %bitcast.16, bf16[512,1024]{1,0:T(8,128)(2,1)S(1)} %bitcast.29, bf16[512,1024]{1,0:T(8,128)(2,1)S(1)} %bitcast.30), custom_call_target="tpu_custom_call" | custom-call | flops 17179869184 | bytes 1024 | tf_op jit(solution)/shard_map/prompt_attention/pallas_call | solution.py:94
  20.5 1.1 %collective-permute-done.2.refs_0_ = bf16[320,256]{1,0:T(8,128)(2,1)S(1)} collective-permute-done((bf16[320,256]{1,0:T(8,128)(2,1)S(1)}, bf16[320,256]{1,0:T(8,128)(2,1)S(1)}, u32[]{:S(2)}, u32[]{:S(2)}) %collective-permute-start.2) | collective-permute-done | bytes 163872 | tf_op jit(solution)/shard_map/ppermute | solution.py:318
  21.6 5.0 %collective-permute-start.11 = (bf16[320,256]{1,0:T(8,128)(2,1)S(1)}, bf16[320,256]{1,0:T(8,128)(2,1)S(1)}, u32[]{:S(2)}, u32[]{:S(2)}) collective-permute-start(bf16[320,256]{1,0:T(8,128)(2,1)S(1)} %get-tuple-element.88), channel_id=1, source_target_pairs={{0,16},{8,24},{16,0},{24,8},{1,17},{9,25},{17,1},{25,9},{2,18},{10... | collective-permute-start | bytes 491528 | tf_op jit(solution)/shard_map/ppermute | solution.py:318
  27.2 1.8 %collective-permute-start.5 = (bf16[2,320,256]{2,1,0:T(8,128)(2,1)S(1)}, bf16[2,320,256]{2,1,0:T(8,128)(2,1)S(1)}, u32[]{:S(2)}, u32[]{:S(2)}) collective-permute-start(bf16[2,320,256]{2,1,0:T(8,128)(2,1)S(1)} %pad_maximum_fusion), channel_id=1, source_target_pairs={{0,1},{1,0},{2,3},{3,2},{4,5},{5,4},{6,7},{7,6},{8,9},{9,8},{10,11... | collective-permute-start | bytes 983048 | tf_op jit(solution)/shard_map/ppermute | solution.py:318
  29.4 6.3 %prompt_attention.3 = (f32[128,4096]{1,0:T(8,128)S(1)}, f32[8,4096]{1,0:T(8,128)S(1)}) custom-call(s32[4]{0:T(128)S(1)} %get-tuple-element.110.info, bf16[128,4096]{1,0:T(8,128)(2,1)S(1)} %bitcast.17, bf16[512,1024]{1,0:T(8,128)(2,1)} %collective-permute-done.4.k_ref.v_ref, bf16[512,1024]{1,0:T(8,128)(2,1)} %collective-permute-done.4.k_ref.v_ref, ...), custom_call_target="tpu_custom_call" | custom-call | flops 8589934592 | bytes 1024 | tf_op jit(solution)/shard_map/prompt_attention/pallas_call | solution.py:94
  35.7 0.7 %collective-permute-done.5.refs_2_ = bf16[2,320,256]{2,1,0:T(8,128)(2,1)S(1)} collective-permute-done((bf16[2,320,256]{2,1,0:T(8,128)(2,1)S(1)}, bf16[2,320,256]{2,1,0:T(8,128)(2,1)S(1)}, u32[]{:S(2)}, u32[]{:S(2)}) %collective-permute-start.5) | collective-permute-done | bytes 327712 | tf_op jit(solution)/shard_map/ppermute | solution.py:318
  36.4 1.5 %collective-permute-start.14 = (bf16[640,256]{1,0:T(8,128)(2,1)S(1)}, bf16[640,256]{1,0:T(8,128)(2,1)S(1)}, u32[]{:S(2)}, u32[]{:S(2)}) collective-permute-start(bf16[640,256]{1,0:T(8,128)(2,1)S(1)} %get-tuple-element.91.own), channel_id=1, source_target_pairs={{0,8},{8,0},{16,24},{24,16},{1,9},{9,1},{17,25},{25,17},{2,10},{10... | collective-permute-start | bytes 983048 | tf_op jit(solution)/shard_map/ppermute | solution.py:318
  37.9 1.5 %project.2 = (f32[2,128,256]{2,1,0:T(8,128)S(1)}, f32[2,128,256]{2,1,0:T(8,128)S(1)}) custom-call(s32[4]{0:T(128)S(1)} %pad_add_fusion.1.where, bf16[2,4,128,640]{3,2,1,0:T(8,128)(2,1)S(1)} %get-tuple-element.84.keep, bf16[4,128,640]{2,1,0:T(8,128)(2,1)S(1)} %collective-permute-done.6.other, bf16[4,128,640]{2,1,0:T(8,128)(2,1)S(1)} %collective-permute-done.7.other_2, ...), custom_call_target="tpu_custom_call" | custom-call | flops 1024 | bytes 1024 | tf_op jit(solution)/shard_map/project/pallas_call | solution.py:117
  39.5 1.6 %collective-permute-start.15 = (bf16[2,320,256]{2,1,0:T(8,128)(2,1)S(1)}, bf16[2,320,256]{2,1,0:T(8,128)(2,1)S(1)}, u32[]{:S(2)}, u32[]{:S(2)}) collective-permute-start(bf16[2,320,256]{2,1,0:T(8,128)(2,1)S(1)} %pad_maximum_fusion.1), channel_id=1, source_target_pairs={{0,1},{1,0},{2,3},{3,2},{4,5},{5,4},{6,7},{7,6},{8,9},{9,8},{10,11... | collective-permute-start | bytes 983048 | tf_op jit(solution)/shard_map/ppermute | solution.py:318
  41.1 1.7 %collective-permute-start.10 = (f32[1,128,256]{2,1,0:T(8,128)S(1)}, f32[1,128,256]{2,1,0:T(8,128)S(1)}, u32[]{:S(2)}, u32[]{:S(2)}) collective-permute-start(f32[1,128,256]{2,1,0:T(8,128)S(1)} %get-tuple-element.107), channel_id=1, source_target_pairs={{0,6},{2,4},{4,2},{6,0},{1,7},{3,5},{5,3},{7,1},{8,14},{10,12},{12... | collective-permute-start | bytes 393224 | tf_op jit(solution)/shard_map/ppermute | solution.py:318
  43.3 5.5 %collective-permute-done.15.refs_2_ = bf16[2,320,256]{2,1,0:T(8,128)(2,1)S(1)} collective-permute-done((bf16[2,320,256]{2,1,0:T(8,128)(2,1)S(1)}, bf16[2,320,256]{2,1,0:T(8,128)(2,1)S(1)}, u32[]{:S(2)}, u32[]{:S(2)}) %collective-permute-start.15) | collective-permute-done | bytes 327712 | tf_op jit(solution)/shard_map/ppermute | solution.py:318
  48.8 1.5 %project.3 = (f32[2,128,256]{2,1,0:T(8,128)S(1)}, f32[2,128,256]{2,1,0:T(8,128)S(1)}) custom-call(s32[4]{0:T(128)S(1)} %pad_add_fusion.1.where, bf16[2,4,128,640]{3,2,1,0:T(8,128)(2,1)S(1)} %get-tuple-element.84.keep, bf16[4,128,640]{2,1,0:T(8,128)(2,1)S(1)} %collective-permute-done.6.other, bf16[4,128,640]{2,1,0:T(8,128)(2,1)S(1)} %collective-permute-done.7.other_2, ...), custom_call_target="tpu_custom_call" | custom-call | flops 1024 | bytes 1024 | tf_op jit(solution)/shard_map/project/pallas_call | solution.py:117
  50.4 1.6 %collective-permute-start.16 = (f32[1,128,256]{2,1,0:T(8,128)S(1)}, f32[1,128,256]{2,1,0:T(8,128)S(1)}, u32[]{:S(2)}, u32[]{:S(2)}) collective-permute-start(f32[1,128,256]{2,1,0:T(8,128)S(1)} %get-tuple-element.106), channel_id=1, source_target_pairs={{0,4},{4,0},{1,5},{5,1},{2,6},{6,2},{3,7},{7,3},{8,12},{12,8},{9,1... | collective-permute-start | bytes 393224 | tf_op jit(solution)/shard_map/ppermute | solution.py:318
  52.0 0.7 %collective-permute-start.18 = (f32[1,128,256]{2,1,0:T(8,128)S(1)}, f32[1,128,256]{2,1,0:T(8,128)S(1)}, u32[]{:S(2)}, u32[]{:S(2)}) collective-permute-start(f32[1,128,256]{2,1,0:T(8,128)S(1)} %slice.23), channel_id=1, source_target_pairs={{0,2},{2,0},{1,3},{3,1},{4,6},{6,4},{5,7},{7,5},{8,10},{10,8},{9,1... | collective-permute-start | bytes 393224 | tf_op jit(solution)/shard_map/ppermute | solution.py:318
  52.7 2.2 %final_attention.2.refs_0_ = bf16[128,4096]{1,0:T(8,128)(2,1)} custom-call(s32[3]{0:T(128)S(1)} %pad_add_fusion.info, f32[1,128]{1,0:T(1,128)S(1)} %bitcast.26, bf16[128,4096]{1,0:T(8,128)(2,1)S(1)} %bitcast.18, f32[128,4096]{1,0:T(8,128)S(1)} %get-tuple-element.82.acc_ref, f32[8,4096]{1,0:T(8,128)S(1)} %get-tuple-element.83.ml_ref, ...), custom_call_target="tpu_custom_call" | custom-call | flops 1024 | bytes 1024 | tf_op jit(solution)/shard_map/final_attention/pallas_call | solution.py:304
  54.9 1.0 %collective-permute-done.16.theirs = f32[1,128,256]{2,1,0:T(8,128)S(1)} collective-permute-done((f32[1,128,256]{2,1,0:T(8,128)S(1)}, f32[1,128,256]{2,1,0:T(8,128)S(1)}, u32[]{:S(2)}, u32[]{:S(2)}) %collective-permute-start.16) | collective-permute-done | bytes 131104 | tf_op jit(solution)/shard_map/ppermute | solution.py:318
  55.9 1.9 %collective-permute-done.17.there = f32[1,128,256]{2,1,0:T(8,128)S(1)} collective-permute-done((f32[1,128,256]{2,1,0:T(8,128)S(1)}, f32[1,128,256]{2,1,0:T(8,128)S(1)}, u32[]{:S(2)}, u32[]{:S(2)}) %collective-permute-start.17) | collective-permute-done | bytes 131104 | tf_op jit(solution)/shard_map/ppermute | solution.py:318
  57.7 2.2 %final_attention.3 = bf16[128,4096]{1,0:T(8,128)(2,1)} custom-call(s32[3]{0:T(128)S(1)} %pad_add_fusion.info, f32[1,128]{1,0:T(1,128)S(1)} %bitcast.27, bf16[128,4096]{1,0:T(8,128)(2,1)S(1)} %bitcast.19, f32[128,4096]{1,0:T(8,128)S(1)} %get-tuple-element.82.acc_ref, f32[8,4096]{1,0:T(8,128)S(1)} %get-tuple-element.83.ml_ref, ...), custom_call_target="tpu_custom_call", output_to_operand_aliasing={{}: (9, {})} | custom-call | flops 1024 | bytes 1024 | tf_op jit(solution)/shard_map/final_attention/pallas_call | solution.py:304
  (48 shorter events, 4.7 us)
Async XLA Ops:
  0.0 11.8 %collective-permute-start.1 = (bf16[128,5120]{1,0:T(8,128)(2,1)}, bf16[128,5120]{1,0:T(8,128)(2,1)}, u32[]{:S(2)}, u32[]{:S(2)}) collective-permute-start(bf16[128,5120]{1,0:T(8,128)(2,1)} %bitcast.20), channel_id=1, source_target_pairs={{0,2},{2,0},{1,3},{3,1},{4,6},{6,4},{5,7},{7,5},{8,10},{10,8},{9,1... | collective-permute-start | bytes 3932168 | tf_op jit(solution)/shard_map/ppermute | solution.py:318
  0.5 5.6 %collective-permute-start = (bf16[320,1024]{1,0:T(8,128)(2,1)}, bf16[320,1024]{1,0:T(8,128)(2,1)S(1)}, u32[]{:S(2)}, u32[]{:S(2)}) collective-permute-start(bf16[320,1024]{1,0:T(8,128)(2,1)} %weight_ref.1), channel_id=1, source_target_pairs={{0,2},{2,0},{1,3},{3,1},{4,6},{6,4},{5,7},{7,5},{8,10},{10,8},{9,1... | collective-permute-start | bytes 1966088 | tf_op jit(solution)/shard_map/ppermute | solution.py:318
  0.6 26.6 %collective-permute-start.4 = (bf16[512,1024]{1,0:T(8,128)(2,1)}, bf16[512,1024]{1,0:T(8,128)(2,1)}, u32[]{:S(2)}, u32[]{:S(2)}) collective-permute-start(bf16[512,1024]{1,0:T(8,128)(2,1)} %bitcast.28), channel_id=1, source_target_pairs={{0,1},{1,0},{2,3},{3,2},{4,5},{5,4},{6,7},{7,6},{8,9},{9,8},{10,11... | collective-permute-start | bytes 3145736 | tf_op jit(solution)/shard_map/ppermute | solution.py:337
  5.2 6.3 %copy-start.5 = (s32[1,2,2]{2,1,0:T(2,128)S(1)}, s32[1,2,2]{2,1,0:T(2,128)}, u32[]{:S(2)}) copy-start(s32[1,2,2]{2,1,0:T(2,128)} %param.14) | copy-start | bytes 52
  5.2 6.6 %copy-start.1 = (bf16[1,128,5120]{2,1,0:T(8,128)(2,1)S(1)}, bf16[1,128,5120]{2,1,0:T(8,128)(2,1)}, u32[]{:S(2)}) copy-start(bf16[1,128,5120]{2,1,0:T(8,128)(2,1)} %param.8) | copy-start | bytes 3932164
  6.6 15.0 %collective-permute-start.2 = (bf16[320,256]{1,0:T(8,128)(2,1)S(1)}, bf16[320,256]{1,0:T(8,128)(2,1)S(1)}, u32[]{:S(2)}, u32[]{:S(2)}) collective-permute-start(bf16[320,256]{1,0:T(8,128)(2,1)S(1)} %far_first.1), channel_id=1, source_target_pairs={{0,16},{8,24},{16,0},{24,8},{1,17},{9,25},{17,1},{25,9},{2,18},{10... | collective-permute-start | bytes 491528 | tf_op jit(solution)/shard_map/ppermute | solution.py:318
  9.3 12.4 %collective-permute-start.3 = (bf16[320,256]{1,0:T(8,128)(2,1)S(1)}, bf16[320,256]{1,0:T(8,128)(2,1)S(1)}, u32[]{:S(2)}, u32[]{:S(2)}) collective-permute-start(bf16[320,256]{1,0:T(8,128)(2,1)S(1)} %far_first.1), channel_id=1, source_target_pairs={{0,24},{8,16},{16,8},{24,0},{1,25},{9,17},{17,9},{25,1},{2,26},{10... | collective-permute-start | bytes 491528 | tf_op jit(solution)/shard_map/ppermute | solution.py:318
  11.2 26.6 %collective-permute-start.8 = (bf16[640,256]{1,0:T(8,128)(2,1)S(1)}, bf16[640,256]{1,0:T(8,128)(2,1)S(1)}, u32[]{:S(2)}, u32[]{:S(2)}) collective-permute-start(bf16[640,256]{1,0:T(8,128)(2,1)S(1)} %get-tuple-element.60.own), channel_id=1, source_target_pairs={{0,8},{8,0},{16,24},{24,16},{1,9},{9,1},{17,25},{25,17},{2,10},{10... | collective-permute-start | bytes 983048 | tf_op jit(solution)/shard_map/ppermute | solution.py:318
  11.8 3.3 %copy-start = (bf16[1,128,4096]{2,1,0:T(8,128)(2,1)S(1)}, bf16[1,128,4096]{2,1,0:T(8,128)(2,1)}, u32[]{:S(2)}) copy-start(bf16[1,128,4096]{2,1,0:T(8,128)(2,1)} %param.9) | copy-start | bytes 3145732
  13.5 15.9 %collective-permute-start.6 = (bf16[4,128,640]{2,1,0:T(8,128)(2,1)S(1)}, bf16[4,128,640]{2,1,0:T(8,128)(2,1)S(1)}, u32[]{:S(2)}, u32[]{:S(2)}) collective-permute-start(bf16[4,128,640]{2,1,0:T(8,128)(2,1)S(1)} %get-tuple-element.63), channel_id=1, source_target_pairs={{0,4},{4,0},{1,5},{5,1},{2,6},{6,2},{3,7},{7,3},{8,12},{12,8},{9,1... | collective-permute-start | bytes 1966088 | tf_op jit(solution)/shard_map/ppermute | solution.py:318
  21.6 17.8 %collective-permute-start.11 = (bf16[320,256]{1,0:T(8,128)(2,1)S(1)}, bf16[320,256]{1,0:T(8,128)(2,1)S(1)}, u32[]{:S(2)}, u32[]{:S(2)}) collective-permute-start(bf16[320,256]{1,0:T(8,128)(2,1)S(1)} %get-tuple-element.88), channel_id=1, source_target_pairs={{0,16},{8,24},{16,0},{24,8},{1,17},{9,25},{17,1},{25,9},{2,18},{10... | collective-permute-start | bytes 491528 | tf_op jit(solution)/shard_map/ppermute | solution.py:318
  26.6 12.8 %collective-permute-start.12 = (bf16[320,256]{1,0:T(8,128)(2,1)S(1)}, bf16[320,256]{1,0:T(8,128)(2,1)S(1)}, u32[]{:S(2)}, u32[]{:S(2)}) collective-permute-start(bf16[320,256]{1,0:T(8,128)(2,1)S(1)} %get-tuple-element.88), channel_id=1, source_target_pairs={{0,24},{8,16},{16,8},{24,0},{1,25},{9,17},{17,9},{25,1},{2,26},{10... | collective-permute-start | bytes 491528 | tf_op jit(solution)/shard_map/ppermute | solution.py:318
  27.2 9.1 %collective-permute-start.5 = (bf16[2,320,256]{2,1,0:T(8,128)(2,1)S(1)}, bf16[2,320,256]{2,1,0:T(8,128)(2,1)S(1)}, u32[]{:S(2)}, u32[]{:S(2)}) collective-permute-start(bf16[2,320,256]{2,1,0:T(8,128)(2,1)S(1)} %pad_maximum_fusion), channel_id=1, source_target_pairs={{0,1},{1,0},{2,3},{3,2},{4,5},{5,4},{6,7},{7,6},{8,9},{9,8},{10,11... | collective-permute-start | bytes 983048 | tf_op jit(solution)/shard_map/ppermute | solution.py:318
  29.4 8.5 %collective-permute-start.7 = (bf16[4,128,640]{2,1,0:T(8,128)(2,1)S(1)}, bf16[4,128,640]{2,1,0:T(8,128)(2,1)S(1)}, u32[]{:S(2)}, u32[]{:S(2)}) collective-permute-start(bf16[4,128,640]{2,1,0:T(8,128)(2,1)S(1)} %collective-permute-done.6.other), channel_id=1, source_target_pairs={{0,2},{2,0},{1,3},{3,1},{4,6},{6,4},{5,7},{7,5},{8,10},{10,8},{9,1... | collective-permute-start | bytes 1966088 | tf_op jit(solution)/shard_map/ppermute | solution.py:318
  36.4 12.4 %collective-permute-start.14 = (bf16[640,256]{1,0:T(8,128)(2,1)S(1)}, bf16[640,256]{1,0:T(8,128)(2,1)S(1)}, u32[]{:S(2)}, u32[]{:S(2)}) collective-permute-start(bf16[640,256]{1,0:T(8,128)(2,1)S(1)} %get-tuple-element.91.own), channel_id=1, source_target_pairs={{0,8},{8,0},{16,24},{24,16},{1,9},{9,1},{17,25},{25,17},{2,10},{10... | collective-permute-start | bytes 983048 | tf_op jit(solution)/shard_map/ppermute | solution.py:318
  39.5 9.3 %collective-permute-start.15 = (bf16[2,320,256]{2,1,0:T(8,128)(2,1)S(1)}, bf16[2,320,256]{2,1,0:T(8,128)(2,1)S(1)}, u32[]{:S(2)}, u32[]{:S(2)}) collective-permute-start(bf16[2,320,256]{2,1,0:T(8,128)(2,1)S(1)} %pad_maximum_fusion.1), channel_id=1, source_target_pairs={{0,1},{1,0},{2,3},{3,2},{4,5},{5,4},{6,7},{7,6},{8,9},{9,8},{10,11... | collective-permute-start | bytes 983048 | tf_op jit(solution)/shard_map/ppermute | solution.py:318
  41.0 9.3 %collective-permute-start.13 = (f32[1,128,256]{2,1,0:T(8,128)S(1)}, f32[1,128,256]{2,1,0:T(8,128)S(1)}, u32[]{:S(2)}, u32[]{:S(2)}) collective-permute-start(f32[1,128,256]{2,1,0:T(8,128)S(1)} %slice.20), channel_id=1, source_target_pairs={{0,2},{2,0},{1,3},{3,1},{4,6},{6,4},{5,7},{7,5},{8,10},{10,8},{9,1... | collective-permute-start | bytes 393224 | tf_op jit(solution)/shard_map/ppermute | solution.py:318
  41.1 9.2 %collective-permute-start.10 = (f32[1,128,256]{2,1,0:T(8,128)S(1)}, f32[1,128,256]{2,1,0:T(8,128)S(1)}, u32[]{:S(2)}, u32[]{:S(2)}) collective-permute-start(f32[1,128,256]{2,1,0:T(8,128)S(1)} %get-tuple-element.107), channel_id=1, source_target_pairs={{0,6},{2,4},{4,2},{6,0},{1,7},{3,5},{5,3},{7,1},{8,14},{10,12},{12... | collective-permute-start | bytes 393224 | tf_op jit(solution)/shard_map/ppermute | solution.py:318
  42.8 9.8 %copy-start.6 = (s32[1,2]{1,0:T(1,128)S(1)}, s32[1,2]{1,0:T(1,128)}, u32[]{:S(2)}) copy-start(s32[1,2]{1,0:T(1,128)} %param.15) | copy-start | bytes 28
  42.8 9.9 %copy-start.3 = (f32[128]{0:T(128)S(1)}, f32[128]{0:T(128)}, u32[]{:S(2)}) copy-start(f32[128]{0:T(128)} %param.12) | copy-start | bytes 1540
  42.8 7.5 %collective-permute-start.9 = (f32[1,128,256]{2,1,0:T(8,128)S(1)}, f32[1,128,256]{2,1,0:T(8,128)S(1)}, u32[]{:S(2)}, u32[]{:S(2)}) collective-permute-start(f32[1,128,256]{2,1,0:T(8,128)S(1)} %get-tuple-element.108), channel_id=1, source_target_pairs={{0,4},{4,0},{1,5},{5,1},{2,6},{6,2},{3,7},{7,3},{8,12},{12,8},{9,1... | collective-permute-start | bytes 393224 | tf_op jit(solution)/shard_map/ppermute | solution.py:318
  50.4 5.5 %collective-permute-start.16 = (f32[1,128,256]{2,1,0:T(8,128)S(1)}, f32[1,128,256]{2,1,0:T(8,128)S(1)}, u32[]{:S(2)}, u32[]{:S(2)}) collective-permute-start(f32[1,128,256]{2,1,0:T(8,128)S(1)} %get-tuple-element.106), channel_id=1, source_target_pairs={{0,4},{4,0},{1,5},{5,1},{2,6},{6,2},{3,7},{7,3},{8,12},{12,8},{9,1... | collective-permute-start | bytes 393224 | tf_op jit(solution)/shard_map/ppermute | solution.py:318
  51.9 5.8 %collective-permute-start.17 = (f32[1,128,256]{2,1,0:T(8,128)S(1)}, f32[1,128,256]{2,1,0:T(8,128)S(1)}, u32[]{:S(2)}, u32[]{:S(2)}) collective-permute-start(f32[1,128,256]{2,1,0:T(8,128)S(1)} %get-tuple-element.105), channel_id=1, source_target_pairs={{0,6},{2,4},{4,2},{6,0},{1,7},{3,5},{5,3},{7,1},{8,14},{10,12},{12... | collective-permute-start | bytes 393224 | tf_op jit(solution)/shard_map/ppermute | solution.py:318
  52.0 5.8 %collective-permute-start.18 = (f32[1,128,256]{2,1,0:T(8,128)S(1)}, f32[1,128,256]{2,1,0:T(8,128)S(1)}, u32[]{:S(2)}, u32[]{:S(2)}) collective-permute-start(f32[1,128,256]{2,1,0:T(8,128)S(1)} %slice.23), channel_id=1, source_target_pairs={{0,2},{2,0},{1,3},{3,1},{4,6},{6,4},{5,7},{7,5},{8,10},{10,8},{9,1... | collective-permute-start | bytes 393224 | tf_op jit(solution)/shard_map/ppermute | solution.py:318
  (2 other events, 4.3 us)

commit v17 on v16

--- a/solution.py
+++ b/solution.py
@@ -331,14 +331,14 @@
     tie = lax.optimization_barrier
 
     got_weight = xor_swap(kv_weight, "core", 1)
-    got_x = xor_swap(x, "core", 1)
     caches = [prompt_cache[0]]
     for _ in range(cycle - 1):
         caches.append(lax.ppermute(caches[-1], "blk", [(i, (i + 1) % cycle) for i in range(cycle)]))
 
     wholes, got_weight = tie((own_rows(where, kv_weight), got_weight))
     far = far_first(where, wholes[0], got_weight)
-    got_weight, far = tie((got_weight, far))
+    got_weight, far, own_x = tie((got_weight, far, x))
+    got_x = xor_swap(own_x, "core", 1)
     whole, rest = pack_weight(where, got_weight, wholes)
     far = [far, *rest]
 

time: 60.6 us -> 62.8 us (1.036)
  waiting for transfers between devices: 10.6 us -> 13.1 us
    ppermute x1, waiting for transfers between devices: 0.14 us -> 2.58 us  [per_device(): lax.ppermute(caches[-1], 'blk', [(i, (i + 1) % cycle) for i in range(cycl...]
    ppermute x18, starting transfers between devices: 21.2 us -> 21.9 us  [xor_swap(): lax.ppermute(array, axis, [(i, i ^ by) for i in range(lax.axis_size(axis))])]
  transfers between devices with their start and end apart: 19 -> 19, of which waited for: 7 -> 8; matrix products, arithmetic and copies ran while one was open for 1% -> 1% of each run, Pallas kernels for 34% -> 31%
where the time goes in v17:
time: 62.8 us; the launch traced here: 62.7 us
  starting transfers between devices  24.6 us (39%)
  Pallas kernels  22.5 us (36%)
  waiting for transfers between devices  13.1 us (21%)
  local copies, waits for them, and re-layouts  1.39 us (2%)
  between operations  0.85 us (1%)
    ppermute x18, starting transfers between devices, xor_swap(): lax.ppermute(array, axis, [(i, i ^ by) for i in range(lax.axis_size(axis))])  21.9 us
    pallas_call x2, Pallas kernels, prompt_attention(): pl.pallas_call(functools.partial(prompt_kernel, first), grid_spec=pltpu.P...  11.7 us
    ppermute x18, waiting for transfers between devices, xor_swap(): lax.ppermute(array, axis, [(i, i ^ by) for i in range(lax.axis_size(axis))])  10.5 us
    pallas_call x5, Pallas kernels, on_chip(): pl.pallas_call(kernel, in_specs=[SMEM] + [VMEM] * len(operands), out_spec...  5.81 us
    pallas_call x2, Pallas kernels, final_attention(): pl.pallas_call(functools.partial(final_kernel, chunk, offset), in_specs=s...  4.32 us
    ppermute x1, starting transfers between devices, per_device(): lax.ppermute(caches[-1], 'blk', [(i, (i + 1) % cycle) for i in range(cycl...  2.63 us
    ppermute x1, waiting for transfers between devices, per_device(): lax.ppermute(caches[-1], 'blk', [(i, (i + 1) % cycle) for i in range(cycl...  2.58 us
  transfers between devices with their start and end apart: 19, of which 8 were waited for; matrix products, arithmetic and copies ran while one was open for 1% of the time, Pallas kernels for 31%

profile of v17, /device:TPU:0, one launch (start us, length us, event | category | flops | bytes accessed | tf_op | source)
XLA Modules:
  0.0 62.7 jit_solution(17192904767479571265)
XLA Ops:
  0.5 1.1 %copy-done.2 = bf16[320,1024]{1,0:T(8,128)(2,1)S(1)} copy-done((bf16[320,1024]{1,0:T(8,128)(2,1)S(1)}, bf16[320,1024]{1,0:T(8,128)(2,1)}, u32[]{:S(2)}) %copy-start.2) | copy-done | bytes 655384
  3.4 2.6 %collective-permute-start.4 = (bf16[512,1024]{1,0:T(8,128)(2,1)}, bf16[512,1024]{1,0:T(8,128)(2,1)}, u32[]{:S(2)}, u32[]{:S(2)}) collective-permute-start(bf16[512,1024]{1,0:T(8,128)(2,1)} %bitcast.28), channel_id=1, source_target_pairs={{0,1},{1,0},{2,3},{3,2},{4,5},{5,4},{6,7},{7,6},{8,9},{9,8},{10,11... | collective-permute-start | bytes 3145736 | tf_op jit(solution)/shard_map/ppermute | solution.py:336
  6.7 2.7 %collective-permute-start.2 = (bf16[320,256]{1,0:T(8,128)(2,1)S(1)}, bf16[320,256]{1,0:T(8,128)(2,1)S(1)}, u32[]{:S(2)}, u32[]{:S(2)}) collective-permute-start(bf16[320,256]{1,0:T(8,128)(2,1)S(1)} %far_first.1), channel_id=1, source_target_pairs={{0,16},{8,24},{16,0},{24,8},{1,17},{9,25},{17,1},{25,9},{2,18},{10... | collective-permute-start | bytes 491528 | tf_op jit(solution)/shard_map/ppermute | solution.py:318
  9.4 1.3 %collective-permute-start.3 = (bf16[320,256]{1,0:T(8,128)(2,1)S(1)}, bf16[320,256]{1,0:T(8,128)(2,1)S(1)}, u32[]{:S(2)}, u32[]{:S(2)}) collective-permute-start(bf16[320,256]{1,0:T(8,128)(2,1)S(1)} %far_first.1), channel_id=1, source_target_pairs={{0,24},{8,16},{16,8},{24,0},{1,25},{9,17},{17,9},{25,1},{2,26},{10... | collective-permute-start | bytes 491528 | tf_op jit(solution)/shard_map/ppermute | solution.py:318
  11.9 1.6 %pack_rows.1 = (bf16[2,4,128,640]{3,2,1,0:T(8,128)(2,1)S(1)}, bf16[4,128,640]{2,1,0:T(8,128)(2,1)S(1)}) custom-call(s32[4]{0:T(128)S(1)} %pad_add_fusion.1.where, bf16[128,5120]{1,0:T(8,128)(2,1)S(1)} %bitcast.21, bf16[128,5120]{1,0:T(8,128)(2,1)} %collective-permute-done.1.got_ref), custom_call_target="tpu_custom_call" | custom-call | flops 1024 | bytes 1024 | tf_op jit(solution)/shard_map/pack_rows/pallas_call | solution.py:117
  13.6 1.6 %collective-permute-start.6 = (bf16[4,128,640]{2,1,0:T(8,128)(2,1)S(1)}, bf16[4,128,640]{2,1,0:T(8,128)(2,1)S(1)}, u32[]{:S(2)}, u32[]{:S(2)}) collective-permute-start(bf16[4,128,640]{2,1,0:T(8,128)(2,1)S(1)} %get-tuple-element.65), channel_id=1, source_target_pairs={{0,4},{4,0},{1,5},{5,1},{2,6},{6,2},{3,7},{7,3},{8,12},{12,8},{9,1... | collective-permute-start | bytes 1966088 | tf_op jit(solution)/shard_map/ppermute | solution.py:318
  15.2 5.4 %prompt_attention.2 = (f32[128,4096]{1,0:T(8,128)S(1)}, f32[8,4096]{1,0:T(8,128)S(1)}) custom-call(s32[4]{0:T(128)S(1)} %get-tuple-element.111.info, bf16[128,4096]{1,0:T(8,128)(2,1)S(1)} %bitcast.16, bf16[512,1024]{1,0:T(8,128)(2,1)S(1)} %bitcast.29, bf16[512,1024]{1,0:T(8,128)(2,1)S(1)} %bitcast.30), custom_call_target="tpu_custom_call" | custom-call | flops 17179869184 | bytes 1024 | tf_op jit(solution)/shard_map/prompt_attention/pallas_call | solution.py:94
  20.6 1.2 %collective-permute-done.2.refs_0_ = bf16[320,256]{1,0:T(8,128)(2,1)S(1)} collective-permute-done((bf16[320,256]{1,0:T(8,128)(2,1)S(1)}, bf16[320,256]{1,0:T(8,128)(2,1)S(1)}, u32[]{:S(2)}, u32[]{:S(2)}) %collective-permute-start.2) | collective-permute-done | bytes 163872 | tf_op jit(solution)/shard_map/ppermute | solution.py:318
  21.8 5.2 %collective-permute-start.11 = (bf16[320,256]{1,0:T(8,128)(2,1)S(1)}, bf16[320,256]{1,0:T(8,128)(2,1)S(1)}, u32[]{:S(2)}, u32[]{:S(2)}) collective-permute-start(bf16[320,256]{1,0:T(8,128)(2,1)S(1)} %get-tuple-element.90), channel_id=1, source_target_pairs={{0,16},{8,24},{16,0},{24,8},{1,17},{9,25},{17,1},{25,9},{2,18},{10... | collective-permute-start | bytes 491528 | tf_op jit(solution)/shard_map/ppermute | solution.py:318
  27.5 2.6 %collective-permute-done.4.k_ref.v_ref = bf16[512,1024]{1,0:T(8,128)(2,1)} collective-permute-done((bf16[512,1024]{1,0:T(8,128)(2,1)}, bf16[512,1024]{1,0:T(8,128)(2,1)}, u32[]{:S(2)}, u32[]{:S(2)}) %collective-permute-start.4) | collective-permute-done | bytes 1048608 | tf_op jit(solution)/shard_map/ppermute | solution.py:336
  30.1 1.8 %collective-permute-start.5 = (bf16[2,320,256]{2,1,0:T(8,128)(2,1)S(1)}, bf16[2,320,256]{2,1,0:T(8,128)(2,1)S(1)}, u32[]{:S(2)}, u32[]{:S(2)}) collective-permute-start(bf16[2,320,256]{2,1,0:T(8,128)(2,1)S(1)} %pad_maximum_fusion), channel_id=1, source_target_pairs={{0,1},{1,0},{2,3},{3,2},{4,5},{5,4},{6,7},{7,6},{8,9},{9,8},{10,11... | collective-permute-start | bytes 983048 | tf_op jit(solution)/shard_map/ppermute | solution.py:318
  31.9 6.3 %prompt_attention.3 = (f32[128,4096]{1,0:T(8,128)S(1)}, f32[8,4096]{1,0:T(8,128)S(1)}) custom-call(s32[4]{0:T(128)S(1)} %get-tuple-element.112.info, bf16[128,4096]{1,0:T(8,128)(2,1)S(1)} %bitcast.17, bf16[512,1024]{1,0:T(8,128)(2,1)} %collective-permute-done.4.k_ref.v_ref, bf16[512,1024]{1,0:T(8,128)(2,1)} %collective-permute-done.4.k_ref.v_ref, ...), custom_call_target="tpu_custom_call" | custom-call | flops 8589934592 | bytes 1024 | tf_op jit(solution)/shard_map/prompt_attention/pallas_call | solution.py:94
  38.2 1.4 %collective-permute-done.5.refs_2_ = bf16[2,320,256]{2,1,0:T(8,128)(2,1)S(1)} collective-permute-done((bf16[2,320,256]{2,1,0:T(8,128)(2,1)S(1)}, bf16[2,320,256]{2,1,0:T(8,128)(2,1)S(1)}, u32[]{:S(2)}, u32[]{:S(2)}) %collective-permute-start.5) | collective-permute-done | bytes 327712 | tf_op jit(solution)/shard_map/ppermute | solution.py:318
  39.6 1.6 %collective-permute-start.14 = (bf16[640,256]{1,0:T(8,128)(2,1)S(1)}, bf16[640,256]{1,0:T(8,128)(2,1)S(1)}, u32[]{:S(2)}, u32[]{:S(2)}) collective-permute-start(bf16[640,256]{1,0:T(8,128)(2,1)S(1)} %get-tuple-element.93.own), channel_id=1, source_target_pairs={{0,8},{8,0},{16,24},{24,16},{1,9},{9,1},{17,25},{25,17},{2,10},{10... | collective-permute-start | bytes 983048 | tf_op jit(solution)/shard_map/ppermute | solution.py:318
  41.1 1.5 %project.2 = (f32[2,128,256]{2,1,0:T(8,128)S(1)}, f32[2,128,256]{2,1,0:T(8,128)S(1)}) custom-call(s32[4]{0:T(128)S(1)} %pad_add_fusion.1.where, bf16[2,4,128,640]{3,2,1,0:T(8,128)(2,1)S(1)} %get-tuple-element.86.keep, bf16[4,128,640]{2,1,0:T(8,128)(2,1)S(1)} %collective-permute-done.6.other, bf16[4,128,640]{2,1,0:T(8,128)(2,1)S(1)} %collective-permute-done.7.other_2, ...), custom_call_target="tpu_custom_call" | custom-call | flops 1024 | bytes 1024 | tf_op jit(solution)/shard_map/project/pallas_call | solution.py:117
  42.7 1.6 %collective-permute-start.15 = (bf16[2,320,256]{2,1,0:T(8,128)(2,1)S(1)}, bf16[2,320,256]{2,1,0:T(8,128)(2,1)S(1)}, u32[]{:S(2)}, u32[]{:S(2)}) collective-permute-start(bf16[2,320,256]{2,1,0:T(8,128)(2,1)S(1)} %pad_maximum_fusion.1), channel_id=1, source_target_pairs={{0,1},{1,0},{2,3},{3,2},{4,5},{5,4},{6,7},{7,6},{8,9},{9,8},{10,11... | collective-permute-start | bytes 983048 | tf_op jit(solution)/shard_map/ppermute | solution.py:318
  44.4 1.7 %collective-permute-start.10 = (f32[1,128,256]{2,1,0:T(8,128)S(1)}, f32[1,128,256]{2,1,0:T(8,128)S(1)}, u32[]{:S(2)}, u32[]{:S(2)}) collective-permute-start(f32[1,128,256]{2,1,0:T(8,128)S(1)} %get-tuple-element.109), channel_id=1, source_target_pairs={{0,6},{2,4},{4,2},{6,0},{1,7},{3,5},{5,3},{7,1},{8,14},{10,12},{12... | collective-permute-start | bytes 393224 | tf_op jit(solution)/shard_map/ppermute | solution.py:318
  46.6 4.7 %collective-permute-done.15.refs_2_ = bf16[2,320,256]{2,1,0:T(8,128)(2,1)S(1)} collective-permute-done((bf16[2,320,256]{2,1,0:T(8,128)(2,1)S(1)}, bf16[2,320,256]{2,1,0:T(8,128)(2,1)S(1)}, u32[]{:S(2)}, u32[]{:S(2)}) %collective-permute-start.15) | collective-permute-done | bytes 327712 | tf_op jit(solution)/shard_map/ppermute | solution.py:318
  51.4 1.5 %project.3 = (f32[2,128,256]{2,1,0:T(8,128)S(1)}, f32[2,128,256]{2,1,0:T(8,128)S(1)}) custom-call(s32[4]{0:T(128)S(1)} %pad_add_fusion.1.where, bf16[2,4,128,640]{3,2,1,0:T(8,128)(2,1)S(1)} %get-tuple-element.86.keep, bf16[4,128,640]{2,1,0:T(8,128)(2,1)S(1)} %collective-permute-done.6.other, bf16[4,128,640]{2,1,0:T(8,128)(2,1)S(1)} %collective-permute-done.7.other_2, ...), custom_call_target="tpu_custom_call" | custom-call | flops 1024 | bytes 1024 | tf_op jit(solution)/shard_map/project/pallas_call | solution.py:117
  53.1 1.6 %collective-permute-start.16 = (f32[1,128,256]{2,1,0:T(8,128)S(1)}, f32[1,128,256]{2,1,0:T(8,128)S(1)}, u32[]{:S(2)}, u32[]{:S(2)}) collective-permute-start(f32[1,128,256]{2,1,0:T(8,128)S(1)} %get-tuple-element.108), channel_id=1, source_target_pairs={{0,4},{4,0},{1,5},{5,1},{2,6},{6,2},{3,7},{7,3},{8,12},{12,8},{9,1... | collective-permute-start | bytes 393224 | tf_op jit(solution)/shard_map/ppermute | solution.py:318
  55.5 2.2 %final_attention.2.refs_0_ = bf16[128,4096]{1,0:T(8,128)(2,1)} custom-call(s32[3]{0:T(128)S(1)} %pad_add_fusion.info, f32[1,128]{1,0:T(1,128)S(1)} %bitcast.26, bf16[128,4096]{1,0:T(8,128)(2,1)S(1)} %bitcast.18, f32[128,4096]{1,0:T(8,128)S(1)} %get-tuple-element.84.acc_ref, f32[8,4096]{1,0:T(8,128)S(1)} %get-tuple-element.85.ml_ref, ...), custom_call_target="tpu_custom_call" | custom-call | flops 1024 | bytes 1024 | tf_op jit(solution)/shard_map/final_attention/pallas_call | solution.py:304
  57.7 1.0 %collective-permute-done.16.theirs = f32[1,128,256]{2,1,0:T(8,128)S(1)} collective-permute-done((f32[1,128,256]{2,1,0:T(8,128)S(1)}, f32[1,128,256]{2,1,0:T(8,128)S(1)}, u32[]{:S(2)}, u32[]{:S(2)}) %collective-permute-start.16) | collective-permute-done | bytes 131104 | tf_op jit(solution)/shard_map/ppermute | solution.py:318
  58.6 1.9 %collective-permute-done.17.there = f32[1,128,256]{2,1,0:T(8,128)S(1)} collective-permute-done((f32[1,128,256]{2,1,0:T(8,128)S(1)}, f32[1,128,256]{2,1,0:T(8,128)S(1)}, u32[]{:S(2)}, u32[]{:S(2)}) %collective-permute-start.17) | collective-permute-done | bytes 131104 | tf_op jit(solution)/shard_map/ppermute | solution.py:318
  60.5 2.2 %final_attention.3 = bf16[128,4096]{1,0:T(8,128)(2,1)} custom-call(s32[3]{0:T(128)S(1)} %pad_add_fusion.info, f32[1,128]{1,0:T(1,128)S(1)} %bitcast.27, bf16[128,4096]{1,0:T(8,128)(2,1)S(1)} %bitcast.19, f32[128,4096]{1,0:T(8,128)S(1)} %get-tuple-element.84.acc_ref, f32[8,4096]{1,0:T(8,128)S(1)} %get-tuple-element.85.ml_ref, ...), custom_call_target="tpu_custom_call", output_to_operand_aliasing={{}: (9, {})} | custom-call | flops 1024 | bytes 1024 | tf_op jit(solution)/shard_map/final_attention/pallas_call | solution.py:304
  (48 shorter events, 5.6 us)
Async XLA Ops:
  0.0 2.4 %collective-permute-start = (bf16[320,1024]{1,0:T(8,128)(2,1)}, bf16[320,1024]{1,0:T(8,128)(2,1)S(1)}, u32[]{:S(2)}, u32[]{:S(2)}) collective-permute-start(bf16[320,1024]{1,0:T(8,128)(2,1)} %weight_ref.1), channel_id=1, source_target_pairs={{0,2},{2,0},{1,3},{3,1},{4,6},{6,4},{5,7},{7,5},{8,10},{10,8},{9,1... | collective-permute-start | bytes 1966088 | tf_op jit(solution)/shard_map/ppermute | solution.py:318
  2.2 9.4 %copy-start.5 = (s32[1,2,2]{2,1,0:T(2,128)S(1)}, s32[1,2,2]{2,1,0:T(2,128)}, u32[]{:S(2)}) copy-start(s32[1,2,2]{2,1,0:T(2,128)} %param.14) | copy-start | bytes 52
  3.0 8.9 %collective-permute-start.1 = (bf16[128,5120]{1,0:T(8,128)(2,1)S(1)}, bf16[128,5120]{1,0:T(8,128)(2,1)}, u32[]{:S(2)}, u32[]{:S(2)}) collective-permute-start(bf16[128,5120]{1,0:T(8,128)(2,1)S(1)} %bitcast.20), channel_id=1, source_target_pairs={{0,2},{2,0},{1,3},{3,1},{4,6},{6,4},{5,7},{7,5},{8,10},{10,8},{9,1... | collective-permute-start | bytes 3932168 | tf_op jit(solution)/shard_map/ppermute | solution.py:318
  3.4 26.6 %collective-permute-start.4 = (bf16[512,1024]{1,0:T(8,128)(2,1)}, bf16[512,1024]{1,0:T(8,128)(2,1)}, u32[]{:S(2)}, u32[]{:S(2)}) collective-permute-start(bf16[512,1024]{1,0:T(8,128)(2,1)} %bitcast.28), channel_id=1, source_target_pairs={{0,1},{1,0},{2,3},{3,2},{4,5},{5,4},{6,7},{7,6},{8,9},{9,8},{10,11... | collective-permute-start | bytes 3145736 | tf_op jit(solution)/shard_map/ppermute | solution.py:336
  6.7 15.1 %collective-permute-start.2 = (bf16[320,256]{1,0:T(8,128)(2,1)S(1)}, bf16[320,256]{1,0:T(8,128)(2,1)S(1)}, u32[]{:S(2)}, u32[]{:S(2)}) collective-permute-start(bf16[320,256]{1,0:T(8,128)(2,1)S(1)} %far_first.1), channel_id=1, source_target_pairs={{0,16},{8,24},{16,0},{24,8},{1,17},{9,25},{17,1},{25,9},{2,18},{10... | collective-permute-start | bytes 491528 | tf_op jit(solution)/shard_map/ppermute | solution.py:318
  9.4 12.4 %collective-permute-start.3 = (bf16[320,256]{1,0:T(8,128)(2,1)S(1)}, bf16[320,256]{1,0:T(8,128)(2,1)S(1)}, u32[]{:S(2)}, u32[]{:S(2)}) collective-permute-start(bf16[320,256]{1,0:T(8,128)(2,1)S(1)} %far_first.1), channel_id=1, source_target_pairs={{0,24},{8,16},{16,8},{24,0},{1,25},{9,17},{17,9},{25,1},{2,26},{10... | collective-permute-start | bytes 491528 | tf_op jit(solution)/shard_map/ppermute | solution.py:318
  11.3 29.8 %collective-permute-start.8 = (bf16[640,256]{1,0:T(8,128)(2,1)S(1)}, bf16[640,256]{1,0:T(8,128)(2,1)S(1)}, u32[]{:S(2)}, u32[]{:S(2)}) collective-permute-start(bf16[640,256]{1,0:T(8,128)(2,1)S(1)} %get-tuple-element.61.own), channel_id=1, source_target_pairs={{0,8},{8,0},{16,24},{24,16},{1,9},{9,1},{17,25},{25,17},{2,10},{10... | collective-permute-start | bytes 983048 | tf_op jit(solution)/shard_map/ppermute | solution.py:318
  11.9 3.2 %copy-start = (bf16[1,128,4096]{2,1,0:T(8,128)(2,1)S(1)}, bf16[1,128,4096]{2,1,0:T(8,128)(2,1)}, u32[]{:S(2)}) copy-start(bf16[1,128,4096]{2,1,0:T(8,128)(2,1)} %param.9) | copy-start | bytes 3145732
  11.9 3.2 %copy-start.4 = (bf16[1,512,1024]{2,1,0:T(8,128)(2,1)S(1)}, bf16[1,512,1024]{2,1,0:T(8,128)(2,1)}, u32[]{:S(2)}) copy-start(bf16[1,512,1024]{2,1,0:T(8,128)(2,1)} %param.10) | copy-start | bytes 3145732
  13.6 18.3 %collective-permute-start.6 = (bf16[4,128,640]{2,1,0:T(8,128)(2,1)S(1)}, bf16[4,128,640]{2,1,0:T(8,128)(2,1)S(1)}, u32[]{:S(2)}, u32[]{:S(2)}) collective-permute-start(bf16[4,128,640]{2,1,0:T(8,128)(2,1)S(1)} %get-tuple-element.65), channel_id=1, source_target_pairs={{0,4},{4,0},{1,5},{5,1},{2,6},{6,2},{3,7},{7,3},{8,12},{12,8},{9,1... | collective-permute-start | bytes 1966088 | tf_op jit(solution)/shard_map/ppermute | solution.py:318
  21.8 20.9 %collective-permute-start.11 = (bf16[320,256]{1,0:T(8,128)(2,1)S(1)}, bf16[320,256]{1,0:T(8,128)(2,1)S(1)}, u32[]{:S(2)}, u32[]{:S(2)}) collective-permute-start(bf16[320,256]{1,0:T(8,128)(2,1)S(1)} %get-tuple-element.90), channel_id=1, source_target_pairs={{0,16},{8,24},{16,0},{24,8},{1,17},{9,25},{17,1},{25,9},{2,18},{10... | collective-permute-start | bytes 491528 | tf_op jit(solution)/shard_map/ppermute | solution.py:318
  27.0 15.6 %collective-permute-start.12 = (bf16[320,256]{1,0:T(8,128)(2,1)S(1)}, bf16[320,256]{1,0:T(8,128)(2,1)S(1)}, u32[]{:S(2)}, u32[]{:S(2)}) collective-permute-start(bf16[320,256]{1,0:T(8,128)(2,1)S(1)} %get-tuple-element.90), channel_id=1, source_target_pairs={{0,24},{8,16},{16,8},{24,0},{1,25},{9,17},{17,9},{25,1},{2,26},{10... | collective-permute-start | bytes 491528 | tf_op jit(solution)/shard_map/ppermute | solution.py:318
  30.1 9.5 %collective-permute-start.5 = (bf16[2,320,256]{2,1,0:T(8,128)(2,1)S(1)}, bf16[2,320,256]{2,1,0:T(8,128)(2,1)S(1)}, u32[]{:S(2)}, u32[]{:S(2)}) collective-permute-start(bf16[2,320,256]{2,1,0:T(8,128)(2,1)S(1)} %pad_maximum_fusion), channel_id=1, source_target_pairs={{0,1},{1,0},{2,3},{3,2},{4,5},{5,4},{6,7},{7,6},{8,9},{9,8},{10,11... | collective-permute-start | bytes 983048 | tf_op jit(solution)/shard_map/ppermute | solution.py:318
  31.9 9.2 %collective-permute-start.7 = (bf16[4,128,640]{2,1,0:T(8,128)(2,1)S(1)}, bf16[4,128,640]{2,1,0:T(8,128)(2,1)S(1)}, u32[]{:S(2)}, u32[]{:S(2)}) collective-permute-start(bf16[4,128,640]{2,1,0:T(8,128)(2,1)S(1)} %collective-permute-done.6.other), channel_id=1, source_target_pairs={{0,2},{2,0},{1,3},{3,1},{4,6},{6,4},{5,7},{7,5},{8,10},{10,8},{9,1... | collective-permute-start | bytes 1966088 | tf_op jit(solution)/shard_map/ppermute | solution.py:318
  39.6 11.8 %collective-permute-start.14 = (bf16[640,256]{1,0:T(8,128)(2,1)S(1)}, bf16[640,256]{1,0:T(8,128)(2,1)S(1)}, u32[]{:S(2)}, u32[]{:S(2)}) collective-permute-start(bf16[640,256]{1,0:T(8,128)(2,1)S(1)} %get-tuple-element.93.own), channel_id=1, source_target_pairs={{0,8},{8,0},{16,24},{24,16},{1,9},{9,1},{17,25},{25,17},{2,10},{10... | collective-permute-start | bytes 983048 | tf_op jit(solution)/shard_map/ppermute | solution.py:318
  42.7 8.6 %collective-permute-start.15 = (bf16[2,320,256]{2,1,0:T(8,128)(2,1)S(1)}, bf16[2,320,256]{2,1,0:T(8,128)(2,1)S(1)}, u32[]{:S(2)}, u32[]{:S(2)}) collective-permute-start(bf16[2,320,256]{2,1,0:T(8,128)(2,1)S(1)} %pad_maximum_fusion.1), channel_id=1, source_target_pairs={{0,1},{1,0},{2,3},{3,2},{4,5},{5,4},{6,7},{7,6},{8,9},{9,8},{10,11... | collective-permute-start | bytes 983048 | tf_op jit(solution)/shard_map/ppermute | solution.py:318
  44.3 8.6 %collective-permute-start.13 = (f32[1,128,256]{2,1,0:T(8,128)S(1)}, f32[1,128,256]{2,1,0:T(8,128)S(1)}, u32[]{:S(2)}, u32[]{:S(2)}) collective-permute-start(f32[1,128,256]{2,1,0:T(8,128)S(1)} %slice.20), channel_id=1, source_target_pairs={{0,2},{2,0},{1,3},{3,1},{4,6},{6,4},{5,7},{7,5},{8,10},{10,8},{9,1... | collective-permute-start | bytes 393224 | tf_op jit(solution)/shard_map/ppermute | solution.py:318
  44.4 8.5 %collective-permute-start.10 = (f32[1,128,256]{2,1,0:T(8,128)S(1)}, f32[1,128,256]{2,1,0:T(8,128)S(1)}, u32[]{:S(2)}, u32[]{:S(2)}) collective-permute-start(f32[1,128,256]{2,1,0:T(8,128)S(1)} %get-tuple-element.109), channel_id=1, source_target_pairs={{0,6},{2,4},{4,2},{6,0},{1,7},{3,5},{5,3},{7,1},{8,14},{10,12},{12... | collective-permute-start | bytes 393224 | tf_op jit(solution)/shard_map/ppermute | solution.py:318
  46.1 9.3 %copy-start.6 = (s32[1,2]{1,0:T(1,128)S(1)}, s32[1,2]{1,0:T(1,128)}, u32[]{:S(2)}) copy-start(s32[1,2]{1,0:T(1,128)} %param.15) | copy-start | bytes 28
  46.1 9.4 %copy-start.3 = (f32[128]{0:T(128)S(1)}, f32[128]{0:T(128)}, u32[]{:S(2)}) copy-start(f32[128]{0:T(128)} %param.12) | copy-start | bytes 1540
  46.1 7.0 %collective-permute-start.9 = (f32[1,128,256]{2,1,0:T(8,128)S(1)}, f32[1,128,256]{2,1,0:T(8,128)S(1)}, u32[]{:S(2)}, u32[]{:S(2)}) collective-permute-start(f32[1,128,256]{2,1,0:T(8,128)S(1)} %get-tuple-element.110), channel_id=1, source_target_pairs={{0,4},{4,0},{1,5},{5,1},{2,6},{6,2},{3,7},{7,3},{8,12},{12,8},{9,1... | collective-permute-start | bytes 393224 | tf_op jit(solution)/shard_map/ppermute | solution.py:318
  53.1 5.5 %collective-permute-start.16 = (f32[1,128,256]{2,1,0:T(8,128)S(1)}, f32[1,128,256]{2,1,0:T(8,128)S(1)}, u32[]{:S(2)}, u32[]{:S(2)}) collective-permute-start(f32[1,128,256]{2,1,0:T(8,128)S(1)} %get-tuple-element.108), channel_id=1, source_target_pairs={{0,4},{4,0},{1,5},{5,1},{2,6},{6,2},{3,7},{7,3},{8,12},{12,8},{9,1... | collective-permute-start | bytes 393224 | tf_op jit(solution)/shard_map/ppermute | solution.py:318
  54.7 5.8 %collective-permute-start.17 = (f32[1,128,256]{2,1,0:T(8,128)S(1)}, f32[1,128,256]{2,1,0:T(8,128)S(1)}, u32[]{:S(2)}, u32[]{:S(2)}) collective-permute-start(f32[1,128,256]{2,1,0:T(8,128)S(1)} %get-tuple-element.107), channel_id=1, source_target_pairs={{0,6},{2,4},{4,2},{6,0},{1,7},{3,5},{5,3},{7,1},{8,14},{10,12},{12... | collective-permute-start | bytes 393224 | tf_op jit(solution)/shard_map/ppermute | solution.py:318
  54.7 5.8 %collective-permute-start.18 = (f32[1,128,256]{2,1,0:T(8,128)S(1)}, f32[1,128,256]{2,1,0:T(8,128)S(1)}, u32[]{:S(2)}, u32[]{:S(2)}) collective-permute-start(f32[1,128,256]{2,1,0:T(8,128)S(1)} %slice.23), channel_id=1, source_target_pairs={{0,2},{2,0},{1,3},{3,1},{4,6},{6,4},{5,7},{7,5},{8,10},{10,8},{9,1... | collective-permute-start | bytes 393224 | tf_op jit(solution)/shard_map/ppermute | solution.py:318
  (2 other events, 4.1 us)

commit v18 on v15

--- a/solution.py
+++ b/solution.py
@@ -206,47 +206,50 @@
     return list(outs[:count]), list(outs[count:])
 
 
-def project_kernel(where, keep, other, other_2, own, near, *refs):
-    mine, theirs, whole = refs[-3:]
-    far = whole.shape[0]
-    direct, forwarded = refs[:far], refs[far:-3]
+def project_kernel(counts, where, keep, other, other_2, *refs):
+    parts = []
+    for count in counts:
+        parts.append(refs[:count])
+        refs = refs[count:]
+    near, direct, forwarded, before = parts
+    mine, theirs = refs[:2]
     plane = where[3]
-    count, extra = direct[0].shape[0], whole.shape[1] - direct[0].shape[0]
+    weights = list(enumerate(near))
+    for i, piece in enumerate(direct):
+        count, rows = piece.shape[0], refs[2].shape[1]
+        whole = refs[2].at[i]
+        whole[pl.ds(pl.multiple_of(plane * (rows - count), 16), count), :] = piece[...]
+        whole[pl.ds(pl.multiple_of((1 - plane) * count, 16), rows - count), :] = forwarded[0][i]
+        weights.append((2 + i, whole))
     total = None
-    for j in range(2 + far):
-        if j == 0:
-            weight = own[...]
-        elif j == 1:
-            weight = near[...]
-        else:
-            piece = whole.at[j - 2]
-            piece[pl.ds(pl.multiple_of(plane * extra, 16), count), :] = direct[j - 2][...]
-            rest = forwarded[0][j - 2] if len(forwarded) == 1 else forwarded[j - 2][...]
-            piece[pl.ds(pl.multiple_of((1 - plane) * count, 16), extra), :] = rest
-            weight = piece[...]
+    if before:
+        total = jnp.concatenate([ref[i] for ref in before for i in range(2)], axis=0)
+    for j, weight in weights:
         place = where[0] ^ j
         left = jnp.concatenate([keep[0, place], keep[1, place], other[place], other_2[place]], axis=0)
-        product = jnp.dot(left, weight, preferred_element_type=jnp.float32)
+        product = jnp.dot(left, weight[...], preferred_element_type=jnp.float32)
         total = product if total is None else total + product
     for i in range(2):
         mine[i] = total[i * ROWS : (i + 1) * ROWS]
         theirs[i] = total[(2 + i) * ROWS : (3 + i) * ROWS]
 
 
-def project(where, rows_of_x, own, near, direct, forwarded):
-    width = own.shape[1]
+def project(where, rows_of_x, near=(), direct=(), forwarded=(), before=()):
+    width = (near or direct)[0].shape[1]
     out = jax.ShapeDtypeStruct((2, ROWS, width), jnp.float32)
+    scratch = []
+    if direct:
+        rows = direct[0].shape[0] + forwarded[0].shape[1]
+        scratch.append(pltpu.VMEM((len(direct), rows, width), jnp.bfloat16))
+    operands = [near, direct, forwarded, before]
     return on_chip(
-        project_kernel,
+        functools.partial(project_kernel, [len(part) for part in operands]),
         "project",
         [out, out],
         where,
         *rows_of_x,
-        own,
-        near,
-        *direct,
-        *forwarded,
-        scratch=[pltpu.VMEM((len(direct), own.shape[0], width), jnp.bfloat16)],
+        *[array for part in operands for array in part],
+        scratch=scratch,
     )
 
 
@@ -343,8 +346,8 @@
     def send(far):
         return [xor_swap(far, "z", j) for j in range(2, steps)]
 
-    def forward(i):
-        return [xor_swap(jnp.stack(sent[i]), "blk", 1)]
+    def forward(stacked):
+        return [xor_swap(stacked, "blk", 1)]
 
     sent = [send(far[0])]
     near = [xor_swap(whole[0], "z", 1)]
@@ -367,26 +370,25 @@
     sent.append(send(far[1]))
     near.append(xor_swap(whole[1], "z", 1))
     sent[0], caches = tie((sent[0], caches))
-    forwarded = [forward(0)]
+    forwarded = [forward(jnp.stack(sent[0]))]
     state, other = tie((state, other))
     rows_of_x = [keep, other, xor_swap(other, "core", 1)]
     for stride in range(1, cycle):
         state = prompt_attention(infos[stride], query, caches[stride], state, 0, KVH)
 
-    def sums(i):
-        return project(where, rows_of_x, whole[i], near[i], sent[i], forwarded[i])
-
     def owners(mine, theirs):
         there = [xor_swap(theirs[1:], ("y", "core"), 3), xor_swap(mine[1:], "core", 1)]
         return xor_swap(theirs[:1], "y", 1), there
 
     forwarded[0], state = tie((forwarded[0], state))
-    mine_0, theirs_0 = sums(0)
+    mine_0, theirs_0 = project(where, rows_of_x, [whole[0], near[0]], sent[0], forwarded[0])
     sent[1], mine_0 = tie((sent[1], mine_0))
-    forwarded.append(forward(1))
+    stacked, mine_0, theirs_0 = tie((jnp.stack(sent[1]), mine_0, theirs_0))
+    forwarded.append(forward(stacked))
     here_0, there_0 = owners(mine_0, theirs_0)
-    forwarded[1], mine_0 = tie((forwarded[1], mine_0))
-    mine_1, theirs_1 = sums(1)
+    early = project(where, rows_of_x, [whole[1], near[1]])
+    forwarded[1], early = tie((forwarded[1], early))
+    mine_1, theirs_1 = project(where, rows_of_x, (), sent[1], forwarded[1], early)
     here_0, there_0, mine_1, theirs_1 = tie((here_0, there_0, mine_1, theirs_1))
     here_1, there_1 = owners(mine_1, theirs_1)
     info = jnp.concatenate([resp_lengths[0], core[None]]).astype(jnp.int32)

time: 60.8 us -> 62.2 us (1.023)
  waiting for transfers between devices: 10.4 us -> 14.5 us
  starting transfers between devices: 24.1 us -> 21.2 us
  Pallas kernels: 22.8 us -> 23.6 us
    ppermute x18, waiting for transfers between devices: 10.3 us -> 14.2 us  [xor_swap(): lax.ppermute(array, axis, [(i, i ^ by) for i in range(lax.axis_size(axis))])]
    ppermute x18, starting transfers between devices: 21.2 us -> 18.3 us  [xor_swap(): lax.ppermute(array, axis, [(i, i ^ by) for i in range(lax.axis_size(axis))])]
    pallas_call x5 -> x6, Pallas kernels: 5.81 us -> 6.57 us  [on_chip(): pl.pallas_call(kernel, in_specs=[SMEM] + [VMEM] * len(operands), out_spec...]
  transfers between devices with their start and end apart: 19 -> 19, of which waited for: 7 -> 8; matrix products, arithmetic and copies ran while one was open for 1% -> 1% of each run, Pallas kernels for 34% -> 34%
where the time goes in v18:
time: 62.2 us; the launch traced here: 62 us
  Pallas kernels  23.6 us (38%)
  starting transfers between devices  21.2 us (34%)
  waiting for transfers between devices  14.5 us (23%)
  local copies, waits for them, and re-layouts  1.39 us (2%)
  between operations  1.05 us (2%)
    ppermute x18, starting transfers between devices, xor_swap(): lax.ppermute(array, axis, [(i, i ^ by) for i in range(lax.axis_size(axis))])  18.3 us
    ppermute x18, waiting for transfers between devices, xor_swap(): lax.ppermute(array, axis, [(i, i ^ by) for i in range(lax.axis_size(axis))])  14.2 us
    pallas_call x2, Pallas kernels, prompt_attention(): pl.pallas_call(functools.partial(prompt_kernel, first), grid_spec=pltpu.P...  11.7 us
    pallas_call x6, Pallas kernels, on_chip(): pl.pallas_call(kernel, in_specs=[SMEM] + [VMEM] * len(operands), out_spec...  6.57 us
    pallas_call x2, Pallas kernels, final_attention(): pl.pallas_call(functools.partial(final_kernel, chunk, offset), in_specs=s...  4.69 us
    ppermute x1, starting transfers between devices, per_device(): lax.ppermute(caches[-1], 'blk', [(i, (i + 1) % cycle) for i in range(cycl...  2.94 us
  transfers between devices with their start and end apart: 19, of which 8 were waited for; matrix products, arithmetic and copies ran while one was open for 1% of the time, Pallas kernels for 34%

profile of v18, /device:TPU:0, one launch (start us, length us, event | category | flops | bytes accessed | tf_op | source)
XLA Modules:
  0.0 62.0 jit_solution(749594459471853434)
XLA Ops:
  0.6 2.9 %collective-permute-start.4 = (bf16[512,1024]{1,0:T(8,128)(2,1)}, bf16[512,1024]{1,0:T(8,128)(2,1)}, u32[]{:S(2)}, u32[]{:S(2)}) collective-permute-start(bf16[512,1024]{1,0:T(8,128)(2,1)} %bitcast.28), channel_id=1, source_target_pairs={{0,1},{1,0},{2,3},{3,2},{4,5},{5,4},{6,7},{7,6},{8,9},{9,8},{10,11... | collective-permute-start | bytes 3145736 | tf_op jit(solution)/shard_map/ppermute | solution.py:338
  3.5 1.1 %copy-done.2 = bf16[320,1024]{1,0:T(8,128)(2,1)S(1)} copy-done((bf16[320,1024]{1,0:T(8,128)(2,1)S(1)}, bf16[320,1024]{1,0:T(8,128)(2,1)}, u32[]{:S(2)}) %copy-start.2) | copy-done | bytes 655384
  6.6 3.7 %collective-permute-start.3 = (bf16[320,256]{1,0:T(8,128)(2,1)S(1)}, bf16[320,256]{1,0:T(8,128)(2,1)S(1)}, u32[]{:S(2)}, u32[]{:S(2)}) collective-permute-start(bf16[320,256]{1,0:T(8,128)(2,1)S(1)} %far_first.1), channel_id=1, source_target_pairs={{0,24},{8,16},{16,8},{24,0},{1,25},{9,17},{17,9},{25,1},{2,26},{10... | collective-permute-start | bytes 491528 | tf_op jit(solution)/shard_map/ppermute | solution.py:319
  10.9 0.8 %collective-permute-start.10 = (bf16[640,256]{1,0:T(8,128)(2,1)S(1)}, bf16[640,256]{1,0:T(8,128)(2,1)S(1)}, u32[]{:S(2)}, u32[]{:S(2)}) collective-permute-start(bf16[640,256]{1,0:T(8,128)(2,1)S(1)} %get-tuple-element.66.refs_0_), channel_id=1, source_target_pairs={{0,8},{8,0},{16,24},{24,16},{1,9},{9,1},{17,25},{25,17},{2,10},{10... | collective-permute-start | bytes 983048 | tf_op jit(solution)/shard_map/ppermute | solution.py:319
  12.1 1.6 %pack_rows.1 = (bf16[2,4,128,640]{3,2,1,0:T(8,128)(2,1)S(1)}, bf16[4,128,640]{2,1,0:T(8,128)(2,1)S(1)}) custom-call(s32[4]{0:T(128)S(1)} %pad_add_fusion.1.where, bf16[128,5120]{1,0:T(8,128)(2,1)S(1)} %bitcast.21, bf16[128,5120]{1,0:T(8,128)(2,1)} %collective-permute-done.1.got_ref), custom_call_target="tpu_custom_call" | custom-call | flops 1024 | bytes 1024 | tf_op jit(solution)/shard_map/pack_rows/pallas_call | solution.py:117
  13.7 1.6 %collective-permute-start.6 = (bf16[4,128,640]{2,1,0:T(8,128)(2,1)S(1)}, bf16[4,128,640]{2,1,0:T(8,128)(2,1)S(1)}, u32[]{:S(2)}, u32[]{:S(2)}) collective-permute-start(bf16[4,128,640]{2,1,0:T(8,128)(2,1)S(1)} %get-tuple-element.69), channel_id=1, source_target_pairs={{0,4},{4,0},{1,5},{5,1},{2,6},{6,2},{3,7},{7,3},{8,12},{12,8},{9,1... | collective-permute-start | bytes 1966088 | tf_op jit(solution)/shard_map/ppermute | solution.py:319
  15.3 5.4 %prompt_attention.2 = (f32[128,4096]{1,0:T(8,128)S(1)}, f32[8,4096]{1,0:T(8,128)S(1)}) custom-call(s32[4]{0:T(128)S(1)} %get-tuple-element.121.info, bf16[128,4096]{1,0:T(8,128)(2,1)S(1)} %bitcast.16, bf16[512,1024]{1,0:T(8,128)(2,1)S(1)} %bitcast.29, bf16[512,1024]{1,0:T(8,128)(2,1)S(1)} %bitcast.30), custom_call_target="tpu_custom_call" | custom-call | flops 17179869184 | bytes 1024 | tf_op jit(solution)/shard_map/prompt_attention/pallas_call | solution.py:94
  20.8 3.4 %collective-permute-done.2.refs_2_ = bf16[320,256]{1,0:T(8,128)(2,1)S(1)} collective-permute-done((bf16[320,256]{1,0:T(8,128)(2,1)S(1)}, bf16[320,256]{1,0:T(8,128)(2,1)S(1)}, u32[]{:S(2)}, u32[]{:S(2)}) %collective-permute-start.2) | collective-permute-done | bytes 163872 | tf_op jit(solution)/shard_map/ppermute | solution.py:319
  24.2 2.7 %collective-permute-start.8 = (bf16[320,256]{1,0:T(8,128)(2,1)S(1)}, bf16[320,256]{1,0:T(8,128)(2,1)S(1)}, u32[]{:S(2)}, u32[]{:S(2)}) collective-permute-start(bf16[320,256]{1,0:T(8,128)(2,1)S(1)} %get-tuple-element.90), channel_id=1, source_target_pairs={{0,24},{8,16},{16,8},{24,0},{1,25},{9,17},{17,9},{25,1},{2,26},{10... | collective-permute-start | bytes 491528 | tf_op jit(solution)/shard_map/ppermute | solution.py:319
  27.2 1.8 %collective-permute-start.5 = (bf16[2,320,256]{2,1,0:T(8,128)(2,1)S(1)}, bf16[2,320,256]{2,1,0:T(8,128)(2,1)S(1)}, u32[]{:S(2)}, u32[]{:S(2)}) collective-permute-start(bf16[2,320,256]{2,1,0:T(8,128)(2,1)S(1)} %pad_maximum_fusion), channel_id=1, source_target_pairs={{0,1},{1,0},{2,3},{3,2},{4,5},{5,4},{6,7},{7,6},{8,9},{9,8},{10,11... | collective-permute-start | bytes 983048 | tf_op jit(solution)/shard_map/ppermute | solution.py:319
  29.4 6.3 %prompt_attention.3 = (f32[128,4096]{1,0:T(8,128)S(1)}, f32[8,4096]{1,0:T(8,128)S(1)}) custom-call(s32[4]{0:T(128)S(1)} %get-tuple-element.122.info, bf16[128,4096]{1,0:T(8,128)(2,1)S(1)} %bitcast.17, bf16[512,1024]{1,0:T(8,128)(2,1)} %collective-permute-done.4.k_ref.v_ref, bf16[512,1024]{1,0:T(8,128)(2,1)} %collective-permute-done.4.k_ref.v_ref, ...), custom_call_target="tpu_custom_call" | custom-call | flops 8589934592 | bytes 1024 | tf_op jit(solution)/shard_map/prompt_attention/pallas_call | solution.py:94
  36.4 1.5 %collective-permute-start.15 = (bf16[640,256]{1,0:T(8,128)(2,1)S(1)}, bf16[640,256]{1,0:T(8,128)(2,1)S(1)}, u32[]{:S(2)}, u32[]{:S(2)}) collective-permute-start(bf16[640,256]{1,0:T(8,128)(2,1)S(1)} %get-tuple-element.102.refs_0_), channel_id=1, source_target_pairs={{0,8},{8,0},{16,24},{24,16},{1,9},{9,1},{17,25},{25,17},{2,10},{10... | collective-permute-start | bytes 983048 | tf_op jit(solution)/shard_map/ppermute | solution.py:319
  37.9 1.5 %project.3 = (f32[2,128,256]{2,1,0:T(8,128)S(1)}, f32[2,128,256]{2,1,0:T(8,128)S(1)}) custom-call(s32[4]{0:T(128)S(1)} %pad_add_fusion.1.where, bf16[2,4,128,640]{3,2,1,0:T(8,128)(2,1)S(1)} %get-tuple-element.91.keep, bf16[4,128,640]{2,1,0:T(8,128)(2,1)S(1)} %collective-permute-done.6.other, bf16[4,128,640]{2,1,0:T(8,128)(2,1)S(1)} %collective-permute-done.9.other_2, ...), custom_call_target="tpu_custom_call" | custom-call | flops 1024 | bytes 1024 | tf_op jit(solution)/shard_map/project/pallas_call | solution.py:117
  39.6 1.6 %collective-permute-start.14 = (bf16[2,320,256]{2,1,0:T(8,128)(2,1)S(1)}, bf16[2,320,256]{2,1,0:T(8,128)(2,1)S(1)}, u32[]{:S(2)}, u32[]{:S(2)}) collective-permute-start(bf16[2,320,256]{2,1,0:T(8,128)(2,1)S(1)} %pad_maximum_fusion.1), channel_id=1, source_target_pairs={{0,1},{1,0},{2,3},{3,2},{4,5},{5,4},{6,7},{7,6},{8,9},{9,8},{10,11... | collective-permute-start | bytes 983048 | tf_op jit(solution)/shard_map/ppermute | solution.py:319
  41.2 1.4 %collective-permute-start.12 = (f32[1,128,256]{2,1,0:T(8,128)S(1)}, f32[1,128,256]{2,1,0:T(8,128)S(1)}, u32[]{:S(2)}, u32[]{:S(2)}) collective-permute-start(f32[1,128,256]{2,1,0:T(8,128)S(1)} %get-tuple-element.119), channel_id=1, source_target_pairs={{0,6},{2,4},{4,2},{6,0},{1,7},{3,5},{5,3},{7,1},{8,14},{10,12},{12... | collective-permute-start | bytes 393224 | tf_op jit(solution)/shard_map/ppermute | solution.py:319
  43.0 3.3 %collective-permute-done.15.refs_1_ = bf16[640,256]{1,0:T(8,128)(2,1)S(1)} collective-permute-done((bf16[640,256]{1,0:T(8,128)(2,1)S(1)}, bf16[640,256]{1,0:T(8,128)(2,1)S(1)}, u32[]{:S(2)}, u32[]{:S(2)}) %collective-permute-start.15) | collective-permute-done | bytes 327712 | tf_op jit(solution)/shard_map/ppermute | solution.py:319
  46.3 1.1 %project.4 = (f32[2,128,256]{2,1,0:T(8,128)S(1)}, f32[2,128,256]{2,1,0:T(8,128)S(1)}) custom-call(s32[4]{0:T(128)S(1)} %pad_add_fusion.1.where, bf16[2,4,128,640]{3,2,1,0:T(8,128)(2,1)S(1)} %get-tuple-element.91.keep, bf16[4,128,640]{2,1,0:T(8,128)(2,1)S(1)} %collective-permute-done.6.other, bf16[4,128,640]{2,1,0:T(8,128)(2,1)S(1)} %collective-permute-done.9.other_2, ...), custom_call_target="tpu_custom_call" | custom-call | flops 1024 | bytes 1024 | tf_op jit(solution)/shard_map/project/pallas_call | solution.py:117
  47.4 2.3 %collective-permute-done.14.refs_2_ = bf16[2,320,256]{2,1,0:T(8,128)(2,1)S(1)} collective-permute-done((bf16[2,320,256]{2,1,0:T(8,128)(2,1)S(1)}, bf16[2,320,256]{2,1,0:T(8,128)(2,1)S(1)}, u32[]{:S(2)}, u32[]{:S(2)}) %collective-permute-start.14) | collective-permute-done | bytes 327712 | tf_op jit(solution)/shard_map/ppermute | solution.py:319
  49.7 1.1 %project.5 = (f32[2,128,256]{2,1,0:T(8,128)S(1)}, f32[2,128,256]{2,1,0:T(8,128)S(1)}) custom-call(s32[4]{0:T(128)S(1)} %pad_add_fusion.1.where, bf16[2,4,128,640]{3,2,1,0:T(8,128)(2,1)S(1)} %get-tuple-element.91.keep, bf16[4,128,640]{2,1,0:T(8,128)(2,1)S(1)} %collective-permute-done.6.other, bf16[4,128,640]{2,1,0:T(8,128)(2,1)S(1)} %collective-permute-done.9.other_2, ...), custom_call_target="tpu_custom_call" | custom-call | flops 1024 | bytes 1024 | tf_op jit(solution)/shard_map/project/pallas_call | solution.py:117
  51.0 1.6 %collective-permute-start.17 = (f32[1,128,256]{2,1,0:T(8,128)S(1)}, f32[1,128,256]{2,1,0:T(8,128)S(1)}, u32[]{:S(2)}, u32[]{:S(2)}) collective-permute-start(f32[1,128,256]{2,1,0:T(8,128)S(1)} %get-tuple-element.117), channel_id=1, source_target_pairs={{0,6},{2,4},{4,2},{6,0},{1,7},{3,5},{5,3},{7,1},{8,14},{10,12},{12... | collective-permute-start | bytes 393224 | tf_op jit(solution)/shard_map/ppermute | solution.py:319
  53.2 2.3 %final_attention.2.refs_0_ = bf16[128,4096]{1,0:T(8,128)(2,1)} custom-call(s32[3]{0:T(128)S(1)} %pad_add_fusion.info, f32[1,128]{1,0:T(1,128)S(1)} %bitcast.26, bf16[128,4096]{1,0:T(8,128)(2,1)S(1)} %bitcast.18, f32[128,4096]{1,0:T(8,128)S(1)} %get-tuple-element.88.acc_ref, f32[8,4096]{1,0:T(8,128)S(1)} %get-tuple-element.89.ml_ref, ...), custom_call_target="tpu_custom_call" | custom-call | flops 1024 | bytes 1024 | tf_op jit(solution)/shard_map/final_attention/pallas_call | solution.py:305
  55.6 0.9 %collective-permute-done.17.there = f32[1,128,256]{2,1,0:T(8,128)S(1)} collective-permute-done((f32[1,128,256]{2,1,0:T(8,128)S(1)}, f32[1,128,256]{2,1,0:T(8,128)S(1)}, u32[]{:S(2)}, u32[]{:S(2)}) %collective-permute-start.17) | collective-permute-done | bytes 131104 | tf_op jit(solution)/shard_map/ppermute | solution.py:319
  56.5 3.2 %collective-permute-done.16.theirs = f32[1,128,256]{2,1,0:T(8,128)S(1)} collective-permute-done((f32[1,128,256]{2,1,0:T(8,128)S(1)}, f32[1,128,256]{2,1,0:T(8,128)S(1)}, u32[]{:S(2)}, u32[]{:S(2)}) %collective-permute-start.16) | collective-permute-done | bytes 131104 | tf_op jit(solution)/shard_map/ppermute | solution.py:319
  59.7 2.3 %final_attention.3 = bf16[128,4096]{1,0:T(8,128)(2,1)} custom-call(s32[3]{0:T(128)S(1)} %pad_add_fusion.info, f32[1,128]{1,0:T(1,128)S(1)} %bitcast.27, bf16[128,4096]{1,0:T(8,128)(2,1)S(1)} %bitcast.19, f32[128,4096]{1,0:T(8,128)S(1)} %get-tuple-element.88.acc_ref, f32[8,4096]{1,0:T(8,128)S(1)} %get-tuple-element.89.ml_ref, ...), custom_call_target="tpu_custom_call", output_to_operand_aliasing={{}: (9, {})} | custom-call | flops 1024 | bytes 1024 | tf_op jit(solution)/shard_map/final_attention/pallas_call | solution.py:305
  (49 shorter events, 5.5 us)
Async XLA Ops:
  0.0 12.0 %collective-permute-start.1 = (bf16[128,5120]{1,0:T(8,128)(2,1)}, bf16[128,5120]{1,0:T(8,128)(2,1)}, u32[]{:S(2)}, u32[]{:S(2)}) collective-permute-start(bf16[128,5120]{1,0:T(8,128)(2,1)} %bitcast.20), channel_id=1, source_target_pairs={{0,2},{2,0},{1,3},{3,1},{4,6},{6,4},{5,7},{7,5},{8,10},{10,8},{9,1... | collective-permute-start | bytes 3932168 | tf_op jit(solution)/shard_map/ppermute | solution.py:319
  0.5 5.6 %collective-permute-start = (bf16[320,1024]{1,0:T(8,128)(2,1)}, bf16[320,1024]{1,0:T(8,128)(2,1)S(1)}, u32[]{:S(2)}, u32[]{:S(2)}) collective-permute-start(bf16[320,1024]{1,0:T(8,128)(2,1)} %weight_ref.1), channel_id=1, source_target_pairs={{0,2},{2,0},{1,3},{3,1},{4,6},{6,4},{5,7},{7,5},{8,10},{10,8},{9,1... | collective-permute-start | bytes 1966088 | tf_op jit(solution)/shard_map/ppermute | solution.py:319
  0.6 26.6 %collective-permute-start.4 = (bf16[512,1024]{1,0:T(8,128)(2,1)}, bf16[512,1024]{1,0:T(8,128)(2,1)}, u32[]{:S(2)}, u32[]{:S(2)}) collective-permute-start(bf16[512,1024]{1,0:T(8,128)(2,1)} %bitcast.28), channel_id=1, source_target_pairs={{0,1},{1,0},{2,3},{3,2},{4,5},{5,4},{6,7},{7,6},{8,9},{9,8},{10,11... | collective-permute-start | bytes 3145736 | tf_op jit(solution)/shard_map/ppermute | solution.py:338
  5.2 6.5 %copy-start.5 = (s32[1,2,2]{2,1,0:T(2,128)S(1)}, s32[1,2,2]{2,1,0:T(2,128)}, u32[]{:S(2)}) copy-start(s32[1,2,2]{2,1,0:T(2,128)} %param.14) | copy-start | bytes 52
  5.2 6.8 %copy-start.1 = (bf16[1,128,5120]{2,1,0:T(8,128)(2,1)S(1)}, bf16[1,128,5120]{2,1,0:T(8,128)(2,1)}, u32[]{:S(2)}) copy-start(bf16[1,128,5120]{2,1,0:T(8,128)(2,1)} %param.8) | copy-start | bytes 3932164
  6.6 14.1 %collective-permute-start.3 = (bf16[320,256]{1,0:T(8,128)(2,1)S(1)}, bf16[320,256]{1,0:T(8,128)(2,1)S(1)}, u32[]{:S(2)}, u32[]{:S(2)}) collective-permute-start(bf16[320,256]{1,0:T(8,128)(2,1)S(1)} %far_first.1), channel_id=1, source_target_pairs={{0,24},{8,16},{16,8},{24,0},{1,25},{9,17},{17,9},{25,1},{2,26},{10... | collective-permute-start | bytes 491528 | tf_op jit(solution)/shard_map/ppermute | solution.py:319
  10.3 13.9 %collective-permute-start.2 = (bf16[320,256]{1,0:T(8,128)(2,1)S(1)}, bf16[320,256]{1,0:T(8,128)(2,1)S(1)}, u32[]{:S(2)}, u32[]{:S(2)}) collective-permute-start(bf16[320,256]{1,0:T(8,128)(2,1)S(1)} %far_first.1), channel_id=1, source_target_pairs={{0,16},{8,24},{16,0},{24,8},{1,17},{9,25},{17,1},{25,9},{2,18},{10... | collective-permute-start | bytes 491528 | tf_op jit(solution)/shard_map/ppermute | solution.py:319
  10.9 27.0 %collective-permute-start.10 = (bf16[640,256]{1,0:T(8,128)(2,1)S(1)}, bf16[640,256]{1,0:T(8,128)(2,1)S(1)}, u32[]{:S(2)}, u32[]{:S(2)}) collective-permute-start(bf16[640,256]{1,0:T(8,128)(2,1)S(1)} %get-tuple-element.66.refs_0_), channel_id=1, source_target_pairs={{0,8},{8,0},{16,24},{24,16},{1,9},{9,1},{17,25},{25,17},{2,10},{10... | collective-permute-start | bytes 983048 | tf_op jit(solution)/shard_map/ppermute | solution.py:319
  12.0 3.3 %copy-start = (bf16[1,128,4096]{2,1,0:T(8,128)(2,1)S(1)}, bf16[1,128,4096]{2,1,0:T(8,128)(2,1)}, u32[]{:S(2)}) copy-start(bf16[1,128,4096]{2,1,0:T(8,128)(2,1)} %param.9) | copy-start | bytes 3145732
  13.7 15.7 %collective-permute-start.6 = (bf16[4,128,640]{2,1,0:T(8,128)(2,1)S(1)}, bf16[4,128,640]{2,1,0:T(8,128)(2,1)S(1)}, u32[]{:S(2)}, u32[]{:S(2)}) collective-permute-start(bf16[4,128,640]{2,1,0:T(8,128)(2,1)S(1)} %get-tuple-element.69), channel_id=1, source_target_pairs={{0,4},{4,0},{1,5},{5,1},{2,6},{6,2},{3,7},{7,3},{8,12},{12,8},{9,1... | collective-permute-start | bytes 1966088 | tf_op jit(solution)/shard_map/ppermute | solution.py:319
  24.2 15.2 %collective-permute-start.8 = (bf16[320,256]{1,0:T(8,128)(2,1)S(1)}, bf16[320,256]{1,0:T(8,128)(2,1)S(1)}, u32[]{:S(2)}, u32[]{:S(2)}) collective-permute-start(bf16[320,256]{1,0:T(8,128)(2,1)S(1)} %get-tuple-element.90), channel_id=1, source_target_pairs={{0,24},{8,16},{16,8},{24,0},{1,25},{9,17},{17,9},{25,1},{2,26},{10... | collective-permute-start | bytes 491528 | tf_op jit(solution)/shard_map/ppermute | solution.py:319
  26.8 12.6 %collective-permute-start.7 = (bf16[320,256]{1,0:T(8,128)(2,1)S(1)}, bf16[320,256]{1,0:T(8,128)(2,1)S(1)}, u32[]{:S(2)}, u32[]{:S(2)}) collective-permute-start(bf16[320,256]{1,0:T(8,128)(2,1)S(1)} %get-tuple-element.90), channel_id=1, source_target_pairs={{0,16},{8,24},{16,0},{24,8},{1,17},{9,25},{17,1},{25,9},{2,18},{10... | collective-permute-start | bytes 491528 | tf_op jit(solution)/shard_map/ppermute | solution.py:319
  27.2 9.1 %collective-permute-start.5 = (bf16[2,320,256]{2,1,0:T(8,128)(2,1)S(1)}, bf16[2,320,256]{2,1,0:T(8,128)(2,1)S(1)}, u32[]{:S(2)}, u32[]{:S(2)}) collective-permute-start(bf16[2,320,256]{2,1,0:T(8,128)(2,1)S(1)} %pad_maximum_fusion), channel_id=1, source_target_pairs={{0,1},{1,0},{2,3},{3,2},{4,5},{5,4},{6,7},{7,6},{8,9},{9,8},{10,11... | collective-permute-start | bytes 983048 | tf_op jit(solution)/shard_map/ppermute | solution.py:319
  29.4 8.4 %collective-permute-start.9 = (bf16[4,128,640]{2,1,0:T(8,128)(2,1)S(1)}, bf16[4,128,640]{2,1,0:T(8,128)(2,1)S(1)}, u32[]{:S(2)}, u32[]{:S(2)}) collective-permute-start(bf16[4,128,640]{2,1,0:T(8,128)(2,1)S(1)} %collective-permute-done.6.other), channel_id=1, source_target_pairs={{0,2},{2,0},{1,3},{3,1},{4,6},{6,4},{5,7},{7,5},{8,10},{10,8},{9,1... | collective-permute-start | bytes 1966088 | tf_op jit(solution)/shard_map/ppermute | solution.py:319
  36.4 10.0 %collective-permute-start.15 = (bf16[640,256]{1,0:T(8,128)(2,1)S(1)}, bf16[640,256]{1,0:T(8,128)(2,1)S(1)}, u32[]{:S(2)}, u32[]{:S(2)}) collective-permute-start(bf16[640,256]{1,0:T(8,128)(2,1)S(1)} %get-tuple-element.102.refs_0_), channel_id=1, source_target_pairs={{0,8},{8,0},{16,24},{24,16},{1,9},{9,1},{17,25},{25,17},{2,10},{10... | collective-permute-start | bytes 983048 | tf_op jit(solution)/shard_map/ppermute | solution.py:319
  39.5 11.4 %collective-permute-start.13 = (f32[1,128,256]{2,1,0:T(8,128)S(1)}, f32[1,128,256]{2,1,0:T(8,128)S(1)}, u32[]{:S(2)}, u32[]{:S(2)}) collective-permute-start(f32[1,128,256]{2,1,0:T(8,128)S(1)} %slice.20), channel_id=1, source_target_pairs={{0,2},{2,0},{1,3},{3,1},{4,6},{6,4},{5,7},{7,5},{8,10},{10,8},{9,1... | collective-permute-start | bytes 393224 | tf_op jit(solution)/shard_map/ppermute | solution.py:319
  39.6 10.1 %collective-permute-start.14 = (bf16[2,320,256]{2,1,0:T(8,128)(2,1)S(1)}, bf16[2,320,256]{2,1,0:T(8,128)(2,1)S(1)}, u32[]{:S(2)}, u32[]{:S(2)}) collective-permute-start(bf16[2,320,256]{2,1,0:T(8,128)(2,1)S(1)} %pad_maximum_fusion.1), channel_id=1, source_target_pairs={{0,1},{1,0},{2,3},{3,2},{4,5},{5,4},{6,7},{7,6},{8,9},{9,8},{10,11... | collective-permute-start | bytes 983048 | tf_op jit(solution)/shard_map/ppermute | solution.py:319
  41.2 9.7 %collective-permute-start.12 = (f32[1,128,256]{2,1,0:T(8,128)S(1)}, f32[1,128,256]{2,1,0:T(8,128)S(1)}, u32[]{:S(2)}, u32[]{:S(2)}) collective-permute-start(f32[1,128,256]{2,1,0:T(8,128)S(1)} %get-tuple-element.119), channel_id=1, source_target_pairs={{0,6},{2,4},{4,2},{6,0},{1,7},{3,5},{5,3},{7,1},{8,14},{10,12},{12... | collective-permute-start | bytes 393224 | tf_op jit(solution)/shard_map/ppermute | solution.py:319
  42.5 8.4 %collective-permute-start.11 = (f32[1,128,256]{2,1,0:T(8,128)S(1)}, f32[1,128,256]{2,1,0:T(8,128)S(1)}, u32[]{:S(2)}, u32[]{:S(2)}) collective-permute-start(f32[1,128,256]{2,1,0:T(8,128)S(1)} %get-tuple-element.120), channel_id=1, source_target_pairs={{0,4},{4,0},{1,5},{5,1},{2,6},{6,2},{3,7},{7,3},{8,12},{12,8},{9,1... | collective-permute-start | bytes 393224 | tf_op jit(solution)/shard_map/ppermute | solution.py:319
  49.7 3.5 %copy-start.6 = (s32[1,2]{1,0:T(1,128)S(1)}, s32[1,2]{1,0:T(1,128)}, u32[]{:S(2)}) copy-start(s32[1,2]{1,0:T(1,128)} %param.15) | copy-start | bytes 28
  49.7 3.5 %copy-start.3 = (f32[128]{0:T(128)S(1)}, f32[128]{0:T(128)}, u32[]{:S(2)}) copy-start(f32[128]{0:T(128)} %param.12) | copy-start | bytes 1540
  50.9 4.7 %collective-permute-start.18 = (f32[1,128,256]{2,1,0:T(8,128)S(1)}, f32[1,128,256]{2,1,0:T(8,128)S(1)}, u32[]{:S(2)}, u32[]{:S(2)}) collective-permute-start(f32[1,128,256]{2,1,0:T(8,128)S(1)} %slice.23), channel_id=1, source_target_pairs={{0,2},{2,0},{1,3},{3,1},{4,6},{6,4},{5,7},{7,5},{8,10},{10,8},{9,1... | collective-permute-start | bytes 393224 | tf_op jit(solution)/shard_map/ppermute | solution.py:319
  51.0 5.5 %collective-permute-start.17 = (f32[1,128,256]{2,1,0:T(8,128)S(1)}, f32[1,128,256]{2,1,0:T(8,128)S(1)}, u32[]{:S(2)}, u32[]{:S(2)}) collective-permute-start(f32[1,128,256]{2,1,0:T(8,128)S(1)} %get-tuple-element.117), channel_id=1, source_target_pairs={{0,6},{2,4},{4,2},{6,0},{1,7},{3,5},{5,3},{7,1},{8,14},{10,12},{12... | collective-permute-start | bytes 393224 | tf_op jit(solution)/shard_map/ppermute | solution.py:319
  52.7 7.0 %collective-permute-start.16 = (f32[1,128,256]{2,1,0:T(8,128)S(1)}, f32[1,128,256]{2,1,0:T(8,128)S(1)}, u32[]{:S(2)}, u32[]{:S(2)}) collective-permute-start(f32[1,128,256]{2,1,0:T(8,128)S(1)} %get-tuple-element.118), channel_id=1, source_target_pairs={{0,4},{4,0},{1,5},{5,1},{2,6},{6,2},{3,7},{7,3},{8,12},{12,8},{9,1... | collective-permute-start | bytes 393224 | tf_op jit(solution)/shard_map/ppermute | solution.py:319
  (2 other events, 4.3 us)
